TPU v7x, 32 devices: a whole 2x2x4 slice. The times are simulated.
32 devices in a mesh: dp: 2 (over y), ctx: 4 (over x, core), tp: 4 (over z).
Axes of the slice: x: 2, y: 2, z: 4, core: 2. Of those that a mesh axis runs over, the one named last changes fastest.
Arguments:
- tokens: bfloat16 [2, 2, 2, 2048, 1152], P(None, 'dp', None, 'ctx'), may hold values from -6 to 6
- segments: int32 [2, 2, 2, 2048], P(None, 'dp', None, 'ctx'), may hold values from 0 to 66, as said below
- cotangent: bfloat16 [2, 2, 2, 2048, 1152], P(None, 'dp', None, 'ctx'), may hold values from -6 to 6
- w_query: bfloat16 [1152, 1024], P(('dp', 'ctx'), 'tp'), may hold values from -0.1875 to 0.1875
- w_key: bfloat16 [1152, 256], P(('dp', 'ctx')), may hold values from -0.1875 to 0.1875
- w_value: bfloat16 [1152, 256], P(('dp', 'ctx')), may hold values from -0.1875 to 0.1875
- w_out: bfloat16 [1024, 1152], P('tp', ('dp', 'ctx')), may hold values from -0.375 to 0.375
- w_gate: bfloat16 [1152, 6912], P(('dp', 'ctx'), 'tp'), may hold values from -0.1875 to 0.1875
- w_up: bfloat16 [1152, 6912], P(('dp', 'ctx'), 'tp'), may hold values from -0.1875 to 0.1875
- w_down: bfloat16 [6912, 1152], P('tp', ('dp', 'ctx')), may hold values from -0.078125 to 0.078125
- g_input: bfloat16 [1152], P(('dp', 'ctx')), may hold values from -0.59765625 to 0.59765625
- g_post_attn: bfloat16 [1152], P(('dp', 'ctx')), may hold values from -0.59765625 to 0.59765625
- g_pre_ffn: bfloat16 [1152], P(('dp', 'ctx')), may hold values from -0.59765625 to 0.59765625
- g_post_ffn: bfloat16 [1152], P(('dp', 'ctx')), may hold values from -0.59765625 to 0.59765625
- g_query: bfloat16 [256], P(('dp', 'ctx')), may hold values from -0.59765625 to 0.59765625
- g_key: bfloat16 [256], P(('dp', 'ctx')), may hold values from -0.59765625 to 0.59765625
Outputs:
- output: bfloat16 [2, 2, 2, 2048, 1152], P(None, 'dp', None, 'ctx')
- d_tokens: float32 [2, 2, 2, 2048, 1152], P(None, 'dp', None, 'ctx')
- grad_w_query: float32 [1152, 1024], P(('dp', 'ctx'), 'tp')
- grad_w_key: float32 [1152, 256], P(('dp', 'ctx'))
- grad_w_value: float32 [1152, 256], P(('dp', 'ctx'))
- grad_w_out: float32 [1024, 1152], P('tp', ('dp', 'ctx'))
- grad_w_gate: float32 [1152, 6912], P(('dp', 'ctx'), 'tp')
- grad_w_up: float32 [1152, 6912], P(('dp', 'ctx'), 'tp')
- grad_w_down: float32 [6912, 1152], P('tp', ('dp', 'ctx'))
- grad_g_input: float32 [1152], P(('dp', 'ctx'))
- grad_g_post_attn: float32 [1152], P(('dp', 'ctx'))
- grad_g_pre_ffn: float32 [1152], P(('dp', 'ctx'))
- grad_g_post_ffn: float32 [1152], P(('dp', 'ctx'))
- grad_g_query: float32 [256], P(('dp', 'ctx'))
- grad_g_key: float32 [256], P(('dp', 'ctx'))
Inputs may be any that keep to these rules, and one draw needn't show every extreme that they name: `segments`: read in each sequence's true order, ids never fall before the padding; id 0 marks padding, which fills the last positions of every sequence; the last token before the padding has the largest id.
All inputs are finite; a program needn't handle non-finite values.
Results may differ from a plain program's by a relative error of at most 0.025.
Values may be sent and summed in bfloat16 or wider, within the bound.
A program may use at most 320 MiB of HBM per device.

v0:
```python
import jax
import jax.numpy as jnp
from jax import lax
from jax.sharding import PartitionSpec as P

EPS = 1e-06
THETA = 1000000.0
SCALE = 0.0625
NEGATIVE = -1e30


def angles(position, half_size, full_size):
    frequency = THETA ** (-2.0 * jnp.arange(half_size, dtype=jnp.float32) / full_size)
    turned = position[:, None] * frequency[None, :]
    return (jnp.cos(turned), jnp.sin(turned))


def rotate(tensor, cosine, sine_table):
    half_size = tensor.shape[-1] // 2
    first_half = tensor[..., :half_size]
    second_half = tensor[..., half_size:]
    return jnp.concatenate(
        [
            first_half * cosine - second_half * sine_table,
            second_half * cosine + first_half * sine_table,
        ],
        axis=-1,
    )


def norm_parts(values):
    scale_inv = lax.rsqrt(jnp.mean(values * values, axis=-1, keepdims=True) + EPS)
    return (values * scale_inv, scale_inv)


def norm_back(upstream, normalized, scale_inv, gain_vec):
    d_norm = upstream * (1.0 + gain_vec)
    d_values = scale_inv * (
        d_norm - normalized * jnp.mean(d_norm * normalized, axis=-1, keepdims=True)
    )
    d_gain = jnp.sum((upstream * normalized).reshape(-1, upstream.shape[-1]), axis=0)
    return (d_values, d_gain)


def matmul(left_side, right_side):
    return jnp.dot(left_side, right_side, preferred_element_type=jnp.float32)


def matmul_tn(left_side, right_side):
    return lax.dot_general(
        left_side, right_side, (((0,), (0,)), ((), ())), preferred_element_type=jnp.float32
    )


def matmul_nt(left_side, right_side):
    return lax.dot_general(
        left_side, right_side, (((1,), (1,)), ((), ())), preferred_element_type=jnp.float32
    )


def gelu_tanh(values):
    return jax.nn.gelu(values, approximate=True)


def shards(
    tokens,
    segments,
    cotangent,
    w_query,
    w_key,
    w_value,
    w_out,
    w_gate,
    w_up,
    w_down,
    g_input,
    g_post_attn,
    g_pre_ffn,
    g_post_ffn,
    g_query,
    g_key,
):
    batches = tokens.shape[0]
    seq_local = tokens.shape[1]
    block_len = tokens.shape[3]
    width = tokens.shape[4]
    head_size = w_key.shape[1]
    head_local = w_query.shape[1] // head_size
    seq_length = 2 * block_len * lax.axis_size("ctx")
    tok_rows = seq_local * 2 * block_len
    ctx_rank = lax.axis_index("ctx")
    offsets = ctx_rank * block_len + jnp.arange(block_len, dtype=jnp.int32)
    query_position = jnp.stack([offsets, seq_length - 1 - offsets], axis=0).reshape(2 * block_len)
    row_position = (
        jnp.broadcast_to(query_position, (seq_local, 2 * block_len))
        .reshape(tok_rows)
        .astype(jnp.float32)
    )
    cosine, sine_table = angles(row_position, head_size // 2, head_size)
    gathered_half = jnp.arange(seq_length // 2, dtype=jnp.int32)
    key_position = jnp.concatenate([gathered_half, seq_length - 1 - gathered_half])
    earlier_ok = key_position[None, :] <= query_position[:, None]
    diagonal = key_position[None, :] == query_position[:, None]
    key_ids = lax.all_gather(segments, "ctx", axis=3, tiled=True).reshape(
        batches, seq_local, seq_length
    )
    outputs_list = []
    d_tokens_list = []
    totals = None
    for micro_idx in range(batches):
        full_set = (
            lax.all_gather(w_query, ("dp", "ctx"), axis=0, tiled=True),
            lax.all_gather(w_key, ("dp", "ctx"), axis=0, tiled=True),
            lax.all_gather(w_value, ("dp", "ctx"), axis=0, tiled=True),
            lax.all_gather(w_out, ("dp", "ctx"), axis=1, tiled=True),
            lax.all_gather(w_gate, ("dp", "ctx"), axis=0, tiled=True),
            lax.all_gather(w_up, ("dp", "ctx"), axis=0, tiled=True),
            lax.all_gather(w_down, ("dp", "ctx"), axis=1, tiled=True),
            lax.all_gather(g_input, ("dp", "ctx"), axis=0, tiled=True),
            lax.all_gather(g_post_attn, ("dp", "ctx"), axis=0, tiled=True),
            lax.all_gather(g_pre_ffn, ("dp", "ctx"), axis=0, tiled=True),
            lax.all_gather(g_post_ffn, ("dp", "ctx"), axis=0, tiled=True),
            lax.all_gather(g_query, ("dp", "ctx"), axis=0, tiled=True),
            lax.all_gather(g_key, ("dp", "ctx"), axis=0, tiled=True),
        )
        tok_part = tokens[micro_idx]
        key_seg = key_ids[micro_idx]
        mat_query, mat_key, mat_value, mat_out, mat_gate, mat_up, mat_down = full_set[:7]
        gain_input = full_set[7].astype(jnp.float32)
        gain_post_attn = full_set[8].astype(jnp.float32)
        gain_pre_ffn = full_set[9].astype(jnp.float32)
        gain_post_ffn = full_set[10].astype(jnp.float32)
        gain_query = full_set[11].astype(jnp.float32)
        gain_key = full_set[12].astype(jnp.float32)
        inputs = tok_part.reshape(tok_rows, width).astype(jnp.float32)
        upstream = cotangent[micro_idx].reshape(tok_rows, width).astype(jnp.float32)
        query_seg = segments[micro_idx].reshape(seq_local, 2 * block_len)
        allowed = (key_seg[:, None, :] == query_seg[:, :, None]) & (
            key_seg[:, None, :] != 0
        ) & earlier_ok[None] | diagonal[None]
        allowed = allowed[:, None]
        norm_one, scale_one = norm_parts(inputs)
        hidden_one = (norm_one * (1.0 + gain_input)).astype(jnp.bfloat16)
        q_raw = matmul(hidden_one, mat_query).reshape(tok_rows, head_local, head_size)
        k_raw = matmul(hidden_one, mat_key)
        v_raw = matmul(hidden_one, mat_value)
        q_hat, q_scale = norm_parts(q_raw)
        k_hat, k_scale = norm_parts(k_raw)
        queries = rotate(
            q_hat * (1.0 + gain_query), cosine[:, None, :], sine_table[:, None, :]
        ).astype(jnp.bfloat16)
        key_rows = rotate(k_hat * (1.0 + gain_key), cosine, sine_table).astype(jnp.bfloat16)
        value_rows = v_raw.astype(jnp.bfloat16)
        key_all = lax.all_gather(
            key_rows.reshape(seq_local, 2, block_len, head_size), "ctx", axis=2, tiled=True
        )
        value_all = lax.all_gather(
            value_rows.reshape(seq_local, 2, block_len, head_size), "ctx", axis=2, tiled=True
        )
        key_all = key_all.reshape(seq_local, seq_length, head_size)
        value_all = value_all.reshape(seq_local, seq_length, head_size)
        query_seq = queries.reshape(seq_local, 2 * block_len, head_local, head_size)
        scores = SCALE * jnp.einsum(
            "sqhd,skd->shqk", query_seq, key_all, preferred_element_type=jnp.float32
        )
        masked = jnp.where(allowed, scores, NEGATIVE)
        top_score = jnp.max(masked, axis=-1, keepdims=True)
        shifted = jnp.exp(masked - top_score)
        total_mass = jnp.sum(shifted, axis=-1, keepdims=True)
        prob_low = (shifted / total_mass).astype(jnp.bfloat16)
        log_total = top_score + jnp.log(total_mass)
        head_out = jnp.einsum(
            "shqk,skd->sqhd", prob_low, value_all, preferred_element_type=jnp.float32
        )
        head_out = head_out.reshape(tok_rows, head_local * head_size).astype(jnp.bfloat16)
        attn_out = lax.psum(matmul(head_out, mat_out).astype(jnp.bfloat16), "tp").astype(
            jnp.float32
        )
        norm_attn, scale_attn = norm_parts(attn_out)
        middle = inputs + norm_attn * (1.0 + gain_post_attn)
        norm_two, scale_two = norm_parts(middle)
        hidden_two = (norm_two * (1.0 + gain_pre_ffn)).astype(jnp.bfloat16)
        gate_proj = matmul(hidden_two, mat_gate)
        up_proj = matmul(hidden_two, mat_up)
        activated, gelu_pull = jax.vjp(gelu_tanh, gate_proj)
        hidden_ffn = (activated * up_proj).astype(jnp.bfloat16)
        ffn_out = lax.psum(matmul(hidden_ffn, mat_down).astype(jnp.bfloat16), "tp").astype(
            jnp.float32
        )
        norm_ffn, scale_ffn = norm_parts(ffn_out)
        output = (middle + norm_ffn * (1.0 + gain_post_ffn)).astype(jnp.bfloat16)
        d_ffn, d_gain_post_ffn = norm_back(upstream, norm_ffn, scale_ffn, gain_post_ffn)
        d_ffn_low = d_ffn.astype(jnp.bfloat16)
        grad_down = matmul_tn(hidden_ffn, d_ffn_low)
        d_hidden = matmul_nt(d_ffn_low, mat_down)
        (d_gate,) = gelu_pull(d_hidden * up_proj)
        d_gate_low = d_gate.astype(jnp.bfloat16)
        d_up_low = (d_hidden * activated).astype(jnp.bfloat16)
        grad_gate = matmul_tn(hidden_two, d_gate_low)
        grad_up = matmul_tn(hidden_two, d_up_low)
        d_hidden_two = lax.psum(
            (matmul_nt(d_gate_low, mat_gate) + matmul_nt(d_up_low, mat_up)).astype(jnp.bfloat16),
            "tp",
        ).astype(jnp.float32)
        d_middle_part, d_gain_pre_ffn = norm_back(d_hidden_two, norm_two, scale_two, gain_pre_ffn)
        d_middle = upstream + d_middle_part
        d_attn, d_gain_post_attn = norm_back(d_middle, norm_attn, scale_attn, gain_post_attn)
        d_attn_low = d_attn.astype(jnp.bfloat16)
        grad_out = matmul_tn(head_out, d_attn_low)
        d_heads = (
            matmul_nt(d_attn_low, mat_out)
            .astype(jnp.bfloat16)
            .reshape(seq_local, 2 * block_len, head_local, head_size)
        )
        scores_again = SCALE * jnp.einsum(
            "sqhd,skd->shqk", query_seq, key_all, preferred_element_type=jnp.float32
        )
        probabilities = jnp.exp(jnp.where(allowed, scores_again, NEGATIVE) - log_total)
        d_probs = jnp.einsum(
            "sqhd,skd->shqk", d_heads, value_all, preferred_element_type=jnp.float32
        )
        delta = jnp.sum(probabilities * d_probs, axis=-1, keepdims=True)
        d_scores = (probabilities * (d_probs - delta)).astype(jnp.bfloat16)
        d_query = SCALE * jnp.einsum(
            "shqk,skd->sqhd", d_scores, key_all, preferred_element_type=jnp.float32
        )
        prob_again = probabilities.astype(jnp.bfloat16)
        d_value_all = jnp.einsum(
            "shqk,sqhd->skd", prob_again, d_heads, preferred_element_type=jnp.float32
        )
        d_key_all = SCALE * jnp.einsum(
            "shqk,sqhd->skd", d_scores, query_seq, preferred_element_type=jnp.float32
        )
        d_key_own = lax.psum_scatter(
            d_key_all.reshape(seq_local, 2, seq_length // 2, head_size).astype(jnp.bfloat16),
            "ctx",
            scatter_dimension=2,
            tiled=True,
        ).astype(jnp.float32)
        d_value_own = lax.psum_scatter(
            d_value_all.reshape(seq_local, 2, seq_length // 2, head_size).astype(jnp.bfloat16),
            "ctx",
            scatter_dimension=2,
            tiled=True,
        ).astype(jnp.float32)
        d_q_rot = rotate(
            d_query.reshape(tok_rows, head_local, head_size),
            cosine[:, None, :],
            -sine_table[:, None, :],
        )
        d_q_raw, d_gain_query_part = norm_back(d_q_rot, q_hat, q_scale, gain_query)
        q_grad_low = d_q_raw.astype(jnp.bfloat16).reshape(tok_rows, head_local * head_size)
        grad_query = matmul_tn(hidden_one, q_grad_low)
        d_hidden_q = matmul_nt(q_grad_low, mat_query)
        d_hidden_q, d_key_sum, d_value_sum, d_gain_query = (
            lax.psum(d_hidden_q.astype(jnp.bfloat16), "tp").astype(jnp.float32),
            lax.psum(d_key_own.reshape(tok_rows, head_size).astype(jnp.bfloat16), "tp").astype(
                jnp.float32
            ),
            lax.psum(d_value_own.reshape(tok_rows, head_size).astype(jnp.bfloat16), "tp").astype(
                jnp.float32
            ),
            lax.psum(d_gain_query_part.astype(jnp.bfloat16), "tp").astype(jnp.float32),
        )
        d_k_rot = rotate(d_key_sum, cosine, -sine_table)
        d_k_raw, d_gain_key = norm_back(d_k_rot, k_hat, k_scale, gain_key)
        k_grad_low = d_k_raw.astype(jnp.bfloat16)
        v_grad_low = d_value_sum.astype(jnp.bfloat16)
        grad_key = matmul_tn(hidden_one, k_grad_low)
        grad_value = matmul_tn(hidden_one, v_grad_low)
        d_hidden_one = (
            d_hidden_q + matmul_nt(k_grad_low, mat_key) + matmul_nt(v_grad_low, mat_value)
        )
        d_input_part, d_gain_input = norm_back(d_hidden_one, norm_one, scale_one, gain_input)
        d_inputs = d_middle + d_input_part
        grad_set = (
            grad_query,
            grad_key,
            grad_value,
            grad_out,
            grad_gate,
            grad_up,
            grad_down,
            d_gain_input,
            d_gain_post_attn,
            d_gain_pre_ffn,
            d_gain_post_ffn,
            d_gain_query,
            d_gain_key,
        )
        result_out, result_grad, grad_set = (
            output.reshape(tok_part.shape),
            d_inputs.reshape(tok_part.shape),
            grad_set,
        )
        outputs_list.append(result_out)
        d_tokens_list.append(result_grad)
        pending = (
            lax.psum_scatter(
                grad_set[0].astype(jnp.bfloat16), ("dp", "ctx"), scatter_dimension=0, tiled=True
            ).astype(jnp.float32),
            lax.psum_scatter(
                grad_set[1].astype(jnp.bfloat16), ("dp", "ctx"), scatter_dimension=0, tiled=True
            ).astype(jnp.float32),
            lax.psum_scatter(
                grad_set[2].astype(jnp.bfloat16), ("dp", "ctx"), scatter_dimension=0, tiled=True
            ).astype(jnp.float32),
            lax.psum_scatter(
                grad_set[3].astype(jnp.bfloat16), ("dp", "ctx"), scatter_dimension=1, tiled=True
            ).astype(jnp.float32),
            lax.psum_scatter(
                grad_set[4].astype(jnp.bfloat16), ("dp", "ctx"), scatter_dimension=0, tiled=True
            ).astype(jnp.float32),
            lax.psum_scatter(
                grad_set[5].astype(jnp.bfloat16), ("dp", "ctx"), scatter_dimension=0, tiled=True
            ).astype(jnp.float32),
            lax.psum_scatter(
                grad_set[6].astype(jnp.bfloat16), ("dp", "ctx"), scatter_dimension=1, tiled=True
            ).astype(jnp.float32),
            lax.psum_scatter(
                grad_set[7].astype(jnp.bfloat16), ("dp", "ctx"), scatter_dimension=0, tiled=True
            ).astype(jnp.float32),
            lax.psum_scatter(
                grad_set[8].astype(jnp.bfloat16), ("dp", "ctx"), scatter_dimension=0, tiled=True
            ).astype(jnp.float32),
            lax.psum_scatter(
                grad_set[9].astype(jnp.bfloat16), ("dp", "ctx"), scatter_dimension=0, tiled=True
            ).astype(jnp.float32),
            lax.psum_scatter(
                grad_set[10].astype(jnp.bfloat16), ("dp", "ctx"), scatter_dimension=0, tiled=True
            ).astype(jnp.float32),
            lax.psum_scatter(
                grad_set[11].astype(jnp.bfloat16), ("dp", "ctx"), scatter_dimension=0, tiled=True
            ).astype(jnp.float32),
            lax.psum_scatter(
                grad_set[12].astype(jnp.bfloat16), ("dp", "ctx"), scatter_dimension=0, tiled=True
            ).astype(jnp.float32),
        )
        totals = pending if totals is None else jax.tree.map(jnp.add, totals, pending)
    return (
        jnp.stack(outputs_list),
        jnp.stack(d_tokens_list),
        totals[0],
        totals[1],
        totals[2],
        totals[3],
        totals[4],
        totals[5],
        totals[6],
        totals[7],
        totals[8],
        totals[9],
        totals[10],
        totals[11],
        totals[12],
    )


def solution(mesh):
    return jax.shard_map(
        shards,
        mesh=mesh,
        in_specs=(
            P(None, "dp", None, "ctx", None),
            P(None, "dp", None, "ctx"),
            P(None, "dp", None, "ctx", None),
            P(("dp", "ctx"), "tp"),
            P(("dp", "ctx"), None),
            P(("dp", "ctx"), None),
            P("tp", ("dp", "ctx")),
            P(("dp", "ctx"), "tp"),
            P(("dp", "ctx"), "tp"),
            P("tp", ("dp", "ctx")),
            P(("dp", "ctx")),
            P(("dp", "ctx")),
            P(("dp", "ctx")),
            P(("dp", "ctx")),
            P(("dp", "ctx")),
            P(("dp", "ctx")),
        ),
        out_specs=(
            P(None, "dp", None, "ctx", None),
            P(None, "dp", None, "ctx", None),
            P(("dp", "ctx"), "tp"),
            P(("dp", "ctx"), None),
            P(("dp", "ctx"), None),
            P("tp", ("dp", "ctx")),
            P(("dp", "ctx"), "tp"),
            P(("dp", "ctx"), "tp"),
            P("tp", ("dp", "ctx")),
            P(("dp", "ctx")),
            P(("dp", "ctx")),
            P(("dp", "ctx")),
            P(("dp", "ctx")),
            P(("dp", "ctx")),
            P(("dp", "ctx")),
        ),
        check_vma=False,
    )
```

profile of v0, /device:TPU:0, one launch (start us, length us, event | category | flops | bytes accessed | tf_op | source)
XLA Modules:
  0.0 1917.7 jit_solution(7947380345968917817)
XLA Ops:
  15.9 26.1 %all-reduce.19 = (bf16[1152]{0:T(1024)(128)(2,1)}, bf16[1152]{0:T(1024)(128)(2,1)S(1)}, bf16[256]{0:T(256)(128)(2,1)S(1)}, bf16[256]{0:T(256)(128)(2,1)}, bf16[1...) all-reduce(bf16[1152]{0:T(1024)(128)(2,1)S(1)} %dynamic-update-slice, ...), channel_id=1, replica_groups=mesh['dp'=2,'ctx'=4,'tp'=4] {'dp','ctx'}, use_global_device_ids=true, to_apply=%add.3 | all-reduce | flops 5120 | bytes 20480
  95.5 13.1 all_gather.76
  176.8 171.3 %all-reduce.36.cloned.1.call-done = (bf16[1024,1152]{1,0:T(8,128)(2,1)}, bf16[1024,1152]{1,0:T(8,128)(2,1)}) async-done(((bf16[1024,1152]{1,0:T(8,128)(2,1)}, bf16[1024,1152]{1,0:T(8,128)(2,1)}), (bf16[1024,1152]{1,0:T(8,128)(2,1)}, bf16[1024,1152]{1,0:T(8,128)(2,1)})) %all-reduce.36.cloned.1.call-update) | async-done | bytes 4718608 | tf_op jit(solution)/shard_map/psum | solution.py:176
  379.8 13.0 multiply_convert_fusion.2
  424.3 165.6 %all-reduce.34.cloned.1.call-done = (bf16[1024,1152]{1,0:T(8,128)(2,1)}, bf16[1024,1152]{1,0:T(8,128)(2,1)}) async-done(((bf16[1024,1152]{1,0:T(8,128)(2,1)}, bf16[1024,1152]{1,0:T(8,128)(2,1)}), (bf16[1024,1152]{1,0:T(8,128)(2,1)}, bf16[1024,1152]{1,0:T(8,128)(2,1)})) %all-reduce.34.cloned.1.call-update) | async-done | bytes 4718608 | tf_op jit(solution)/shard_map/psum | solution.py:187
  603.1 17.3 multiply_convert_fusion
  629.7 16.2 multiply_convert_fusion.1
  668.1 171.4 %all-reduce.32.cloned.1.call-done = (bf16[1024,1152]{1,0:T(8,128)(2,1)}, bf16[1024,1152]{1,0:T(8,128)(2,1)}) async-done(((bf16[1024,1152]{1,0:T(8,128)(2,1)}, bf16[1024,1152]{1,0:T(8,128)(2,1)}), (bf16[1024,1152]{1,0:T(8,128)(2,1)}, bf16[1024,1152]{1,0:T(8,128)(2,1)})) %all-reduce.32.cloned.1.call-update) | async-done | bytes 4718608 | tf_op jit(solution)/shard_map/psum | solution.py:201
  883.5 13.3 fusion.8
  917.5 13.9 fusion
  933.6 13.2 fusion.9
  1074.1 37.5 %reduce-scatter.41.cloned.1.call-done = bf16[256,144]{0,1:T(8,128)(2,1)} async-done(((bf16[256,1152]{0,1:T(8,128)(2,1)}), bf16[256,144]{0,1:T(8,128)(2,1)}) %reduce-scatter.41.cloned.1.call-update) | async-done | bytes 73744 | tf_op jit(solution)/shard_map/reduce_scatter | solution.py:308
  1113.2 36.3 %reduce-scatter.27.cloned.1.call-done = bf16[144,256]{1,0:T(8,128)(2,1)} async-done(((bf16[1152,256]{1,0:T(8,128)(2,1)}), bf16[144,256]{1,0:T(8,128)(2,1)}) %reduce-scatter.27.cloned.1.call-update) | async-done | bytes 73744 | tf_op jit(solution)/shard_map/reduce_scatter | solution.py:299
  1149.6 37.9 %reduce-scatter.29.cloned.1.call-done = bf16[144,256]{1,0:T(8,128)(2,1)} async-done(((bf16[1152,256]{1,0:T(8,128)(2,1)}), bf16[144,256]{1,0:T(8,128)(2,1)}) %reduce-scatter.29.cloned.1.call-update) | async-done | bytes 73744 | tf_op jit(solution)/shard_map/reduce_scatter | solution.py:299
  1189.1 52.7 %reduce-scatter.51.cloned.1.call-done = bf16[1728,144]{0,1:T(8,128)(2,1)} async-done(((bf16[1728,1152]{0,1:T(8,128)(2,1)}), bf16[1728,144]{0,1:T(8,128)(2,1)}) %reduce-scatter.51.cloned.1.call-update) | async-done | bytes 497680 | tf_op jit(solution)/shard_map/reduce_scatter | solution.py:317
  1241.8 54.3 %reduce-scatter.53.cloned.1.call-done = bf16[1728,144]{0,1:T(8,128)(2,1)} async-done(((bf16[1728,1152]{0,1:T(8,128)(2,1)}), bf16[1728,144]{0,1:T(8,128)(2,1)}) %reduce-scatter.53.cloned.1.call-update) | async-done | bytes 497680 | tf_op jit(solution)/shard_map/reduce_scatter | solution.py:317
  1298.4 52.6 %reduce-scatter.45.cloned.1.call-done = bf16[144,1728]{1,0:T(8,128)(2,1)} async-done(((bf16[1152,1728]{1,0:T(8,128)(2,1)}), bf16[144,1728]{1,0:T(8,128)(2,1)}) %reduce-scatter.45.cloned.1.call-update) | async-done | bytes 497680 | tf_op jit(solution)/shard_map/reduce_scatter | solution.py:311
  1351.1 54.5 %reduce-scatter.43.cloned.1.call-done = bf16[144,1728]{1,0:T(8,128)(2,1)} async-done(((bf16[1152,1728]{1,0:T(8,128)(2,1)}), bf16[144,1728]{1,0:T(8,128)(2,1)}) %reduce-scatter.43.cloned.1.call-update) | async-done | bytes 497680 | tf_op jit(solution)/shard_map/reduce_scatter | solution.py:311
  1407.8 52.1 %reduce-scatter.49.cloned.1.call-done = bf16[144,1728]{1,0:T(8,128)(2,1)} async-done(((bf16[1152,1728]{1,0:T(8,128)(2,1)}), bf16[144,1728]{1,0:T(8,128)(2,1)}) %reduce-scatter.49.cloned.1.call-update) | async-done | bytes 497680 | tf_op jit(solution)/shard_map/reduce_scatter | solution.py:314
  1459.9 54.5 %reduce-scatter.47.cloned.1.call-done = bf16[144,1728]{1,0:T(8,128)(2,1)} async-done(((bf16[1152,1728]{1,0:T(8,128)(2,1)}), bf16[144,1728]{1,0:T(8,128)(2,1)}) %reduce-scatter.47.cloned.1.call-update) | async-done | bytes 497680 | tf_op jit(solution)/shard_map/reduce_scatter | solution.py:314
  1516.6 242.2 %all-reduce.30.cloned.1.call-done = (bf16[1024,256]{1,0:T(8,128)(2,1)}, bf16[1024,1152]{1,0:T(8,128)(2,1)}, bf16[1024,256]{1,0:T(8,128)(2,1)}, bf16[1024,256]{1,...) async-done(((bf16[1024,256]{1,0:T(8,128)(2,1)}, bf16[1024,1152]{1,0:T(8,128)(2,1)}, bf16[1024,256]{1,0:T(8,128)(2,1)}, bf16[1024,256]{1,0:T(8,128)(2,1)}, ...) | async-done | bytes 6815760 | tf_op jit(solution)/shard_map/psum | solution.py:257
  1790.3 24.5 %all-reduce.18 = (bf16[1152]{0:T(1024)(128)(2,1)S(1)}, bf16[1152]{0:T(1024)(128)(2,1)S(1)}, bf16[1152]{0:T(1024)(128)(2,1)S(1)}, bf16[1152]{0:T(1024)(128)(2,1)S...) all-reduce(bf16[1152]{0:T(1024)(128)(2,1)S(1)} %get-tuple-element.2, ...), channel_id=21, replica_groups=mesh['dp'=2,'ctx'=4,'tp'=4] {'dp','ctx'}, use_global_device_ids=true, to_apply=%region_63.64.clone | all-reduce | flops 10240 | bytes 40960
  1846.1 25.0 %reduce-scatter.31.cloned.1.call-done = bf16[144,256]{1,0:T(8,128)(2,1)} async-done(((bf16[1152,256]{1,0:T(8,128)(2,1)}), bf16[144,256]{1,0:T(8,128)(2,1)}) %reduce-scatter.31.cloned.1.call-update) | async-done | bytes 73744 | tf_op jit(solution)/shard_map/reduce_scatter | solution.py:302
  1871.1 37.4 %reduce-scatter.33.cloned.1.call-done = bf16[144,256]{1,0:T(8,128)(2,1)} async-done(((bf16[1152,256]{1,0:T(8,128)(2,1)}), bf16[144,256]{1,0:T(8,128)(2,1)}) %reduce-scatter.33.cloned.1.call-update) | async-done | bytes 73744 | tf_op jit(solution)/shard_map/reduce_scatter | solution.py:302
  (517 shorter events, 501.4 us)
Async XLA Ops:
  8.0 103.8 %all-gather.20.cloned.1.call-start = ((), (), s32[]{:S(2)}) async-start(), calls=%async_computation.24 | async-start | bytes 2621440 | tf_op jit(solution)/shard_map/all_gather | solution.py:154
  79.0 269.1 %all-reduce.36.cloned.1.call-start = ((), (), s32[]{:S(2)}) async-start(), calls=%async_computation.46 | async-start | bytes 9437184 | tf_op jit(solution)/shard_map/psum | solution.py:176
  175.0 187.3 %all-gather.12.cloned.1.call-start = ((), (), s32[]{:S(2)}) async-start(), calls=%async_computation.20 | async-start | bytes 4644864 | tf_op jit(solution)/shard_map/all_gather | solution.py:116
  175.5 204.3 %all-gather.14.cloned.1.call-start = ((), (), s32[]{:S(2)}) async-start(), calls=%async_computation.21 | async-start | bytes 4644864 | tf_op jit(solution)/shard_map/all_gather | solution.py:117
  176.1 225.9 %all-gather.16.cloned.1.call-start = ((), (), s32[]{:S(2)}) async-start(), calls=%async_computation.22 | async-start | bytes 4644864 | tf_op jit(solution)/shard_map/all_gather | solution.py:118
  176.7 413.2 %all-reduce.34.cloned.1.call-start = ((), (), s32[]{:S(2)}) async-start(), calls=%async_computation.45 | async-start | bytes 9437184 | tf_op jit(solution)/shard_map/psum | solution.py:187
  418.4 421.1 %all-reduce.32.cloned.1.call-start = ((), (), s32[]{:S(2)}) async-start(), calls=%async_computation.44 | async-start | bytes 9437184 | tf_op jit(solution)/shard_map/psum | solution.py:201
  668.0 389.3 %reduce-scatter.21.cloned.1.call-start = ((), (), s32[]{:S(2)}) async-start(), calls=%async_computation.26 | async-start | bytes 2621440 | tf_op jit(solution)/shard_map/reduce_scatter | solution.py:240
  904.0 153.3 %reduce-scatter.19.cloned.1.call-start = ((), (), s32[]{:S(2)}) async-start(), calls=%async_computation.25 | async-start | bytes 2621440 | tf_op jit(solution)/shard_map/reduce_scatter | solution.py:234
  911.2 146.1 %reduce-scatter.25.cloned.1.call-start = ((), (), s32[]{:S(2)}) async-start(), calls=%async_computation.28 | async-start | bytes 2621440 | tf_op jit(solution)/shard_map/reduce_scatter | solution.py:240
  953.9 103.4 %reduce-scatter.23.cloned.1.call-start = ((), (), s32[]{:S(2)}) async-start(), calls=%async_computation.27 | async-start | bytes 2621440 | tf_op jit(solution)/shard_map/reduce_scatter | solution.py:234
  961.3 112.8 %reduce-scatter.39.cloned.1.call-start = ((), (), s32[]{:S(2)}) async-start(), calls=%async_computation.35 | async-start | bytes 663552 | tf_op jit(solution)/shard_map/reduce_scatter | solution.py:308
  975.0 136.7 %reduce-scatter.41.cloned.1.call-start = ((), (), s32[]{:S(2)}) async-start(), calls=%async_computation.36 | async-start | bytes 663552 | tf_op jit(solution)/shard_map/reduce_scatter | solution.py:308
  986.0 163.6 %reduce-scatter.27.cloned.1.call-start = ((), (), s32[]{:S(2)}) async-start(), calls=%async_computation.29 | async-start | bytes 663552 | tf_op jit(solution)/shard_map/reduce_scatter | solution.py:299
  993.8 193.7 %reduce-scatter.29.cloned.1.call-start = ((), (), s32[]{:S(2)}) async-start(), calls=%async_computation.30 | async-start | bytes 663552 | tf_op jit(solution)/shard_map/reduce_scatter | solution.py:299
  997.6 244.2 %reduce-scatter.51.cloned.1.call-start = ((), (), s32[]{:S(2)}) async-start(), calls=%async_computation.41 | async-start | bytes 4644864 | tf_op jit(solution)/shard_map/reduce_scatter | solution.py:317
  1007.6 288.6 %reduce-scatter.53.cloned.1.call-start = ((), (), s32[]{:S(2)}) async-start(), calls=%async_computation.42 | async-start | bytes 4644864 | tf_op jit(solution)/shard_map/reduce_scatter | solution.py:317
  1015.9 335.2 %reduce-scatter.45.cloned.1.call-start = ((), (), s32[]{:S(2)}) async-start(), calls=%async_computation.38 | async-start | bytes 4644864 | tf_op jit(solution)/shard_map/reduce_scatter | solution.py:311
  1025.3 380.2 %reduce-scatter.43.cloned.1.call-start = ((), (), s32[]{:S(2)}) async-start(), calls=%async_computation.37 | async-start | bytes 4644864 | tf_op jit(solution)/shard_map/reduce_scatter | solution.py:311
  1033.8 426.0 %reduce-scatter.49.cloned.1.call-start = ((), (), s32[]{:S(2)}) async-start(), calls=%async_computation.40 | async-start | bytes 4644864 | tf_op jit(solution)/shard_map/reduce_scatter | solution.py:314
  1043.1 471.3 %reduce-scatter.47.cloned.1.call-start = ((), (), s32[]{:S(2)}) async-start(), calls=%async_computation.39 | async-start | bytes 4644864 | tf_op jit(solution)/shard_map/reduce_scatter | solution.py:314
  1051.4 707.4 %all-reduce.30.cloned.1.call-start = ((), (), s32[]{:S(2)}) async-start(), calls=%async_computation.43 | async-start | bytes 13631488 | tf_op jit(solution)/shard_map/psum | solution.py:257
  1057.3 787.1 %reduce-scatter.37.cloned.1.call-start = ((), (), s32[]{:S(2)}) async-start(), calls=%async_computation.34 | async-start | bytes 663552 | tf_op jit(solution)/shard_map/reduce_scatter | solution.py:305
  1780.5 128.0 %reduce-scatter.33.cloned.1.call-start = ((), (), s32[]{:S(2)}) async-start(), calls=%async_computation.32 | async-start | bytes 663552 | tf_op jit(solution)/shard_map/reduce_scatter | solution.py:302
  (140 other events, 2480.8 us)
Sparse Core Ops, SparseCore 0:
  63.0 23.1 all-gather.19
  88.3 24.9 all-gather.17
  115.4 22.5 all-gather.9
  140.0 22.5 all-gather.7
  175.1 172.9 all-reduce.35
  418.5 171.3 all-reduce.33
  668.1 171.3 all-reduce.31
  904.1 30.4 reduce-scatter.20
  937.2 31.4 reduce-scatter.18
  971.1 31.3 reduce-scatter.24
  1005.2 31.4 reduce-scatter.22
  1039.7 34.3 reduce-scatter.38
  1077.2 34.3 reduce-scatter.40
  1115.2 34.3 reduce-scatter.26
  1153.1 34.3 reduce-scatter.28
  1190.8 50.9 reduce-scatter.50
  1245.1 51.0 reduce-scatter.52
  1300.0 50.9 reduce-scatter.44
  1354.5 50.9 reduce-scatter.42
  1408.8 50.9 reduce-scatter.48
  1463.3 51.0 reduce-scatter.46
  1517.2 241.5 all-reduce.29
Sparse Core Ops, SparseCore 1:
  177.3 36.9 all-gather.11
  216.0 36.2 all-gather.13
  254.1 36.2 all-gather.15
  1762.7 33.2 reduce-scatter.36
  1799.1 34.4 reduce-scatter.34
  1836.6 34.4 reduce-scatter.30
  1874.0 34.3 reduce-scatter.32
where the time goes:
time: 1930 us; the launch traced here: 1920 us
  waiting for transfers between devices  1260 us (65%)
  matrix products  341 us (18%)
  other arithmetic  168 us (9%)
  blocking collectives  107 us (6%)
  local copies, waits for them, and re-layouts  20.9 us (1%)
  between operations  20.5 us (1%)
    psum x1, waiting for transfers between devices, shards(): lax.psum(d_key_own.reshape(tok_rows, head_size).astype(jnp.bfloat16), 'tp')  242 us
    psum x1, waiting for transfers between devices, shards(): lax.psum((matmul_nt(d_gate_low, mat_gate) + matmul_nt(d_up_low, mat_up))....  171 us
    psum x1, waiting for transfers between devices, shards(): lax.psum(matmul(head_out, mat_out).astype(jnp.bfloat16), 'tp')  171 us
    psum x1, waiting for transfers between devices, shards(): lax.psum(matmul(hidden_ffn, mat_down).astype(jnp.bfloat16), 'tp')  166 us
    reduce_scatter x2, waiting for transfers between devices, shards(): lax.psum_scatter(grad_set[4].astype(jnp.bfloat16), ('dp', 'ctx'), scatter...  107 us
    reduce_scatter x2, waiting for transfers between devices, shards(): lax.psum_scatter(grad_set[6].astype(jnp.bfloat16), ('dp', 'ctx'), scatter...  107 us
    reduce_scatter x2, waiting for transfers between devices, shards(): lax.psum_scatter(grad_set[5].astype(jnp.bfloat16), ('dp', 'ctx'), scatter...  107 us
    dot_general x14, matrix products, matmul_nt(): lax.dot_general(left_side, right_side, (((1,), (1,)), ((), ())), preferre...  90.8 us
  transfers between devices with their start and end apart: 29, of which 16 were waited for; matrix products, arithmetic and copies ran while one was open for 17% of the time, Pallas kernels for 0%

commit v1 on v0

v1 whole, which is shorter than its diff:
```python
import functools

import jax
import jax.numpy as jnp
from jax import lax
from jax.experimental import pallas as pl
from jax.experimental.pallas import tpu as pltpu
from jax.sharding import PartitionSpec as P

EPS = 1e-06
THETA = 1000000.0
SCALE = 0.0625
NEGATIVE = -1e30
BF16 = jnp.bfloat16
F32 = jnp.float32
MESH = pl.DeviceIdType.MESH
NN = (((1,), (0,)), ((), ()))
NT = (((1,), (1,)), ((), ()))
TN = (((0,), (0,)), ((), ()))


def dot(a, b, dims=NN):
    return lax.dot_general(a, b, dims, preferred_element_type=F32)


def barrier_line(z):
    bar = pltpu.get_barrier_semaphore()

    @pl.when(z > 0)
    def _():
        pl.semaphore_signal(bar, inc=1, device_id={"tp": z - 1}, device_id_type=MESH)

    @pl.when(z < 3)
    def _():
        pl.semaphore_signal(bar, inc=1, device_id={"tp": z + 1}, device_id_type=MESH)

    pl.semaphore_wait(bar, jnp.where((z == 0) | (z == 3), 1, 2))


def sum_kernel(n, tile, x_ref, o_ref, own, got, pair, other, *sems):
    lsem, ssem1, rsem1, ssem2, rsem2, ssem3, rsem3, osem = sems
    z = lax.axis_index("tp")
    hub = (z == 1) | (z == 2)
    leaf = jnp.logical_not(hub)
    other_hub = jnp.where(z == 1, 2, 1)
    my_hub = jnp.where(z == 0, 1, 2)
    my_leaf = jnp.where(z == 1, 0, 3)
    barrier_line(z)

    def rows(t):
        return pl.ds(t * tile, tile)

    def up(t):
        return pltpu.make_async_remote_copy(
            x_ref.at[rows(t)], got.at[rows(t)], ssem1.at[t], rsem1.at[t],
            device_id={"tp": my_hub}, device_id_type=MESH)

    def across(t):
        return pltpu.make_async_remote_copy(
            pair.at[rows(t)], other.at[rows(t)], ssem2.at[t], rsem2.at[t],
            device_id={"tp": other_hub}, device_id_type=MESH)

    def back(t):
        return pltpu.make_async_remote_copy(
            own.at[rows(t)], o_ref.at[rows(t)], ssem3.at[t], rsem3.at[t],
            device_id={"tp": my_leaf}, device_id_type=MESH)

    def load(t):
        return pltpu.make_async_copy(x_ref.at[rows(t)], own.at[rows(t)], lsem.at[t])

    def store(t):
        return pltpu.make_async_copy(own.at[rows(t)], o_ref.at[rows(t)], osem.at[t])

    @pl.when(leaf)
    def _():
        for t in range(n):
            up(t).start()
        for t in range(n):
            back(t).wait_recv()
        for t in range(n):
            up(t).wait_send()

    @pl.when(hub)
    def _():
        for t in range(n):
            load(t).start()

        def finish(t):
            across(t).wait_recv()
            own[rows(t), :] = (pair[rows(t), :].astype(F32) + other[rows(t), :].astype(F32)).astype(BF16)
            back(t).start()
            store(t).start()

        for t in range(n):
            load(t).wait()
            up(t).wait_recv()
            pair[rows(t), :] = (own[rows(t), :].astype(F32) + got[rows(t), :].astype(F32)).astype(BF16)
            across(t).start()
            if t > 0:
                finish(t - 1)
        finish(n - 1)
        for t in range(n):
            across(t).wait_send()
            back(t).wait_send()
            store(t).wait()


def sum_tp(x, ident):
    rows, cols = x.shape
    tile = 128 if rows % 128 == 0 else rows
    n = rows // tile
    dma = pltpu.SemaphoreType.DMA((n,))
    return pl.pallas_call(
        functools.partial(sum_kernel, n, tile),
        out_shape=jax.ShapeDtypeStruct((rows, cols), BF16),
        in_specs=[pl.BlockSpec(memory_space=pl.ANY)],
        out_specs=pl.BlockSpec(memory_space=pl.ANY),
        scratch_shapes=[pltpu.VMEM((rows, cols), BF16)] * 4 + [dma] * 8,
        compiler_params=pltpu.CompilerParams(
            collective_id=ident, has_side_effects=True, vmem_limit_bytes=40 * 2**20),
        name=f"sum_tp_{ident}",
    )(x)


def gather_kernel(n, tile, width, x_ref, o_ref, lsem, *sems):
    su, ru, sd, rd = sems
    z = lax.axis_index("tp")
    barrier_line(z)

    def place(src, t):
        return o_ref.at[pl.ds(t * tile, tile), pl.ds(pl.multiple_of(src * width, width), width)]

    def send(src, t, k, way):
        ss, rs = (su, ru) if way > 0 else (sd, rd)
        here = x_ref.at[pl.ds(t * tile, tile)] if k == 0 else place(src, t)
        return pltpu.make_async_remote_copy(
            here, place(src, t), ss.at[k, t], rs.at[k, t],
            device_id={"tp": z + way}, device_id_type=MESH)

    own = pltpu.make_async_copy(x_ref, o_ref.at[:, pl.ds(pl.multiple_of(z * width, width), width)], lsem)
    own.start()
    for k in range(3):
        for t in range(n):
            for way in (1, -1):
                src = z - way * k
                ok = (z + way >= 0) & (z + way <= 3) & (src >= 0) & (src <= 3)
                if k > 0:
                    came = (src >= 0) & (src <= 3)

                    @pl.when(came)
                    def _():
                        send(src, t, k - 1, way).wait_recv()

                @pl.when(ok)
                def _():
                    send(src, t, k, way).start()
    for way in (1, -1):
        src = z - way * 3
        came = (src >= 0) & (src <= 3)

        @pl.when(came)
        def _():
            for t in range(n):
                send(src, t, 2, way).wait_recv()

    for k in range(3):
        for way in (1, -1):
            src = z - way * k
            ok = (z + way >= 0) & (z + way <= 3) & (src >= 0) & (src <= 3)

            @pl.when(ok)
            def _():
                for t in range(n):
                    send(src, t, k, way).wait_send()
    own.wait()


def gather_tp(x, ident):
    rows, width = x.shape
    tile = 256 if rows % 256 == 0 else rows
    n = rows // tile
    dma = pltpu.SemaphoreType.DMA((3, n))
    return pl.pallas_call(
        functools.partial(gather_kernel, n, tile, width),
        out_shape=jax.ShapeDtypeStruct((rows, 4 * width), x.dtype),
        in_specs=[pl.BlockSpec(memory_space=pl.ANY)],
        out_specs=pl.BlockSpec(memory_space=pl.ANY),
        scratch_shapes=[pltpu.SemaphoreType.DMA] + [dma] * 4,
        compiler_params=pltpu.CompilerParams(collective_id=ident, has_side_effects=True),
        name=f"gather_tp_{ident}",
    )(x)


def block_starts(half, t, blocks, rank):
    if half == 0:
        return t
    return jnp.where(t < blocks, t, t + rank + 1)


def attend_kernel(blocks, q_ref, k_ref, v_ref, qs_ref, ks_ref, o_ref, l_ref):
    rank = lax.axis_index("ctx")
    size = q_ref.shape[2]
    row = lax.broadcasted_iota(jnp.int32, (size, size), 0)
    col = lax.broadcasted_iota(jnp.int32, (size, size), 1)
    for half in range(2):
        q = q_ref[0, half] * jnp.asarray(SCALE, BF16)
        qseg = qs_ref[0, half]

        def part(block):
            start = pl.multiple_of(block * size, size)
            k = k_ref[0, pl.ds(start, size), :]
            v = v_ref[0, pl.ds(start, size), :]
            same = qseg == ks_ref[0, :, pl.ds(start, size)]
            return dot(q, k, NT), v, same

        s, v, same = part(rank + half * blocks)
        order = (col <= row) if half == 0 else (col >= row)
        s = jnp.where((same & order) | (col == row), s, NEGATIVE)
        top = jnp.max(s, axis=1, keepdims=True)
        p = jnp.exp(s - top)
        mass = jnp.sum(p, axis=1, keepdims=True)
        acc = dot(p.astype(BF16), v)

        def step(t, carry):
            top, mass, acc = carry
            s, v, same = part(block_starts(half, t, blocks, rank))
            s = jnp.where(same, s, NEGATIVE)
            new = jnp.maximum(top, jnp.max(s, axis=1, keepdims=True))
            keep = jnp.exp(top - new)
            p = jnp.exp(s - new)
            mass = mass * keep + jnp.sum(p, axis=1, keepdims=True)
            acc = acc * keep + dot(p.astype(BF16), v)
            return new, mass, acc

        count = rank if half == 0 else 2 * blocks - 1 - rank
        top, mass, acc = lax.fori_loop(0, count, step, (top, mass, acc))
        o_ref[0, half] = (acc / mass).astype(BF16)
        l_ref[0, half] = top + jnp.log(mass)


def attend(q, k, v, qseg, kseg):
    groups, _, size, head = q.shape
    length = k.shape[1]
    blocks = length // (2 * size)
    return pl.pallas_call(
        functools.partial(attend_kernel, blocks),
        grid=(groups,),
        out_shape=(
            jax.ShapeDtypeStruct(q.shape, BF16),
            jax.ShapeDtypeStruct((groups, 2, size, 1), F32),
        ),
        in_specs=[
            pl.BlockSpec((1, 2, size, head), lambda g: (g, 0, 0, 0)),
            pl.BlockSpec((1, length, head), lambda g: (g, 0, 0)),
            pl.BlockSpec((1, length, head), lambda g: (g, 0, 0)),
            pl.BlockSpec((1, 2, size, 1), lambda g: (g, 0, 0, 0)),
            pl.BlockSpec((1, 1, length), lambda g: (g, 0, 0)),
        ],
        out_specs=(
            pl.BlockSpec((1, 2, size, head), lambda g: (g, 0, 0, 0)),
            pl.BlockSpec((1, 2, size, 1), lambda g: (g, 0, 0, 0)),
        ),
        compiler_params=pltpu.CompilerParams(vmem_limit_bytes=48 * 2**20),
        name="attend",
    )(q, k, v, qseg, kseg)


def attend_back_kernel(blocks, q_ref, k_ref, v_ref, do_ref, l_ref, d_ref, qs_ref, ks_ref,
                       dq_ref, dkv_ref, dk_acc, dv_acc):
    rank = lax.axis_index("ctx")
    size = q_ref.shape[2]
    head = q_ref.shape[3]
    row = lax.broadcasted_iota(jnp.int32, (size, size), 0)
    col = lax.broadcasted_iota(jnp.int32, (size, size), 1)
    dk_acc[...] = jnp.zeros_like(dk_acc)
    dv_acc[...] = jnp.zeros_like(dv_acc)
    for half in range(2):
        q = q_ref[0, half] * jnp.asarray(SCALE, BF16)
        do = do_ref[0, half]
        qseg = qs_ref[0, half]
        log_mass = l_ref[0, half]
        delta = d_ref[0, half]

        def part(block, own):
            rows = pl.ds(pl.multiple_of(block * size, size), size)
            k = k_ref[0, rows, :]
            v = v_ref[0, rows, :]
            allowed = ks_ref[0, rows, :] == qseg
            if own:
                order = (row <= col) if half == 0 else (row >= col)
                allowed = (allowed & order) | (col == row)
            s = jnp.where(allowed, dot(k, q, NT), NEGATIVE)
            p = jnp.exp(s - log_mass)
            ds = (p * (dot(v, do, NT) - delta)).astype(BF16)
            dv_acc[rows, :] += dot(p.astype(BF16), do)
            dk_acc[rows, :] += dot(ds, q)
            return dot(ds, k, TN)

        def step(t, dq):
            return dq + part(block_starts(half, t, blocks, rank), False)

        dq = part(rank + half * blocks, True)
        count = rank if half == 0 else 2 * blocks - 1 - rank
        dq_ref[0, half] = SCALE * lax.fori_loop(0, count, step, dq)
    dkv_ref[0, :, :head] = dk_acc[...].astype(BF16)
    dkv_ref[0, :, head:] = dv_acc[...].astype(BF16)


def attend_back(q, k, v, do, log_mass, delta, qseg, kseg):
    groups, _, size, head = q.shape
    length = k.shape[1]
    blocks = length // (2 * size)
    halves = pl.BlockSpec((1, 2, size, head), lambda g: (g, 0, 0, 0))
    whole = pl.BlockSpec((1, length, head), lambda g: (g, 0, 0))
    line = pl.BlockSpec((1, 2, 1, size), lambda g: (g, 0, 0, 0))
    return pl.pallas_call(
        functools.partial(attend_back_kernel, blocks),
        grid=(groups,),
        out_shape=(
            jax.ShapeDtypeStruct(q.shape, F32),
            jax.ShapeDtypeStruct((groups, length, 2 * head), BF16),
        ),
        in_specs=[halves, whole, whole, halves, line, line, line,
                  pl.BlockSpec((1, length, 1), lambda g: (g, 0, 0))],
        out_specs=(halves, pl.BlockSpec((1, length, 2 * head), lambda g: (g, 0, 0))),
        scratch_shapes=[pltpu.VMEM((length, head), F32)] * 2,
        compiler_params=pltpu.CompilerParams(vmem_limit_bytes=56 * 2**20),
        name="attend_back",
    )(q, k, v, do, log_mass, delta, qseg, kseg)


def angles(position, half_size, full_size):
    frequency = THETA ** (-2.0 * jnp.arange(half_size, dtype=F32) / full_size)
    turned = position[:, None] * frequency[None, :]
    return (jnp.cos(turned), jnp.sin(turned))


def rotate(tensor, cosine, sine):
    half_size = tensor.shape[-1] // 2
    a = tensor[..., :half_size]
    b = tensor[..., half_size:]
    return jnp.concatenate([a * cosine - b * sine, b * cosine + a * sine], axis=-1)


def norm_parts(values):
    inv = lax.rsqrt(jnp.mean(values * values, axis=-1, keepdims=True) + EPS)
    return (values * inv, inv)


def norm_back(upstream, normalized, inv, gain):
    d_norm = upstream * (1.0 + gain)
    d_values = inv * (d_norm - normalized * jnp.mean(d_norm * normalized, axis=-1, keepdims=True))
    return (d_values, jnp.sum(upstream * normalized, axis=0))


def gelu_tanh(values):
    return jax.nn.gelu(values, approximate=True)


def shards(tokens, segments, cotangent, w_query, w_key, w_value, w_out, w_gate, w_up, w_down,
           g_input, g_post_attn, g_pre_ffn, g_post_ffn, g_query, g_key):
    batches, seq_local, _, size, width = tokens.shape
    head = w_key.shape[1]
    groups = batches * seq_local
    per_group = 2 * size
    rows = groups * per_group
    ctx = lax.axis_size("ctx")
    length = per_group * ctx
    rank = lax.axis_index("ctx")
    shared = ("dp", "ctx")
    own_rows = g_input.shape[0]
    hidden = w_gate.shape[1]

    def column(gain):
        return jnp.pad(gain, (0, own_rows - gain.shape[0]))[:, None]

    gains = jnp.concatenate([column(g) for g in (g_input, g_post_attn, g_pre_ffn, g_post_ffn, g_query, g_key)], axis=1)
    gains = jnp.pad(gains, ((0, 0), (0, 128 - gains.shape[1])))
    first = lax.all_gather(
        jnp.concatenate([w_query, w_key, w_value, gains], axis=1), shared, axis=0, tiled=True)
    key_ids = lax.all_gather(segments, "ctx", axis=3, tiled=True).reshape(groups, length)
    both = lax.all_gather(
        jnp.concatenate([w_query, w_out.T], axis=1), ("dp", "ctx", "tp"), axis=0, tiled=True)
    both = both.reshape(width // own_rows, 4, own_rows, 2 * head)
    both = both.transpose(0, 2, 3, 1).reshape(width, 2, head, 4).transpose(0, 1, 3, 2)
    query_full = both[:, 0].reshape(width, 4 * head)
    out_full = both[:, 1].reshape(width, 4 * head)
    ffn = lax.all_gather(
        jnp.concatenate([w_gate, w_up, w_down.T], axis=1), shared, axis=0, tiled=True)
    mat_qkv = first[:, : 3 * head]
    gain_cols = first[:, 3 * head :].astype(F32)
    gain_input, gain_post_attn, gain_pre_ffn, gain_post_ffn = (gain_cols[:, i] for i in range(4))
    short = g_query.shape[0]
    gain_query, gain_key = (
        gain_cols[:, i].reshape(-1, own_rows)[:, :short].reshape(-1) for i in (4, 5))
    mat_gate, mat_up, mat_down_t = ffn[:, :hidden], ffn[:, hidden : 2 * hidden], ffn[:, 2 * hidden :]
    tp_rank = lax.axis_index("tp")
    mat_out_t = lax.dynamic_slice_in_dim(out_full, tp_rank * head, head, axis=1)

    offsets = rank * size + jnp.arange(size, dtype=jnp.int32)
    position = jnp.concatenate([offsets, length - 1 - offsets]).astype(F32)
    cosine, sine = angles(position, head // 2, head)
    cosine = jnp.broadcast_to(cosine, (groups, per_group, head // 2)).reshape(rows, head // 2)
    sine = jnp.broadcast_to(sine, (groups, per_group, head // 2)).reshape(rows, head // 2)
    key_ids = jnp.where(key_ids == 0, -1, key_ids)
    own_ids = segments.reshape(groups, 2, size)

    inputs = tokens.reshape(rows, width).astype(F32)
    upstream = cotangent.reshape(rows, width).astype(F32)

    norm_one, scale_one = norm_parts(inputs)
    hidden_one = (norm_one * (1.0 + gain_input)).astype(BF16)
    raw = dot(hidden_one, mat_qkv)
    q_hat, q_scale = norm_parts(raw[:, :head])
    k_hat, k_scale = norm_parts(raw[:, head : 2 * head])
    queries = rotate(q_hat * (1.0 + gain_query), cosine, sine).astype(BF16)
    keys = rotate(k_hat * (1.0 + gain_key), cosine, sine).astype(BF16)
    values = raw[:, 2 * head :].astype(BF16)
    queries = queries.reshape(groups, 2, size, head)
    key_all = lax.all_gather(keys.reshape(groups, 2, size, head), "ctx", axis=2, tiled=True)
    value_all = lax.all_gather(values.reshape(groups, 2, size, head), "ctx", axis=2, tiled=True)
    key_all = key_all.reshape(groups, length, head)
    value_all = value_all.reshape(groups, length, head)
    heads, log_mass = attend(queries, key_all, value_all, own_ids[..., None], key_ids[:, None, :])
    heads_own = heads.reshape(rows, head)
    heads_all = gather_tp(heads_own, 0)
    attn = dot(heads_all, out_full, NT)
    norm_attn, scale_attn = norm_parts(attn)
    middle = inputs + norm_attn * (1.0 + gain_post_attn)
    norm_two, scale_two = norm_parts(middle)
    hidden_two = (norm_two * (1.0 + gain_pre_ffn)).astype(BF16)

    gate = dot(hidden_two, mat_gate)
    up = dot(hidden_two, mat_up)
    activated, gelu_pull = jax.vjp(gelu_tanh, gate)
    hidden_ffn = (activated * up).astype(BF16)
    ffn_out = sum_tp(dot(hidden_ffn, mat_down_t, NT).astype(BF16), 1).astype(F32)
    norm_ffn, scale_ffn = norm_parts(ffn_out)
    output = (middle + norm_ffn * (1.0 + gain_post_ffn)).astype(BF16)
    d_ffn, d_gain_post_ffn = norm_back(upstream, norm_ffn, scale_ffn, gain_post_ffn)
    d_ffn = d_ffn.astype(BF16)
    d_hidden = dot(d_ffn, mat_down_t)
    (d_gate,) = gelu_pull(d_hidden * up)
    d_gate = d_gate.astype(BF16)
    d_up = (d_hidden * activated).astype(BF16)
    d_two = sum_tp((dot(d_gate, mat_gate, NT) + dot(d_up, mat_up, NT)).astype(BF16), 2).astype(F32)
    grad_ffn = jnp.concatenate(
        [dot(hidden_two, d_gate, TN).astype(BF16), dot(hidden_two, d_up, TN).astype(BF16),
         dot(d_ffn, hidden_ffn, TN).astype(BF16)], axis=1)
    grad_ffn = lax.psum_scatter(grad_ffn, shared, scatter_dimension=0, tiled=True).astype(F32)
    d_part, d_gain_pre_ffn = norm_back(d_two, norm_two, scale_two, gain_pre_ffn)
    d_middle = upstream + d_part
    d_attn, d_gain_post_attn = norm_back(d_middle, norm_attn, scale_attn, gain_post_attn)
    d_attn = d_attn.astype(BF16)

    grad_out_t = dot(d_attn, heads_own, TN)
    d_heads = dot(d_attn, mat_out_t).astype(BF16)
    delta = jnp.sum(d_heads.astype(F32) * heads_own.astype(F32), axis=-1)
    d_query, d_kv = attend_back(
        queries, key_all, value_all, d_heads.reshape(groups, 2, size, head),
        log_mass.reshape(groups, 2, 1, size), delta.reshape(groups, 2, 1, size),
        own_ids[:, :, None, :], key_ids[:, :, None])
    d_kv = lax.psum_scatter(
        d_kv.reshape(groups, 2, length // 2, 2 * head), "ctx", scatter_dimension=2, tiled=True)
    d_kv = sum_tp(d_kv.reshape(rows, 2 * head), 3).astype(F32)
    d_q_rot = rotate(d_query.reshape(rows, head), cosine, -sine)
    d_q_raw, d_gain_query = norm_back(d_q_rot, q_hat, q_scale, gain_query)
    d_q_raw = d_q_raw.astype(BF16)
    d_q_all = gather_tp(d_q_raw, 4)
    d_k_rot = rotate(d_kv[:, :head], cosine, -sine)
    d_k_raw, d_gain_key = norm_back(d_k_rot, k_hat, k_scale, gain_key)
    d_kv_raw = jnp.concatenate([d_k_raw.astype(BF16), d_kv[:, head:].astype(BF16)], axis=1)
    d_one = dot(d_q_all, query_full, NT) + dot(d_kv_raw, mat_qkv[:, head:], NT)
    d_part, d_gain_input = norm_back(d_one, norm_one, scale_one, gain_input)
    d_tokens = d_middle + d_part
    d_gain_query = lax.psum(d_gain_query, "tp")

    def spread(vector):
        return jnp.pad(vector.reshape(-1, short), ((0, 0), (0, own_rows - short))).reshape(-1)

    d_gains = jnp.stack(
        [d_gain_input, d_gain_post_attn, d_gain_pre_ffn, d_gain_post_ffn, spread(d_gain_query), spread(d_gain_key)], axis=1)
    d_gains = jnp.pad(d_gains, ((0, 0), (0, 128 - d_gains.shape[1]))).astype(BF16)
    last = jnp.concatenate(
        [dot(hidden_one, d_q_raw, TN).astype(BF16), dot(hidden_one, d_kv_raw, TN).astype(BF16),
         grad_out_t.astype(BF16), d_gains], axis=1)
    last = lax.psum_scatter(last, shared, scatter_dimension=0, tiled=True).astype(F32)
    g = last[:, 4 * head :]
    return (
        output.reshape(tokens.shape),
        d_tokens.reshape(tokens.shape),
        last[:, :head],
        last[:, head : 2 * head],
        last[:, 2 * head : 3 * head],
        last[:, 3 * head : 4 * head].T,
        grad_ffn[:, :hidden],
        grad_ffn[:, hidden : 2 * hidden],
        grad_ffn[:, 2 * hidden :].T,
        g[:, 0],
        g[:, 1],
        g[:, 2],
        g[:, 3],
        g[:short, 4],
        g[:short, 5],
    )


def solution(mesh):
    shared = ("dp", "ctx")
    rows = P(None, "dp", None, "ctx", None)
    weights = (
        P(shared, "tp"), P(shared, None), P(shared, None), P("tp", shared),
        P(shared, "tp"), P(shared, "tp"), P("tp", shared),
    )
    gains = (P(shared),) * 6
    return jax.shard_map(
        shards,
        mesh=mesh,
        in_specs=(rows, P(None, "dp", None, "ctx"), rows) + weights + gains,
        out_specs=(rows, rows) + weights + gains,
        check_vma=False,
    )
```

time: 1930 us -> 1060 us (0.55)
  waiting for transfers between devices: 1260 us -> 101 us
  Pallas kernels: 0 us -> 478 us
  matrix products: 341 us -> 197 us
  local copies, waits for them, and re-layouts: 20.9 us -> 116 us
  blocking collectives: 107 us -> 15.3 us
  other arithmetic: 168 us -> 124 us
    psum x4 -> x0, waiting for transfers between devices: 750 us -> none  [the longest x1 242 us: shards(): lax.psum(d_key_own.reshape(tok_rows, head_size).astype(jnp.bfloat16), 'tp')]
    reduce_scatter x18 -> x1, waiting for transfers between devices: 506 us -> 0.01 us  [shards(): lax.psum_scatter(d_kv.reshape(groups, 2, length // 2, 2 * head), 'ctx', s...]
    pallas_call x0 -> x7, Pallas kernels: none -> 478 us  [the longest x3 293 us: sum_tp(): pl.pallas_call(functools.partial(sum_kernel, n, tile), out_shape=jax.Shap...]
    dot_general x54 -> x17, matrix products: 341 us -> 197 us  [dot(): return lax.dot_general(a, b, dims, preferred_element_type=F32)]
    all_gather x7 -> x5, waiting for transfers between devices: 0.06 us -> 88.5 us  [the longest x1 35.9 us: shards(): lax.all_gather(values.reshape(groups, 2, size, head), 'ctx', axis=2, tile...]
    unnamed x2 -> x0, blocking collectives: 50.6 us -> none
    all_gather x5 -> x1, blocking collectives: 46.6 us -> 5.41 us  [shards(): lax.all_gather(segments, 'ctx', axis=3, tiled=True).reshape(groups, length)]
    reduce_sum x17 -> x8, other arithmetic: 73.2 us -> 32.7 us  [the longest x4 25.4 us: norm_back(): return (d_values, jnp.sum(upstream * normalized, axis=0))]
  transfers between devices with their start and end apart: 29 -> 8, of which waited for: 16 -> 5; matrix products, arithmetic and copies ran while one was open for 17% -> 25% of each run, Pallas kernels for 0% -> 21%
where the time goes in v1:
time: 1060 us; the launch traced here: 1050 us
  Pallas kernels  478 us (45%)
  matrix products  197 us (19%)
  other arithmetic  124 us (12%)
  local copies, waits for them, and re-layouts  116 us (11%)
  waiting for transfers between devices  101 us (10%)
  between operations  15.7 us (1%)
  blocking collectives  15.3 us (1%)
    pallas_call x3, Pallas kernels, sum_tp(): pl.pallas_call(functools.partial(sum_kernel, n, tile), out_shape=jax.Shap...  293 us
    dot_general x17, matrix products, dot(): return lax.dot_general(a, b, dims, preferred_element_type=F32)  197 us
    pallas_call x2, Pallas kernels, gather_tp(): pl.pallas_call(functools.partial(gather_kernel, n, tile, width), out_shap...  140 us
    unnamed x111, local copies, waits for them, and re-layouts  48 us
    all_gather x1, waiting for transfers between devices, shards(): lax.all_gather(values.reshape(groups, 2, size, head), 'ctx', axis=2, tile...  35.9 us
    concatenate x1, other arithmetic, shards(): jnp.concatenate([dot(hidden_two, d_gate, TN).astype(BF16), dot(hidden_two...  34.5 us
    all_gather x1, waiting for transfers between devices, shards(): lax.all_gather(jnp.concatenate([w_query, w_out.T], axis=1), ('dp', 'ctx',...  28.7 us
    reduce_sum x4, other arithmetic, norm_back(): return (d_values, jnp.sum(upstream * normalized, axis=0))  25.4 us
  transfers between devices with their start and end apart: 8, of which 5 were waited for; matrix products, arithmetic and copies ran while one was open for 25% of the time, Pallas kernels for 21%

profile of v1, /device:TPU:0, one launch (start us, length us, event | category | flops | bytes accessed | tf_op | source)
XLA Modules:
  0.0 1047.8 jit_solution(12052840585919243698)
XLA Ops:
  20.1 23.5 %all-gather.6.cloned.1.call-done = bf16[1152,896]{1,0:T(8,128)(2,1)} async-done(((bf16[144,896]{1,0:T(8,128)(2,1)}), bf16[1152,896]{1,0:T(8,128)(2,1)}) %all-gather.6.cloned.1.call-update) | async-done | bytes 2064400 | tf_op jit(solution)/shard_map/all_gather | solution.py:379
  82.0 28.7 %all-gather.12.cloned.1.call-done = bf16[4608,512]{1,0:T(8,128)(2,1)} async-done(((bf16[144,512]{1,0:T(8,128)(2,1)}), bf16[4608,512]{1,0:T(8,128)(2,1)}) %all-gather.12.cloned.1.call-update) | async-done | bytes 4718608 | tf_op jit(solution)/shard_map/all_gather | solution.py:382
  145.5 35.9 %all-gather.10.cloned.1.call-done = bf16[2,2,2048,256]{3,2,1,0:T(8,128)(2,1)} async-done(((bf16[2,2,512,256]{3,2,1,0:T(8,128)(2,1)}), bf16[2,2,2048,256]{3,2,1,0:T(8,128)(2,1)}) %all-gather.10.cloned.1.call-update) | async-done | bytes 4194320 | tf_op jit(solution)/shard_map/all_gather | solution.py:421
  181.5 20.1 %attend.1 = (bf16[2,2,512,256]{3,2,1,0:T(8,128)(2,1)S(1)}, f32[2,2,512,1]{3,2,1,0:T(8,128)S(1)}) custom-call(bf16[2,2,512,256]{3,2,1,0:T(8,128)(2,1)S(1)} %pad_maximum_fusion.6.q_ref, bf16[2,4096,256]{2,1,0:T(8,128)(2,1)} %bitcast.165, bf16[2,4096,256]{2,1,0:T(8,128)(2,1)} %bitcast.167, s32[2,2,512,1]{3,2,1,0:T(8,128)S(1)} %copy.58.qs_ref, ...), custom_call_target="tpu_custom_call" | custom-call | tf_op jit(solution)/shard_map/attend/pallas_call | solution.py:245
  202.6 72.7 %gather_tp_0.1 = bf16[2048,1024]{1,0:T(8,128)(2,1)} custom-call(bf16[2048,256]{1,0:T(8,128)(2,1)} %bitcast.153), custom_call_target="tpu_custom_call" | custom-call | tf_op jit(solution)/shard_map/gather_tp_0/pallas_call | solution.py:183
  294.9 15.4 %fusion.43 = f32[2048,1728]{0,1:T(8,128)} fusion(bf16[2048,1152]{1,0:T(8,128)(2,1)} %multiply_convert_fusion.3, bf16[1152,5184]{1,0:T(8,128)(2,1)} %all-gather.14.cloned.1.call-done), kind=kOutput, calls=%fused_computation.82 | convolution fusion | flops 8153726976 | bytes 23003136 | tf_op jit(solution)/shard_map/dot_general | solution.py:23
  310.3 24.0 %multiply_convert_fusion.1 = (bf16[2048,1728]{0,1:T(8,128)(2,1)}, f32[2048,1728]{0,1:T(8,128)}) fusion(f32[2048,1728]{0,1:T(8,128)} %fusion.43, bf16[2048,1152]{1,0:T(8,128)(2,1)} %multiply_convert_fusion.3, bf16[1152,5184]{1,0:T(8,128)(2,1)} %all-gather.14.cloned.1.call-done), kind=kOutput, calls=%fused_computation.10 | convolution fusion | flops 8189116416 | bytes 44236800 | tf_op jit(solution)/shard_map/dot_general | solution.py:23
  334.3 13.4 %convolution_convert_fusion.x_ref = bf16[2048,1152]{1,0:T(8,128)(2,1)S(1)} fusion(bf16[2048,1728]{0,1:T(8,128)(2,1)} %get-tuple-element.139, bf16[1152,5184]{1,0:T(8,128)(2,1)} %all-gather.14.cloned.1.call-done), kind=kOutput, calls=%fused_computation.59 | convolution fusion | flops 8156086272 | bytes 15925248 | tf_op jit(solution)/shard_map/dot_general | solution.py:23
  347.7 118.8 %sum_tp_1.1 = bf16[2048,1152]{1,0:T(8,128)(2,1)S(1)} custom-call(bf16[2048,1152]{1,0:T(8,128)(2,1)S(1)} %convolution_convert_fusion.x_ref), custom_call_target="tpu_custom_call" | custom-call | tf_op jit(solution)/shard_map/sum_tp_1/pallas_call | solution.py:113
  474.4 27.8 %multiply_convert_fusion = (bf16[2048,1728]{0,1:T(8,128)(2,1)}, bf16[2048,1728]{0,1:T(8,128)(2,1)}) fusion(f32[2048,1728]{0,1:T(8,128)} %fusion.43, f32[2048,1728]{0,1:T(8,128)} %get-tuple-element.140, bf16[2048,1152]{1,0:T(8,128)(2,1)S(1)} %fusion.14, bf16[1152,5184]{1,0:T(8,128)(2,1)} %all-gather.14.cloned.1.call-done), kind=kOutput, calls=%fused_computation.9 | convolution fusion | flops 8238661632 | bytes 51314688 | tf_op jit(solution)/shard_map/dot_general | solution.py:23
  502.1 15.6 %fusion.41 = f32[2048,1152]{1,0:T(8,128)} fusion(bf16[2048,1728]{0,1:T(8,128)(2,1)} %get-tuple-element.94, bf16[1152,5184]{1,0:T(8,128)(2,1)} %all-gather.14.cloned.1.call-done), kind=kOutput, calls=%fused_computation.80 | convolution fusion | flops 8153726976 | bytes 20643840 | tf_op jit(solution)/shard_map/dot_general | solution.py:23
  517.8 17.7 %add_convert_fusion.x_ref = bf16[2048,1152]{1,0:T(8,128)(2,1)S(1)} fusion(f32[2048,1152]{1,0:T(8,128)} %fusion.41, bf16[2048,1728]{0,1:T(8,128)(2,1)} %get-tuple-element.93, bf16[1152,5184]{1,0:T(8,128)(2,1)} %all-gather.14.cloned.1.call-done), kind=kOutput, calls=%fused_computation.54 | convolution fusion | flops 8158445568 | bytes 25362432 | tf_op jit(solution)/shard_map/dot_general | solution.py:23
  535.5 119.1 %sum_tp_2.1 = bf16[2048,1152]{1,0:T(8,128)(2,1)S(1)} custom-call(bf16[2048,1152]{1,0:T(8,128)(2,1)S(1)} %add_convert_fusion.x_ref), custom_call_target="tpu_custom_call" | custom-call | tf_op jit(solution)/shard_map/sum_tp_2/pallas_call | solution.py:113
  659.8 14.4 %multiply_reduce_fusion = (bf16[1152]{0:T(1024)(128)(2,1)S(1)}, f32[2048]{0:T(1024)S(1)}, f32[2048,1152]{1,0:T(8,128)}, bf16[2048,1152]{1,0:T(8,128)(2,1)}) fusion(f32[2048,1152]{1,0:T(8,128)} %copy-done.5, f32[2048]{0:T(1024)S(1)} %add_rsqrt_fusion.2, f32[1152]{0:T(1024)S(1)} %get-tuple-element.86, f32[2048]{0:T(1024)S(1)} %broadcast_multiply_fusion.2, ...), kind=kLoop, calls=%fused_computation.51 | loop fusion | flops 44823424 | bytes 47243008 | tf_op jit(solution)/shard_map/reduce_sum | solution.py:353
  686.4 24.6 %attend_back.1 = (f32[2,2,512,256]{3,2,1,0:T(8,128)}, bf16[2,4096,512]{2,1,0:T(8,128)(2,1)}) custom-call(bf16[2,2,512,256]{3,2,1,0:T(8,128)(2,1)} %copy-done, bf16[2,4096,256]{2,1,0:T(8,128)(2,1)} %bitcast.166, bf16[2,4096,256]{2,1,0:T(8,128)(2,1)} %bitcast.168, bf16[2,2,512,256]{3,2,1,0:T(8,128)(2,1)} %bitcast.184, f32[2,2,1,512]{3,2,1,0:T(1,128)} %reshape.312.l_ref, ...), custom_call_target="tpu_custom_call" | custom-call | tf_op jit(solution)/shard_map/attend_back/pallas_call | solution.py:316
  711.4 12.9 %convolution_convert_fusion.1 = bf16[1152,1728]{0,1:T(8,128)(2,1)S(1)} fusion(bf16[2048,1728]{0,1:T(8,128)(2,1)} %get-tuple-element.139, bf16[2048,1152]{1,0:T(8,128)(2,1)} %copy-done.8), kind=kOutput, calls=%fused_computation.60 | convolution fusion | flops 8155717632 | bytes 15777792 | tf_op jit(solution)/shard_map/dot_general | solution.py:23
  724.3 13.1 %convolution_convert_fusion.2 = bf16[1152,1728]{0,1:T(8,128)(2,1)S(1)} fusion(bf16[2048,1728]{0,1:T(8,128)(2,1)} %get-tuple-element.93, bf16[2048,1152]{1,0:T(8,128)(2,1)} %multiply_convert_fusion.3), kind=kOutput, calls=%fused_computation.61 | convolution fusion | flops 8155717632 | bytes 15777792 | tf_op jit(solution)/shard_map/dot_general | solution.py:23
  737.4 12.9 %convolution_convert_fusion.3 = bf16[1152,1728]{0,1:T(8,128)(2,1)S(1)} fusion(bf16[2048,1728]{0,1:T(8,128)(2,1)} %get-tuple-element.94, bf16[2048,1152]{1,0:T(8,128)(2,1)} %multiply_convert_fusion.3), kind=kOutput, calls=%fused_computation.62 | convolution fusion | flops 8155717632 | bytes 15777792 | tf_op jit(solution)/shard_map/dot_general | solution.py:23
  750.3 34.5 %pad_maximum_fusion = bf16[1152,5184]{0,1:T(8,128)(2,1)} fusion(bf16[1152,1728]{0,1:T(8,128)(2,1)S(1)} %convolution_convert_fusion.1, bf16[1152,1728]{0,1:T(8,128)(2,1)S(1)} %convolution_convert_fusion.2, bf16[1152,1728]{0,1:T(8,128)(2,1)S(1)} %convolution_convert_fusion.3), kind=kLoop, calls=%fused_computation.16 | loop fusion | flops 35831808 | bytes 23887872 | tf_op jit(solution)/shard_map/concatenate | solution.py:447
  784.9 16.6 %copy.76 = bf16[1152,5184]{1,0:T(8,128)(2,1)} copy(bf16[1152,5184]{0,1:T(8,128)(2,1)} %pad_maximum_fusion) | data formatting | bytes 23887872
  819.6 55.6 %sum_tp_3.1 = bf16[2048,512]{1,0:T(8,128)(2,1)S(1)} custom-call(bf16[2048,512]{1,0:T(8,128)(2,1)S(1)} %bitcast.152), custom_call_target="tpu_custom_call" | custom-call | tf_op jit(solution)/shard_map/sum_tp_3/pallas_call | solution.py:113
  884.8 67.6 %gather_tp_4.1 = bf16[2048,1024]{1,0:T(8,128)(2,1)} custom-call(bf16[2048,256]{1,0:T(8,128)(2,1)} %get-tuple-element.97.x_ref), custom_call_target="tpu_custom_call" | custom-call | tf_op jit(solution)/shard_map/gather_tp_4/pallas_call | solution.py:183
  992.7 13.6 %fusion.31 = f32[2048,1152]{1,0:T(8,128)} fusion(f32[2048,1152]{1,0:T(8,128)} %get-tuple-element.90, bf16[2,1,2,512,1152]{4,3,2,1,0:T(8,128)(2,1)} %param.16, f32[2048,1152]{1,0:T(8,128)} %get-tuple-element.143, f32[2048]{0:T(1024)S(1)} %broadcast_multiply_fusion, f32[1152]{0:T(1024)S(1)} %copy-done.29, f32[2048]{0:T(1024)S(1)} %bitcast.190), kind=kLoop, calls=%fused_computation.48 | loop fusion | flops 16515072 | bytes 33051136 | tf_op jit(solution)/shard_map/add | solution.py:475
  1022.7 12.1 %reduce-scatter.10.cloned.1.call-done = bf16[144,1152]{1,0:T(8,128)(2,1)} async-done(((bf16[1152,1152]{1,0:T(8,128)(2,1)}), bf16[144,1152]{1,0:T(8,128)(2,1)}) %reduce-scatter.10.cloned.1.call-update) | async-done | bytes 331792
  (237 shorter events, 221.4 us)
Async XLA Ops:
  7.2 36.5 %all-gather.6.cloned.1.call-start = ((), (), s32[]{:S(2)}) async-start(), calls=%async_computation.3 | async-start | bytes 2322432 | tf_op jit(solution)/shard_map/all_gather | solution.py:379
  13.1 97.6 %all-gather.12.cloned.1.call-start = ((), (), s32[]{:S(2)}) async-start(), calls=%async_computation.6 | async-start | bytes 4866048 | tf_op jit(solution)/shard_map/all_gather | solution.py:382
  14.7 130.8 %all-gather.8.cloned.1.call-start = ((), (), s32[]{:S(2)}) async-start(), calls=%async_computation.4 | async-start | bytes 5242880 | tf_op jit(solution)/shard_map/all_gather | solution.py:420
  18.2 32.3 %copy-start.30 = (f32[2,4,2,128]{3,1,2,0:T(4,128)}, f32[2,4,2,128]{3,1,2,0:T(4,128)S(1)}, u32[]{:S(2)}) copy-start(f32[2,4,2,128]{3,1,2,0:T(4,128)S(1)} %copy.79) | copy-start | bytes 24580
  20.1 37.4 %copy-start.10 = (f32[1024,128]{1,0:T(8,128)}, f32[1024,128]{1,0:T(8,128)S(1)}, u32[]{:S(2)}) copy-start(f32[1024,128]{1,0:T(8,128)S(1)} %get-tuple-element.135) | copy-start | bytes 1572868
  20.1 37.4 %copy-start.12 = (f32[1024,128]{1,0:T(8,128)}, f32[1024,128]{1,0:T(8,128)S(1)}, u32[]{:S(2)}) copy-start(f32[1024,128]{1,0:T(8,128)S(1)} %get-tuple-element.136) | copy-start | bytes 1572868
  46.6 8.9 copy-start.35
  46.8 8.7 copy-start.37
  59.3 122.2 %all-gather.10.cloned.1.call-start = ((), (), s32[]{:S(2)}) async-start(), calls=%async_computation.5 | async-start | bytes 5242880 | tf_op jit(solution)/shard_map/all_gather | solution.py:421
  62.0 232.9 %all-gather.14.cloned.1.call-start = ((), (), s32[]{:S(2)}) async-start(), calls=%async_computation.7 | async-start | bytes 13602816 | tf_op jit(solution)/shard_map/all_gather | solution.py:388
  65.4 752.1 %reduce-scatter.8.cloned.1.call-start = ((), (), s32[]{:S(2)}) async-start(), calls=%async_computation.8 | async-start | bytes 10485760 | tf_op jit(solution)/shard_map/reduce_scatter | solution.py:463
  82.0 99.5 %copy-start = (bf16[2,2,512,256]{3,2,1,0:T(8,128)(2,1)}, bf16[2,2,512,256]{3,2,1,0:T(8,128)(2,1)S(1)}, u32[]{:S(2)}) copy-start(bf16[2,2,512,256]{3,2,1,0:T(8,128)(2,1)S(1)} %pad_maximum_fusion.6.q_ref) | copy-start | bytes 3145732
  202.6 82.0 %slice-start = ((s8[4718592]{0:T(1024)(128)(4,1)}), s8[524288]{0:T(1024)(128)(4,1)S(1)}, s32[]{:S(2)}) async-start(s8[4718592]{0:T(1024)(128)(4,1)} %bitcast.155), calls=%async_computation.11 | async-start | bytes 1048576
  276.2 8.4 slice-start.1
  310.3 157.3 %slice-start.6 = ((s8[4718592]{0:T(1024)(128)(4,1)}), s8[524288]{0:T(1024)(128)(4,1)S(1)}, s32[]{:S(2)}) async-start(s8[4718592]{0:T(1024)(128)(4,1)} %bitcast.161), calls=%async_computation.17 | async-start | bytes 1048576
  334.3 133.3 %slice-start.7 = ((s8[4718592]{0:T(1024)(128)(4,1)}), s8[4194304]{0:T(1024)(128)(4,1)S(1)}, s32[]{:S(2)}) async-start(s8[4718592]{0:T(1024)(128)(4,1)} %bitcast.161), calls=%async_computation.18 | async-start | bytes 8388608
  474.4 27.8 %copy-start.8 = (bf16[2048,1152]{1,0:T(8,128)(2,1)}, bf16[2048,1152]{1,0:T(8,128)(2,1)S(1)}, u32[]{:S(2)}) copy-start(bf16[2048,1152]{1,0:T(8,128)(2,1)S(1)} %fusion.14) | copy-start | bytes 14155780
  710.9 295.4 %reduce-scatter.12.cloned.1.call-start = ((), (), s32[]{:S(2)}) async-start(), calls=%async_computation.10 | async-start | bytes 13602816
  801.5 10.1 copy-start.34
  801.5 233.3 %reduce-scatter.10.cloned.1.call-start = ((), (), s32[]{:S(2)}) async-start(), calls=%async_computation.9 | async-start | bytes 2985984
  884.8 75.2 %slice-start.2 = ((s8[4718592]{0:T(1024)(128)(4,1)}), s8[524288]{0:T(1024)(128)(4,1)S(1)}, s32[]{:S(2)}) async-start(s8[4718592]{0:T(1024)(128)(4,1)} %bitcast.157), calls=%async_computation.13 | async-start | bytes 1048576
  960.0 16.8 %copy-start.14 = (bf16[2048,256]{1,0:T(8,128)(2,1)S(1)}, bf16[2048,256]{1,0:T(8,128)(2,1)}, u32[]{:S(2)}) copy-start(bf16[2048,256]{1,0:T(8,128)(2,1)} %get-tuple-element.97.x_ref) | copy-start | bytes 3145732
  966.5 14.4 %slice-start.8 = ((s8[4718592]{0:T(1024)(128)(4,1)}), s8[524288]{0:T(1024)(128)(4,1)S(1)}, s32[]{:S(2)}) async-start(s8[4718592]{0:T(1024)(128)(4,1)} %bitcast.172), calls=%async_computation.19 | async-start | bytes 1048576
  966.5 14.5 %copy-start.17 = (bf16[2048,256]{1,0:T(8,128)(2,1)S(1)}, bf16[2048,256]{1,0:T(8,128)(2,1)}, u32[]{:S(2)}) copy-start(bf16[2048,256]{1,0:T(8,128)(2,1)} %get-tuple-element.96) | copy-start | bytes 3145732
  (33 other events, 129.8 us)
Sparse Core Ops, SparseCore 0:
  13.2 30.4 all-gather.5
  47.0 63.5 all-gather.11
  112.2 33.2 all-gather.7
  146.9 34.4 all-gather.9
  183.2 70.0 all-gather.13
  711.1 70.2 reduce-scatter.7
  801.6 89.8 reduce-scatter.11
  992.8 42.0 reduce-scatter.9

commit v2 on v1

--- a/solution.py
+++ b/solution.py
@@ -357,6 +357,407 @@
     return jax.nn.gelu(values, approximate=True)
 
 
+class LineSum:
+    def __init__(self, count, chunk, slots, own, near, far, out, sems):
+        self.count, self.chunk, self.slots = count, chunk, slots
+        self.own, self.near, self.far, self.out = own, near, far, out
+        self.sems = sems
+        self.z = z = lax.axis_index("tp")
+        self.hub = (z == 1) | (z == 2)
+        self.leaf = (z == 0) | (z == 3)
+        self.other_hub = jnp.where(z == 1, 2, 1)
+        self.my_hub = jnp.where(z == 0, 1, 2)
+        self.my_leaf = jnp.where(z == 1, 0, 3)
+
+    def slot(self, c):
+        return pl.ds(pl.multiple_of(lax.rem(c, self.slots) * self.chunk, self.chunk), self.chunk)
+
+    def rows(self, c):
+        return pl.ds(pl.multiple_of(c * self.chunk, self.chunk), self.chunk)
+
+    def inwards(self, c):
+        return pltpu.make_async_remote_copy(
+            self.own.at[self.slot(c)], self.near.at[self.slot(c)], self.sems[0].at[c], self.sems[1].at[c],
+            device_id={"tp": self.my_hub}, device_id_type=MESH)
+
+    def across(self, c):
+        return pltpu.make_async_remote_copy(
+            self.own.at[self.slot(c)], self.far.at[self.slot(c)], self.sems[2].at[c], self.sems[3].at[c],
+            device_id={"tp": self.other_hub}, device_id_type=MESH)
+
+    def outwards(self, c):
+        return pltpu.make_async_remote_copy(
+            self.far.at[self.slot(c)], self.out.at[self.rows(c)], self.sems[4].at[c], self.sems[5].at[c],
+            device_id={"tp": self.my_leaf}, device_id_type=MESH)
+
+    def store(self, c):
+        return pltpu.make_async_copy(self.far.at[self.slot(c)], self.out.at[self.rows(c)], self.sems[6].at[c])
+
+    def put(self, c, value):
+        ring = self.slots < self.count
+        if ring:
+            @pl.when(c >= self.slots)
+            def _():
+                @pl.when(self.leaf)
+                def _():
+                    self.inwards(c - self.slots).wait_send()
+
+                @pl.when(self.hub)
+                def _():
+                    self.across(c - self.slots).wait_send()
+
+        self.own[self.slot(c), :] = value
+
+        @pl.when(self.leaf)
+        def _():
+            if ring:
+                @pl.when(c >= self.slots)
+                def _():
+                    pl.semaphore_wait(self.sems[7], 1)
+            self.inwards(c).start()
+
+    def pair(self, c):
+        ring = self.slots < self.count
+
+        @pl.when(self.hub)
+        def _():
+            self.inwards(c).wait_recv()
+            at = self.slot(c)
+            self.own[at, :] = (self.own[at, :].astype(F32) + self.near[at, :].astype(F32)).astype(BF16)
+            if ring:
+                @pl.when(c < self.count - self.slots)
+                def _():
+                    pl.semaphore_signal(self.sems[7], inc=1, device_id={"tp": self.my_leaf}, device_id_type=MESH)
+
+                @pl.when(c >= self.slots)
+                def _():
+                    pl.semaphore_wait(self.sems[8], 1)
+            self.across(c).start()
+
+    def total(self, c):
+        @pl.when(self.hub)
+        def _():
+            self.across(c).wait_recv()
+            at = self.slot(c)
+            self.far[at, :] = (self.own[at, :].astype(F32) + self.far[at, :].astype(F32)).astype(BF16)
+            self.outwards(c).start()
+            self.store(c).start()
+
+    def retire(self, c):
+        @pl.when(self.hub)
+        def _():
+            self.outwards(c).wait_send()
+            self.store(c).wait()
+            if self.slots < self.count:
+                @pl.when(c < self.count - self.slots)
+                def _():
+                    pl.semaphore_signal(self.sems[8], inc=1, device_id={"tp": self.other_hub}, device_id_type=MESH)
+
+    def finish(self):
+        first = max(0, self.count - self.slots)
+
+        @pl.when(self.leaf)
+        def _():
+            for c in range(self.count):
+                self.outwards(c).wait_recv()
+            for c in range(first, self.count):
+                self.inwards(c).wait_send()
+
+        @pl.when(self.hub)
+        def _():
+            for c in range(first, self.count):
+                self.across(c).wait_send()
+
+
+def line_sum_scratch(count, chunk, slots, cols):
+    dma = pltpu.SemaphoreType.DMA((count,))
+    regular = pltpu.SemaphoreType.REGULAR
+    return [pltpu.VMEM((slots * chunk, cols), BF16)] * 3 + [dma] * 7 + [regular] * 2
+
+
+def gelu_parts(v):
+    c = 0.7978845608028654
+    square = v * v
+    t = jnp.tanh(v * (c + (c * 0.044715) * square))
+    half = 0.5 + 0.5 * t
+    value = v * half
+    slope = half + (0.5 * v) * (1.0 - t * t) * (c + (3.0 * c * 0.044715) * square)
+    return value, slope
+
+
+def column_parts(cols):
+    middle = -(-cols // 256) * 128
+    return [(0, middle), (middle, cols)] if middle < cols else [(0, cols)]
+
+
+def middle_of(x, attn, gain_post_attn):
+    hat, inv = norm_parts(attn.astype(F32))
+    return x.astype(F32) + hat * (1.0 + gain_post_attn), hat, inv
+
+
+def ffn_forward_kernel(tiles, tile, chunk, x_ref, h_ref, gain_ref, wo_ref, wg_ref, wu_ref, wd_ref,
+                       attn_ref, two_ref, gate_ref, up_ref, out_ref, own, near, far, *sems):
+    i = pl.program_id(0)
+    per = tile // chunk
+    line = LineSum(tiles * per, chunk, tiles * per, own, near, far, out_ref, sems)
+
+    @pl.when(i == 0)
+    def _():
+        barrier_line(line.z)
+
+    attn = dot(h_ref[...], wo_ref[...], NT).astype(BF16)
+    attn_ref[...] = attn
+    middle, _, _ = middle_of(x_ref[...], attn, gain_ref[1:2, :])
+    hat, _ = norm_parts(middle)
+    two = (hat * (1.0 + gain_ref[2:3, :])).astype(BF16)
+    two_ref[...] = two
+    part = None
+    for a, b in column_parts(wg_ref.shape[1]):
+        gate = dot(two, wg_ref[:, a:b])
+        up = dot(two, wu_ref[:, a:b])
+        gate_ref[:, a:b] = gate.astype(BF16)
+        up_ref[:, a:b] = up.astype(BF16)
+        value, _ = gelu_parts(gate)
+        more = dot((value * up).astype(BF16), wd_ref[:, a:b], NT)
+        part = more if part is None else part + more
+    for j in range(per):
+        line.put(i * per + j, part[j * chunk : (j + 1) * chunk].astype(BF16))
+
+    @pl.when(i >= 1)
+    def _():
+        for j in range(per):
+            line.pair((i - 1) * per + j)
+
+    @pl.when(i >= 2)
+    def _():
+        for j in range(per):
+            line.total((i - 2) * per + j)
+
+    @pl.when(i == tiles - 1)
+    def _():
+        last = tiles * per
+        for j in range(per):
+            line.pair(last - per + j)
+        for c in range(max(0, last - 2 * per), last):
+            line.total(c)
+        for c in range(last):
+            line.retire(c)
+        line.finish()
+
+
+def whole_block(shape):
+    return pl.BlockSpec(shape, lambda i: (0,) * len(shape), pipeline_mode=pl.Buffered(1))
+
+
+def tile_block(tile, cols):
+    return pl.BlockSpec((tile, cols), lambda i: (i, 0))
+
+
+ANY = pl.BlockSpec(memory_space=pl.ANY)
+
+
+def ffn_forward(x, heads, gains, w_out, w_gate, w_up, w_down_t, ident):
+    rows, width = x.shape
+    hidden = w_gate.shape[1]
+    tile, chunk = 256, 128
+    tiles = rows // tile
+    count = rows // chunk
+    return pl.pallas_call(
+        functools.partial(ffn_forward_kernel, tiles, tile, chunk),
+        grid=(tiles,),
+        out_shape=(
+            jax.ShapeDtypeStruct((rows, width), BF16),
+            jax.ShapeDtypeStruct((rows, width), BF16),
+            jax.ShapeDtypeStruct((rows, hidden), BF16),
+            jax.ShapeDtypeStruct((rows, hidden), BF16),
+            jax.ShapeDtypeStruct((rows, width), BF16),
+        ),
+        in_specs=[tile_block(tile, width), tile_block(tile, heads.shape[1])]
+        + [whole_block(w.shape) for w in (gains, w_out, w_gate, w_up, w_down_t)],
+        out_specs=(tile_block(tile, width), tile_block(tile, width), tile_block(tile, hidden), tile_block(tile, hidden), ANY),
+        scratch_shapes=line_sum_scratch(count, chunk, count, width),
+        compiler_params=pltpu.CompilerParams(
+            collective_id=ident, has_side_effects=True, vmem_limit_bytes=60 * 2**20),
+        name="ffn_forward",
+    )(x, heads, gains, w_out, w_gate, w_up, w_down_t)
+
+
+def ffn_backward_kernel(tiles, tile, chunk, slots, x_ref, attn_ref, dy_ref, ffn_ref, two_ref, gate_ref, up_ref,
+                        gain_ref, wg_ref, wu_ref, wd_ref,
+                        y_ref, dgain_ref, gg_ref, gu_ref, gd_ref, out_ref,
+                        acc_g, acc_u, acc_d, keep_g, keep_u, keep_h, stage, stage_sem, own, near, far, *sems):
+    i = pl.program_id(0)
+    per = tile // chunk
+    last = tiles * per
+    line = LineSum(last, chunk, slots, own, near, far, out_ref, sems)
+
+    @pl.when(i == 0)
+    def _():
+        barrier_line(line.z)
+        for acc in (acc_g, acc_u, acc_d, dgain_ref):
+            acc[...] = jnp.zeros_like(acc)
+
+    middle, _, _ = middle_of(x_ref[...], attn_ref[...], gain_ref[1:2, :])
+    hat, inv = norm_parts(ffn_ref[...].astype(F32))
+    gain = gain_ref[3:4, :]
+    y_ref[...] = (middle + hat * (1.0 + gain)).astype(BF16)
+    d_ffn, d_gain = norm_back(dy_ref[...].astype(F32), hat, inv, gain)
+    dgain_ref[...] += d_gain[None]
+    d_ffn = d_ffn.astype(BF16)
+    part = None
+    for a, b in column_parts(wg_ref.shape[1]):
+        d_hidden = dot(d_ffn, wd_ref[:, a:b])
+        up = up_ref[:, a:b].astype(F32)
+        value, slope = gelu_parts(gate_ref[:, a:b].astype(F32))
+        keep_h[:, a:b] = (value * up).astype(BF16)
+        d_gate = (d_hidden * up * slope).astype(BF16)
+        d_up = (d_hidden * value).astype(BF16)
+        keep_g[:, a:b] = d_gate
+        keep_u[:, a:b] = d_up
+        more = dot(d_gate, wg_ref[:, a:b], NT) + dot(d_up, wu_ref[:, a:b], NT)
+        part = more if part is None else part + more
+    for j in range(per):
+        line.put(i * per + j, part[j * chunk : (j + 1) * chunk].astype(BF16))
+
+    @pl.when(i >= 1)
+    def _():
+        for j in range(per):
+            line.pair((i - 1) * per + j)
+
+    acc_g[...] += dot(two_ref[...], keep_g[...], TN)
+    acc_u[...] += dot(two_ref[...], keep_u[...], TN)
+    acc_d[...] += dot(d_ffn, keep_h[...], TN)
+
+    @pl.when(i >= 2)
+    def _():
+        for j in range(per):
+            line.total((i - 2) * per + j)
+
+    @pl.when(i >= 3)
+    def _():
+        for j in range(per):
+            line.retire((i - 3) * per + j)
+
+    @pl.when(i == tiles - 1)
+    def _():
+        for j in range(per):
+            line.pair(last - per + j)
+        step = stage.shape[1]
+        count = acc_g.shape[0] // step
+
+        def piece(acc, out, k, at):
+            @pl.when(k >= 2)
+            def _():
+                pltpu.make_async_copy(stage.at[at], out.at[pl.ds(0, step)], stage_sem.at[at]).wait()
+            rows = pl.ds(pl.multiple_of(k * step, step), step)
+            stage[at] = acc[rows, :].astype(BF16)
+            pltpu.make_async_copy(stage.at[at], out.at[rows], stage_sem.at[at]).start()
+
+        for acc, out in ((acc_g, gg_ref), (acc_u, gu_ref), (acc_d, gd_ref)):
+            def pieces(k, _):
+                piece(acc, out, k, lax.rem(k, 2))
+                return 0
+
+            lax.fori_loop(0, count, pieces, 0)
+            for at in range(2):
+                pltpu.make_async_copy(stage.at[at], out.at[pl.ds(0, step)], stage_sem.at[at]).wait()
+            if acc is acc_g:
+                for c in range(max(0, last - 2 * per), last - per):
+                    line.total(c)
+            if acc is acc_u:
+                for c in range(last - per, last):
+                    line.total(c)
+        for c in range(max(0, last - 3 * per), last):
+            line.retire(c)
+        line.finish()
+
+
+def ffn_backward(x, attn, dy, ffn, two, gate, up, gains, w_gate, w_up, w_down_t, ident):
+    rows, width = x.shape
+    hidden = w_gate.shape[1]
+    tile, chunk = 256, 128
+    tiles = rows // tile
+    count = rows // chunk
+    slots = min(count, 6)
+    step = 144
+    grad = jax.ShapeDtypeStruct((width, hidden), BF16)
+    acc = pltpu.VMEM((width, hidden), F32)
+    keep = pltpu.VMEM((tile, hidden), BF16)
+    return pl.pallas_call(
+        functools.partial(ffn_backward_kernel, tiles, tile, chunk, slots),
+        grid=(tiles,),
+        out_shape=(
+            jax.ShapeDtypeStruct((rows, width), BF16),
+            jax.ShapeDtypeStruct((1, width), F32),
+            grad, grad, grad,
+            jax.ShapeDtypeStruct((rows, width), BF16),
+        ),
+        in_specs=[tile_block(tile, width)] * 5 + [tile_block(tile, hidden)] * 2
+        + [whole_block(w.shape) for w in (gains, w_gate, w_up, w_down_t)],
+        out_specs=(tile_block(tile, width), pl.BlockSpec((1, width), lambda i: (0, 0)), ANY, ANY, ANY, ANY),
+        scratch_shapes=[acc] * 3 + [keep] * 3
+        + [pltpu.VMEM((2, step, hidden), BF16), pltpu.SemaphoreType.DMA((2,))]
+        + line_sum_scratch(count, chunk, slots, width),
+        compiler_params=pltpu.CompilerParams(
+            collective_id=ident, has_side_effects=True, vmem_limit_bytes=63 * 2**20),
+        name="ffn_backward",
+    )(x, attn, dy, ffn, two, gate, up, gains, w_gate, w_up, w_down_t)
+
+
+def middle_back_kernel(x_ref, attn_ref, dy_ref, d2_ref, h_ref, gain_ref, wo_ref,
+                       dm_ref, dh_ref, delta_ref, dgain_ref, go_ref, acc):
+    i = pl.program_id(0)
+
+    @pl.when(i == 0)
+    def _():
+        acc[...] = jnp.zeros_like(acc)
+        dgain_ref[...] = jnp.zeros_like(dgain_ref)
+
+    middle, attn_hat, attn_inv = middle_of(x_ref[...], attn_ref[...], gain_ref[1:2, :])
+    hat, inv = norm_parts(middle)
+    d_part, d_gain = norm_back(d2_ref[...].astype(F32), hat, inv, gain_ref[2:3, :])
+    dgain_ref[1:2, :] += d_gain[None]
+    d_middle = dy_ref[...].astype(F32) + d_part
+    dm_ref[...] = d_middle
+    d_attn, d_gain = norm_back(d_middle, attn_hat, attn_inv, gain_ref[1:2, :])
+    dgain_ref[0:1, :] += d_gain[None]
+    d_attn = d_attn.astype(BF16)
+    d_heads = dot(d_attn, wo_ref[...]).astype(BF16)
+    dh_ref[...] = d_heads
+    heads = h_ref[...]
+    delta_ref[...] = jnp.sum(d_heads.astype(F32) * heads.astype(F32), axis=1, keepdims=True)
+    acc[...] += dot(d_attn, heads, TN)
+
+    @pl.when(i == pl.num_programs(0) - 1)
+    def _():
+        go_ref[...] = acc[...].astype(BF16)
+
+
+def middle_back(x, attn, dy, d_two, heads, gains, w_out_t):
+    rows, width = x.shape
+    head = heads.shape[1]
+    tile = 256
+    return pl.pallas_call(
+        middle_back_kernel,
+        grid=(rows // tile,),
+        out_shape=(
+            jax.ShapeDtypeStruct((rows, width), F32),
+            jax.ShapeDtypeStruct((rows, head), BF16),
+            jax.ShapeDtypeStruct((rows, 1), F32),
+            jax.ShapeDtypeStruct((2, width), F32),
+            jax.ShapeDtypeStruct((width, head), BF16),
+        ),
+        in_specs=[tile_block(tile, width)] * 4 + [tile_block(tile, head)] + [whole_block(w.shape) for w in (gains, w_out_t)],
+        out_specs=(
+            tile_block(tile, width), tile_block(tile, head), tile_block(tile, 1),
+            pl.BlockSpec((2, width), lambda i: (0, 0)), pl.BlockSpec((width, head), lambda i: (0, 0)),
+        ),
+        scratch_shapes=[pltpu.VMEM((width, head), F32)],
+        compiler_params=pltpu.CompilerParams(vmem_limit_bytes=48 * 2**20),
+        name="middle_back",
+    )(x, attn, dy, d_two, heads, gains, w_out_t)
+
+
 def shards(tokens, segments, cotangent, w_query, w_key, w_value, w_out, w_gate, w_up, w_down,
            g_input, g_post_attn, g_pre_ffn, g_post_ffn, g_query, g_key):
     batches, seq_local, _, size, width = tokens.shape
@@ -385,15 +786,13 @@
     both = both.transpose(0, 2, 3, 1).reshape(width, 2, head, 4).transpose(0, 1, 3, 2)
     query_full = both[:, 0].reshape(width, 4 * head)
     out_full = both[:, 1].reshape(width, 4 * head)
-    ffn = lax.all_gather(
-        jnp.concatenate([w_gate, w_up, w_down.T], axis=1), shared, axis=0, tiled=True)
     mat_qkv = first[:, : 3 * head]
     gain_cols = first[:, 3 * head :].astype(F32)
-    gain_input, gain_post_attn, gain_pre_ffn, gain_post_ffn = (gain_cols[:, i] for i in range(4))
+    gain_rows = gain_cols[:, :8].T
+    gain_input = gain_rows[0]
     short = g_query.shape[0]
     gain_query, gain_key = (
         gain_cols[:, i].reshape(-1, own_rows)[:, :short].reshape(-1) for i in (4, 5))
-    mat_gate, mat_up, mat_down_t = ffn[:, :hidden], ffn[:, hidden : 2 * hidden], ffn[:, 2 * hidden :]
     tp_rank = lax.axis_index("tp")
     mat_out_t = lax.dynamic_slice_in_dim(out_full, tp_rank * head, head, axis=1)
 
@@ -406,7 +805,6 @@
     own_ids = segments.reshape(groups, 2, size)
 
     inputs = tokens.reshape(rows, width).astype(F32)
-    upstream = cotangent.reshape(rows, width).astype(F32)
 
     norm_one, scale_one = norm_parts(inputs)
     hidden_one = (norm_one * (1.0 + gain_input)).astype(BF16)
@@ -421,41 +819,24 @@
     value_all = lax.all_gather(values.reshape(groups, 2, size, head), "ctx", axis=2, tiled=True)
     key_all = key_all.reshape(groups, length, head)
     value_all = value_all.reshape(groups, length, head)
+    stacked = jnp.stack([w_gate, w_up, w_down.T])
+    stacked, key_all = lax.optimization_barrier((stacked, key_all))
+    ffn = lax.all_gather(stacked, shared, axis=1, tiled=True)
+    mat_gate, mat_up, mat_down_t = ffn[0], ffn[1], ffn[2]
     heads, log_mass = attend(queries, key_all, value_all, own_ids[..., None], key_ids[:, None, :])
     heads_own = heads.reshape(rows, head)
     heads_all = gather_tp(heads_own, 0)
-    attn = dot(heads_all, out_full, NT)
-    norm_attn, scale_attn = norm_parts(attn)
-    middle = inputs + norm_attn * (1.0 + gain_post_attn)
-    norm_two, scale_two = norm_parts(middle)
-    hidden_two = (norm_two * (1.0 + gain_pre_ffn)).astype(BF16)
-
-    gate = dot(hidden_two, mat_gate)
-    up = dot(hidden_two, mat_up)
-    activated, gelu_pull = jax.vjp(gelu_tanh, gate)
-    hidden_ffn = (activated * up).astype(BF16)
-    ffn_out = sum_tp(dot(hidden_ffn, mat_down_t, NT).astype(BF16), 1).astype(F32)
-    norm_ffn, scale_ffn = norm_parts(ffn_out)
-    output = (middle + norm_ffn * (1.0 + gain_post_ffn)).astype(BF16)
-    d_ffn, d_gain_post_ffn = norm_back(upstream, norm_ffn, scale_ffn, gain_post_ffn)
-    d_ffn = d_ffn.astype(BF16)
-    d_hidden = dot(d_ffn, mat_down_t)
-    (d_gate,) = gelu_pull(d_hidden * up)
-    d_gate = d_gate.astype(BF16)
-    d_up = (d_hidden * activated).astype(BF16)
-    d_two = sum_tp((dot(d_gate, mat_gate, NT) + dot(d_up, mat_up, NT)).astype(BF16), 2).astype(F32)
-    grad_ffn = jnp.concatenate(
-        [dot(hidden_two, d_gate, TN).astype(BF16), dot(hidden_two, d_up, TN).astype(BF16),
-         dot(d_ffn, hidden_ffn, TN).astype(BF16)], axis=1)
-    grad_ffn = lax.psum_scatter(grad_ffn, shared, scatter_dimension=0, tiled=True).astype(F32)
-    d_part, d_gain_pre_ffn = norm_back(d_two, norm_two, scale_two, gain_pre_ffn)
-    d_middle = upstream + d_part
-    d_attn, d_gain_post_attn = norm_back(d_middle, norm_attn, scale_attn, gain_post_attn)
-    d_attn = d_attn.astype(BF16)
-
-    grad_out_t = dot(d_attn, heads_own, TN)
-    d_heads = dot(d_attn, mat_out_t).astype(BF16)
-    delta = jnp.sum(d_heads.astype(F32) * heads_own.astype(F32), axis=-1)
+    x_rows = tokens.reshape(rows, width)
+    dy_rows = cotangent.reshape(rows, width)
+    attn, hidden_two, gate, up, ffn_out = ffn_forward(
+        x_rows, heads_all, gain_rows, out_full, mat_gate, mat_up, mat_down_t, 1)
+    output, d_gain_post_ffn, grad_gate, grad_up, grad_down_t, d_two = ffn_backward(
+        x_rows, attn, dy_rows, ffn_out, hidden_two, gate, up, gain_rows, mat_gate, mat_up, mat_down_t, 2)
+    grad_ffn = lax.psum_scatter(
+        jnp.stack([grad_gate, grad_up, grad_down_t]), shared, scatter_dimension=1, tiled=True).astype(F32)
+    d_middle, d_heads, delta, d_gain_mid, grad_out_t = middle_back(
+        x_rows, attn, dy_rows, d_two, heads_own, gain_rows, mat_out_t)
+
     d_query, d_kv = attend_back(
         queries, key_all, value_all, d_heads.reshape(groups, 2, size, head),
         log_mass.reshape(groups, 2, 1, size), delta.reshape(groups, 2, 1, size),
@@ -479,11 +860,11 @@
         return jnp.pad(vector.reshape(-1, short), ((0, 0), (0, own_rows - short))).reshape(-1)
 
     d_gains = jnp.stack(
-        [d_gain_input, d_gain_post_attn, d_gain_pre_ffn, d_gain_post_ffn, spread(d_gain_query), spread(d_gain_key)], axis=1)
+        [d_gain_input, d_gain_mid[0], d_gain_mid[1], d_gain_post_ffn[0], spread(d_gain_query), spread(d_gain_key)], axis=1)
     d_gains = jnp.pad(d_gains, ((0, 0), (0, 128 - d_gains.shape[1]))).astype(BF16)
     last = jnp.concatenate(
         [dot(hidden_one, d_q_raw, TN).astype(BF16), dot(hidden_one, d_kv_raw, TN).astype(BF16),
-         grad_out_t.astype(BF16), d_gains], axis=1)
+         grad_out_t, d_gains], axis=1)
     last = lax.psum_scatter(last, shared, scatter_dimension=0, tiled=True).astype(F32)
     g = last[:, 4 * head :]
     return (
@@ -493,9 +874,9 @@
         last[:, head : 2 * head],
         last[:, 2 * head : 3 * head],
         last[:, 3 * head : 4 * head].T,
-        grad_ffn[:, :hidden],
-        grad_ffn[:, hidden : 2 * hidden],
-        grad_ffn[:, 2 * hidden :].T,
+        grad_ffn[0],
+        grad_ffn[1],
+        grad_ffn[2].T,
         g[:, 0],
         g[:, 1],
         g[:, 2],

time: 1060 us -> 964 us (0.909)
  matrix products: 197 us -> 28.2 us
  Pallas kernels: 478 us -> 560 us
  waiting for transfers between devices: 101 us -> 183 us
  other arithmetic: 124 us -> 63.4 us
  local copies, waits for them, and re-layouts: 116 us -> 93.5 us
    pallas_call x0 -> x3, Pallas kernels: none -> 316 us  [the longest x1 155 us: ffn_backward(): pl.pallas_call(functools.partial(ffn_backward_kernel, tiles, tile, chunk,...]
    pallas_call x3 -> x1, Pallas kernels: 293 us -> 59.6 us  [sum_tp(): pl.pallas_call(functools.partial(sum_kernel, n, tile), out_shape=jax.Shap...]
    dot_general x17 -> x5, matrix products: 197 us -> 28.2 us  [dot(): return lax.dot_general(a, b, dims, preferred_element_type=F32)]
    reduce_scatter x1, waiting for transfers between devices: 0.01 us -> 47.3 us  [shards(): lax.psum_scatter(d_kv.reshape(groups, 2, length // 2, 2 * head), 'ctx', s...]
    concatenate x1 -> x0, other arithmetic: 34.5 us -> none  [shards(): jnp.concatenate([dot(hidden_two, d_gate, TN).astype(BF16), dot(hidden_two...]
    all_gather x1, waiting for transfers between devices: 35.9 us -> 3.64 us  [shards(): lax.all_gather(values.reshape(groups, 2, size, head), 'ctx', axis=2, tile...]
    all_gather x1, waiting for transfers between devices: 0.31 us -> 29.7 us  [shards(): lax.all_gather(keys.reshape(groups, 2, size, head), 'ctx', axis=2, tiled=...]
    unnamed x111 -> x89, local copies, waits for them, and re-layouts: 48 us -> 23.8 us
  transfers between devices with their start and end apart: 8 -> 8, of which waited for: 5 -> 6; matrix products, arithmetic and copies ran while one was open for 25% -> 14% of each run, Pallas kernels for 21% -> 23%
where the time goes in v2:
time: 964 us; the launch traced here: 959 us
  Pallas kernels  560 us (58%)
  waiting for transfers between devices  183 us (19%)
  local copies, waits for them, and re-layouts  93.5 us (10%)
  other arithmetic  63.4 us (7%)
  matrix products  28.2 us (3%)
  between operations  15.2 us (2%)
  blocking collectives  15.1 us (2%)
    pallas_call x1, Pallas kernels, ffn_backward(): pl.pallas_call(functools.partial(ffn_backward_kernel, tiles, tile, chunk,...  155 us
    pallas_call x1, Pallas kernels, ffn_forward(): pl.pallas_call(functools.partial(ffn_forward_kernel, tiles, tile, chunk),...  143 us
    pallas_call x2, Pallas kernels, gather_tp(): pl.pallas_call(functools.partial(gather_kernel, n, tile, width), out_shap...  140 us
    pallas_call x1, Pallas kernels, sum_tp(): pl.pallas_call(functools.partial(sum_kernel, n, tile), out_shape=jax.Shap...  59.6 us
    all_gather x1, waiting for transfers between devices, shards(): lax.all_gather(jnp.concatenate([w_query, w_out.T], axis=1), ('dp', 'ctx',...  50.3 us
    reduce_scatter x1, waiting for transfers between devices, shards(): lax.psum_scatter(d_kv.reshape(groups, 2, length // 2, 2 * head), 'ctx', s...  47.3 us
    all_gather x1, waiting for transfers between devices, shards(): lax.all_gather(keys.reshape(groups, 2, size, head), 'ctx', axis=2, tiled=...  29.7 us
    dot_general x5, matrix products, dot(): return lax.dot_general(a, b, dims, preferred_element_type=F32)  28.2 us
  transfers between devices with their start and end apart: 8, of which 6 were waited for; matrix products, arithmetic and copies ran while one was open for 14% of the time, Pallas kernels for 23%

profile of v2, /device:TPU:0, one launch (start us, length us, event | category | flops | bytes accessed | tf_op | source)
XLA Modules:
  0.0 958.7 jit_solution(8286465608727683505)
XLA Ops:
  18.4 25.2 %all-gather.6.cloned.1.call-done = bf16[1152,896]{1,0:T(8,128)(2,1)} async-done(((bf16[144,896]{1,0:T(8,128)(2,1)}), bf16[1152,896]{1,0:T(8,128)(2,1)}) %all-gather.6.cloned.1.call-update) | async-done | bytes 2064400 | tf_op jit(solution)/shard_map/all_gather | solution.py:780
  62.7 29.7 %all-gather.8.cloned.1.call-done = bf16[2,2,2048,256]{3,2,1,0:T(8,128)(2,1)} async-done(((bf16[2,2,512,256]{3,2,1,0:T(8,128)(2,1)}), bf16[2,2,2048,256]{3,2,1,0:T(8,128)(2,1)}) %all-gather.8.cloned.1.call-update) | async-done | bytes 4194320 | tf_op jit(solution)/shard_map/all_gather | solution.py:818
  109.1 50.3 %all-gather.12.cloned.1.call-done = bf16[4608,512]{1,0:T(8,128)(2,1)} async-done(((bf16[144,512]{1,0:T(8,128)(2,1)}), bf16[4608,512]{1,0:T(8,128)(2,1)}) %all-gather.12.cloned.1.call-update) | async-done | bytes 4718608 | tf_op jit(solution)/shard_map/all_gather | solution.py:783
  164.3 7.9 reshape.236
  172.2 10.6 %fusion.24 = (bf16[1152,1,4,256]{3,1,0,2:T(2,128)(2,1)}, bf16[1152,1,4,256]{3,1,0,2:T(2,128)(2,1)S(1)}) fusion(bf16[1152,2,4,256]{3,1,0,2:T(2,128)(2,1)} %bitcast.149), kind=kLoop, calls=%fused_computation.101 | loop fusion | bytes 9437184 | tf_op jit(solution)/shard_map/slice | solution.py:787
  182.8 5.6 copy.96
  194.1 20.1 %attend.1 = (bf16[2,2,512,256]{3,2,1,0:T(8,128)(2,1)S(1)}, f32[2,2,512,1]{3,2,1,0:T(8,128)S(1)}) custom-call(bf16[2,2,512,256]{3,2,1,0:T(8,128)(2,1)S(1)} %pad_maximum_fusion.7.q_ref, bf16[2,4096,256]{2,1,0:T(8,128)(2,1)} %bitcast.153, bf16[2,4096,256]{2,1,0:T(8,128)(2,1)} %bitcast.155, s32[2,2,512,1]{3,2,1,0:T(8,128)S(1)} %copy.94.qs_ref, ...), custom_call_target="tpu_custom_call" | custom-call | tf_op jit(solution)/shard_map/attend/pallas_call | solution.py:245
  218.4 72.6 %gather_tp_0.1.h_ref = bf16[2048,1024]{1,0:T(8,128)(2,1)} custom-call(bf16[2048,256]{1,0:T(8,128)(2,1)} %bitcast.138), custom_call_target="tpu_custom_call" | custom-call | tf_op jit(solution)/shard_map/gather_tp_0/pallas_call | solution.py:183
  291.1 8.9 slice_bitcast_fusion
  300.0 143.2 %ffn_forward.1 = (bf16[2048,1152]{1,0:T(8,128)(2,1)}, bf16[2048,1152]{1,0:T(8,128)(2,1)}, bf16[2048,1728]{1,0:T(8,128)(2,1)}, bf16[2048,1728]{1,0:T(8,128)(2,1)}, bf16[2048,1152]{1,0:T(8,128)(2,1)}) custom-call(bf16[2048,1152]{1,0:T(8,128)(2,1)} %bitcast.142, bf16[2048,1024]{1,0:T(8,128)(2,1)} %gather_tp_0.1.h_ref, f32[8,1152]{1,0:T(8,128)} %copy-done.6, ...), custom_call_target="tpu_custom_call" | custom-call | tf_op jit(solution)/shard_map/ffn_forward/pallas_call | solution.py:565
  443.2 155.2 %ffn_backward.1 = (bf16[2048,1152]{1,0:T(8,128)(2,1)}, f32[1,1152]{1,0:T(1,128)}, bf16[1152,1728]{1,0:T(8,128)(2,1)}, bf16[1152,1728]{1,0:T(8,128)(2,1)}, bf16[1...) custom-call(bf16[2048,1152]{1,0:T(8,128)(2,1)} %bitcast.143, bf16[2048,1152]{1,0:T(8,128)(2,1)} %get-tuple-element.40.attn_ref, ...), custom_call_target="tpu_custom_call" | custom-call | tf_op jit(solution)/shard_map/ffn_backward/pallas_call | solution.py:686
  599.6 17.7 %middle_back.1 = (f32[2048,1152]{1,0:T(8,128)}, bf16[2048,256]{1,0:T(8,128)(2,1)S(1)}, f32[2048,1]{1,0:T(8,128)S(1)}, f32[2,1152]{1,0:T(2,128)S(1)}, bf16[1152,256]{1,0:T(8,128)(2,1)S(1)}) custom-call(bf16[2048,1152]{1,0:T(8,128)(2,1)} %bitcast.144, bf16[2048,1152]{1,0:T(8,128)(2,1)} %get-tuple-element.40.attn_ref, bf16[2048,1152]{1,0:T(8,128)(2,1)} %bitcast.152, ...), custom_call_target="tpu_custom_call" | custom-call | tf_op jit(solution)/shard_map/middle_back/pallas_call | solution.py:740
  619.1 24.6 %attend_back.1 = (f32[2,2,512,256]{3,2,1,0:T(8,128)}, bf16[2,4096,512]{2,1,0:T(8,128)(2,1)}) custom-call(bf16[2,2,512,256]{3,2,1,0:T(8,128)(2,1)} %copy-done, bf16[2,4096,256]{2,1,0:T(8,128)(2,1)} %bitcast.154, bf16[2,4096,256]{2,1,0:T(8,128)(2,1)} %bitcast.156, bf16[2,2,512,256]{3,2,1,0:T(8,128)(2,1)} %bitcast.141, f32[2,2,1,512]{3,2,1,0:T(1,128)} %reshape.249.l_ref, ...), custom_call_target="tpu_custom_call" | custom-call | tf_op jit(solution)/shard_map/attend_back/pallas_call | solution.py:316
  643.7 11.1 %pad_maximum_fusion = bf16[3,1152,1728]{2,1,0:T(8,128)(2,1)} fusion(bf16[1,1152,1728]{2,1,0:T(8,128)(2,1)} %bitcast.167, bf16[1,1152,1728]{2,1,0:T(8,128)(2,1)} %bitcast.166, bf16[1,1152,1728]{2,1,0:T(8,128)(2,1)} %bitcast.165), kind=kLoop, calls=%fused_computation.1 | loop fusion | flops 11943936 | bytes 23887872 | tf_op jit(solution)/shard_map/stack | solution.py:836
  655.0 11.3 %copy.101 = bf16[1152,1,4,256]{0,3,2,1:T(8,128)(2,1)} copy(bf16[1152,1,4,256]{3,1,0,2:T(2,128)(2,1)} %get-tuple-element.153) | data formatting | bytes 4718592 | tf_op jit(solution)/shard_map/slice | solution.py:787
  667.3 47.3 %reduce-scatter.6.cloned.1.call-done = bf16[2,2,512,512]{3,2,1,0:T(8,128)(2,1)} async-done(((bf16[2,2,2048,512]{3,2,1,0:T(8,128)(2,1)}), bf16[2,2,512,512]{3,2,1,0:T(8,128)(2,1)}) %reduce-scatter.6.cloned.1.call-update) | async-done | bytes 2097168 | tf_op jit(solution)/shard_map/reduce_scatter | solution.py:844
  716.3 59.6 %sum_tp_3.1 = bf16[2048,512]{1,0:T(8,128)(2,1)S(1)} custom-call(bf16[2048,512]{1,0:T(8,128)(2,1)S(1)} %bitcast.140), custom_call_target="tpu_custom_call" | custom-call | tf_op jit(solution)/shard_map/sum_tp_3/pallas_call | solution.py:113
  782.3 9.7 %psum.7 = bf16[256]{0:T(256)(128)(2,1)S(1)} all-reduce(f32[256]{0:T(256)S(1)} %get-tuple-element.141), channel_id=1, replica_groups=mesh['dp'=2,'ctx'=4,'tp'=4] {'tp'}, use_global_device_ids=true, to_apply=%region_9.10 | all-reduce | flops 256 | bytes 1536 | tf_op jit(solution)/shard_map/psum | solution.py:857
  797.7 67.4 %gather_tp_4.1 = bf16[2048,1024]{1,0:T(8,128)(2,1)} custom-call(bf16[2048,256]{1,0:T(8,128)(2,1)} %get-tuple-element.150.x_ref), custom_call_target="tpu_custom_call" | custom-call | tf_op jit(solution)/shard_map/gather_tp_4/pallas_call | solution.py:183
  865.2 7.5 fusion.27
  872.8 6.9 multiply_reduce_fusion
  889.3 5.4 fusion.1
  898.2 13.4 %multiply_add_fusion = f32[2048,1152]{1,0:T(8,128)} fusion(f32[2048,1152]{1,0:T(8,128)} %get-tuple-element.47, f32[2048,1152]{1,0:T(8,128)} %get-tuple-element.193, f32[2048]{0:T(1024)S(1)} %broadcast_multiply_fusion, f32[1152]{0:T(1024)S(1)} %fusion.21, f32[2048]{0:T(1024)S(1)} %bitcast.181, bf16[2,1,2,512,1152]{4,3,2,1,0:T(8,128)(2,1)} %param.16), kind=kLoop, calls=%fused_computation.3 | loop fusion | flops 16515072 | bytes 33051136 | tf_op jit(solution)/shard_map/add | solution.py:856
  915.0 26.2 %reduce-scatter.10.cloned.1.call-done = bf16[144,1152]{1,0:T(8,128)(2,1)} async-done(((bf16[1152,1152]{1,0:T(8,128)(2,1)}), bf16[144,1152]{1,0:T(8,128)(2,1)}) %reduce-scatter.10.cloned.1.call-update) | async-done | bytes 331792
  (193 shorter events, 105.9 us)
Async XLA Ops:
  7.2 36.5 %all-gather.6.cloned.1.call-start = ((), (), s32[]{:S(2)}) async-start(), calls=%async_computation.3 | async-start | bytes 2322432 | tf_op jit(solution)/shard_map/all_gather | solution.py:780
  13.1 79.4 %all-gather.8.cloned.1.call-start = ((), (), s32[]{:S(2)}) async-start(), calls=%async_computation.4 | async-start | bytes 5242880 | tf_op jit(solution)/shard_map/all_gather | solution.py:818
  18.4 37.7 %copy-start.14 = (f32[1024,128]{1,0:T(8,128)}, f32[1024,128]{1,0:T(8,128)S(1)}, u32[]{:S(2)}) copy-start(f32[1024,128]{1,0:T(8,128)S(1)} %get-tuple-element.191) | copy-start | bytes 1572868
  18.4 37.7 %copy-start.16 = (f32[1024,128]{1,0:T(8,128)}, f32[1024,128]{1,0:T(8,128)S(1)}, u32[]{:S(2)}) copy-start(f32[1024,128]{1,0:T(8,128)S(1)} %get-tuple-element.192) | copy-start | bytes 1572868
  56.6 4.7 copy-start.26
  57.8 34.7 %copy-start.30 = (s32[2,1,2,512]{3,2,1,0:T(2,128)S(1)}, s32[2,1,2,512]{3,2,1,0:T(2,128)}, u32[]{:S(2)}) copy-start(s32[2,1,2,512]{3,2,1,0:T(2,128)} %param.17) | copy-start | bytes 24580
  57.8 101.6 %all-gather.12.cloned.1.call-start = ((), (), s32[]{:S(2)}) async-start(), calls=%async_computation.6 | async-start | bytes 4866048 | tf_op jit(solution)/shard_map/all_gather | solution.py:783
  58.6 135.6 %all-gather.10.cloned.1.call-start = ((), (), s32[]{:S(2)}) async-start(), calls=%async_computation.5 | async-start | bytes 5242880 | tf_op jit(solution)/shard_map/all_gather | solution.py:819
  61.3 229.7 %all-gather.14.cloned.1.call-start = ((), (), s32[]{:S(2)}) async-start(), calls=%async_computation.7 | async-start | bytes 13934592 | tf_op jit(solution)/shard_map/all_gather | solution.py:824
  92.5 622.2 %reduce-scatter.6.cloned.1.call-start = ((), (), s32[]{:S(2)}) async-start(), calls=%async_computation.8 | async-start | bytes 10485760 | tf_op jit(solution)/shard_map/reduce_scatter | solution.py:844
  109.1 85.0 %copy-start = (bf16[2,2,512,256]{3,2,1,0:T(8,128)(2,1)}, bf16[2,2,512,256]{3,2,1,0:T(8,128)(2,1)S(1)}, u32[]{:S(2)}) copy-start(bf16[2,2,512,256]{3,2,1,0:T(8,128)(2,1)S(1)} %pad_maximum_fusion.7.q_ref) | copy-start | bytes 3145732
  443.2 155.2 %copy-start.7 = (f32[8,1152]{1,0:T(8,128)S(1)}, f32[8,1152]{1,0:T(8,128)}, u32[]{:S(2)}) copy-start(f32[8,1152]{1,0:T(8,128)} %copy-done.6) | copy-start | bytes 110596
  643.7 267.9 %reduce-scatter.8.cloned.1.call-start = ((), (), s32[]{:S(2)}) async-start(), calls=%async_computation.9 | async-start | bytes 13934592 | tf_op jit(solution)/shard_map/reduce_scatter | solution.py:835
  654.9 11.4 %copy-start.9 = (bf16[1152,256]{1,0:T(8,128)(2,1)S(1)}, bf16[1152,256]{1,0:T(8,128)(2,1)}, u32[]{:S(2)}) copy-start(bf16[1152,256]{1,0:T(8,128)(2,1)} %copy-done.8) | copy-start | bytes 1769476
  654.9 286.3 %reduce-scatter.10.cloned.1.call-start = ((), (), s32[]{:S(2)}) async-start(), calls=%async_computation.10 | async-start | bytes 2985984
  655.0 12.4 %copy-start.34 = (f32[1,1152]{1,0:T(1,128)S(1)}, f32[1,1152]{1,0:T(1,128)}, u32[]{:S(2)}) copy-start(f32[1,1152]{1,0:T(1,128)} %get-tuple-element.55) | copy-start | bytes 13828
  797.7 67.4 %copy-start.20 = (bf16[1152,1,4,256]{0,3,2,1:T(8,128)(2,1)S(1)}, bf16[1152,1,4,256]{0,3,2,1:T(8,128)(2,1)}, u32[]{:S(2)}) copy-start(bf16[1152,1,4,256]{0,3,2,1:T(8,128)(2,1)} %copy.101) | copy-start | bytes 7077892
  797.7 75.0 %slice-start = ((s8[4718592]{0:T(1024)(128)(4,1)}), s8[524288]{0:T(1024)(128)(4,1)S(1)}, s32[]{:S(2)}) async-start(s8[4718592]{0:T(1024)(128)(4,1)} %bitcast.145), calls=%async_computation.11 | async-start | bytes 1048576
  865.2 7.6 slice-start.1
  865.2 7.6 copy-start.22
  865.2 7.6 copy-start.24
  865.2 7.6 copy-start.33
  872.8 7.0 copy-start.18
  883.9 5.3 copy-start.19
  (23 other events, 56.0 us)
Sparse Core Ops, SparseCore 0:
  13.2 30.4 all-gather.5
  57.9 34.4 all-gather.7
  95.8 63.5 all-gather.11
  160.8 33.2 all-gather.9
  195.9 71.2 all-gather.13
  643.8 70.8 reduce-scatter.5
  718.8 91.3 reduce-scatter.7
  898.3 42.8 reduce-scatter.9

commit v3 on v2

--- a/solution.py
+++ b/solution.py
@@ -197,9 +197,9 @@
     return jnp.where(t < blocks, t, t + rank + 1)
 
 
-def attend_kernel(blocks, q_ref, k_ref, v_ref, qs_ref, ks_ref, o_ref, l_ref):
+def attend_kernel(blocks, q_ref, kv_ref, qs_ref, ks_ref, o_ref, l_ref):
     rank = lax.axis_index("ctx")
-    size = q_ref.shape[2]
+    size, head = q_ref.shape[2:]
     row = lax.broadcasted_iota(jnp.int32, (size, size), 0)
     col = lax.broadcasted_iota(jnp.int32, (size, size), 1)
     for half in range(2):
@@ -208,8 +208,8 @@
 
         def part(block):
             start = pl.multiple_of(block * size, size)
-            k = k_ref[0, pl.ds(start, size), :]
-            v = v_ref[0, pl.ds(start, size), :]
+            k = kv_ref[0, pl.ds(start, size), :head]
+            v = kv_ref[0, pl.ds(start, size), head:]
             same = qseg == ks_ref[0, :, pl.ds(start, size)]
             return dot(q, k, NT), v, same
 
@@ -238,9 +238,9 @@
         l_ref[0, half] = top + jnp.log(mass)
 
 
-def attend(q, k, v, qseg, kseg):
+def attend(q, kv, qseg, kseg):
     groups, _, size, head = q.shape
-    length = k.shape[1]
+    length = kv.shape[1]
     blocks = length // (2 * size)
     return pl.pallas_call(
         functools.partial(attend_kernel, blocks),
@@ -251,8 +251,7 @@
         ),
         in_specs=[
             pl.BlockSpec((1, 2, size, head), lambda g: (g, 0, 0, 0)),
-            pl.BlockSpec((1, length, head), lambda g: (g, 0, 0)),
-            pl.BlockSpec((1, length, head), lambda g: (g, 0, 0)),
+            pl.BlockSpec((1, length, 2 * head), lambda g: (g, 0, 0)),
             pl.BlockSpec((1, 2, size, 1), lambda g: (g, 0, 0, 0)),
             pl.BlockSpec((1, 1, length), lambda g: (g, 0, 0)),
         ],
@@ -262,10 +261,10 @@
         ),
         compiler_params=pltpu.CompilerParams(vmem_limit_bytes=48 * 2**20),
         name="attend",
-    )(q, k, v, qseg, kseg)
-
-
-def attend_back_kernel(blocks, q_ref, k_ref, v_ref, do_ref, l_ref, d_ref, qs_ref, ks_ref,
+    )(q, kv, qseg, kseg)
+
+
+def attend_back_kernel(blocks, q_ref, kv_ref, do_ref, l_ref, d_ref, qs_ref, ks_ref,
                        dq_ref, dkv_ref, dk_acc, dv_acc):
     rank = lax.axis_index("ctx")
     size = q_ref.shape[2]
@@ -283,8 +282,8 @@
 
         def part(block, own):
             rows = pl.ds(pl.multiple_of(block * size, size), size)
-            k = k_ref[0, rows, :]
-            v = v_ref[0, rows, :]
+            k = kv_ref[0, rows, :head]
+            v = kv_ref[0, rows, head:]
             allowed = ks_ref[0, rows, :] == qseg
             if own:
                 order = (row <= col) if half == 0 else (row >= col)
@@ -306,12 +305,12 @@
     dkv_ref[0, :, head:] = dv_acc[...].astype(BF16)
 
 
-def attend_back(q, k, v, do, log_mass, delta, qseg, kseg):
+def attend_back(q, kv, do, log_mass, delta, qseg, kseg):
     groups, _, size, head = q.shape
-    length = k.shape[1]
+    length = kv.shape[1]
     blocks = length // (2 * size)
     halves = pl.BlockSpec((1, 2, size, head), lambda g: (g, 0, 0, 0))
-    whole = pl.BlockSpec((1, length, head), lambda g: (g, 0, 0))
+    whole = pl.BlockSpec((1, length, 2 * head), lambda g: (g, 0, 0))
     line = pl.BlockSpec((1, 2, 1, size), lambda g: (g, 0, 0, 0))
     return pl.pallas_call(
         functools.partial(attend_back_kernel, blocks),
@@ -320,13 +319,13 @@
             jax.ShapeDtypeStruct(q.shape, F32),
             jax.ShapeDtypeStruct((groups, length, 2 * head), BF16),
         ),
-        in_specs=[halves, whole, whole, halves, line, line, line,
+        in_specs=[halves, whole, halves, line, line, line,
                   pl.BlockSpec((1, length, 1), lambda g: (g, 0, 0))],
         out_specs=(halves, pl.BlockSpec((1, length, 2 * head), lambda g: (g, 0, 0))),
         scratch_shapes=[pltpu.VMEM((length, head), F32)] * 2,
         compiler_params=pltpu.CompilerParams(vmem_limit_bytes=56 * 2**20),
         name="attend_back",
-    )(q, k, v, do, log_mass, delta, qseg, kseg)
+    )(q, kv, do, log_mass, delta, qseg, kseg)
 
 
 def angles(position, half_size, full_size):
@@ -495,24 +494,45 @@
     return x.astype(F32) + hat * (1.0 + gain_post_attn), hat, inv
 
 
-def ffn_forward_kernel(tiles, tile, chunk, x_ref, h_ref, gain_ref, wo_ref, wg_ref, wu_ref, wd_ref,
-                       attn_ref, two_ref, gate_ref, up_ref, out_ref, own, near, far, *sems):
+def load_ffn_weights(weights, refs, sem):
+    wide = refs[0].shape[1]
+    base = weights.shape[1] - 3 * wide
+    return [
+        pltpu.make_async_copy(weights.at[:, pl.ds(base + j * wide, wide)], ref, sem.at[j])
+        for j, ref in enumerate(refs)
+    ]
+
+
+def ffn_forward_kernel(tiles, tile, chunk, hidden, x_ref, h0_ref, h1_ref, gain_ref, w_ref,
+                       attn_ref, two_ref, gate_ref, up_ref, out_ref, wo_ref, wg_ref, wu_ref, wd_ref, w_sem, own, near, far, *sems):
     i = pl.program_id(0)
     per = tile // chunk
     line = LineSum(tiles * per, chunk, tiles * per, own, near, far, out_ref, sems)
+    head = wo_ref.shape[1] // 4
 
     @pl.when(i == 0)
     def _():
+        copies = load_ffn_weights(w_ref, (wg_ref, wu_ref, wd_ref), w_sem)
+        copies += [
+            pltpu.make_async_copy(
+                w_ref.at[:, pl.ds((2 * j + 1) * head, head)], wo_ref.at[:, pl.ds(j * head, head)], w_sem.at[3 + j])
+            for j in range(4)
+        ]
+        for copy in copies:
+            copy.start()
         barrier_line(line.z)
-
-    attn = dot(h_ref[...], wo_ref[...], NT).astype(BF16)
+        for copy in copies:
+            copy.wait()
+
+    heads = jnp.where(i < tiles // 2, h0_ref[...], h1_ref[...])
+    attn = dot(heads, wo_ref[...], NT).astype(BF16)
     attn_ref[...] = attn
     middle, _, _ = middle_of(x_ref[...], attn, gain_ref[1:2, :])
     hat, _ = norm_parts(middle)
     two = (hat * (1.0 + gain_ref[2:3, :])).astype(BF16)
     two_ref[...] = two
     part = None
-    for a, b in column_parts(wg_ref.shape[1]):
+    for a, b in column_parts(hidden):
         gate = dot(two, wg_ref[:, a:b])
         up = dot(two, wu_ref[:, a:b])
         gate_ref[:, a:b] = gate.astype(BF16)
@@ -556,14 +576,20 @@
 ANY = pl.BlockSpec(memory_space=pl.ANY)
 
 
-def ffn_forward(x, heads, gains, w_out, w_gate, w_up, w_down_t, ident):
+def wide_of(hidden):
+    return -(-hidden // 128) * 128
+
+
+def ffn_forward(x, heads, gains, weights, hidden, ident):
     rows, width = x.shape
-    hidden = w_gate.shape[1]
+    all_heads = heads[0].shape[1]
     tile, chunk = 256, 128
     tiles = rows // tile
+    half = tiles // 2
     count = rows // chunk
+    wide = wide_of(hidden)
     return pl.pallas_call(
-        functools.partial(ffn_forward_kernel, tiles, tile, chunk),
+        functools.partial(ffn_forward_kernel, tiles, tile, chunk, hidden),
         grid=(tiles,),
         out_shape=(
             jax.ShapeDtypeStruct((rows, width), BF16),
@@ -572,19 +598,26 @@
             jax.ShapeDtypeStruct((rows, hidden), BF16),
             jax.ShapeDtypeStruct((rows, width), BF16),
         ),
-        in_specs=[tile_block(tile, width), tile_block(tile, heads.shape[1])]
-        + [whole_block(w.shape) for w in (gains, w_out, w_gate, w_up, w_down_t)],
+        in_specs=[
+            tile_block(tile, width),
+            pl.BlockSpec((tile, all_heads), lambda i: (jnp.minimum(i, half - 1), 0)),
+            pl.BlockSpec((tile, all_heads), lambda i: (jnp.maximum(i - half, 0), 0)),
+            whole_block(gains.shape),
+            ANY,
+        ],
         out_specs=(tile_block(tile, width), tile_block(tile, width), tile_block(tile, hidden), tile_block(tile, hidden), ANY),
-        scratch_shapes=line_sum_scratch(count, chunk, count, width),
+        scratch_shapes=[pltpu.VMEM((width, all_heads), BF16)] + [pltpu.VMEM((width, wide), BF16)] * 3
+        + [pltpu.SemaphoreType.DMA((7,))]
+        + line_sum_scratch(count, chunk, count, width),
         compiler_params=pltpu.CompilerParams(
             collective_id=ident, has_side_effects=True, vmem_limit_bytes=60 * 2**20),
         name="ffn_forward",
-    )(x, heads, gains, w_out, w_gate, w_up, w_down_t)
-
-
-def ffn_backward_kernel(tiles, tile, chunk, slots, x_ref, attn_ref, dy_ref, ffn_ref, two_ref, gate_ref, up_ref,
-                        gain_ref, wg_ref, wu_ref, wd_ref,
-                        y_ref, dgain_ref, gg_ref, gu_ref, gd_ref, out_ref,
+    )(x, heads[0], heads[1], gains, weights)
+
+
+def ffn_backward_kernel(tiles, tile, chunk, slots, hidden, x_ref, attn_ref, dy_ref, ffn_ref, two_ref, gate_ref, up_ref,
+                        gain_ref, w_ref,
+                        y_ref, dgain_ref, grad_ref, out_ref, wg_ref, wu_ref, wd_ref, w_sem,
                         acc_g, acc_u, acc_d, keep_g, keep_u, keep_h, stage, stage_sem, own, near, far, *sems):
     i = pl.program_id(0)
     per = tile // chunk
@@ -593,9 +626,14 @@
 
     @pl.when(i == 0)
     def _():
+        copies = load_ffn_weights(w_ref, (wg_ref, wu_ref, wd_ref), w_sem)
+        for copy in copies:
+            copy.start()
         barrier_line(line.z)
         for acc in (acc_g, acc_u, acc_d, dgain_ref):
             acc[...] = jnp.zeros_like(acc)
+        for copy in copies:
+            copy.wait()
 
     middle, _, _ = middle_of(x_ref[...], attn_ref[...], gain_ref[1:2, :])
     hat, inv = norm_parts(ffn_ref[...].astype(F32))
@@ -605,7 +643,7 @@
     dgain_ref[...] += d_gain[None]
     d_ffn = d_ffn.astype(BF16)
     part = None
-    for a, b in column_parts(wg_ref.shape[1]):
+    for a, b in column_parts(hidden):
         d_hidden = dot(d_ffn, wd_ref[:, a:b])
         up = up_ref[:, a:b].astype(F32)
         value, slope = gelu_parts(gate_ref[:, a:b].astype(F32))
@@ -653,7 +691,7 @@
             stage[at] = acc[rows, :].astype(BF16)
             pltpu.make_async_copy(stage.at[at], out.at[rows], stage_sem.at[at]).start()
 
-        for acc, out in ((acc_g, gg_ref), (acc_u, gu_ref), (acc_d, gd_ref)):
+        for acc, out in ((acc_g, grad_ref.at[0]), (acc_u, grad_ref.at[1]), (acc_d, grad_ref.at[2])):
             def pieces(k, _):
                 piece(acc, out, k, lax.rem(k, 2))
                 return 0
@@ -672,44 +710,49 @@
         line.finish()
 
 
-def ffn_backward(x, attn, dy, ffn, two, gate, up, gains, w_gate, w_up, w_down_t, ident):
+def ffn_backward(x, attn, dy, ffn, two, gate, up, gains, weights, ident):
     rows, width = x.shape
-    hidden = w_gate.shape[1]
+    hidden = gate.shape[1]
+    wide = wide_of(hidden)
     tile, chunk = 256, 128
     tiles = rows // tile
     count = rows // chunk
     slots = min(count, 6)
     step = 144
-    grad = jax.ShapeDtypeStruct((width, hidden), BF16)
     acc = pltpu.VMEM((width, hidden), F32)
     keep = pltpu.VMEM((tile, hidden), BF16)
     return pl.pallas_call(
-        functools.partial(ffn_backward_kernel, tiles, tile, chunk, slots),
+        functools.partial(ffn_backward_kernel, tiles, tile, chunk, slots, hidden),
         grid=(tiles,),
         out_shape=(
             jax.ShapeDtypeStruct((rows, width), BF16),
             jax.ShapeDtypeStruct((1, width), F32),
-            grad, grad, grad,
+            jax.ShapeDtypeStruct((3, width, hidden), BF16),
             jax.ShapeDtypeStruct((rows, width), BF16),
         ),
         in_specs=[tile_block(tile, width)] * 5 + [tile_block(tile, hidden)] * 2
-        + [whole_block(w.shape) for w in (gains, w_gate, w_up, w_down_t)],
-        out_specs=(tile_block(tile, width), pl.BlockSpec((1, width), lambda i: (0, 0)), ANY, ANY, ANY, ANY),
-        scratch_shapes=[acc] * 3 + [keep] * 3
+        + [whole_block(gains.shape), ANY],
+        out_specs=(tile_block(tile, width), pl.BlockSpec((1, width), lambda i: (0, 0)), ANY, ANY),
+        scratch_shapes=[pltpu.VMEM((width, wide), BF16)] * 3 + [pltpu.SemaphoreType.DMA((3,))] + [acc] * 3 + [keep] * 3
         + [pltpu.VMEM((2, step, hidden), BF16), pltpu.SemaphoreType.DMA((2,))]
         + line_sum_scratch(count, chunk, slots, width),
         compiler_params=pltpu.CompilerParams(
             collective_id=ident, has_side_effects=True, vmem_limit_bytes=63 * 2**20),
         name="ffn_backward",
-    )(x, attn, dy, ffn, two, gate, up, gains, w_gate, w_up, w_down_t)
-
-
-def middle_back_kernel(x_ref, attn_ref, dy_ref, d2_ref, h_ref, gain_ref, wo_ref,
-                       dm_ref, dh_ref, delta_ref, dgain_ref, go_ref, acc):
+    )(x, attn, dy, ffn, two, gate, up, gains, weights)
+
+
+def middle_back_kernel(x_ref, attn_ref, dy_ref, d2_ref, h_ref, gain_ref, w_ref,
+                       dm_ref, dh_ref, delta_ref, dgain_ref, go_ref, acc, wo_ref, w_sem):
     i = pl.program_id(0)
 
     @pl.when(i == 0)
     def _():
+        head = wo_ref.shape[1]
+        at = pl.multiple_of((2 * lax.axis_index("tp") + 1) * head, head)
+        copy = pltpu.make_async_copy(w_ref.at[:, pl.ds(at, head)], wo_ref, w_sem)
+        copy.start()
+        copy.wait()
         acc[...] = jnp.zeros_like(acc)
         dgain_ref[...] = jnp.zeros_like(dgain_ref)
 
@@ -733,7 +776,7 @@
         go_ref[...] = acc[...].astype(BF16)
 
 
-def middle_back(x, attn, dy, d_two, heads, gains, w_out_t):
+def middle_back(x, attn, dy, d_two, heads, gains, weights):
     rows, width = x.shape
     head = heads.shape[1]
     tile = 256
@@ -747,15 +790,15 @@
             jax.ShapeDtypeStruct((2, width), F32),
             jax.ShapeDtypeStruct((width, head), BF16),
         ),
-        in_specs=[tile_block(tile, width)] * 4 + [tile_block(tile, head)] + [whole_block(w.shape) for w in (gains, w_out_t)],
+        in_specs=[tile_block(tile, width)] * 4 + [tile_block(tile, head)] + [whole_block(gains.shape), ANY],
         out_specs=(
             tile_block(tile, width), tile_block(tile, head), tile_block(tile, 1),
             pl.BlockSpec((2, width), lambda i: (0, 0)), pl.BlockSpec((width, head), lambda i: (0, 0)),
         ),
-        scratch_shapes=[pltpu.VMEM((width, head), F32)],
+        scratch_shapes=[pltpu.VMEM((width, head), F32), pltpu.VMEM((width, head), BF16), pltpu.SemaphoreType.DMA],
         compiler_params=pltpu.CompilerParams(vmem_limit_bytes=48 * 2**20),
         name="middle_back",
-    )(x, attn, dy, d_two, heads, gains, w_out_t)
+    )(x, attn, dy, d_two, heads, gains, weights)
 
 
 def shards(tokens, segments, cotangent, w_query, w_key, w_value, w_out, w_gate, w_up, w_down,
@@ -775,34 +818,40 @@
     def column(gain):
         return jnp.pad(gain, (0, own_rows - gain.shape[0]))[:, None]
 
-    gains = jnp.concatenate([column(g) for g in (g_input, g_post_attn, g_pre_ffn, g_post_ffn, g_query, g_key)], axis=1)
-    gains = jnp.pad(gains, ((0, 0), (0, 128 - gains.shape[1])))
+    own_ids = segments.reshape(groups, 2, size)
+    id_cols = -(-own_ids.size // own_rows)
+    ids = jnp.pad(own_ids.reshape(-1), (0, own_rows * id_cols - own_ids.size)).reshape(own_rows, id_cols)
+    extra = jnp.concatenate(
+        [column(g) for g in (g_input, g_post_attn, g_pre_ffn, g_post_ffn, g_query, g_key)] + [ids.astype(BF16)], axis=1)
+    extra = jnp.pad(extra, ((0, 0), (0, 128 - extra.shape[1])))
     first = lax.all_gather(
-        jnp.concatenate([w_query, w_key, w_value, gains], axis=1), shared, axis=0, tiled=True)
-    key_ids = lax.all_gather(segments, "ctx", axis=3, tiled=True).reshape(groups, length)
-    both = lax.all_gather(
-        jnp.concatenate([w_query, w_out.T], axis=1), ("dp", "ctx", "tp"), axis=0, tiled=True)
-    both = both.reshape(width // own_rows, 4, own_rows, 2 * head)
-    both = both.transpose(0, 2, 3, 1).reshape(width, 2, head, 4).transpose(0, 1, 3, 2)
-    query_full = both[:, 0].reshape(width, 4 * head)
-    out_full = both[:, 1].reshape(width, 4 * head)
+        jnp.concatenate([w_query, w_key, w_value, extra], axis=1), shared, axis=0, tiled=True)
     mat_qkv = first[:, : 3 * head]
-    gain_cols = first[:, 3 * head :].astype(F32)
-    gain_rows = gain_cols[:, :8].T
+    side = first[:, 3 * head :]
+    gain_cols = side[:, :8].astype(F32)
+    gain_rows = gain_cols.T
     gain_input = gain_rows[0]
     short = g_query.shape[0]
     gain_query, gain_key = (
         gain_cols[:, i].reshape(-1, own_rows)[:, :short].reshape(-1) for i in (4, 5))
-    tp_rank = lax.axis_index("tp")
-    mat_out_t = lax.dynamic_slice_in_dim(out_full, tp_rank * head, head, axis=1)
+    ids = side[:, 6 : 6 + id_cols].reshape(-1, ctx, own_rows * id_cols)[:, :, : own_ids.size]
+    ids = lax.dynamic_index_in_dim(ids, lax.axis_index("dp"), 0, keepdims=False).astype(jnp.int32)
+    key_ids = ids.reshape(ctx, groups, 2, size).transpose(1, 2, 0, 3).reshape(groups, length)
+    key_ids = jnp.where(key_ids == 0, -1, key_ids)
+
+    def rows_of_16(w):
+        return jnp.pad(w, ((0, -own_rows % 16), (0, 0)))
+
+    wide = wide_of(hidden)
+    line = gather_tp(rows_of_16(jnp.concatenate([w_query, w_out.T], axis=1)), 5)[:own_rows]
+    second = jnp.concatenate(
+        [line] + [jnp.pad(w, ((0, 0), (0, wide - hidden))) for w in (w_gate, w_up, w_down.T)], axis=1)
 
     offsets = rank * size + jnp.arange(size, dtype=jnp.int32)
     position = jnp.concatenate([offsets, length - 1 - offsets]).astype(F32)
     cosine, sine = angles(position, head // 2, head)
     cosine = jnp.broadcast_to(cosine, (groups, per_group, head // 2)).reshape(rows, head // 2)
     sine = jnp.broadcast_to(sine, (groups, per_group, head // 2)).reshape(rows, head // 2)
-    key_ids = jnp.where(key_ids == 0, -1, key_ids)
-    own_ids = segments.reshape(groups, 2, size)
 
     inputs = tokens.reshape(rows, width).astype(F32)
 
@@ -815,42 +864,44 @@
     keys = rotate(k_hat * (1.0 + gain_key), cosine, sine).astype(BF16)
     values = raw[:, 2 * head :].astype(BF16)
     queries = queries.reshape(groups, 2, size, head)
-    key_all = lax.all_gather(keys.reshape(groups, 2, size, head), "ctx", axis=2, tiled=True)
-    value_all = lax.all_gather(values.reshape(groups, 2, size, head), "ctx", axis=2, tiled=True)
-    key_all = key_all.reshape(groups, length, head)
-    value_all = value_all.reshape(groups, length, head)
-    stacked = jnp.stack([w_gate, w_up, w_down.T])
-    stacked, key_all = lax.optimization_barrier((stacked, key_all))
-    ffn = lax.all_gather(stacked, shared, axis=1, tiled=True)
-    mat_gate, mat_up, mat_down_t = ffn[0], ffn[1], ffn[2]
-    heads, log_mass = attend(queries, key_all, value_all, own_ids[..., None], key_ids[:, None, :])
-    heads_own = heads.reshape(rows, head)
-    heads_all = gather_tp(heads_own, 0)
+    pairs = jnp.concatenate([keys, values], axis=1).reshape(batches, seq_local, 2, size, 2 * head)
+    kv = [lax.all_gather(pairs[m], "ctx", axis=2, tiled=True).reshape(seq_local, length, 2 * head) for m in range(batches)]
+    *kv, second = lax.optimization_barrier((*kv, second))
+    weights = lax.all_gather(second, shared, axis=0, tiled=True)
+    heads, heads_all, log_mass = [], [], []
+    for m in range(batches):
+        part = slice(m * seq_local, (m + 1) * seq_local)
+        out, log = attend(queries[part], kv[m], own_ids[part, :, :, None], key_ids[part, None, :])
+        heads.append(out.reshape(rows // batches, head))
+        heads_all.append(gather_tp(heads[m], m * 6))
+        log_mass.append(log)
+    heads_own = jnp.concatenate(heads)
+    log_mass = jnp.concatenate(log_mass)
     x_rows = tokens.reshape(rows, width)
     dy_rows = cotangent.reshape(rows, width)
-    attn, hidden_two, gate, up, ffn_out = ffn_forward(
-        x_rows, heads_all, gain_rows, out_full, mat_gate, mat_up, mat_down_t, 1)
-    output, d_gain_post_ffn, grad_gate, grad_up, grad_down_t, d_two = ffn_backward(
-        x_rows, attn, dy_rows, ffn_out, hidden_two, gate, up, gain_rows, mat_gate, mat_up, mat_down_t, 2)
-    grad_ffn = lax.psum_scatter(
-        jnp.stack([grad_gate, grad_up, grad_down_t]), shared, scatter_dimension=1, tiled=True).astype(F32)
+    attn, hidden_two, gate, up, ffn_out = ffn_forward(x_rows, heads_all, gain_rows, weights, hidden, 1)
+    output, d_gain_post_ffn, grad_ffn, d_two = ffn_backward(
+        x_rows, attn, dy_rows, ffn_out, hidden_two, gate, up, gain_rows, weights, 2)
+    grad_ffn = lax.psum_scatter(grad_ffn, shared, scatter_dimension=1, tiled=True).astype(F32)
     d_middle, d_heads, delta, d_gain_mid, grad_out_t = middle_back(
-        x_rows, attn, dy_rows, d_two, heads_own, gain_rows, mat_out_t)
+        x_rows, attn, dy_rows, d_two, heads_own, gain_rows, weights)
 
     d_query, d_kv = attend_back(
-        queries, key_all, value_all, d_heads.reshape(groups, 2, size, head),
+        queries, jnp.concatenate(kv), d_heads.reshape(groups, 2, size, head),
         log_mass.reshape(groups, 2, 1, size), delta.reshape(groups, 2, 1, size),
         own_ids[:, :, None, :], key_ids[:, :, None])
     d_kv = lax.psum_scatter(
         d_kv.reshape(groups, 2, length // 2, 2 * head), "ctx", scatter_dimension=2, tiled=True)
-    d_kv = sum_tp(d_kv.reshape(rows, 2 * head), 3).astype(F32)
     d_q_rot = rotate(d_query.reshape(rows, head), cosine, -sine)
     d_q_raw, d_gain_query = norm_back(d_q_rot, q_hat, q_scale, gain_query)
     d_q_raw = d_q_raw.astype(BF16)
     d_q_all = gather_tp(d_q_raw, 4)
+    d_kv, d_q_all = lax.optimization_barrier((d_kv, d_q_all))
+    d_kv = sum_tp(d_kv.reshape(rows, 2 * head), 3).astype(F32)
     d_k_rot = rotate(d_kv[:, :head], cosine, -sine)
     d_k_raw, d_gain_key = norm_back(d_k_rot, k_hat, k_scale, gain_key)
     d_kv_raw = jnp.concatenate([d_k_raw.astype(BF16), d_kv[:, head:].astype(BF16)], axis=1)
+    query_full = weights[:, : 8 * head].reshape(width, 4, 2, head)[:, :, 0].reshape(width, 4 * head)
     d_one = dot(d_q_all, query_full, NT) + dot(d_kv_raw, mat_qkv[:, head:], NT)
     d_part, d_gain_input = norm_back(d_one, norm_one, scale_one, gain_input)
     d_tokens = d_middle + d_part

time: 964 us -> 871 us (0.904)
  waiting for transfers between devices: 183 us -> 103 us
  local copies, waits for them, and re-layouts: 93.5 us -> 72.7 us
    reduce_scatter x1, waiting for transfers between devices: 47.3 us -> 0.01 us  [shards(): lax.psum_scatter(d_kv.reshape(groups, 2, length // 2, 2 * head), 'ctx', s...]
    all_gather x5 -> x4, waiting for transfers between devices: 109 us -> 76 us  [the longest x2 50.8 us: shards(): lax.all_gather(pairs[m], 'ctx', axis=2, tiled=True)]
    slice x4 -> x5, local copies, waits for them, and re-layouts: 28.5 us -> 9 us  [the longest x1 5.36 us: shards(): weights[:, :8 * head].reshape(width, 4, 2, head)[:, :, 0]]
    pallas_call x2 -> x4, Pallas kernels: 140 us -> 159 us  [gather_tp(): pl.pallas_call(functools.partial(gather_kernel, n, tile, width), out_shap...]
    unnamed x89 -> x83, local copies, waits for them, and re-layouts: 23.8 us -> 36 us
    another operation x4 -> x2, other arithmetic: 13 us -> 1.52 us  [the longest x1 11.1 us: shards(): jnp.stack([grad_gate, grad_up, grad_down_t])]
    concatenate x1 -> x5, other arithmetic: 1.69 us -> 12.9 us  [the longest x1 7.57 us: shards(): jnp.concatenate(kv)]
    pallas_call x1, Pallas kernels: 155 us -> 145 us  [ffn_backward(): pl.pallas_call(functools.partial(ffn_backward_kernel, tiles, tile, chunk,...]
  transfers between devices with their start and end apart: 8 -> 7, of which waited for: 6 -> 4; matrix products, arithmetic and copies ran while one was open for 14% -> 14% of each run, Pallas kernels for 23% -> 27%
where the time goes in v3:
time: 871 us; the launch traced here: 861 us
  Pallas kernels  566 us (65%)
  waiting for transfers between devices  103 us (12%)
  local copies, waits for them, and re-layouts  72.7 us (8%)
  other arithmetic  65.1 us (7%)
  matrix products  27.8 us (3%)
  between operations  15.3 us (2%)
  blocking collectives  10.9 us (1%)
    pallas_call x4, Pallas kernels, gather_tp(): pl.pallas_call(functools.partial(gather_kernel, n, tile, width), out_shap...  159 us
    pallas_call x1, Pallas kernels, ffn_backward(): pl.pallas_call(functools.partial(ffn_backward_kernel, tiles, tile, chunk,...  145 us
    pallas_call x1, Pallas kernels, ffn_forward(): pl.pallas_call(functools.partial(ffn_forward_kernel, tiles, tile, chunk,...  142 us
    pallas_call x1, Pallas kernels, sum_tp(): pl.pallas_call(functools.partial(sum_kernel, n, tile), out_shape=jax.Shap...  53.9 us
    all_gather x2, waiting for transfers between devices, shards(): lax.all_gather(pairs[m], 'ctx', axis=2, tiled=True)  50.8 us
    unnamed x83, local copies, waits for them, and re-layouts  36 us
    dot_general x5, matrix products, dot(): return lax.dot_general(a, b, dims, preferred_element_type=F32)  27.8 us
    unnamed x8, waiting for transfers between devices  26.5 us
  transfers between devices with their start and end apart: 7, of which 4 were waited for; matrix products, arithmetic and copies ran while one was open for 14% of the time, Pallas kernels for 27%

profile of v3, /device:TPU:0, one launch (start us, length us, event | category | flops | bytes accessed | tf_op | source)
XLA Modules:
  0.0 861.1 jit_solution(12336455098957611361)
XLA Ops:
  19.9 25.2 %all-gather.5.cloned.1.call-done = bf16[1152,896]{1,0:T(8,128)(2,1)} async-done(((bf16[144,896]{1,0:T(8,128)(2,1)}), bf16[1152,896]{1,0:T(8,128)(2,1)}) %all-gather.5.cloned.1.call-update) | async-done | bytes 2064400 | tf_op jit(solution)/shard_map/all_gather | solution.py:827
  65.0 16.6 %gather_tp_5.1 = bf16[144,2048]{1,0:T(8,128)(2,1)} custom-call(bf16[144,512]{1,0:T(8,128)(2,1)} %pad_maximum_fusion.10.x_ref), custom_call_target="tpu_custom_call" | custom-call | tf_op jit(solution)/shard_map/gather_tp_5/pallas_call | solution.py:183
  84.0 14.1 %all-gather.7.cloned.1.call-done = bf16[1,2,2048,512]{3,2,1,0:T(8,128)(2,1)} async-done(((bf16[1,2,512,512]{3,2,1,0:T(8,128)(2,1)}), bf16[1,2,2048,512]{3,2,1,0:T(8,128)(2,1)}) %all-gather.7.cloned.1.call-update) | async-done | bytes 4194320 | tf_op jit(solution)/shard_map/all_gather | solution.py:868
  98.1 36.7 %all-gather.9.cloned.1.call-done = bf16[1,2,2048,512]{3,2,1,0:T(8,128)(2,1)} async-done(((bf16[1,2,512,512]{3,2,1,0:T(8,128)(2,1)}), bf16[1,2,2048,512]{3,2,1,0:T(8,128)(2,1)}) %all-gather.9.cloned.1.call-update) | async-done | bytes 4194320 | tf_op jit(solution)/shard_map/all_gather | solution.py:868
  148.8 11.1 %attend.3 = (bf16[1,2,512,256]{3,2,1,0:T(8,128)(2,1)S(1)}, f32[1,2,512,1]{3,2,1,0:T(8,128)S(1)}) custom-call(bf16[1,2,512,256]{3,2,1,0:T(8,128)(2,1)S(1)} %bitcast.135, bf16[1,4096,512]{2,1,0:T(8,128)(2,1)} %bitcast.151, s32[1,2,512,1]{3,2,1,0:T(8,128)S(1)} %copy.132.qs_ref, s32[1,1,4096]{2,1,0:T(1,128)S(1)} %get-tuple-element.201.ks_ref), custom_call_target="tpu_custom_call" | custom-call | tf_op jit(solution)/shard_map/attend/pallas_call | solution.py:245
  160.7 38.5 %gather_tp_6.1.h1_ref = bf16[1024,1024]{1,0:T(8,128)(2,1)} custom-call(bf16[1024,256]{1,0:T(8,128)(2,1)} %bitcast.133), custom_call_target="tpu_custom_call" | custom-call | tf_op jit(solution)/shard_map/gather_tp_6/pallas_call | solution.py:183
  199.2 11.1 %attend.2 = (bf16[1,2,512,256]{3,2,1,0:T(8,128)(2,1)S(1)}, f32[1,2,512,1]{3,2,1,0:T(8,128)S(1)}) custom-call(bf16[1,2,512,256]{3,2,1,0:T(8,128)(2,1)S(1)} %bitcast.132, bf16[1,4096,512]{2,1,0:T(8,128)(2,1)} %bitcast.149, s32[1,2,512,1]{3,2,1,0:T(8,128)S(1)} %copy.131.qs_ref, s32[1,1,4096]{2,1,0:T(1,128)S(1)} %get-tuple-element.202.ks_ref), custom_call_target="tpu_custom_call" | custom-call | tf_op jit(solution)/shard_map/attend/pallas_call | solution.py:245
  211.1 36.7 %gather_tp_0.1.h0_ref = bf16[1024,1024]{1,0:T(8,128)(2,1)} custom-call(bf16[1024,256]{1,0:T(8,128)(2,1)} %bitcast.136), custom_call_target="tpu_custom_call" | custom-call | tf_op jit(solution)/shard_map/gather_tp_0/pallas_call | solution.py:183
  249.9 7.6 pad_maximum_fusion.kv_ref
  257.5 142.4 %ffn_forward.1 = (bf16[2048,1152]{1,0:T(8,128)(2,1)}, bf16[2048,1152]{1,0:T(8,128)(2,1)}, bf16[2048,1728]{1,0:T(8,128)(2,1)}, bf16[2048,1728]{1,0:T(8,128)(2,1)}, bf16[2048,1152]{1,0:T(8,128)(2,1)}) custom-call(bf16[2048,1152]{1,0:T(8,128)(2,1)} %bitcast.139, bf16[1024,1024]{1,0:T(8,128)(2,1)} %gather_tp_0.1.h0_ref, bf16[1024,1024]{1,0:T(8,128)(2,1)} %gather_tp_6.1.h1_ref, ...), custom_call_target="tpu_custom_call" | custom-call | tf_op jit(solution)/shard_map/ffn_forward/pallas_call | solution.py:591
  399.9 145.1 %ffn_backward.1 = (bf16[2048,1152]{1,0:T(8,128)(2,1)}, f32[1,1152]{1,0:T(1,128)}, bf16[3,1152,1728]{2,1,0:T(8,128)(2,1)}, bf16[2048,1152]{1,0:T(8,128)(2,1)}) custom-call(bf16[2048,1152]{1,0:T(8,128)(2,1)} %bitcast.140, bf16[2048,1152]{1,0:T(8,128)(2,1)} %get-tuple-element.45.attn_ref, bf16[2048,1152]{1,0:T(8,128)(2,1)} %bitcast.146, ...), custom_call_target="tpu_custom_call" | custom-call | tf_op jit(solution)/shard_map/ffn_backward/pallas_call | solution.py:724
  546.2 19.3 %middle_back.1 = (f32[2048,1152]{1,0:T(8,128)}, bf16[2048,256]{1,0:T(8,128)(2,1)S(1)}, f32[2048,1]{1,0:T(8,128)S(1)}, f32[2,1152]{1,0:T(2,128)S(1)}, bf16[1152,256]{1,0:T(8,128)(2,1)S(1)}) custom-call(bf16[2048,1152]{1,0:T(8,128)(2,1)} %bitcast.141, bf16[2048,1152]{1,0:T(8,128)(2,1)} %get-tuple-element.45.attn_ref, bf16[2048,1152]{1,0:T(8,128)(2,1)} %bitcast.147, ...), custom_call_target="tpu_custom_call" | custom-call | tf_op jit(solution)/shard_map/middle_back/pallas_call | solution.py:783
  567.5 24.5 %attend_back.1 = (f32[2,2,512,256]{3,2,1,0:T(8,128)}, bf16[2,4096,512]{2,1,0:T(8,128)(2,1)}) custom-call(bf16[2,2,512,256]{3,2,1,0:T(8,128)(2,1)} %pad_maximum_fusion.8.q_ref, bf16[2,4096,512]{2,1,0:T(8,128)(2,1)} %pad_maximum_fusion.kv_ref, bf16[2,2,512,256]{3,2,1,0:T(8,128)(2,1)} %bitcast.138, f32[2,2,1,512]{3,2,1,0:T(1,128)} %maximum_bitcast_fusion.l_ref, ...), custom_call_target="tpu_custom_call" | custom-call | tf_op jit(solution)/shard_map/attend_back/pallas_call | solution.py:315
  601.3 67.2 %gather_tp_4.1 = bf16[2048,1024]{1,0:T(8,128)(2,1)} custom-call(bf16[2048,256]{1,0:T(8,128)(2,1)} %multiply_convert_fusion.2.x_ref), custom_call_target="tpu_custom_call" | custom-call | tf_op jit(solution)/shard_map/gather_tp_4/pallas_call | solution.py:183
  673.9 9.4 %reshape.238 = bf16[1152,4,2,256]{3,2,1,0:T(2,128)(2,1)} reshape(bf16[1152,2048]{1,0:T(8,128)(2,1)} %slice.242) | data formatting | bytes 9437184 | tf_op jit(solution)/shard_map/reshape | solution.py:904
  683.2 11.2 %copy.149 = bf16[1152,4,1,256]{0,3,1,2:T(8,128)(2,1)} copy(bf16[1152,4,1,256]{3,2,1,0:T(2,128)(2,1)} %bitcast.148) | data formatting | bytes 4718592
  694.4 10.9 %psum.7 = bf16[256]{0:T(256)(128)(2,1)S(1)} all-reduce(f32[256]{0:T(256)S(1)} %get-tuple-element.159), channel_id=1, replica_groups=mesh['dp'=2,'ctx'=4,'tp'=4] {'tp'}, use_global_device_ids=true, to_apply=%region_9.10 | all-reduce | flops 256 | bytes 1536 | tf_op jit(solution)/shard_map/psum | solution.py:908
  713.4 53.9 %sum_tp_3.1 = bf16[2048,512]{1,0:T(8,128)(2,1)S(1)} custom-call(bf16[2048,512]{1,0:T(8,128)(2,1)S(1)} %bitcast.131), custom_call_target="tpu_custom_call" | custom-call | tf_op jit(solution)/shard_map/sum_tp_3/pallas_call | solution.py:113
  773.8 5.8 fusion.37
  779.7 6.9 multiply_reduce_fusion
  786.9 5.7 convolution_convert_fusion
  792.5 5.7 fusion.6
  801.5 13.5 %multiply_add_fusion = f32[2048,1152]{1,0:T(8,128)} fusion(f32[2048,1152]{1,0:T(8,128)} %get-tuple-element.52, f32[2048,1152]{1,0:T(8,128)} %get-tuple-element.211, f32[2048]{0:T(1024)S(1)} %broadcast_multiply_fusion, f32[1152]{0:T(1024)S(1)} %fusion.30, f32[2048]{0:T(1024)S(1)} %bitcast.166, bf16[2,1,2,512,1152]{4,3,2,1,0:T(8,128)(2,1)} %param.16), kind=kLoop, calls=%fused_computation.2 | loop fusion | flops 16515072 | bytes 33051136 | tf_op jit(solution)/shard_map/add | solution.py:907
  818.3 25.2 %reduce-scatter.10.cloned.1.call-done = bf16[144,1152]{1,0:T(8,128)(2,1)} async-done(((bf16[1152,1152]{1,0:T(8,128)(2,1)}), bf16[144,1152]{1,0:T(8,128)(2,1)}) %reduce-scatter.10.cloned.1.call-update) | async-done | bytes 331792
  (198 shorter events, 101.7 us)
Async XLA Ops:
  7.2 38.0 %all-gather.5.cloned.1.call-start = ((), (), s32[]{:S(2)}) async-start(), calls=%async_computation.3 | async-start | bytes 2322432 | tf_op jit(solution)/shard_map/all_gather | solution.py:827
  14.5 83.6 %all-gather.7.cloned.1.call-start = ((), (), s32[]{:S(2)}) async-start(), calls=%async_computation.4 | async-start | bytes 5242880 | tf_op jit(solution)/shard_map/all_gather | solution.py:868
  19.9 40.4 %copy-start.11 = (f32[1024,128]{1,0:T(8,128)}, f32[1024,128]{1,0:T(8,128)S(1)}, u32[]{:S(2)}) copy-start(f32[1024,128]{1,0:T(8,128)S(1)} %get-tuple-element.210) | copy-start | bytes 1572868
  62.0 19.6 %copy-start.23 = (bf16[1728,144]{0,1:T(8,128)(2,1)S(1)}, bf16[1728,144]{0,1:T(8,128)(2,1)}, u32[]{:S(2)}) copy-start(bf16[1728,144]{0,1:T(8,128)(2,1)} %param.25) | copy-start | bytes 1492996
  62.0 19.6 %copy-start.24 = (bf16[144,1728]{1,0:T(8,128)(2,1)S(1)}, bf16[144,1728]{1,0:T(8,128)(2,1)}, u32[]{:S(2)}) copy-start(bf16[144,1728]{1,0:T(8,128)(2,1)} %param.24) | copy-start | bytes 1492996
  62.0 19.6 %copy-start.25 = (bf16[144,1728]{1,0:T(8,128)(2,1)S(1)}, bf16[144,1728]{1,0:T(8,128)(2,1)}, u32[]{:S(2)}) copy-start(bf16[144,1728]{1,0:T(8,128)(2,1)} %param.23) | copy-start | bytes 1492996
  63.5 71.3 %all-gather.9.cloned.1.call-start = ((), (), s32[]{:S(2)}) async-start(), calls=%async_computation.5 | async-start | bytes 5242880 | tf_op jit(solution)/shard_map/all_gather | solution.py:868
  64.3 193.2 %all-gather.11.cloned.1.call-start = ((), (), s32[]{:S(2)}) async-start(), calls=%async_computation.6 | async-start | bytes 19243008 | tf_op jit(solution)/shard_map/all_gather | solution.py:870
  81.7 53.4 %copy-start.29 = (s32[2,1,2,512]{3,2,1,0:T(2,128)S(1)}, s32[2,1,2,512]{3,2,1,0:T(2,128)}, u32[]{:S(2)}) copy-start(s32[2,1,2,512]{3,2,1,0:T(2,128)} %param.17) | copy-start | bytes 24580
  134.8 577.0 %reduce-scatter.6.cloned.1.call-start = ((), (), s32[]{:S(2)}) async-start(), calls=%async_computation.7 | async-start | bytes 10485760 | tf_op jit(solution)/shard_map/reduce_scatter | solution.py:893
  136.2 6.9 copy-start.13
  136.2 6.9 copy-start.14
  211.1 37.8 %copy-start.3 = (bf16[1,2,512,256]{3,2,1,0:T(8,128)(2,1)S(1)}, bf16[1,2,512,256]{3,2,1,0:T(8,128)(2,1)}, u32[]{:S(2)}) copy-start(bf16[1,2,512,256]{3,2,1,0:T(8,128)(2,1)} %copy-done.2) | copy-start | bytes 1572868
  211.1 37.8 %copy-start.5 = (bf16[1,2,512,256]{3,2,1,0:T(8,128)(2,1)S(1)}, bf16[1,2,512,256]{3,2,1,0:T(8,128)(2,1)}, u32[]{:S(2)}) copy-start(bf16[1,2,512,256]{3,2,1,0:T(8,128)(2,1)} %copy-done.4) | copy-start | bytes 1572868
  399.9 145.1 %copy-start.8 = (f32[8,1152]{1,0:T(8,128)S(1)}, f32[8,1152]{1,0:T(8,128)}, u32[]{:S(2)}) copy-start(f32[8,1152]{1,0:T(8,128)} %copy-done.7) | copy-start | bytes 110596
  592.0 223.0 %reduce-scatter.8.cloned.1.call-start = ((), (), s32[]{:S(2)}) async-start(), calls=%async_computation.8 | async-start | bytes 13934592 | tf_op jit(solution)/shard_map/reduce_scatter | solution.py:885
  592.6 251.0 %reduce-scatter.10.cloned.1.call-start = ((), (), s32[]{:S(2)}) async-start(), calls=%async_computation.9 | async-start | bytes 2985984
  683.2 23.4 %copy-start.31 = (f32[1,1152]{1,0:T(1,128)S(1)}, f32[1,1152]{1,0:T(1,128)}, u32[]{:S(2)}) copy-start(f32[1,1152]{1,0:T(1,128)} %get-tuple-element.63) | copy-start | bytes 13828
  683.2 23.4 %copy-start.17 = (bf16[2048,256]{1,0:T(8,128)(2,1)S(1)}, bf16[2048,256]{1,0:T(8,128)(2,1)}, u32[]{:S(2)}) copy-start(bf16[2048,256]{1,0:T(8,128)(2,1)} %multiply_convert_fusion.2.x_ref) | copy-start | bytes 3145732
  768.0 11.7 %copy-start.21 = (bf16[2048,256]{1,0:T(8,128)(2,1)}, bf16[2048,256]{1,0:T(8,128)(2,1)S(1)}, u32[]{:S(2)}) copy-start(bf16[2048,256]{1,0:T(8,128)(2,1)S(1)} %slice.201) | copy-start | bytes 3145732
  771.5 8.2 slice-start
  773.8 5.8 slice-start.1
  773.8 5.8 copy-start.28
  786.9 5.7 copy-start.22
  (19 other events, 45.7 us)
Sparse Core Ops, SparseCore 0:
  14.6 30.4 all-gather.4
  63.6 34.4 all-gather.6
  100.3 34.4 all-gather.8
  137.1 91.2 all-gather.10
  592.1 70.6 reduce-scatter.5
  666.8 91.3 reduce-scatter.7
  801.6 41.9 reduce-scatter.9

commit v4 on v3

--- a/solution.py
+++ b/solution.py
@@ -35,91 +35,6 @@
         pl.semaphore_signal(bar, inc=1, device_id={"tp": z + 1}, device_id_type=MESH)
 
     pl.semaphore_wait(bar, jnp.where((z == 0) | (z == 3), 1, 2))
-
-
-def sum_kernel(n, tile, x_ref, o_ref, own, got, pair, other, *sems):
-    lsem, ssem1, rsem1, ssem2, rsem2, ssem3, rsem3, osem = sems
-    z = lax.axis_index("tp")
-    hub = (z == 1) | (z == 2)
-    leaf = jnp.logical_not(hub)
-    other_hub = jnp.where(z == 1, 2, 1)
-    my_hub = jnp.where(z == 0, 1, 2)
-    my_leaf = jnp.where(z == 1, 0, 3)
-    barrier_line(z)
-
-    def rows(t):
-        return pl.ds(t * tile, tile)
-
-    def up(t):
-        return pltpu.make_async_remote_copy(
-            x_ref.at[rows(t)], got.at[rows(t)], ssem1.at[t], rsem1.at[t],
-            device_id={"tp": my_hub}, device_id_type=MESH)
-
-    def across(t):
-        return pltpu.make_async_remote_copy(
-            pair.at[rows(t)], other.at[rows(t)], ssem2.at[t], rsem2.at[t],
-            device_id={"tp": other_hub}, device_id_type=MESH)
-
-    def back(t):
-        return pltpu.make_async_remote_copy(
-            own.at[rows(t)], o_ref.at[rows(t)], ssem3.at[t], rsem3.at[t],
-            device_id={"tp": my_leaf}, device_id_type=MESH)
-
-    def load(t):
-        return pltpu.make_async_copy(x_ref.at[rows(t)], own.at[rows(t)], lsem.at[t])
-
-    def store(t):
-        return pltpu.make_async_copy(own.at[rows(t)], o_ref.at[rows(t)], osem.at[t])
-
-    @pl.when(leaf)
-    def _():
-        for t in range(n):
-            up(t).start()
-        for t in range(n):
-            back(t).wait_recv()
-        for t in range(n):
-            up(t).wait_send()
-
-    @pl.when(hub)
-    def _():
-        for t in range(n):
-            load(t).start()
-
-        def finish(t):
-            across(t).wait_recv()
-            own[rows(t), :] = (pair[rows(t), :].astype(F32) + other[rows(t), :].astype(F32)).astype(BF16)
-            back(t).start()
-            store(t).start()
-
-        for t in range(n):
-            load(t).wait()
-            up(t).wait_recv()
-            pair[rows(t), :] = (own[rows(t), :].astype(F32) + got[rows(t), :].astype(F32)).astype(BF16)
-            across(t).start()
-            if t > 0:
-                finish(t - 1)
-        finish(n - 1)
-        for t in range(n):
-            across(t).wait_send()
-            back(t).wait_send()
-            store(t).wait()
-
-
-def sum_tp(x, ident):
-    rows, cols = x.shape
-    tile = 128 if rows % 128 == 0 else rows
-    n = rows // tile
-    dma = pltpu.SemaphoreType.DMA((n,))
-    return pl.pallas_call(
-        functools.partial(sum_kernel, n, tile),
-        out_shape=jax.ShapeDtypeStruct((rows, cols), BF16),
-        in_specs=[pl.BlockSpec(memory_space=pl.ANY)],
-        out_specs=pl.BlockSpec(memory_space=pl.ANY),
-        scratch_shapes=[pltpu.VMEM((rows, cols), BF16)] * 4 + [dma] * 8,
-        compiler_params=pltpu.CompilerParams(
-            collective_id=ident, has_side_effects=True, vmem_limit_bytes=40 * 2**20),
-        name=f"sum_tp_{ident}",
-    )(x)
 
 
 def gather_kernel(n, tile, width, x_ref, o_ref, lsem, *sems):
@@ -801,6 +716,367 @@
     )(x, attn, dy, d_two, heads, gains, weights)
 
 
+class ResidentSum(LineSum):
+    def outwards(self, c):
+        return pltpu.make_async_remote_copy(
+            self.out.at[self.rows(c)], self.out.at[self.rows(c)], self.sems[4].at[c], self.sems[5].at[c],
+            device_id={"tp": self.my_leaf}, device_id_type=MESH)
+
+    def total(self, c):
+        @pl.when(self.hub)
+        def _():
+            self.across(c).wait_recv()
+            at = self.rows(c)
+            self.out[at, :] = (self.own[at, :].astype(F32) + self.far[at, :].astype(F32)).astype(BF16)
+            self.outwards(c).start()
+
+    def arrived(self, c):
+        @pl.when(self.leaf)
+        def _():
+            self.outwards(c).wait_recv()
+
+    def finish(self):
+        @pl.when(self.leaf)
+        def _():
+            for c in range(self.count):
+                self.inwards(c).wait_send()
+
+        @pl.when(self.hub)
+        def _():
+            for c in range(self.count):
+                self.across(c).wait_send()
+                self.outwards(c).wait_send()
+
+
+class LineGather:
+    def __init__(self, whole, tile, width, sems):
+        self.whole, self.tile, self.width, self.sems = whole, tile, width, sems
+        self.z = lax.axis_index("tp")
+
+    def send(self, src, t, hop, way):
+        ss, rs = self.sems[:2] if way > 0 else self.sems[2:]
+        place = self.whole.at[
+            pl.ds(pl.multiple_of(t * self.tile, self.tile), self.tile),
+            pl.ds(pl.multiple_of(src * self.width, self.width), self.width)]
+        return pltpu.make_async_remote_copy(
+            place, place, ss.at[hop, t], rs.at[hop, t],
+            device_id={"tp": self.z + way}, device_id_type=MESH)
+
+    def going(self, hop, way):
+        src = self.z - way * hop
+        return src, (self.z + way >= 0) & (self.z + way <= 3) & (src >= 0) & (src <= 3)
+
+    def coming(self, hop, way):
+        src = self.z - way * (hop + 1)
+        return src, (src >= 0) & (src <= 3)
+
+    def forward(self, t, hop):
+        for way in (1, -1):
+            if hop > 0:
+                self.wait(t, hop - 1, way)
+            src, ok = self.going(hop, way)
+
+            @pl.when(ok)
+            def _():
+                self.send(src, t, hop, way).start()
+
+    def wait(self, t, hop, way):
+        src, ok = self.coming(hop, way)
+
+        @pl.when(ok)
+        def _():
+            self.send(src, t, hop, way).wait_recv()
+
+    def arrived(self, t):
+        for way in (1, -1):
+            self.wait(t, 2, way)
+
+    def finish(self, tiles):
+        for hop in range(3):
+            for way in (1, -1):
+                src, ok = self.going(hop, way)
+
+                @pl.when(ok)
+                def _():
+                    def one(t, _):
+                        self.send(src, t, hop, way).wait_send()
+                        return 0
+
+                    lax.fori_loop(0, tiles, one, 0)
+
+
+def query_back_kernel(tiles, tile, dq_ref, hat_ref, inv_ref, cos_ref, sin_ref, x_ref, gain_ref, gq_ref, w_ref,
+                      one_ref, grad_ref, dgain_ref, acc, wq_ref, w_sem, whole, *sems):
+    i = pl.program_id(0)
+    head = hat_ref.shape[1]
+    line = LineGather(whole, tile, head, sems)
+
+    @pl.when(i == 0)
+    def _():
+        copies = [
+            pltpu.make_async_copy(w_ref.at[:, pl.ds(2 * j * head, head)], wq_ref.at[:, pl.ds(j * head, head)], w_sem.at[j])
+            for j in range(4)
+        ]
+        for copy in copies:
+            copy.start()
+        barrier_line(line.z)
+        acc[...] = jnp.zeros_like(acc)
+        dgain_ref[...] = jnp.zeros_like(dgain_ref)
+        for copy in copies:
+            copy.wait()
+
+    @pl.when(i < tiles)
+    def _():
+        d_rot = rotate(dq_ref[...], cos_ref[...], -sin_ref[...])
+        d_raw, d_gain = norm_back(d_rot, hat_ref[...], inv_ref[...], gq_ref[...])
+        d_raw = d_raw.astype(BF16)
+        at = pl.ds(pl.multiple_of(line.z * head, head), head)
+        whole[pl.ds(pl.multiple_of(i * tile, tile), tile), at] = d_raw
+        line.forward(i, 0)
+        dgain_ref[...] += d_gain[None]
+        hat, _ = norm_parts(x_ref[...].astype(F32))
+        one = (hat * (1.0 + gain_ref[0:1, :])).astype(BF16)
+        acc[...] += dot(one, d_raw, TN)
+
+    @pl.when((i >= 1) & (i <= tiles))
+    def _():
+        line.forward(i - 1, 1)
+
+    @pl.when((i >= 2) & (i <= tiles + 1))
+    def _():
+        line.forward(i - 2, 2)
+
+    @pl.when(i >= 3)
+    def _():
+        line.arrived(i - 3)
+        one_ref[...] = dot(whole[pl.ds(pl.multiple_of((i - 3) * tile, tile), tile), :], wq_ref[...], NT)
+
+    @pl.when(i == tiles + 2)
+    def _():
+        grad_ref[...] = acc[...].astype(BF16)
+        line.finish(tiles)
+
+
+def query_back(dq, hat, inv, cosine, sine, x, gains, gain_query, weights, ident):
+    rows, width = x.shape
+    head = hat.shape[1]
+    tile = 256
+    tiles = rows // tile
+    dma = pltpu.SemaphoreType.DMA((3, tiles))
+
+    def early(cols):
+        return pl.BlockSpec((tile, cols), lambda i: (jnp.minimum(i, tiles - 1), 0))
+
+    return pl.pallas_call(
+        functools.partial(query_back_kernel, tiles, tile),
+        grid=(tiles + 3,),
+        out_shape=(
+            jax.ShapeDtypeStruct((rows, width), F32),
+            jax.ShapeDtypeStruct((width, head), BF16),
+            jax.ShapeDtypeStruct((1, head), F32),
+        ),
+        in_specs=[early(head), early(head), early(1), early(head // 2), early(head // 2), early(width),
+                  whole_block(gains.shape), whole_block(gain_query.shape), ANY],
+        out_specs=(
+            pl.BlockSpec((tile, width), lambda i: (jnp.maximum(i - 3, 0), 0)),
+            pl.BlockSpec((width, head), lambda i: (0, 0)),
+            pl.BlockSpec((1, head), lambda i: (0, 0)),
+        ),
+        scratch_shapes=[
+            pltpu.VMEM((width, head), F32), pltpu.VMEM((width, 4 * head), BF16), pltpu.SemaphoreType.DMA((4,)),
+            pltpu.VMEM((rows, 4 * head), BF16)] + [dma] * 4,
+        compiler_params=pltpu.CompilerParams(
+            collective_id=ident, has_side_effects=True, vmem_limit_bytes=48 * 2**20),
+        name="query_back",
+    )(dq, hat, inv, cosine, sine, x, gains, gain_query, weights)
+
+
+def key_back_kernel(tiles, tile, chunk, own_rows, dkv_ref, hat_ref, inv_ref, cos_ref, sin_ref, x_ref, dm_ref, part_ref,
+                    gain_ref, gk_ref, w_ref, dgq_ref, dg_mid_ref, dg_post_ref, grad_q_ref, grad_o_ref,
+                    dx_ref, last_ref, acc, acc_in, acc_key, w_kv, w_sem, out, own, near, far, *sems):
+    i = pl.program_id(0)
+    head = hat_ref.shape[1]
+    per = tile // chunk
+    count = tiles * per + 1
+    line = ResidentSum(count, chunk, count, own, near, far, out, sems)
+
+    @pl.when(i == 0)
+    def _():
+        copy = pltpu.make_async_copy(w_ref.at[:, pl.ds(head, 2 * head)], w_kv, w_sem)
+        copy.start()
+        barrier_line(line.z)
+        for ref in (acc, acc_in, acc_key):
+            ref[...] = jnp.zeros_like(ref)
+        copy.wait()
+        line.put(count - 1, jnp.broadcast_to(
+            jnp.concatenate([dgq_ref[...], dgq_ref[...]], axis=1).astype(BF16), (chunk, 2 * head)))
+
+    @pl.when(i < tiles)
+    def _():
+        for j in range(per):
+            line.put(i * per + j, dkv_ref[j * chunk : (j + 1) * chunk, :])
+
+    @pl.when((i >= 1) & (i <= tiles))
+    def _():
+        for j in range(per):
+            line.pair((i - 1) * per + j)
+
+    @pl.when((i >= 2) & (i <= tiles + 1))
+    def _():
+        for j in range(per):
+            line.total((i - 2) * per + j)
+
+    @pl.when(i == 1)
+    def _():
+        line.pair(count - 1)
+
+    @pl.when(i == 2)
+    def _():
+        line.total(count - 1)
+
+    @pl.when(i >= 3)
+    def _():
+        for j in range(per):
+            line.arrived((i - 3) * per + j)
+        d_kv = out[pl.ds(pl.multiple_of((i - 3) * tile, tile), tile), :]
+        d_rot = rotate(d_kv[:, :head].astype(F32), cos_ref[...], -sin_ref[...])
+        d_raw, d_gain = norm_back(d_rot, hat_ref[...], inv_ref[...], gk_ref[...])
+        acc_key[...] += d_gain[None]
+        d_raw = jnp.concatenate([d_raw.astype(BF16), d_kv[:, head:]], axis=1)
+        d_one = part_ref[...] + dot(d_raw, w_kv[...], NT)
+        hat, inv = norm_parts(x_ref[...].astype(F32))
+        gain = gain_ref[0:1, :]
+        d_part, d_gain = norm_back(d_one, hat, inv, gain)
+        acc_in[...] += d_gain[None]
+        dx_ref[...] = dm_ref[...] + d_part
+        acc[...] += dot((hat * (1.0 + gain)).astype(BF16), d_raw, TN)
+
+    @pl.when(i == tiles + 2)
+    def _():
+        line.arrived(count - 1)
+        width = x_ref.shape[1]
+        short = head * own_rows // width
+        last_ref[:, :head] = grad_q_ref[...]
+        last_ref[:, head : 3 * head] = acc[...].astype(BF16)
+        last_ref[:, 3 * head : 4 * head] = grad_o_ref[...]
+        d_query = out[pl.ds((count - 1) * chunk, 16), :head][0:1].astype(F32)
+        pair = jnp.concatenate([d_query, acc_key[...], jnp.zeros((14, head), F32)], axis=0).astype(BF16)
+        col = lax.broadcasted_iota(jnp.int32, (head, width), 1)
+        row = lax.broadcasted_iota(jnp.int32, (head, width), 0)
+        shift = short.bit_length() - 1
+        spot = lax.shift_right_logical(row, shift) * own_rows + (row & (short - 1))
+        spread = dot(pair, jnp.where(col == spot, 1.0, 0.0).astype(BF16))
+        gains = jnp.concatenate(
+            [acc_in[...], dg_mid_ref[...], dg_post_ref[...], spread[0:2], jnp.zeros((122, width), F32)], axis=0)
+        last_ref[:, 4 * head :] = jnp.transpose(gains).astype(BF16)
+        line.finish()
+
+
+def key_back(d_kv, hat, inv, cosine, sine, x, d_middle, part, gains, gain_key, first, dg_query, dg_mid, dg_post,
+             grad_q, grad_o, own_rows, ident):
+    rows, width = x.shape
+    head = hat.shape[1]
+    tile, chunk = 256, 128
+    tiles = rows // tile
+    count = rows // chunk + 1
+    dma = pltpu.SemaphoreType.DMA((count,))
+
+    def late(cols):
+        return pl.BlockSpec((tile, cols), lambda i: (jnp.maximum(i - 3, 0), 0))
+
+    comm = pltpu.VMEM((count * chunk, 2 * head), BF16)
+    return pl.pallas_call(
+        functools.partial(key_back_kernel, tiles, tile, chunk, own_rows),
+        grid=(tiles + 3,),
+        out_shape=(
+            jax.ShapeDtypeStruct((rows, width), F32),
+            jax.ShapeDtypeStruct((width, 4 * head + 128), BF16),
+        ),
+        in_specs=[pl.BlockSpec((tile, 2 * head), lambda i: (jnp.minimum(i, tiles - 1), 0)),
+                  late(head), late(1), late(head // 2), late(head // 2), late(width), late(width), late(width),
+                  whole_block(gains.shape), whole_block(gain_key.shape), ANY]
+        + [whole_block(a.shape) for a in (dg_query, dg_mid, dg_post, grad_q, grad_o)],
+        out_specs=(late(width), pl.BlockSpec((width, 4 * head + 128), lambda i: (0, 0))),
+        scratch_shapes=[
+            pltpu.VMEM((width, 2 * head), F32), pltpu.VMEM((1, width), F32), pltpu.VMEM((1, head), F32),
+            pltpu.VMEM((width, 2 * head), BF16), pltpu.SemaphoreType.DMA] + [comm] * 4 + [dma] * 7
+        + [pltpu.SemaphoreType.REGULAR] * 2,
+        compiler_params=pltpu.CompilerParams(
+            collective_id=ident, has_side_effects=True, vmem_limit_bytes=56 * 2**20),
+        name="key_back",
+    )(d_kv, hat, inv, cosine, sine, x, d_middle, part, gains, gain_key, first, dg_query, dg_mid, dg_post, grad_q, grad_o)
+
+
+def scatter_kernel(chips, own_rows, x_ref, o_ref, near, pair, far, *sems):
+    ss1, rs1, ss2, rs2 = sems
+    ctx = lax.axis_size("ctx")
+    me = lax.axis_index("dp") * ctx + lax.axis_index("ctx")
+    core = lax.rem(me, 2)
+    chip = lax.div(me, 2)
+    bar = pltpu.get_barrier_semaphore()
+
+    def device(d):
+        return {"dp": lax.div(d, ctx), "ctx": lax.rem(d, ctx)}
+
+    partner = device(2 * chip + 1 - core)
+    pl.semaphore_signal(bar, inc=1, device_id=partner, device_id_type=MESH)
+    for k in range(1, chips):
+        other = lax.rem(chip + k, chips)
+        pl.semaphore_signal(bar, inc=1, device_id=device(2 * other + core), device_id_type=MESH)
+    pl.semaphore_wait(bar, chips)
+
+    def block(d):
+        return pl.ds(pl.multiple_of(d * own_rows, 16), own_rows)
+
+    def within(k):
+        q = lax.rem(chip + k, chips)
+        return pltpu.make_async_remote_copy(
+            x_ref.at[block(2 * q + 1 - core)], near.at[k], ss1.at[k], rs1.at[k], device_id=partner, device_id_type=MESH)
+
+    def between(k):
+        q = lax.rem(chip + k, chips)
+        return pltpu.make_async_remote_copy(
+            pair.at[k], far.at[k], ss2.at[k], rs2.at[k], device_id=device(2 * q + core), device_id_type=MESH)
+
+    order = list(range(1, chips)) + [0]
+    for k in order:
+        within(k).start()
+    for k in order:
+        within(k).wait_recv()
+        q = lax.rem(chip + k, chips)
+        both = x_ref[block(2 * q + core), :].astype(F32) + near[k].astype(F32)
+        if k > 0:
+            pair[k] = both.astype(BF16)
+            between(k).start()
+        else:
+            o_ref[...] = both
+    for k in range(1, chips):
+        between(k).wait_recv()
+        o_ref[...] += far[k].astype(F32)
+    for k in range(1, chips):
+        between(k).wait_send()
+    for k in order:
+        within(k).wait_send()
+
+
+def scatter(x, own_rows, ident):
+    n = x.shape[0] // own_rows
+    chips = n // 2
+    cols = x.shape[1]
+    buf = pltpu.VMEM((chips, own_rows, cols), BF16)
+    vmem = pl.BlockSpec(memory_space=pltpu.VMEM)
+    return pl.pallas_call(
+        functools.partial(scatter_kernel, chips, own_rows),
+        out_shape=jax.ShapeDtypeStruct((own_rows, cols), F32),
+        in_specs=[vmem],
+        out_specs=vmem,
+        scratch_shapes=[buf] * 3 + [pltpu.SemaphoreType.DMA((chips,))] * 4,
+        compiler_params=pltpu.CompilerParams(
+            collective_id=ident, has_side_effects=True, vmem_limit_bytes=40 * 2**20),
+        name="scatter",
+    )(x)
+
+
 def shards(tokens, segments, cotangent, w_query, w_key, w_value, w_out, w_gate, w_up, w_down,
            g_input, g_post_attn, g_pre_ffn, g_post_ffn, g_query, g_key):
     batches, seq_local, _, size, width = tokens.shape
@@ -866,7 +1142,7 @@
     queries = queries.reshape(groups, 2, size, head)
     pairs = jnp.concatenate([keys, values], axis=1).reshape(batches, seq_local, 2, size, 2 * head)
     kv = [lax.all_gather(pairs[m], "ctx", axis=2, tiled=True).reshape(seq_local, length, 2 * head) for m in range(batches)]
-    *kv, second = lax.optimization_barrier((*kv, second))
+    kv[-1], second = lax.optimization_barrier((kv[-1], second))
     weights = lax.all_gather(second, shared, axis=0, tiled=True)
     heads, heads_all, log_mass = [], [], []
     for m in range(batches):
@@ -892,31 +1168,16 @@
         own_ids[:, :, None, :], key_ids[:, :, None])
     d_kv = lax.psum_scatter(
         d_kv.reshape(groups, 2, length // 2, 2 * head), "ctx", scatter_dimension=2, tiled=True)
-    d_q_rot = rotate(d_query.reshape(rows, head), cosine, -sine)
-    d_q_raw, d_gain_query = norm_back(d_q_rot, q_hat, q_scale, gain_query)
-    d_q_raw = d_q_raw.astype(BF16)
-    d_q_all = gather_tp(d_q_raw, 4)
-    d_kv, d_q_all = lax.optimization_barrier((d_kv, d_q_all))
-    d_kv = sum_tp(d_kv.reshape(rows, 2 * head), 3).astype(F32)
-    d_k_rot = rotate(d_kv[:, :head], cosine, -sine)
-    d_k_raw, d_gain_key = norm_back(d_k_rot, k_hat, k_scale, gain_key)
-    d_kv_raw = jnp.concatenate([d_k_raw.astype(BF16), d_kv[:, head:].astype(BF16)], axis=1)
-    query_full = weights[:, : 8 * head].reshape(width, 4, 2, head)[:, :, 0].reshape(width, 4 * head)
-    d_one = dot(d_q_all, query_full, NT) + dot(d_kv_raw, mat_qkv[:, head:], NT)
-    d_part, d_gain_input = norm_back(d_one, norm_one, scale_one, gain_input)
-    d_tokens = d_middle + d_part
-    d_gain_query = lax.psum(d_gain_query, "tp")
-
-    def spread(vector):
-        return jnp.pad(vector.reshape(-1, short), ((0, 0), (0, own_rows - short))).reshape(-1)
-
-    d_gains = jnp.stack(
-        [d_gain_input, d_gain_mid[0], d_gain_mid[1], d_gain_post_ffn[0], spread(d_gain_query), spread(d_gain_key)], axis=1)
-    d_gains = jnp.pad(d_gains, ((0, 0), (0, 128 - d_gains.shape[1]))).astype(BF16)
-    last = jnp.concatenate(
-        [dot(hidden_one, d_q_raw, TN).astype(BF16), dot(hidden_one, d_kv_raw, TN).astype(BF16),
-         grad_out_t, d_gains], axis=1)
-    last = lax.psum_scatter(last, shared, scatter_dimension=0, tiled=True).astype(F32)
+    d_one, grad_q, d_gain_query = query_back(
+        d_query.reshape(rows, head), q_hat, q_scale, cosine, sine, x_rows, gain_rows, gain_query[None], weights, 4)
+    d_kv, d_one = lax.optimization_barrier((d_kv, d_one))
+    d_tokens, last = key_back(
+        d_kv.reshape(rows, 2 * head), k_hat, k_scale, cosine, sine, x_rows, d_middle, d_one, gain_rows, gain_key[None],
+        first, d_gain_query, d_gain_mid, d_gain_post_ffn, grad_q, grad_out_t, own_rows, 3)
+    if own_rows % 16 == 0:
+        last = scatter(last, own_rows, 7)
+    else:
+        last = lax.psum_scatter(last, shared, scatter_dimension=0, tiled=True).astype(F32)
     g = last[:, 4 * head :]
     return (
         output.reshape(tokens.shape),

time: 871 us -> 787 us (0.904)
  waiting for transfers between devices: 103 us -> 45.9 us
  Pallas kernels: 566 us -> 621 us
  other arithmetic: 65.1 us -> 36.2 us
  local copies, waits for them, and re-layouts: 72.7 us -> 49.7 us
  matrix products: 27.8 us -> 9.94 us
  blocking collectives: 10.9 us -> 0 us
    pallas_call x1 -> x3, Pallas kernels: 53.9 us -> 170 us  [the longest x1 73.1 us: query_back(): pl.pallas_call(functools.partial(query_back_kernel, tiles, tile), grid=(t...]
    pallas_call x4 -> x3, Pallas kernels: 159 us -> 91.8 us  [gather_tp(): pl.pallas_call(functools.partial(gather_kernel, n, tile, width), out_shap...]
    all_gather x2, waiting for transfers between devices: 50.8 us -> 14.1 us  [shards(): lax.all_gather(pairs[m], 'ctx', axis=2, tiled=True)]
    unnamed x8 -> x6, waiting for transfers between devices: 26.5 us -> 1.24 us
    dot_general x5 -> x1, matrix products: 27.8 us -> 9.94 us  [dot(): return lax.dot_general(a, b, dims, preferred_element_type=F32)]
    add x5 -> x0, other arithmetic: 13.8 us -> none  [the longest x1 13.5 us: shards(): d_tokens = d_middle + d_part]
    unnamed x83 -> x60, local copies, waits for them, and re-layouts: 36 us -> 22.6 us
    psum x1 -> x0, blocking collectives: 10.9 us -> none  [shards(): d_gain_query = lax.psum(d_gain_query, 'tp')]
  transfers between devices with their start and end apart: 7 -> 6, of which waited for: 4 -> 3; matrix products, arithmetic and copies ran while one was open for 14% -> 5% of each run, Pallas kernels for 27% -> 36%
where the time goes in v4:
time: 787 us; the launch traced here: 778 us
  Pallas kernels  621 us (79%)
  local copies, waits for them, and re-layouts  49.7 us (6%)
  waiting for transfers between devices  45.9 us (6%)
  other arithmetic  36.2 us (5%)
  between operations  15.2 us (2%)
  matrix products  9.94 us (1%)
    pallas_call x1, Pallas kernels, ffn_backward(): pl.pallas_call(functools.partial(ffn_backward_kernel, tiles, tile, chunk,...  148 us
    pallas_call x1, Pallas kernels, ffn_forward(): pl.pallas_call(functools.partial(ffn_forward_kernel, tiles, tile, chunk,...  146 us
    pallas_call x3, Pallas kernels, gather_tp(): pl.pallas_call(functools.partial(gather_kernel, n, tile, width), out_shap...  91.8 us
    pallas_call x1, Pallas kernels, query_back(): pl.pallas_call(functools.partial(query_back_kernel, tiles, tile), grid=(t...  73.1 us
    pallas_call x1, Pallas kernels, key_back(): pl.pallas_call(functools.partial(key_back_kernel, tiles, tile, chunk, own...  69.7 us
    pallas_call x1, Pallas kernels, scatter(): pl.pallas_call(functools.partial(scatter_kernel, chips, own_rows), out_sh...  26.9 us
    all_gather x1, waiting for transfers between devices, shards(): lax.all_gather(jnp.concatenate([w_query, w_key, w_value, extra], axis=1),...  25.2 us
    pallas_call x1, Pallas kernels, attend_back(): pl.pallas_call(functools.partial(attend_back_kernel, blocks), grid=(group...  24.5 us
  transfers between devices with their start and end apart: 6, of which 3 were waited for; matrix products, arithmetic and copies ran while one was open for 5% of the time, Pallas kernels for 36%

profile of v4, /device:TPU:0, one launch (start us, length us, event | category | flops | bytes accessed | tf_op | source)
XLA Modules:
  0.0 778.3 jit_solution(2117077731003812988)
XLA Ops:
  14.6 3.3 multiply_reduce_fusion
  19.9 25.2 %all-gather.5.cloned.1.call-done.w_ref = bf16[1152,896]{1,0:T(8,128)(2,1)} async-done(((bf16[144,896]{1,0:T(8,128)(2,1)}), bf16[1152,896]{1,0:T(8,128)(2,1)}) %all-gather.5.cloned.1.call-update) | async-done | bytes 2064400 | tf_op jit(solution)/shard_map/all_gather | solution.py:1103
  46.4 9.9 %fusion = f32[2048,768]{1,0:T(8,128)} fusion(bf16[2048,1152]{1,0:T(8,128)(2,1)} %bitcast.105, f32[1152]{0:T(1024)S(1)} %fusion.20, f32[2048]{0:T(1024)S(1)} %bitcast.134, bf16[1152,896]{1,0:T(8,128)(2,1)} %all-gather.5.cloned.1.call-done.w_ref), kind=kOutput, calls=%fused_computation.8 | convolution fusion | flops 3633315840 | bytes 12792320 | tf_op jit(solution)/shard_map/dot_general | solution.py:23
  56.4 2.9 multiply_reduce_fusion.1
  59.2 2.7 slice.241
  62.9 4.0 broadcast_multiply_fusion
  71.4 16.6 %gather_tp_5.1 = bf16[144,2048]{1,0:T(8,128)(2,1)} custom-call(bf16[144,512]{1,0:T(8,128)(2,1)} %pad_maximum_fusion.5.x_ref), custom_call_target="tpu_custom_call" | custom-call | tf_op jit(solution)/shard_map/gather_tp_5/pallas_call | solution.py:98
  90.4 14.1 %all-gather.9.cloned.1.call-done = bf16[1,2,2048,512]{3,2,1,0:T(8,128)(2,1)} async-done(((bf16[1,2,512,512]{3,2,1,0:T(8,128)(2,1)}), bf16[1,2,2048,512]{3,2,1,0:T(8,128)(2,1)}) %all-gather.9.cloned.1.call-update) | async-done | bytes 4194320 | tf_op jit(solution)/shard_map/all_gather | solution.py:1144
  108.2 5.3 reshape.251
  119.1 11.1 %attend.3 = (bf16[1,2,512,256]{3,2,1,0:T(8,128)(2,1)S(1)}, f32[1,2,512,1]{3,2,1,0:T(8,128)S(1)}) custom-call(bf16[1,2,512,256]{3,2,1,0:T(8,128)(2,1)S(1)} %bitcast.100, bf16[1,4096,512]{2,1,0:T(8,128)(2,1)} %bitcast.113, s32[1,2,512,1]{3,2,1,0:T(8,128)S(1)} %copy.91.qs_ref, s32[1,1,4096]{2,1,0:T(1,128)S(1)} %get-tuple-element.168.ks_ref), custom_call_target="tpu_custom_call" | custom-call | tf_op jit(solution)/shard_map/attend/pallas_call | solution.py:160
  131.1 38.4 %gather_tp_6.1.h1_ref = bf16[1024,1024]{1,0:T(8,128)(2,1)} custom-call(bf16[1024,256]{1,0:T(8,128)(2,1)} %bitcast.98), custom_call_target="tpu_custom_call" | custom-call | tf_op jit(solution)/shard_map/gather_tp_6/pallas_call | solution.py:98
  169.5 11.1 %attend.2 = (bf16[1,2,512,256]{3,2,1,0:T(8,128)(2,1)S(1)}, f32[1,2,512,1]{3,2,1,0:T(8,128)S(1)}) custom-call(bf16[1,2,512,256]{3,2,1,0:T(8,128)(2,1)S(1)} %bitcast.97, bf16[1,4096,512]{2,1,0:T(8,128)(2,1)} %bitcast.115, s32[1,2,512,1]{3,2,1,0:T(8,128)S(1)} %copy.90.qs_ref, s32[1,1,4096]{2,1,0:T(1,128)S(1)} %get-tuple-element.169.ks_ref), custom_call_target="tpu_custom_call" | custom-call | tf_op jit(solution)/shard_map/attend/pallas_call | solution.py:160
  181.5 36.7 %gather_tp_0.1.h0_ref = bf16[1024,1024]{1,0:T(8,128)(2,1)} custom-call(bf16[1024,256]{1,0:T(8,128)(2,1)} %bitcast.101), custom_call_target="tpu_custom_call" | custom-call | tf_op jit(solution)/shard_map/gather_tp_0/pallas_call | solution.py:98
  221.3 7.6 pad_maximum_fusion.kv_ref
  228.9 5.3 all-gather.11.cloned.1.call-done.w_ref
  234.2 145.5 %ffn_forward.1 = (bf16[2048,1152]{1,0:T(8,128)(2,1)}, bf16[2048,1152]{1,0:T(8,128)(2,1)}, bf16[2048,1728]{1,0:T(8,128)(2,1)}, bf16[2048,1728]{1,0:T(8,128)(2,1)}, bf16[2048,1152]{1,0:T(8,128)(2,1)}) custom-call(bf16[2048,1152]{1,0:T(8,128)(2,1)} %bitcast.106, bf16[1024,1024]{1,0:T(8,128)(2,1)} %gather_tp_0.1.h0_ref, bf16[1024,1024]{1,0:T(8,128)(2,1)} %gather_tp_6.1.h1_ref, ...), custom_call_target="tpu_custom_call" | custom-call | tf_op jit(solution)/shard_map/ffn_forward/pallas_call | solution.py:506
  379.7 148.0 %ffn_backward.1 = (bf16[2048,1152]{1,0:T(8,128)(2,1)}, f32[1,1152]{1,0:T(1,128)}, bf16[3,1152,1728]{2,1,0:T(8,128)(2,1)}, bf16[2048,1152]{1,0:T(8,128)(2,1)}) custom-call(bf16[2048,1152]{1,0:T(8,128)(2,1)} %bitcast.107, bf16[2048,1152]{1,0:T(8,128)(2,1)} %get-tuple-element.48.attn_ref, bf16[2048,1152]{1,0:T(8,128)(2,1)} %bitcast.111, ...), custom_call_target="tpu_custom_call" | custom-call | tf_op jit(solution)/shard_map/ffn_backward/pallas_call | solution.py:639
  528.9 19.2 %middle_back.1 = (f32[2048,1152]{1,0:T(8,128)}, bf16[2048,256]{1,0:T(8,128)(2,1)S(1)}, f32[2048,1]{1,0:T(8,128)S(1)}, f32[2,1152]{1,0:T(2,128)S(1)}, bf16[1152,256]{1,0:T(8,128)(2,1)S(1)}) custom-call(bf16[2048,1152]{1,0:T(8,128)(2,1)} %bitcast.108, bf16[2048,1152]{1,0:T(8,128)(2,1)} %get-tuple-element.48.attn_ref, bf16[2048,1152]{1,0:T(8,128)(2,1)} %bitcast.112, ...), custom_call_target="tpu_custom_call" | custom-call | tf_op jit(solution)/shard_map/middle_back/pallas_call | solution.py:698
  551.4 24.5 %attend_back.1 = (f32[2,2,512,256]{3,2,1,0:T(8,128)}, bf16[2,4096,512]{2,1,0:T(8,128)(2,1)}) custom-call(bf16[2,2,512,256]{3,2,1,0:T(8,128)(2,1)} %pad_maximum_fusion.2.q_ref, bf16[2,4096,512]{2,1,0:T(8,128)(2,1)} %pad_maximum_fusion.kv_ref, bf16[2,2,512,256]{3,2,1,0:T(8,128)(2,1)} %bitcast.104, f32[2,2,1,512]{3,2,1,0:T(1,128)} %maximum_bitcast_fusion.l_ref, ...), custom_call_target="tpu_custom_call" | custom-call | tf_op jit(solution)/shard_map/attend_back/pallas_call | solution.py:230
  583.0 73.1 %query_back.1 = (f32[2048,1152]{1,0:T(8,128)}, bf16[1152,256]{1,0:T(8,128)(2,1)S(1)}, f32[1,256]{1,0:T(1,128)S(1)}) custom-call(f32[2048,256]{1,0:T(8,128)S(1)} %bitcast.103, f32[2048,256]{1,0:T(8,128)} %get-tuple-element.148.hat_ref, f32[2048,1]{1,0:T(8,128)S(1)} %copy.100.inv_ref, f32[2048,128]{1,0:T(8,128)S(1)} %bitcast.93, f32[2048,128]{1,0:T(8,128)S(1)} %bitcast.95, ...), custom_call_target="tpu_custom_call" | custom-call | tf_op jit(solution)/shard_map/query_back/pallas_call | solution.py:870
  657.5 69.7 %key_back.1 = (f32[2048,1152]{1,0:T(8,128)}, bf16[1152,1152]{1,0:T(8,128)(2,1)}) custom-call(bf16[2048,512]{1,0:T(8,128)(2,1)} %bitcast.126, f32[2048,256]{1,0:T(8,128)} %get-tuple-element.144.hat_ref, f32[2048,1]{1,0:T(8,128)} %copy.102.inv_ref, f32[2048,128]{1,0:T(8,128)} %bitcast.94, f32[2048,128]{1,0:T(8,128)} %bitcast.96, bf16[2048,1152]{1,0:T(8,128)(2,1)} %bitcast.110, ...), custom_call_target="tpu_custom_call" | custom-call | tf_op jit(solution)/shard_map/key_back/pallas_call | solution.py:988
  728.9 26.9 %scatter.1 = f32[144,1152]{1,0:T(8,128)S(1)} custom-call(bf16[1152,1152]{1,0:T(8,128)(2,1)S(1)} %copy-done.3), custom_call_target="tpu_custom_call" | custom-call | tf_op jit(solution)/shard_map/scatter/pallas_call | solution.py:1068
  761.8 5.5 copy.110
  767.3 3.7 copy.111
  (139 shorter events, 52.7 us)
Async XLA Ops:
  7.2 38.0 %all-gather.5.cloned.1.call-start = ((), (), s32[]{:S(2)}) async-start(), calls=%async_computation.2 | async-start | bytes 2322432 | tf_op jit(solution)/shard_map/all_gather | solution.py:1103
  14.5 90.0 %all-gather.9.cloned.1.call-start = ((), (), s32[]{:S(2)}) async-start(), calls=%async_computation.4 | async-start | bytes 5242880 | tf_op jit(solution)/shard_map/all_gather | solution.py:1144
  19.9 47.1 %copy-start.15 = (f32[1024,128]{1,0:T(8,128)}, f32[1024,128]{1,0:T(8,128)S(1)}, u32[]{:S(2)}) copy-start(f32[1024,128]{1,0:T(8,128)S(1)} %get-tuple-element.177) | copy-start | bytes 1572868
  19.9 47.0 %copy-start.16 = (f32[1024,128]{1,0:T(8,128)}, f32[1024,128]{1,0:T(8,128)S(1)}, u32[]{:S(2)}) copy-start(f32[1024,128]{1,0:T(8,128)S(1)} %get-tuple-element.176) | copy-start | bytes 1572868
  68.3 2.3 copy-start.22
  68.4 2.3 copy-start.24
  68.4 19.6 %copy-start.19 = (bf16[1728,144]{0,1:T(8,128)(2,1)S(1)}, bf16[1728,144]{0,1:T(8,128)(2,1)}, u32[]{:S(2)}) copy-start(bf16[1728,144]{0,1:T(8,128)(2,1)} %param.25) | copy-start | bytes 1492996
  68.4 19.6 %copy-start.20 = (bf16[144,1728]{1,0:T(8,128)(2,1)S(1)}, bf16[144,1728]{1,0:T(8,128)(2,1)}, u32[]{:S(2)}) copy-start(bf16[144,1728]{1,0:T(8,128)(2,1)} %param.24) | copy-start | bytes 1492996
  68.4 19.6 %copy-start.21 = (bf16[144,1728]{1,0:T(8,128)(2,1)S(1)}, bf16[144,1728]{1,0:T(8,128)(2,1)}, u32[]{:S(2)}) copy-start(bf16[144,1728]{1,0:T(8,128)(2,1)} %param.23) | copy-start | bytes 1492996
  69.9 99.6 %all-gather.7.cloned.1.call-start = ((), (), s32[]{:S(2)}) async-start(), calls=%async_computation.3 | async-start | bytes 5242880 | tf_op jit(solution)/shard_map/all_gather | solution.py:1144
  69.9 34.9 %copy-start.23 = (s32[2,1,2,512]{3,2,1,0:T(2,128)S(1)}, s32[2,1,2,512]{3,2,1,0:T(2,128)}, u32[]{:S(2)}) copy-start(s32[2,1,2,512]{3,2,1,0:T(2,128)} %param.17) | copy-start | bytes 24580
  70.6 163.6 %all-gather.11.cloned.1.call-start = ((), (), s32[]{:S(2)}) async-start(), calls=%async_computation.5 | async-start | bytes 19243008 | tf_op jit(solution)/shard_map/all_gather | solution.py:1146
  104.5 552.9 %reduce-scatter.3.cloned.1.call-start = ((), (), s32[]{:S(2)}) async-start(), calls=%async_computation.6 | async-start | bytes 10485760 | tf_op jit(solution)/shard_map/reduce_scatter | solution.py:1169
  113.5 3.2 copy-start.14
  169.5 49.7 %copy-start.5 = (bf16[1,2,512,256]{3,2,1,0:T(8,128)(2,1)S(1)}, bf16[1,2,512,256]{3,2,1,0:T(8,128)(2,1)}, u32[]{:S(2)}) copy-start(bf16[1,2,512,256]{3,2,1,0:T(8,128)(2,1)} %copy-done.4) | copy-start | bytes 1572868
  379.7 148.0 %copy-start.8 = (f32[8,1152]{1,0:T(8,128)S(1)}, f32[8,1152]{1,0:T(8,128)}, u32[]{:S(2)}) copy-start(f32[8,1152]{1,0:T(8,128)} %copy.92.gain_ref) | copy-start | bytes 110596
  576.0 182.3 %reduce-scatter.5.cloned.1.call-start = ((), (), s32[]{:S(2)}) async-start(), calls=%async_computation.7 | async-start | bytes 13934592 | tf_op jit(solution)/shard_map/reduce_scatter | solution.py:1161
  576.0 3.0 copy-start.17
  579.1 77.0 %copy-start = (f32[2,1024,128]{2,1,0:T(8,128)}, f32[2,1024,128]{2,1,0:T(8,128)S(1)}, u32[]{:S(2)}) copy-start(f32[2,1024,128]{2,1,0:T(8,128)S(1)} %broadcast_in_dim.57) | copy-start | bytes 3145732
  580.6 75.5 %copy-start.1 = (f32[2,1024,128]{2,1,0:T(8,128)}, f32[2,1024,128]{2,1,0:T(8,128)S(1)}, u32[]{:S(2)}) copy-start(f32[2,1024,128]{2,1,0:T(8,128)S(1)} %broadcast_in_dim.58) | copy-start | bytes 3145732
  580.6 2.4 copy-start.7
  758.3 9.0 %slice-start = ((s8[9437184]{0:T(1024)(128)(4,1)}), s8[4194304]{0:T(1024)(128)(4,1)S(1)}, s32[]{:S(2)}) async-start(s8[9437184]{0:T(1024)(128)(4,1)} %bitcast.117), calls=%async_computation.8 | async-start | bytes 8388608
  760.0 7.2 slice-start.1
  761.8 5.5 slice-start.2
  (10 other events, 9.6 us)
Sparse Core Ops, SparseCore 0:
  14.6 30.4 all-gather.4
  70.0 34.4 all-gather.8
  106.1 34.4 all-gather.6
  142.9 91.2 all-gather.10
  576.1 71.8 reduce-scatter.2
  651.9 105.4 reduce-scatter.4

commit v5 on v4

--- a/solution.py
+++ b/solution.py
@@ -37,146 +37,10 @@
     pl.semaphore_wait(bar, jnp.where((z == 0) | (z == 3), 1, 2))
 
 
-def gather_kernel(n, tile, width, x_ref, o_ref, lsem, *sems):
-    su, ru, sd, rd = sems
-    z = lax.axis_index("tp")
-    barrier_line(z)
-
-    def place(src, t):
-        return o_ref.at[pl.ds(t * tile, tile), pl.ds(pl.multiple_of(src * width, width), width)]
-
-    def send(src, t, k, way):
-        ss, rs = (su, ru) if way > 0 else (sd, rd)
-        here = x_ref.at[pl.ds(t * tile, tile)] if k == 0 else place(src, t)
-        return pltpu.make_async_remote_copy(
-            here, place(src, t), ss.at[k, t], rs.at[k, t],
-            device_id={"tp": z + way}, device_id_type=MESH)
-
-    own = pltpu.make_async_copy(x_ref, o_ref.at[:, pl.ds(pl.multiple_of(z * width, width), width)], lsem)
-    own.start()
-    for k in range(3):
-        for t in range(n):
-            for way in (1, -1):
-                src = z - way * k
-                ok = (z + way >= 0) & (z + way <= 3) & (src >= 0) & (src <= 3)
-                if k > 0:
-                    came = (src >= 0) & (src <= 3)
-
-                    @pl.when(came)
-                    def _():
-                        send(src, t, k - 1, way).wait_recv()
-
-                @pl.when(ok)
-                def _():
-                    send(src, t, k, way).start()
-    for way in (1, -1):
-        src = z - way * 3
-        came = (src >= 0) & (src <= 3)
-
-        @pl.when(came)
-        def _():
-            for t in range(n):
-                send(src, t, 2, way).wait_recv()
-
-    for k in range(3):
-        for way in (1, -1):
-            src = z - way * k
-            ok = (z + way >= 0) & (z + way <= 3) & (src >= 0) & (src <= 3)
-
-            @pl.when(ok)
-            def _():
-                for t in range(n):
-                    send(src, t, k, way).wait_send()
-    own.wait()
-
-
-def gather_tp(x, ident):
-    rows, width = x.shape
-    tile = 256 if rows % 256 == 0 else rows
-    n = rows // tile
-    dma = pltpu.SemaphoreType.DMA((3, n))
-    return pl.pallas_call(
-        functools.partial(gather_kernel, n, tile, width),
-        out_shape=jax.ShapeDtypeStruct((rows, 4 * width), x.dtype),
-        in_specs=[pl.BlockSpec(memory_space=pl.ANY)],
-        out_specs=pl.BlockSpec(memory_space=pl.ANY),
-        scratch_shapes=[pltpu.SemaphoreType.DMA] + [dma] * 4,
-        compiler_params=pltpu.CompilerParams(collective_id=ident, has_side_effects=True),
-        name=f"gather_tp_{ident}",
-    )(x)
-
-
 def block_starts(half, t, blocks, rank):
     if half == 0:
         return t
     return jnp.where(t < blocks, t, t + rank + 1)
-
-
-def attend_kernel(blocks, q_ref, kv_ref, qs_ref, ks_ref, o_ref, l_ref):
-    rank = lax.axis_index("ctx")
-    size, head = q_ref.shape[2:]
-    row = lax.broadcasted_iota(jnp.int32, (size, size), 0)
-    col = lax.broadcasted_iota(jnp.int32, (size, size), 1)
-    for half in range(2):
-        q = q_ref[0, half] * jnp.asarray(SCALE, BF16)
-        qseg = qs_ref[0, half]
-
-        def part(block):
-            start = pl.multiple_of(block * size, size)
-            k = kv_ref[0, pl.ds(start, size), :head]
-            v = kv_ref[0, pl.ds(start, size), head:]
-            same = qseg == ks_ref[0, :, pl.ds(start, size)]
-            return dot(q, k, NT), v, same
-
-        s, v, same = part(rank + half * blocks)
-        order = (col <= row) if half == 0 else (col >= row)
-        s = jnp.where((same & order) | (col == row), s, NEGATIVE)
-        top = jnp.max(s, axis=1, keepdims=True)
-        p = jnp.exp(s - top)
-        mass = jnp.sum(p, axis=1, keepdims=True)
-        acc = dot(p.astype(BF16), v)
-
-        def step(t, carry):
-            top, mass, acc = carry
-            s, v, same = part(block_starts(half, t, blocks, rank))
-            s = jnp.where(same, s, NEGATIVE)
-            new = jnp.maximum(top, jnp.max(s, axis=1, keepdims=True))
-            keep = jnp.exp(top - new)
-            p = jnp.exp(s - new)
-            mass = mass * keep + jnp.sum(p, axis=1, keepdims=True)
-            acc = acc * keep + dot(p.astype(BF16), v)
-            return new, mass, acc
-
-        count = rank if half == 0 else 2 * blocks - 1 - rank
-        top, mass, acc = lax.fori_loop(0, count, step, (top, mass, acc))
-        o_ref[0, half] = (acc / mass).astype(BF16)
-        l_ref[0, half] = top + jnp.log(mass)
-
-
-def attend(q, kv, qseg, kseg):
-    groups, _, size, head = q.shape
-    length = kv.shape[1]
-    blocks = length // (2 * size)
-    return pl.pallas_call(
-        functools.partial(attend_kernel, blocks),
-        grid=(groups,),
-        out_shape=(
-            jax.ShapeDtypeStruct(q.shape, BF16),
-            jax.ShapeDtypeStruct((groups, 2, size, 1), F32),
-        ),
-        in_specs=[
-            pl.BlockSpec((1, 2, size, head), lambda g: (g, 0, 0, 0)),
-            pl.BlockSpec((1, length, 2 * head), lambda g: (g, 0, 0)),
-            pl.BlockSpec((1, 2, size, 1), lambda g: (g, 0, 0, 0)),
-            pl.BlockSpec((1, 1, length), lambda g: (g, 0, 0)),
-        ],
-        out_specs=(
-            pl.BlockSpec((1, 2, size, head), lambda g: (g, 0, 0, 0)),
-            pl.BlockSpec((1, 2, size, 1), lambda g: (g, 0, 0, 0)),
-        ),
-        compiler_params=pltpu.CompilerParams(vmem_limit_bytes=48 * 2**20),
-        name="attend",
-    )(q, kv, qseg, kseg)
 
 
 def attend_back_kernel(blocks, q_ref, kv_ref, do_ref, l_ref, d_ref, qs_ref, ks_ref,
@@ -418,7 +282,7 @@
     ]
 
 
-def ffn_forward_kernel(tiles, tile, chunk, hidden, x_ref, h0_ref, h1_ref, gain_ref, w_ref,
+def ffn_forward_kernel(tiles, tile, chunk, hidden, x_ref, h_ref, gain_ref, w_ref,
                        attn_ref, two_ref, gate_ref, up_ref, out_ref, wo_ref, wg_ref, wu_ref, wd_ref, w_sem, own, near, far, *sems):
     i = pl.program_id(0)
     per = tile // chunk
@@ -439,8 +303,7 @@
         for copy in copies:
             copy.wait()
 
-    heads = jnp.where(i < tiles // 2, h0_ref[...], h1_ref[...])
-    attn = dot(heads, wo_ref[...], NT).astype(BF16)
+    attn = dot(h_ref[...], wo_ref[...], NT).astype(BF16)
     attn_ref[...] = attn
     middle, _, _ = middle_of(x_ref[...], attn, gain_ref[1:2, :])
     hat, _ = norm_parts(middle)
@@ -497,10 +360,9 @@
 
 def ffn_forward(x, heads, gains, weights, hidden, ident):
     rows, width = x.shape
-    all_heads = heads[0].shape[1]
+    all_heads = heads.shape[1]
     tile, chunk = 256, 128
     tiles = rows // tile
-    half = tiles // 2
     count = rows // chunk
     wide = wide_of(hidden)
     return pl.pallas_call(
@@ -515,8 +377,7 @@
         ),
         in_specs=[
             tile_block(tile, width),
-            pl.BlockSpec((tile, all_heads), lambda i: (jnp.minimum(i, half - 1), 0)),
-            pl.BlockSpec((tile, all_heads), lambda i: (jnp.maximum(i - half, 0), 0)),
+            tile_block(tile, all_heads),
             whole_block(gains.shape),
             ANY,
         ],
@@ -527,7 +388,7 @@
         compiler_params=pltpu.CompilerParams(
             collective_id=ident, has_side_effects=True, vmem_limit_bytes=60 * 2**20),
         name="ffn_forward",
-    )(x, heads[0], heads[1], gains, weights)
+    )(x, heads, gains, weights)
 
 
 def ffn_backward_kernel(tiles, tile, chunk, slots, hidden, x_ref, attn_ref, dy_ref, ffn_ref, two_ref, gate_ref, up_ref,
@@ -716,38 +577,6 @@
     )(x, attn, dy, d_two, heads, gains, weights)
 
 
-class ResidentSum(LineSum):
-    def outwards(self, c):
-        return pltpu.make_async_remote_copy(
-            self.out.at[self.rows(c)], self.out.at[self.rows(c)], self.sems[4].at[c], self.sems[5].at[c],
-            device_id={"tp": self.my_leaf}, device_id_type=MESH)
-
-    def total(self, c):
-        @pl.when(self.hub)
-        def _():
-            self.across(c).wait_recv()
-            at = self.rows(c)
-            self.out[at, :] = (self.own[at, :].astype(F32) + self.far[at, :].astype(F32)).astype(BF16)
-            self.outwards(c).start()
-
-    def arrived(self, c):
-        @pl.when(self.leaf)
-        def _():
-            self.outwards(c).wait_recv()
-
-    def finish(self):
-        @pl.when(self.leaf)
-        def _():
-            for c in range(self.count):
-                self.inwards(c).wait_send()
-
-        @pl.when(self.hub)
-        def _():
-            for c in range(self.count):
-                self.across(c).wait_send()
-                self.outwards(c).wait_send()
-
-
 class LineGather:
     def __init__(self, whole, tile, width, sems):
         self.whole, self.tile, self.width, self.sems = whole, tile, width, sems
@@ -803,6 +632,306 @@
                         return 0
 
                     lax.fori_loop(0, tiles, one, 0)
+
+
+class Shared:
+    def __init__(self, over_dp):
+        self.ctx = ctx = lax.axis_size("ctx")
+        me = lax.axis_index("ctx")
+        self.devices = ctx
+        if over_dp:
+            me = me + lax.axis_index("dp") * ctx
+            self.devices = ctx * lax.axis_size("dp")
+        self.over_dp = over_dp
+        self.me = me
+        self.chips = self.devices // 2
+        self.core = lax.rem(me, 2)
+        self.chip = lax.div(me, 2)
+
+    def ident(self, device):
+        if self.over_dp:
+            return {"dp": lax.div(device, self.ctx), "ctx": lax.rem(device, self.ctx)}
+        return {"ctx": device}
+
+    def other(self, k):
+        return 2 * lax.rem(self.chip + k + self.chips, self.chips) + self.core
+
+    def partner(self):
+        return self.me + 1 - 2 * self.core
+
+    def greet(self, z):
+        bar = pltpu.get_barrier_semaphore()
+        for device in [self.partner()] + [self.other(k) for k in range(1, self.chips)]:
+            pl.semaphore_signal(bar, inc=1, device_id=self.ident(device), device_id_type=MESH)
+
+        @pl.when(z > 0)
+        def _():
+            pl.semaphore_signal(bar, inc=1, device_id={"tp": z - 1}, device_id_type=MESH)
+
+        @pl.when(z < 3)
+        def _():
+            pl.semaphore_signal(bar, inc=1, device_id={"tp": z + 1}, device_id_type=MESH)
+
+        pl.semaphore_wait(bar, self.chips + jnp.where((z == 0) | (z == 3), 1, 2))
+
+    def copy(self, source, target, send, recv, device):
+        return pltpu.make_async_remote_copy(
+            source, target, send, recv, device_id=self.ident(device), device_id_type=MESH)
+
+
+def first_gather_kernel(a_ref, b_ref, all_ref, line_ref, lsem, ss1, rs1, ss2, rs2, *sems):
+    group = Shared(True)
+    line = LineGather(line_ref, b_ref.shape[0], b_ref.shape[1], sems)
+    width = b_ref.shape[1]
+    own = [
+        pltpu.make_async_copy(a_ref, all_ref.at[group.me], lsem.at[0]),
+        pltpu.make_async_copy(b_ref, line_ref.at[:, pl.ds(pl.multiple_of(line.z * width, width), width)], lsem.at[1]),
+    ]
+    for copy in own:
+        copy.start()
+    group.greet(line.z)
+
+    def direct(k, incoming=False):
+        at = all_ref.at[group.other(-k)] if incoming else all_ref.at[group.me]
+        return group.copy(a_ref, at, ss1.at[k], rs1.at[k], group.other(k))
+
+    def inner(k, incoming=False):
+        at = all_ref.at[group.other(-k)]
+        if incoming:
+            at = all_ref.at[group.other(-k) + 1 - 2 * group.core]
+        return group.copy(a_ref if k == 0 else at, at, ss2.at[k], rs2.at[k], group.partner())
+
+    for k in range(1, group.chips):
+        direct(k).start()
+    inner(0).start()
+    for copy in own:
+        copy.wait()
+    line.forward(0, 0)
+    line.forward(0, 1)
+    line.forward(0, 2)
+    for k in range(1, group.chips):
+        direct(k, True).wait_recv()
+        inner(k).start()
+    for k in range(group.chips):
+        inner(k, True).wait_recv()
+    line.arrived(0)
+    for k in range(1, group.chips):
+        direct(k).wait_send()
+    for k in range(group.chips):
+        inner(k).wait_send()
+    line.finish(1)
+
+
+def first_gather(a, b, devices, ident):
+    dma = pltpu.SemaphoreType.DMA((devices // 2,))
+    hop = pltpu.SemaphoreType.DMA((3, 1))
+    return pl.pallas_call(
+        first_gather_kernel,
+        out_shape=(
+            jax.ShapeDtypeStruct((devices,) + a.shape, a.dtype),
+            jax.ShapeDtypeStruct((b.shape[0], 4 * b.shape[1]), b.dtype),
+        ),
+        in_specs=[ANY, ANY],
+        out_specs=(ANY, ANY),
+        scratch_shapes=[pltpu.SemaphoreType.DMA((2,))] + [dma] * 4 + [hop] * 4,
+        compiler_params=pltpu.CompilerParams(collective_id=ident, has_side_effects=True),
+        name="first_gather",
+    )(a, b)
+
+
+def attention_kernel(groups, size, x_ref, w_ref, gain_ref, gq_ref, gk_ref, cos_ref, sin_ref, qs_ref, ks_ref,
+                     q_ref, qhat_ref, qinv_ref, khat_ref, kinv_ref, heads_ref, log_ref, kv_out, all_out,
+                     kv, whole, store_kv, store_all, ss1, rs1, ss2, rs2, *sems):
+    head = q_ref.shape[1]
+    length = kv.shape[1]
+    blocks = length // (2 * size)
+    group = Shared(False)
+    rank = group.me
+    line = LineGather(whole, size, head, sems)
+    z = line.z
+    tile = min(256, size)
+    group.greet(z)
+
+    def place(g, half, c):
+        return kv.at[g, pl.ds(pl.multiple_of(half * (length // 2) + c * size, size), size)]
+
+    def direct(g, half, k, incoming=False):
+        at = place(g, half, group.other(-k) if incoming else rank)
+        return group.copy(at, at, ss1.at[g, half, k], rs1.at[g, half, k], group.other(k))
+
+    def inner(g, half, k, incoming=False):
+        block = group.other(-k)
+        at = place(g, half, block + 1 - 2 * group.core if incoming else block)
+        return group.copy(at, at, ss2.at[g, half, k], rs2.at[g, half, k], group.partner())
+
+    def project(g, half, u):
+        rows = pl.ds((2 * g + half) * size + u * tile, tile)
+        spot = pl.ds(half * size + u * tile, tile)
+        cosine, sine = cos_ref[spot, :], sin_ref[spot, :]
+        hat, _ = norm_parts(x_ref[rows, :].astype(F32))
+        raw = dot((hat * (1.0 + gain_ref[0:1, :])).astype(BF16), w_ref[...])
+        hat, inv = norm_parts(raw[:, :head])
+        qhat_ref[rows, :] = hat
+        qinv_ref[rows, :] = inv
+        q_ref[rows, :] = rotate(hat * (1.0 + gq_ref[...]), cosine, sine).astype(BF16)
+        hat, inv = norm_parts(raw[:, head : 2 * head])
+        khat_ref[rows, :] = hat
+        kinv_ref[rows, :] = inv
+        at = pl.ds(pl.multiple_of(half * (length // 2) + rank * size + u * tile, tile), tile)
+        kv[g, at, :head] = rotate(hat * (1.0 + gk_ref[...]), cosine, sine).astype(BF16)
+        kv[g, at, head:] = raw[:, 2 * head :].astype(BF16)
+
+    def attend(g, half):
+        row = lax.broadcasted_iota(jnp.int32, (size, size), 0)
+        col = lax.broadcasted_iota(jnp.int32, (size, size), 1)
+        rows = pl.ds((2 * g + half) * size, size)
+        q = q_ref[rows, :] * jnp.asarray(SCALE, BF16)
+        qseg = qs_ref[g, half]
+
+        def part(block):
+            at = pl.ds(pl.multiple_of(block * size, size), size)
+            same = qseg == ks_ref[g, :, at]
+            return dot(q, kv[g, at, :head], NT), kv[g, at, head:], same
+
+        s, v, same = part(rank + half * blocks)
+        order = (col <= row) if half == 0 else (col >= row)
+        s = jnp.where((same & order) | (col == row), s, NEGATIVE)
+        top = jnp.max(s, axis=1, keepdims=True)
+        p = jnp.exp(s - top)
+        mass = jnp.sum(p, axis=1, keepdims=True)
+        acc = dot(p.astype(BF16), v)
+
+        def step(t, carry):
+            top, mass, acc = carry
+            s, v, same = part(block_starts(half, t, blocks, rank))
+            s = jnp.where(same, s, NEGATIVE)
+            new = jnp.maximum(top, jnp.max(s, axis=1, keepdims=True))
+            keep = jnp.exp(top - new)
+            p = jnp.exp(s - new)
+            mass = mass * keep + jnp.sum(p, axis=1, keepdims=True)
+            return new, mass, acc * keep + dot(p.astype(BF16), v)
+
+        count = rank if half == 0 else 2 * blocks - 1 - rank
+        top, mass, acc = lax.fori_loop(0, count, step, (top, mass, acc))
+        out = (acc / mass).astype(BF16)
+        heads_ref[rows, :] = out
+        whole[rows, pl.ds(pl.multiple_of(z * head, head), head)] = out
+        log_ref[g, half] = top + jnp.log(mass)
+
+    chips = range(1, group.chips)
+    for g in range(groups):
+        for half in range(2):
+            for u in range(size // tile):
+                project(g, half, u)
+            for k in chips:
+                direct(g, half, k).start()
+            inner(g, half, 0).start()
+    tiles = 2 * groups
+
+    def hops(t):
+        for hop in range(3):
+            if 0 <= t - hop < tiles:
+                line.forward(t - hop, hop)
+
+    def keep(t):
+        at = pl.ds(t * size, size)
+        return pltpu.make_async_copy(whole.at[at], all_out.at[at], store_all.at[t])
+
+    def save(g):
+        return pltpu.make_async_copy(kv.at[g], kv_out.at[g], store_kv.at[g])
+
+    for g in range(groups):
+        for half in range(2):
+            for k in chips:
+                direct(g, half, k, True).wait_recv()
+                inner(g, half, k).start()
+        for half in range(2):
+            for k in range(group.chips):
+                inner(g, half, k, True).wait_recv()
+        save(g).start()
+        for half in range(2):
+            attend(g, half)
+            hops(2 * g + half)
+    for t in range(tiles, tiles + 2):
+        hops(t)
+    for t in range(tiles):
+        line.arrived(t)
+        keep(t).start()
+    for g in range(groups):
+        save(g).wait()
+        for half in range(2):
+            for k in chips:
+                direct(g, half, k).wait_send()
+            for k in range(group.chips):
+                inner(g, half, k).wait_send()
+    line.finish(tiles)
+    for t in range(tiles):
+        keep(t).wait()
+
+
+def attention(x, w, gains, gain_query, gain_key, cosine, sine, qseg, kseg, ident):
+    rows, width = x.shape
+    groups, _, size, _ = qseg.shape
+    length = kseg.shape[2]
+    head = gain_query.shape[1]
+    chips = length // (4 * size)
+    tiles = 2 * groups
+    vmem = pl.BlockSpec(memory_space=pltpu.VMEM)
+    dma = pltpu.SemaphoreType.DMA
+    return pl.pallas_call(
+        functools.partial(attention_kernel, groups, size),
+        out_shape=(
+            jax.ShapeDtypeStruct((rows, head), BF16),
+            jax.ShapeDtypeStruct((rows, head), F32),
+            jax.ShapeDtypeStruct((rows, 1), F32),
+            jax.ShapeDtypeStruct((rows, head), F32),
+            jax.ShapeDtypeStruct((rows, 1), F32),
+            jax.ShapeDtypeStruct((rows, head), BF16),
+            jax.ShapeDtypeStruct((groups, 2, size, 1), F32),
+            jax.ShapeDtypeStruct((groups, length, 2 * head), BF16),
+            jax.ShapeDtypeStruct((rows, 4 * head), BF16),
+        ),
+        in_specs=[vmem] * 9,
+        out_specs=(vmem,) * 7 + (ANY, ANY),
+        scratch_shapes=[
+            pltpu.VMEM((groups, length, 2 * head), BF16), pltpu.VMEM((rows, 4 * head), BF16),
+            dma((groups,)), dma((tiles,))] + [dma((groups, 2, chips))] * 4 + [dma((3, tiles))] * 4,
+        compiler_params=pltpu.CompilerParams(
+            collective_id=ident, has_side_effects=True, vmem_limit_bytes=60 * 2**20),
+        name="attention",
+    )(x, w, gains, gain_query, gain_key, cosine, sine, qseg, kseg)
+
+
+class ResidentSum(LineSum):
+    def outwards(self, c):
+        return pltpu.make_async_remote_copy(
+            self.out.at[self.rows(c)], self.out.at[self.rows(c)], self.sems[4].at[c], self.sems[5].at[c],
+            device_id={"tp": self.my_leaf}, device_id_type=MESH)
+
+    def total(self, c):
+        @pl.when(self.hub)
+        def _():
+            self.across(c).wait_recv()
+            at = self.rows(c)
+            self.out[at, :] = (self.own[at, :].astype(F32) + self.far[at, :].astype(F32)).astype(BF16)
+            self.outwards(c).start()
+
+    def arrived(self, c):
+        @pl.when(self.leaf)
+        def _():
+            self.outwards(c).wait_recv()
+
+    def finish(self):
+        @pl.when(self.leaf)
+        def _():
+            for c in range(self.count):
+                self.inwards(c).wait_send()
+
+        @pl.when(self.hub)
+        def _():
+            for c in range(self.count):
+                self.across(c).wait_send()
+                self.outwards(c).wait_send()
 
 
 def query_back_kernel(tiles, tile, dq_ref, hat_ref, inv_ref, cos_ref, sin_ref, x_ref, gain_ref, gq_ref, w_ref,
@@ -1100,8 +1229,15 @@
     extra = jnp.concatenate(
         [column(g) for g in (g_input, g_post_attn, g_pre_ffn, g_post_ffn, g_query, g_key)] + [ids.astype(BF16)], axis=1)
     extra = jnp.pad(extra, ((0, 0), (0, 128 - extra.shape[1])))
-    first = lax.all_gather(
-        jnp.concatenate([w_query, w_key, w_value, extra], axis=1), shared, axis=0, tiled=True)
+
+    def rows_of_16(w):
+        return jnp.pad(w, ((0, -own_rows % 16), (0, 0)))
+
+    first, line = first_gather(
+        rows_of_16(jnp.concatenate([w_query, w_key, w_value, extra], axis=1)),
+        rows_of_16(jnp.concatenate([w_query, w_out.T], axis=1)), width // own_rows, 5)
+    first = first[:, :own_rows].reshape(width, -1)
+    line = line[:own_rows]
     mat_qkv = first[:, : 3 * head]
     side = first[:, 3 * head :]
     gain_cols = side[:, :8].astype(F32)
@@ -1115,46 +1251,23 @@
     key_ids = ids.reshape(ctx, groups, 2, size).transpose(1, 2, 0, 3).reshape(groups, length)
     key_ids = jnp.where(key_ids == 0, -1, key_ids)
 
-    def rows_of_16(w):
-        return jnp.pad(w, ((0, -own_rows % 16), (0, 0)))
-
     wide = wide_of(hidden)
-    line = gather_tp(rows_of_16(jnp.concatenate([w_query, w_out.T], axis=1)), 5)[:own_rows]
     second = jnp.concatenate(
         [line] + [jnp.pad(w, ((0, 0), (0, wide - hidden))) for w in (w_gate, w_up, w_down.T)], axis=1)
+    weights = lax.all_gather(second, shared, axis=0, tiled=True)
 
     offsets = rank * size + jnp.arange(size, dtype=jnp.int32)
     position = jnp.concatenate([offsets, length - 1 - offsets]).astype(F32)
     cosine, sine = angles(position, head // 2, head)
+    turn = (cosine, sine)
     cosine = jnp.broadcast_to(cosine, (groups, per_group, head // 2)).reshape(rows, head // 2)
     sine = jnp.broadcast_to(sine, (groups, per_group, head // 2)).reshape(rows, head // 2)
 
-    inputs = tokens.reshape(rows, width).astype(F32)
-
-    norm_one, scale_one = norm_parts(inputs)
-    hidden_one = (norm_one * (1.0 + gain_input)).astype(BF16)
-    raw = dot(hidden_one, mat_qkv)
-    q_hat, q_scale = norm_parts(raw[:, :head])
-    k_hat, k_scale = norm_parts(raw[:, head : 2 * head])
-    queries = rotate(q_hat * (1.0 + gain_query), cosine, sine).astype(BF16)
-    keys = rotate(k_hat * (1.0 + gain_key), cosine, sine).astype(BF16)
-    values = raw[:, 2 * head :].astype(BF16)
-    queries = queries.reshape(groups, 2, size, head)
-    pairs = jnp.concatenate([keys, values], axis=1).reshape(batches, seq_local, 2, size, 2 * head)
-    kv = [lax.all_gather(pairs[m], "ctx", axis=2, tiled=True).reshape(seq_local, length, 2 * head) for m in range(batches)]
-    kv[-1], second = lax.optimization_barrier((kv[-1], second))
-    weights = lax.all_gather(second, shared, axis=0, tiled=True)
-    heads, heads_all, log_mass = [], [], []
-    for m in range(batches):
-        part = slice(m * seq_local, (m + 1) * seq_local)
-        out, log = attend(queries[part], kv[m], own_ids[part, :, :, None], key_ids[part, None, :])
-        heads.append(out.reshape(rows // batches, head))
-        heads_all.append(gather_tp(heads[m], m * 6))
-        log_mass.append(log)
-    heads_own = jnp.concatenate(heads)
-    log_mass = jnp.concatenate(log_mass)
     x_rows = tokens.reshape(rows, width)
     dy_rows = cotangent.reshape(rows, width)
+    queries, q_hat, q_scale, k_hat, k_scale, heads_own, log_mass, kv, heads_all = attention(
+        x_rows, mat_qkv, gain_rows, gain_query[None], gain_key[None], *turn, own_ids[..., None], key_ids[:, None, :], 0)
+
     attn, hidden_two, gate, up, ffn_out = ffn_forward(x_rows, heads_all, gain_rows, weights, hidden, 1)
     output, d_gain_post_ffn, grad_ffn, d_two = ffn_backward(
         x_rows, attn, dy_rows, ffn_out, hidden_two, gate, up, gain_rows, weights, 2)
@@ -1163,7 +1276,7 @@
         x_rows, attn, dy_rows, d_two, heads_own, gain_rows, weights)
 
     d_query, d_kv = attend_back(
-        queries, jnp.concatenate(kv), d_heads.reshape(groups, 2, size, head),
+        queries.reshape(groups, 2, size, head), kv, d_heads.reshape(groups, 2, size, head),
         log_mass.reshape(groups, 2, 1, size), delta.reshape(groups, 2, 1, size),
         own_ids[:, :, None, :], key_ids[:, :, None])
     d_kv = lax.psum_scatter(

time: 787 us -> 773 us (0.982)
  Pallas kernels: 621 us -> 689 us
  waiting for transfers between devices: 45.9 us -> 0.68 us
  other arithmetic: 36.2 us -> 19.6 us
  local copies, waits for them, and re-layouts: 49.7 us -> 39.4 us
  matrix products: 9.94 us -> 0 us
    pallas_call x5 -> x2, Pallas kernels: 114 us -> 176 us  [the longest x1 145 us: attention(): pl.pallas_call(functools.partial(attention_kernel, groups, size), out_sha...]
    all_gather x3 -> x0, waiting for transfers between devices: 39.4 us -> none  [the longest x1 25.2 us: shards(): lax.all_gather(jnp.concatenate([w_query, w_key, w_value, extra], axis=1),...]
    concatenate x5 -> x0, other arithmetic: 11.1 us -> none  [the longest x1 7.57 us: shards(): jnp.concatenate(kv)]
    dot_general x1 -> x0, matrix products: 9.94 us -> none  [dot(): return lax.dot_general(a, b, dims, preferred_element_type=F32)]
    unnamed x60 -> x43, local copies, waits for them, and re-layouts: 22.6 us -> 17.6 us
  transfers between devices with their start and end apart: 6 -> 3, of which waited for: 3 -> 0; matrix products, arithmetic and copies ran while one was open for 5% -> 3% of each run, Pallas kernels for 36% -> 42%
where the time goes in v5:
time: 773 us; the launch traced here: 764 us
  Pallas kernels  689 us (89%)
  local copies, waits for them, and re-layouts  39.4 us (5%)
  other arithmetic  19.6 us (3%)
  between operations  14.6 us (2%)
    pallas_call x1, Pallas kernels, ffn_backward(): pl.pallas_call(functools.partial(ffn_backward_kernel, tiles, tile, chunk,...  151 us
    pallas_call x1, Pallas kernels, attention(): pl.pallas_call(functools.partial(attention_kernel, groups, size), out_sha...  145 us
    pallas_call x1, Pallas kernels, ffn_forward(): pl.pallas_call(functools.partial(ffn_forward_kernel, tiles, tile, chunk,...  144 us
    pallas_call x1, Pallas kernels, query_back(): pl.pallas_call(functools.partial(query_back_kernel, tiles, tile), grid=(t...  74.5 us
    pallas_call x1, Pallas kernels, key_back(): pl.pallas_call(functools.partial(key_back_kernel, tiles, tile, chunk, own...  71.4 us
    pallas_call x1, Pallas kernels, first_gather(): pl.pallas_call(first_gather_kernel, out_shape=(jax.ShapeDtypeStruct((devi...  31 us
    pallas_call x1, Pallas kernels, scatter(): pl.pallas_call(functools.partial(scatter_kernel, chips, own_rows), out_sh...  28.1 us
    pallas_call x1, Pallas kernels, attend_back(): pl.pallas_call(functools.partial(attend_back_kernel, blocks), grid=(group...  24.6 us
  transfers between devices with their start and end apart: 3, of which 0 were waited for; matrix products, arithmetic and copies ran while one was open for 3% of the time, Pallas kernels for 42%

profile of v5, /device:TPU:0, one launch (start us, length us, event | category | flops | bytes accessed | tf_op | source)
XLA Modules:
  0.0 763.5 jit_solution(4462070289007473197)
XLA Ops:
  12.7 1.6 pad_maximum_fusion.b_ref
  14.4 1.7 fusion.9.a_ref
  16.1 31.0 %first_gather.1 = (bf16[8,144,896]{2,1,0:T(8,128)(2,1)}, bf16[144,2048]{1,0:T(8,128)(2,1)}) custom-call(bf16[144,896]{1,0:T(8,128)(2,1)} %fusion.9.a_ref, bf16[144,512]{1,0:T(8,128)(2,1)} %pad_maximum_fusion.b_ref), custom_call_target="tpu_custom_call" | custom-call | tf_op jit(solution)/shard_map/first_gather/pallas_call | solution.py:728
  47.1 2.9 fusion.6
  50.3 1.3 slice.94.w_ref
  52.1 5.3 reshape.162
  61.0 1.4 copy.84.qs_ref
  62.4 3.1 multiply_sine_fusion
  66.1 145.2 %attention.1 = (bf16[2048,256]{1,0:T(8,128)(2,1)}, f32[2048,256]{1,0:T(8,128)}, f32[2048,1]{1,0:T(8,128)}, f32[2048,256]{1,0:T(8,128)}, f32[2048,1]{1,0:T(8,128)...) custom-call(bf16[2048,1152]{1,0:T(8,128)(2,1)} %bitcast.45, ...), custom_call_target="tpu_custom_call" | custom-call | tf_op jit(solution)/shard_map/attention/pallas_call | solution.py:881
  211.4 1.6 reduce.2
  213.5 4.6 compare_select_fusion.ks_ref
  218.1 144.2 %ffn_forward.1 = (bf16[2048,1152]{1,0:T(8,128)(2,1)}, bf16[2048,1152]{1,0:T(8,128)(2,1)}, bf16[2048,1728]{1,0:T(8,128)(2,1)}, bf16[2048,1728]{1,0:T(8,128)(2,1)}, bf16[2048,1152]{1,0:T(8,128)(2,1)}) custom-call(bf16[2048,1152]{1,0:T(8,128)(2,1)} %bitcast.46, bf16[2048,1024]{1,0:T(8,128)(2,1)} %get-tuple-element.50.h_ref, f32[8,1152]{1,0:T(8,128)} %copy.83.gain_ref, ...), custom_call_target="tpu_custom_call" | custom-call | tf_op jit(solution)/shard_map/ffn_forward/pallas_call | solution.py:368
  362.3 151.1 %ffn_backward.1 = (bf16[2048,1152]{1,0:T(8,128)(2,1)}, f32[1,1152]{1,0:T(1,128)}, bf16[3,1152,1728]{2,1,0:T(8,128)(2,1)}, bf16[2048,1152]{1,0:T(8,128)(2,1)}) custom-call(bf16[2048,1152]{1,0:T(8,128)(2,1)} %bitcast.47, bf16[2048,1152]{1,0:T(8,128)(2,1)} %get-tuple-element.52.attn_ref, bf16[2048,1152]{1,0:T(8,128)(2,1)} %bitcast.51, ...), custom_call_target="tpu_custom_call" | custom-call | tf_op jit(solution)/shard_map/ffn_backward/pallas_call | solution.py:500
  514.6 19.1 %middle_back.1 = (f32[2048,1152]{1,0:T(8,128)}, bf16[2048,256]{1,0:T(8,128)(2,1)S(1)}, f32[2048,1]{1,0:T(8,128)S(1)}, f32[2,1152]{1,0:T(2,128)S(1)}, bf16[1152,256]{1,0:T(8,128)(2,1)S(1)}) custom-call(bf16[2048,1152]{1,0:T(8,128)(2,1)} %bitcast.48, bf16[2048,1152]{1,0:T(8,128)(2,1)} %get-tuple-element.52.attn_ref, bf16[2048,1152]{1,0:T(8,128)(2,1)} %bitcast.52, ...), custom_call_target="tpu_custom_call" | custom-call | tf_op jit(solution)/shard_map/middle_back/pallas_call | solution.py:559
  535.6 24.6 %attend_back.1 = (f32[2,2,512,256]{3,2,1,0:T(8,128)}, bf16[2,4096,512]{2,1,0:T(8,128)(2,1)}) custom-call(bf16[2,2,512,256]{3,2,1,0:T(8,128)(2,1)} %bitcast.63, bf16[2,4096,512]{2,1,0:T(8,128)(2,1)} %get-tuple-element.59.kv_ref, bf16[2,2,512,256]{3,2,1,0:T(8,128)(2,1)} %bitcast.44, f32[2,2,1,512]{3,2,1,0:T(1,128)} %reshape.160.l_ref, ...), custom_call_target="tpu_custom_call" | custom-call | tf_op jit(solution)/shard_map/attend_back/pallas_call | solution.py:94
  561.5 1.5 copy-done.3
  564.3 74.5 %query_back.1 = (f32[2048,1152]{1,0:T(8,128)}, bf16[1152,256]{1,0:T(8,128)(2,1)S(1)}, f32[1,256]{1,0:T(1,128)S(1)}) custom-call(f32[2048,256]{1,0:T(8,128)S(1)} %bitcast.43, f32[2048,256]{1,0:T(8,128)} %get-tuple-element.67.hat_ref, f32[2048,1]{1,0:T(8,128)S(1)} %copy-done.5, f32[2048,128]{1,0:T(8,128)S(1)} %bitcast.39, f32[2048,128]{1,0:T(8,128)S(1)} %bitcast.41, ...), custom_call_target="tpu_custom_call" | custom-call | tf_op jit(solution)/shard_map/query_back/pallas_call | solution.py:999
  640.1 71.4 %key_back.1 = (f32[2048,1152]{1,0:T(8,128)}, bf16[1152,1152]{1,0:T(8,128)(2,1)}) custom-call(bf16[2048,512]{1,0:T(8,128)(2,1)} %bitcast.62, f32[2048,256]{1,0:T(8,128)} %get-tuple-element.71.hat_ref, f32[2048,1]{1,0:T(8,128)} %get-tuple-element.72.inv_ref, f32[2048,128]{1,0:T(8,128)} %bitcast.40, f32[2048,128]{1,0:T(8,128)} %bitcast.42, ...), custom_call_target="tpu_custom_call" | custom-call | tf_op jit(solution)/shard_map/key_back/pallas_call | solution.py:1117
  711.6 1.7 copy-done.2
  713.3 28.1 %scatter.1 = f32[144,1152]{1,0:T(8,128)S(1)} custom-call(bf16[1152,1152]{1,0:T(8,128)(2,1)S(1)} %copy-done.2), custom_call_target="tpu_custom_call" | custom-call | tf_op jit(solution)/shard_map/scatter/pallas_call | solution.py:1197
  743.8 1.8 convert_element_type.35
  745.6 1.7 slice_bitcast_fusion
  747.3 5.5 copy.99
  752.8 3.7 copy.100
  (88 shorter events, 20.5 us)
Async XLA Ops:
  7.2 210.9 %all-gather.2.cloned.1.call-start = ((), (), s32[]{:S(2)}) async-start(), calls=%async_computation.2 | async-start | bytes 19243008 | tf_op jit(solution)/shard_map/all_gather | solution.py:1257
  47.1 3.0 copy-start.13
  50.1 590.1 %reduce-scatter.3.cloned.1.call-start = ((), (), s32[]{:S(2)}) async-start(), calls=%async_computation.3 | async-start | bytes 10485760 | tf_op jit(solution)/shard_map/reduce_scatter | solution.py:1282
  50.3 7.1 copy-start.16
  362.3 151.1 %copy-start.4 = (f32[8,1152]{1,0:T(8,128)S(1)}, f32[8,1152]{1,0:T(8,128)}, u32[]{:S(2)}) copy-start(f32[8,1152]{1,0:T(8,128)} %copy.83.gain_ref) | copy-start | bytes 110596
  513.4 1.2 copy-start.6
  533.8 0.8 copy-start.8
  534.6 1.0 copy-start.7
  534.6 25.6 %copy-start.10 = (f32[2,1152]{1,0:T(2,128)}, f32[2,1152]{1,0:T(2,128)S(1)}, u32[]{:S(2)}) copy-start(f32[2,1152]{1,0:T(2,128)S(1)} %get-tuple-element.76.dg_mid_ref) | copy-start | bytes 27652
  560.2 183.6 %reduce-scatter.5.cloned.1.call-start = ((), (), s32[]{:S(2)}) async-start(), calls=%async_computation.4 | async-start | bytes 13934592 | tf_op jit(solution)/shard_map/reduce_scatter | solution.py:1274
  560.2 1.0 copy-start.15
  560.2 1.2 copy-start.14
  560.2 1.3 copy-start.11
  560.9 2.1 copy-start.3
  561.3 77.4 %copy-start = (f32[2,1024,128]{2,1,0:T(8,128)}, f32[2,1024,128]{2,1,0:T(8,128)S(1)}, u32[]{:S(2)}) copy-start(f32[2,1024,128]{2,1,0:T(8,128)S(1)} %broadcast_in_dim.42) | copy-start | bytes 3145732
  561.5 77.2 %copy-start.1 = (f32[2,1024,128]{2,1,0:T(8,128)}, f32[2,1024,128]{2,1,0:T(8,128)S(1)}, u32[]{:S(2)}) copy-start(f32[2,1024,128]{2,1,0:T(8,128)S(1)} %broadcast_in_dim.43) | copy-start | bytes 3145732
  563.0 1.2 copy-start.5
  638.7 0.8 copy-start.9
  639.6 0.6 copy-start.12
  711.6 1.8 copy-start.2
  743.8 9.0 %slice-start = ((s8[9437184]{0:T(1024)(128)(4,1)}), s8[4194304]{0:T(1024)(128)(4,1)S(1)}, s32[]{:S(2)}) async-start(s8[9437184]{0:T(1024)(128)(4,1)} %bitcast.57), calls=%async_computation.5 | async-start | bytes 8388608
  745.6 7.2 slice-start.1
  747.3 5.5 slice-start.2
Sparse Core Ops, SparseCore 0:
  50.2 125.4 all-gather.1
  560.3 73.2 reduce-scatter.2
  637.7 105.4 reduce-scatter.4

commit v6 on v5

--- a/solution.py
+++ b/solution.py
@@ -63,7 +63,8 @@
             rows = pl.ds(pl.multiple_of(block * size, size), size)
             k = kv_ref[0, rows, :head]
             v = kv_ref[0, rows, head:]
-            allowed = ks_ref[0, rows, :] == qseg
+            ids = jnp.broadcast_to(ks_ref[0, :, rows], (8, size))
+            allowed = jnp.transpose(ids)[:, 0:1] == qseg
             if own:
                 order = (row <= col) if half == 0 else (row >= col)
                 allowed = (allowed & order) | (col == row)
@@ -99,7 +100,7 @@
             jax.ShapeDtypeStruct((groups, length, 2 * head), BF16),
         ),
         in_specs=[halves, whole, halves, line, line, line,
-                  pl.BlockSpec((1, length, 1), lambda g: (g, 0, 0))],
+                  pl.BlockSpec((1, 1, length), lambda g: (g, 0, 0))],
         out_specs=(halves, pl.BlockSpec((1, length, 2 * head), lambda g: (g, 0, 0))),
         scratch_shapes=[pltpu.VMEM((length, head), F32)] * 2,
         compiler_params=pltpu.CompilerParams(vmem_limit_bytes=56 * 2**20),
@@ -292,11 +293,7 @@
     @pl.when(i == 0)
     def _():
         copies = load_ffn_weights(w_ref, (wg_ref, wu_ref, wd_ref), w_sem)
-        copies += [
-            pltpu.make_async_copy(
-                w_ref.at[:, pl.ds((2 * j + 1) * head, head)], wo_ref.at[:, pl.ds(j * head, head)], w_sem.at[3 + j])
-            for j in range(4)
-        ]
+        copies.append(pltpu.make_async_copy(w_ref.at[:, pl.ds(0, 4 * head)], wo_ref, w_sem.at[3]))
         for copy in copies:
             copy.start()
         barrier_line(line.z)
@@ -383,7 +380,7 @@
         ],
         out_specs=(tile_block(tile, width), tile_block(tile, width), tile_block(tile, hidden), tile_block(tile, hidden), ANY),
         scratch_shapes=[pltpu.VMEM((width, all_heads), BF16)] + [pltpu.VMEM((width, wide), BF16)] * 3
-        + [pltpu.SemaphoreType.DMA((7,))]
+        + [pltpu.SemaphoreType.DMA((4,))]
         + line_sum_scratch(count, chunk, count, width),
         compiler_params=pltpu.CompilerParams(
             collective_id=ident, has_side_effects=True, vmem_limit_bytes=60 * 2**20),
@@ -525,7 +522,7 @@
     @pl.when(i == 0)
     def _():
         head = wo_ref.shape[1]
-        at = pl.multiple_of((2 * lax.axis_index("tp") + 1) * head, head)
+        at = pl.multiple_of(lax.axis_index("tp") * head, head)
         copy = pltpu.make_async_copy(w_ref.at[:, pl.ds(at, head)], wo_ref, w_sem)
         copy.start()
         copy.wait()
@@ -582,11 +579,14 @@
         self.whole, self.tile, self.width, self.sems = whole, tile, width, sems
         self.z = lax.axis_index("tp")
 
+    def place(self, src, t):
+        return self.whole.at[
+            pl.ds(pl.multiple_of(t * self.tile, self.tile), self.tile),
+            pl.ds(pl.multiple_of(src * self.width, self.width), self.width)]
+
     def send(self, src, t, hop, way):
         ss, rs = self.sems[:2] if way > 0 else self.sems[2:]
-        place = self.whole.at[
-            pl.ds(pl.multiple_of(t * self.tile, self.tile), self.tile),
-            pl.ds(pl.multiple_of(src * self.width, self.width), self.width)]
+        place = self.place(src, t)
         return pltpu.make_async_remote_copy(
             place, place, ss.at[hop, t], rs.at[hop, t],
             device_id={"tp": self.z + way}, device_id_type=MESH)
@@ -632,6 +632,34 @@
                         return 0
 
                     lax.fori_loop(0, tiles, one, 0)
+
+
+class KeyGather(LineGather):
+    def __init__(self, block, chips, sems):
+        self.block, self.chips, self.sems = block, chips, sems
+        self.z = lax.axis_index("tp")
+
+    def tile_of(self, g, half, k):
+        return (2 * g + half) * (self.chips - 1) + k - 1
+
+    def place(self, src, t):
+        pair, k = divmod(t, self.chips - 1)
+        return self.quarter(pair // 2, pair % 2, k + 1, src)
+
+    def quarter(self, g, half, k, src, own=False):
+        ref, start, size = self.block(g, half, k, own)
+        rows = size // 4
+        return ref.at[pl.ds(pl.multiple_of(start + src * rows, rows), rows)]
+
+    def finish(self, tiles):
+        for hop in range(3):
+            for way in (1, -1):
+                src, ok = self.going(hop, way)
+
+                @pl.when(ok)
+                def _():
+                    for t in range(tiles):
+                        self.send(src, t, hop, way).wait_send()
 
 
 class Shared:
@@ -679,50 +707,63 @@
             source, target, send, recv, device_id=self.ident(device), device_id_type=MESH)
 
 
-def first_gather_kernel(a_ref, b_ref, all_ref, line_ref, lsem, ss1, rs1, ss2, rs2, *sems):
+def first_gather_kernel(a_ref, b_ref, i_ref, all_ref, line_ref, ids_ref, lsem, ss1, rs1, ss2, rs2, si1, ri1, si2, ri2, *sems):
     group = Shared(True)
     line = LineGather(line_ref, b_ref.shape[0], b_ref.shape[1], sems)
     width = b_ref.shape[1]
     own = [
-        pltpu.make_async_copy(a_ref, all_ref.at[group.me], lsem.at[0]),
-        pltpu.make_async_copy(b_ref, line_ref.at[:, pl.ds(pl.multiple_of(line.z * width, width), width)], lsem.at[1]),
+        pltpu.make_async_copy(b_ref, line_ref.at[:, pl.ds(pl.multiple_of(line.z * width, width), width)], lsem.at[0]),
+        pltpu.make_async_copy(a_ref, all_ref.at[group.me], lsem.at[1]),
+        pltpu.make_async_copy(i_ref, ids_ref.at[group.me], lsem.at[2]),
     ]
     for copy in own:
         copy.start()
     group.greet(line.z)
-
-    def direct(k, incoming=False):
-        at = all_ref.at[group.other(-k)] if incoming else all_ref.at[group.me]
-        return group.copy(a_ref, at, ss1.at[k], rs1.at[k], group.other(k))
-
-    def inner(k, incoming=False):
-        at = all_ref.at[group.other(-k)]
+    arrays = ((a_ref, all_ref, ss1, rs1, ss2, rs2), (i_ref, ids_ref, si1, ri1, si2, ri2))
+
+    def direct(n, k, incoming=False):
+        ref, whole, ss, rs = arrays[n][:4]
+        at = whole.at[group.other(-k)] if incoming else whole.at[group.me]
+        return group.copy(ref, at, ss.at[k], rs.at[k], group.other(k))
+
+    def inner(n, k, incoming=False):
+        ref, whole, _, _, ss, rs = arrays[n]
+        at = whole.at[group.other(-k)]
         if incoming:
-            at = all_ref.at[group.other(-k) + 1 - 2 * group.core]
-        return group.copy(a_ref if k == 0 else at, at, ss2.at[k], rs2.at[k], group.partner())
-
+            at = whole.at[group.other(-k) + 1 - 2 * group.core]
+        return group.copy(ref if k == 0 else at, at, ss.at[k], rs.at[k], group.partner())
+
+    both = range(2)
     for k in range(1, group.chips):
-        direct(k).start()
-    inner(0).start()
-    for copy in own:
+        for n in both:
+            direct(n, k).start()
+    own[0].wait()
+    line.forward(0, 0)
+    for n in both:
+        inner(n, 0).start()
+    for k in range(1, group.chips):
+        if k < 3:
+            line.forward(0, k)
+        for n in both:
+            direct(n, k, True).wait_recv()
+            inner(n, k).start()
+    for hop in range(min(3, group.chips), 3):
+        line.forward(0, hop)
+    for k in range(group.chips):
+        for n in both:
+            inner(n, k, True).wait_recv()
+    line.arrived(0)
+    for copy in own[1:]:
         copy.wait()
-    line.forward(0, 0)
-    line.forward(0, 1)
-    line.forward(0, 2)
-    for k in range(1, group.chips):
-        direct(k, True).wait_recv()
-        inner(k).start()
-    for k in range(group.chips):
-        inner(k, True).wait_recv()
-    line.arrived(0)
-    for k in range(1, group.chips):
-        direct(k).wait_send()
-    for k in range(group.chips):
-        inner(k).wait_send()
+    for n in both:
+        for k in range(1, group.chips):
+            direct(n, k).wait_send()
+        for k in range(group.chips):
+            inner(n, k).wait_send()
     line.finish(1)
 
 
-def first_gather(a, b, devices, ident):
+def first_gather(a, b, ids, devices, ident):
     dma = pltpu.SemaphoreType.DMA((devices // 2,))
     hop = pltpu.SemaphoreType.DMA((3, 1))
     return pl.pallas_call(
@@ -730,13 +771,14 @@
         out_shape=(
             jax.ShapeDtypeStruct((devices,) + a.shape, a.dtype),
             jax.ShapeDtypeStruct((b.shape[0], 4 * b.shape[1]), b.dtype),
+            jax.ShapeDtypeStruct((devices,) + ids.shape, ids.dtype),
         ),
-        in_specs=[ANY, ANY],
-        out_specs=(ANY, ANY),
-        scratch_shapes=[pltpu.SemaphoreType.DMA((2,))] + [dma] * 4 + [hop] * 4,
+        in_specs=[ANY] * 3,
+        out_specs=(ANY,) * 3,
+        scratch_shapes=[pltpu.SemaphoreType.DMA((3,))] + [dma] * 8 + [hop] * 4,
         compiler_params=pltpu.CompilerParams(collective_id=ident, has_side_effects=True),
         name="first_gather",
-    )(a, b)
+    )(a, b, ids)
 
 
 def attention_kernel(groups, size, x_ref, w_ref, gain_ref, gq_ref, gk_ref, cos_ref, sin_ref, qs_ref, ks_ref,
@@ -744,19 +786,26 @@
                      kv, whole, store_kv, store_all, ss1, rs1, ss2, rs2, *sems):
     head = q_ref.shape[1]
     length = kv.shape[1]
+    id_rows = size // 128
     blocks = length // (2 * size)
     group = Shared(False)
     rank = group.me
-    line = LineGather(whole, size, head, sems)
+    line = LineGather(whole, size, head, sems[:4])
     z = line.z
     tile = min(256, size)
     group.greet(z)
 
+    def block(g, half, k, own):
+        c = rank if own else group.other(-k)
+        return kv.at[g], half * (length // 2) + c * size, size
+
+    keys = KeyGather(block, group.chips, sems[4:])
+
     def place(g, half, c):
         return kv.at[g, pl.ds(pl.multiple_of(half * (length // 2) + c * size, size), size)]
 
     def direct(g, half, k, incoming=False):
-        at = place(g, half, group.other(-k) if incoming else rank)
+        at = keys.quarter(g, half, k, z, own=not incoming)
         return group.copy(at, at, ss1.at[g, half, k], rs1.at[g, half, k], group.other(k))
 
     def inner(g, half, k, incoming=False):
@@ -790,7 +839,10 @@
 
         def part(block):
             at = pl.ds(pl.multiple_of(block * size, size), size)
-            same = qseg == ks_ref[g, :, at]
+            device = lax.axis_index("dp") * lax.axis_size("ctx") + lax.rem(block, blocks)
+            ids = ks_ref[device, pl.ds((2 * g + lax.div(block, blocks)) * id_rows, id_rows), :]
+            ids = jnp.concatenate([ids[j : j + 1] for j in range(id_rows)], axis=1)
+            same = qseg == jnp.where(ids == 0, -1, ids)
             return dot(q, kv[g, at, :head], NT), kv[g, at, head:], same
 
         s, v, same = part(rank + half * blocks)
@@ -819,14 +871,22 @@
         log_ref[g, half] = top + jnp.log(mass)
 
     chips = range(1, group.chips)
-    for g in range(groups):
-        for half in range(2):
-            for u in range(size // tile):
-                project(g, half, u)
+    tiles = 2 * groups
+
+    def exchange(t):
+        for stage in (4, 3, 2, 1):
+            if not 0 <= t - stage < tiles:
+                continue
+            g, half = divmod(t - stage, 2)
             for k in chips:
-                direct(g, half, k).start()
-            inner(g, half, 0).start()
-    tiles = 2 * groups
+                spot = keys.tile_of(g, half, k)
+                if stage == 1:
+                    direct(g, half, k, True).wait_recv()
+                if stage <= 3:
+                    keys.forward(spot, stage - 1)
+                else:
+                    keys.arrived(spot)
+                    inner(g, half, k).start()
 
     def hops(t):
         for hop in range(3):
@@ -840,17 +900,28 @@
     def save(g):
         return pltpu.make_async_copy(kv.at[g], kv_out.at[g], store_kv.at[g])
 
+    for t in range(tiles):
+        g, half = divmod(t, 2)
+        for u in range(size // tile):
+            project(g, half, u)
+        for k in chips:
+            direct(g, half, k).start()
+        inner(g, half, 0).start()
+        exchange(t)
+    at_step = tiles
     for g in range(groups):
-        for half in range(2):
-            for k in chips:
-                direct(g, half, k, True).wait_recv()
-                inner(g, half, k).start()
+        while at_step < min(2 * g + 6, tiles + 4):
+            exchange(at_step)
+            at_step += 1
         for half in range(2):
             for k in range(group.chips):
                 inner(g, half, k, True).wait_recv()
         save(g).start()
         for half in range(2):
             attend(g, half)
+            if at_step < tiles + 4:
+                exchange(at_step)
+                at_step += 1
             hops(2 * g + half)
     for t in range(tiles, tiles + 2):
         hops(t)
@@ -865,14 +936,14 @@
             for k in range(group.chips):
                 inner(g, half, k).wait_send()
     line.finish(tiles)
+    keys.finish(tiles * (group.chips - 1))
     for t in range(tiles):
         keep(t).wait()
 
 
-def attention(x, w, gains, gain_query, gain_key, cosine, sine, qseg, kseg, ident):
+def attention(x, w, gains, gain_query, gain_key, cosine, sine, qseg, ids, length, ident):
     rows, width = x.shape
     groups, _, size, _ = qseg.shape
-    length = kseg.shape[2]
     head = gain_query.shape[1]
     chips = length // (4 * size)
     tiles = 2 * groups
@@ -895,11 +966,12 @@
         out_specs=(vmem,) * 7 + (ANY, ANY),
         scratch_shapes=[
             pltpu.VMEM((groups, length, 2 * head), BF16), pltpu.VMEM((rows, 4 * head), BF16),
-            dma((groups,)), dma((tiles,))] + [dma((groups, 2, chips))] * 4 + [dma((3, tiles))] * 4,
+            dma((groups,)), dma((tiles,))] + [dma((groups, 2, chips))] * 4 + [dma((3, tiles))] * 4
+        + [dma((3, tiles * (chips - 1)))] * 4,
         compiler_params=pltpu.CompilerParams(
             collective_id=ident, has_side_effects=True, vmem_limit_bytes=60 * 2**20),
         name="attention",
-    )(x, w, gains, gain_query, gain_key, cosine, sine, qseg, kseg)
+    )(x, w, gains, gain_query, gain_key, cosine, sine, qseg, ids)
 
 
 class ResidentSum(LineSum):
@@ -934,25 +1006,17 @@
                 self.outwards(c).wait_send()
 
 
-def query_back_kernel(tiles, tile, dq_ref, hat_ref, inv_ref, cos_ref, sin_ref, x_ref, gain_ref, gq_ref, w_ref,
-                      one_ref, grad_ref, dgain_ref, acc, wq_ref, w_sem, whole, *sems):
+def query_back_kernel(tiles, tile, dq_ref, hat_ref, inv_ref, cos_ref, sin_ref, x_ref, gain_ref, gq_ref, wq_ref,
+                      one_ref, grad_ref, dgain_ref, acc, whole, *sems):
     i = pl.program_id(0)
     head = hat_ref.shape[1]
     line = LineGather(whole, tile, head, sems)
 
     @pl.when(i == 0)
     def _():
-        copies = [
-            pltpu.make_async_copy(w_ref.at[:, pl.ds(2 * j * head, head)], wq_ref.at[:, pl.ds(j * head, head)], w_sem.at[j])
-            for j in range(4)
-        ]
-        for copy in copies:
-            copy.start()
         barrier_line(line.z)
         acc[...] = jnp.zeros_like(acc)
         dgain_ref[...] = jnp.zeros_like(dgain_ref)
-        for copy in copies:
-            copy.wait()
 
     @pl.when(i < tiles)
     def _():
@@ -1005,15 +1069,14 @@
             jax.ShapeDtypeStruct((1, head), F32),
         ),
         in_specs=[early(head), early(head), early(1), early(head // 2), early(head // 2), early(width),
-                  whole_block(gains.shape), whole_block(gain_query.shape), ANY],
+                  whole_block(gains.shape), whole_block(gain_query.shape), whole_block(weights.shape)],
         out_specs=(
             pl.BlockSpec((tile, width), lambda i: (jnp.maximum(i - 3, 0), 0)),
             pl.BlockSpec((width, head), lambda i: (0, 0)),
             pl.BlockSpec((1, head), lambda i: (0, 0)),
         ),
         scratch_shapes=[
-            pltpu.VMEM((width, head), F32), pltpu.VMEM((width, 4 * head), BF16), pltpu.SemaphoreType.DMA((4,)),
-            pltpu.VMEM((rows, 4 * head), BF16)] + [dma] * 4,
+            pltpu.VMEM((width, head), F32), pltpu.VMEM((rows, 4 * head), BF16)] + [dma] * 4,
         compiler_params=pltpu.CompilerParams(
             collective_id=ident, has_side_effects=True, vmem_limit_bytes=48 * 2**20),
         name="query_back",
@@ -1224,20 +1287,20 @@
         return jnp.pad(gain, (0, own_rows - gain.shape[0]))[:, None]
 
     own_ids = segments.reshape(groups, 2, size)
-    id_cols = -(-own_ids.size // own_rows)
-    ids = jnp.pad(own_ids.reshape(-1), (0, own_rows * id_cols - own_ids.size)).reshape(own_rows, id_cols)
+    id_rows = own_ids.size // 128
+    ids = jnp.pad(own_ids.reshape(id_rows, 128), ((0, -id_rows % 16), (0, 0)))
     extra = jnp.concatenate(
-        [column(g) for g in (g_input, g_post_attn, g_pre_ffn, g_post_ffn, g_query, g_key)] + [ids.astype(BF16)], axis=1)
+        [column(g) for g in (g_input, g_post_attn, g_pre_ffn, g_post_ffn, g_query, g_key)], axis=1)
     extra = jnp.pad(extra, ((0, 0), (0, 128 - extra.shape[1])))
 
     def rows_of_16(w):
         return jnp.pad(w, ((0, -own_rows % 16), (0, 0)))
 
-    first, line = first_gather(
+    first, line, ids = first_gather(
         rows_of_16(jnp.concatenate([w_query, w_key, w_value, extra], axis=1)),
-        rows_of_16(jnp.concatenate([w_query, w_out.T], axis=1)), width // own_rows, 5)
+        rows_of_16(jnp.concatenate([w_query, w_out.T], axis=1)), ids, width // own_rows, 5)
     first = first[:, :own_rows].reshape(width, -1)
-    line = line[:own_rows]
+    line = line[:own_rows].reshape(own_rows, 4, 2, head).transpose(2, 0, 1, 3).reshape(2, own_rows, 4 * head)
     mat_qkv = first[:, : 3 * head]
     side = first[:, 3 * head :]
     gain_cols = side[:, :8].astype(F32)
@@ -1246,14 +1309,13 @@
     short = g_query.shape[0]
     gain_query, gain_key = (
         gain_cols[:, i].reshape(-1, own_rows)[:, :short].reshape(-1) for i in (4, 5))
-    ids = side[:, 6 : 6 + id_cols].reshape(-1, ctx, own_rows * id_cols)[:, :, : own_ids.size]
-    ids = lax.dynamic_index_in_dim(ids, lax.axis_index("dp"), 0, keepdims=False).astype(jnp.int32)
-    key_ids = ids.reshape(ctx, groups, 2, size).transpose(1, 2, 0, 3).reshape(groups, length)
+    key_ids = lax.dynamic_index_in_dim(ids.reshape((-1, ctx) + ids.shape[1:]), lax.axis_index("dp"), 0, keepdims=False)
+    key_ids = key_ids[:, :id_rows].reshape(ctx, groups, 2, size).transpose(1, 2, 0, 3).reshape(groups, length)
     key_ids = jnp.where(key_ids == 0, -1, key_ids)
 
     wide = wide_of(hidden)
     second = jnp.concatenate(
-        [line] + [jnp.pad(w, ((0, 0), (0, wide - hidden))) for w in (w_gate, w_up, w_down.T)], axis=1)
+        [line[1]] + [jnp.pad(w, ((0, 0), (0, wide - hidden))) for w in (w_gate, w_up, w_down.T)], axis=1)
     weights = lax.all_gather(second, shared, axis=0, tiled=True)
 
     offsets = rank * size + jnp.arange(size, dtype=jnp.int32)
@@ -1266,8 +1328,10 @@
     x_rows = tokens.reshape(rows, width)
     dy_rows = cotangent.reshape(rows, width)
     queries, q_hat, q_scale, k_hat, k_scale, heads_own, log_mass, kv, heads_all = attention(
-        x_rows, mat_qkv, gain_rows, gain_query[None], gain_key[None], *turn, own_ids[..., None], key_ids[:, None, :], 0)
-
+        x_rows, mat_qkv, gain_rows, gain_query[None], gain_key[None], *turn, own_ids[..., None], ids, length, 0)
+
+    line, heads_all = lax.optimization_barrier((line[0], heads_all))
+    query_full = lax.all_gather(line, shared, axis=0, tiled=True)
     attn, hidden_two, gate, up, ffn_out = ffn_forward(x_rows, heads_all, gain_rows, weights, hidden, 1)
     output, d_gain_post_ffn, grad_ffn, d_two = ffn_backward(
         x_rows, attn, dy_rows, ffn_out, hidden_two, gate, up, gain_rows, weights, 2)
@@ -1278,11 +1342,11 @@
     d_query, d_kv = attend_back(
         queries.reshape(groups, 2, size, head), kv, d_heads.reshape(groups, 2, size, head),
         log_mass.reshape(groups, 2, 1, size), delta.reshape(groups, 2, 1, size),
-        own_ids[:, :, None, :], key_ids[:, :, None])
+        own_ids[:, :, None, :], key_ids[:, None, :])
     d_kv = lax.psum_scatter(
         d_kv.reshape(groups, 2, length // 2, 2 * head), "ctx", scatter_dimension=2, tiled=True)
     d_one, grad_q, d_gain_query = query_back(
-        d_query.reshape(rows, head), q_hat, q_scale, cosine, sine, x_rows, gain_rows, gain_query[None], weights, 4)
+        d_query.reshape(rows, head), q_hat, q_scale, cosine, sine, x_rows, gain_rows, gain_query[None], query_full, 4)
     d_kv, d_one = lax.optimization_barrier((d_kv, d_one))
     d_tokens, last = key_back(
         d_kv.reshape(rows, 2 * head), k_hat, k_scale, cosine, sine, x_rows, d_middle, d_one, gain_rows, gain_key[None],

time: 773 us -> 734 us (0.950)
  Pallas kernels: 689 us -> 655 us
    pallas_call x1, Pallas kernels: 145 us -> 123 us  [attention(): pl.pallas_call(functools.partial(attention_kernel, groups, size), out_sha...]
    unnamed x43 -> x48, local copies, waits for them, and re-layouts: 17.6 us -> 20.9 us
  transfers between devices with their start and end apart: 3 -> 4, of which waited for: 0 -> 0; matrix products, arithmetic and copies ran while one was open for 3% -> 2% of each run, Pallas kernels for 42% -> 87%
where the time goes in v6:
time: 734 us; the launch traced here: 724 us
  Pallas kernels  655 us (89%)
  local copies, waits for them, and re-layouts  40.2 us (5%)
  between operations  14.6 us (2%)
  other arithmetic  13.9 us (2%)
    pallas_call x1, Pallas kernels, ffn_backward(): pl.pallas_call(functools.partial(ffn_backward_kernel, tiles, tile, chunk,...  153 us
    pallas_call x1, Pallas kernels, ffn_forward(): pl.pallas_call(functools.partial(ffn_forward_kernel, tiles, tile, chunk,...  142 us
    pallas_call x1, Pallas kernels, attention(): pl.pallas_call(functools.partial(attention_kernel, groups, size), out_sha...  123 us
    pallas_call x1, Pallas kernels, query_back(): pl.pallas_call(functools.partial(query_back_kernel, tiles, tile), grid=(t...  72.3 us
    pallas_call x1, Pallas kernels, key_back(): pl.pallas_call(functools.partial(key_back_kernel, tiles, tile, chunk, own...  68.9 us
    pallas_call x1, Pallas kernels, scatter(): pl.pallas_call(functools.partial(scatter_kernel, chips, own_rows), out_sh...  28.7 us
    pallas_call x1, Pallas kernels, attend_back(): pl.pallas_call(functools.partial(attend_back_kernel, blocks), grid=(group...  25.6 us
    pallas_call x1, Pallas kernels, first_gather(): pl.pallas_call(first_gather_kernel, out_shape=(jax.ShapeDtypeStruct((devi...  23.4 us
  transfers between devices with their start and end apart: 4, of which 0 were waited for; matrix products, arithmetic and copies ran while one was open for 2% of the time, Pallas kernels for 87%

profile of v6, /device:TPU:0, one launch (start us, length us, event | category | flops | bytes accessed | tf_op | source)
XLA Modules:
  0.0 724.4 jit_solution(2045363286173249063)
XLA Ops:
  12.7 1.6 pad_maximum_fusion.b_ref
  14.3 1.7 fusion.9.a_ref
  16.0 23.4 %first_gather.1 = (bf16[8,144,896]{2,1,0:T(8,128)(2,1)}, bf16[144,2048]{1,0:T(8,128)(2,1)}, s32[8,16,128]{2,1,0:T(8,128)}) custom-call(bf16[144,896]{1,0:T(8,128)(2,1)} %fusion.9.a_ref, bf16[144,512]{1,0:T(8,128)(2,1)} %pad_maximum_fusion.b_ref, s32[16,128]{1,0:T(8,128)} %reshape_reshape.3.i_ref), custom_call_target="tpu_custom_call" | custom-call | tf_op jit(solution)/shard_map/first_gather/pallas_call | solution.py:769
  39.4 2.2 reshape.128
  42.1 2.5 fusion.6
  44.7 1.3 slice.96.w_ref
  49.1 1.3 copy.62.qs_ref
  51.3 3.1 multiply_sine_fusion
  54.3 122.8 %attention.1 = (bf16[2048,256]{1,0:T(8,128)(2,1)}, f32[2048,256]{1,0:T(8,128)}, f32[2048,1]{1,0:T(8,128)}, f32[2048,256]{1,0:T(8,128)}, f32[2048,1]{1,0:T(8,128)...) custom-call(bf16[2048,1152]{1,0:T(8,128)(2,1)} %bitcast.51, ...), custom_call_target="tpu_custom_call" | custom-call | tf_op jit(solution)/shard_map/attention/pallas_call | solution.py:952
  177.8 1.6 reduce.2
  180.7 141.6 %ffn_forward.1 = (bf16[2048,1152]{1,0:T(8,128)(2,1)}, bf16[2048,1152]{1,0:T(8,128)(2,1)}, bf16[2048,1728]{1,0:T(8,128)(2,1)}, bf16[2048,1728]{1,0:T(8,128)(2,1)}, bf16[2048,1152]{1,0:T(8,128)(2,1)}) custom-call(bf16[2048,1152]{1,0:T(8,128)(2,1)} %bitcast.52, bf16[2048,1024]{1,0:T(8,128)(2,1)} %get-tuple-element.56.h_ref, f32[8,1152]{1,0:T(8,128)} %copy.61.gain_ref, ...), custom_call_target="tpu_custom_call" | custom-call | tf_op jit(solution)/shard_map/ffn_forward/pallas_call | solution.py:365
  322.3 152.6 %ffn_backward.1 = (bf16[2048,1152]{1,0:T(8,128)(2,1)}, f32[1,1152]{1,0:T(1,128)}, bf16[3,1152,1728]{2,1,0:T(8,128)(2,1)}, bf16[2048,1152]{1,0:T(8,128)(2,1)}) custom-call(bf16[2048,1152]{1,0:T(8,128)(2,1)} %bitcast.53, bf16[2048,1152]{1,0:T(8,128)(2,1)} %get-tuple-element.57.attn_ref, bf16[2048,1152]{1,0:T(8,128)(2,1)} %bitcast.57, ...), custom_call_target="tpu_custom_call" | custom-call | tf_op jit(solution)/shard_map/ffn_backward/pallas_call | solution.py:497
  476.2 19.2 %middle_back.1 = (f32[2048,1152]{1,0:T(8,128)}, bf16[2048,256]{1,0:T(8,128)(2,1)S(1)}, f32[2048,1]{1,0:T(8,128)S(1)}, f32[2,1152]{1,0:T(2,128)S(1)}, bf16[1152,256]{1,0:T(8,128)(2,1)S(1)}) custom-call(bf16[2048,1152]{1,0:T(8,128)(2,1)} %bitcast.54, bf16[2048,1152]{1,0:T(8,128)(2,1)} %get-tuple-element.57.attn_ref, bf16[2048,1152]{1,0:T(8,128)(2,1)} %bitcast.58, ...), custom_call_target="tpu_custom_call" | custom-call | tf_op jit(solution)/shard_map/middle_back/pallas_call | solution.py:556
  498.7 25.6 %attend_back.1 = (f32[2,2,512,256]{3,2,1,0:T(8,128)}, bf16[2,4096,512]{2,1,0:T(8,128)(2,1)}) custom-call(bf16[2,2,512,256]{3,2,1,0:T(8,128)(2,1)} %bitcast.73, bf16[2,4096,512]{2,1,0:T(8,128)(2,1)} %get-tuple-element.64.kv_ref, bf16[2,2,512,256]{3,2,1,0:T(8,128)(2,1)} %bitcast.50, f32[2,2,1,512]{3,2,1,0:T(1,128)} %reshape.145.l_ref, ...), custom_call_target="tpu_custom_call" | custom-call | tf_op jit(solution)/shard_map/attend_back/pallas_call | solution.py:95
  525.7 2.2 copy-done.3
  527.8 1.4 copy-done.6
  529.2 72.3 %query_back.1 = (f32[2048,1152]{1,0:T(8,128)}, bf16[1152,256]{1,0:T(8,128)(2,1)S(1)}, f32[1,256]{1,0:T(1,128)S(1)}) custom-call(f32[2048,256]{1,0:T(8,128)S(1)} %bitcast.49, f32[2048,256]{1,0:T(8,128)} %get-tuple-element.72.hat_ref, f32[2048,1]{1,0:T(8,128)S(1)} %copy-done.6, f32[2048,128]{1,0:T(8,128)S(1)} %bitcast.45, f32[2048,128]{1,0:T(8,128)S(1)} %bitcast.47, ...), custom_call_target="tpu_custom_call" | custom-call | tf_op jit(solution)/shard_map/query_back/pallas_call | solution.py:1063
  602.9 68.9 %key_back.1 = (f32[2048,1152]{1,0:T(8,128)}, bf16[1152,1152]{1,0:T(8,128)(2,1)}) custom-call(bf16[2048,512]{1,0:T(8,128)(2,1)} %bitcast.68, f32[2048,256]{1,0:T(8,128)} %get-tuple-element.77.hat_ref, f32[2048,1]{1,0:T(8,128)} %get-tuple-element.78.inv_ref, f32[2048,128]{1,0:T(8,128)} %bitcast.46, f32[2048,128]{1,0:T(8,128)} %bitcast.48, ...), custom_call_target="tpu_custom_call" | custom-call | tf_op jit(solution)/shard_map/key_back/pallas_call | solution.py:1180
  671.8 1.7 copy-done.2
  673.5 28.7 %scatter.1 = f32[144,1152]{1,0:T(8,128)S(1)} custom-call(bf16[1152,1152]{1,0:T(8,128)(2,1)S(1)} %copy-done.2), custom_call_target="tpu_custom_call" | custom-call | tf_op jit(solution)/shard_map/scatter/pallas_call | solution.py:1260
  704.6 1.8 convert_element_type.24
  706.4 1.7 slice_bitcast_fusion
  708.1 5.5 copy.79
  713.6 3.7 copy.80
  (94 shorter events, 21.6 us)
Async XLA Ops:
  7.2 34.9 %copy-start.16 = (bf16[1728,144]{0,1:T(8,128)(2,1)S(1)}, bf16[1728,144]{0,1:T(8,128)(2,1)}, u32[]{:S(2)}) copy-start(bf16[1728,144]{0,1:T(8,128)(2,1)} %param.25) | copy-start | bytes 1492996
  7.2 173.5 %all-gather.3.cloned.1.call-start = ((), (), s32[]{:S(2)}) async-start(), calls=%async_computation.2 | async-start | bytes 16588800 | tf_op jit(solution)/shard_map/all_gather | solution.py:1319
  41.8 2.9 copy-start.13
  44.7 4.5 copy-start.18
  44.7 480.2 %all-gather.5.cloned.1.call-start = ((), (), s32[]{:S(2)}) async-start(), calls=%async_computation.4 | async-start | bytes 2654208 | tf_op jit(solution)/shard_map/all_gather | solution.py:1334
  54.3 125.6 %copy-start.17 = (s32[8,16,128]{2,1,0:T(8,128)S(1)}, s32[8,16,128]{2,1,0:T(8,128)}, u32[]{:S(2)}) copy-start(s32[8,16,128]{2,1,0:T(8,128)} %get-tuple-element.54.ks_ref) | copy-start | bytes 196612
  177.1 425.8 %reduce-scatter.3.cloned.1.call-start = ((), (), s32[]{:S(2)}) async-start(), calls=%async_computation.3 | async-start | bytes 10485760 | tf_op jit(solution)/shard_map/reduce_scatter | solution.py:1346
  322.3 152.7 %copy-start.4 = (f32[8,1152]{1,0:T(8,128)S(1)}, f32[8,1152]{1,0:T(8,128)}, u32[]{:S(2)}) copy-start(f32[8,1152]{1,0:T(8,128)} %copy.61.gain_ref) | copy-start | bytes 110596
  475.0 1.2 copy-start.7
  495.4 1.0 copy-start.5
  496.3 0.8 copy-start.8
  524.3 180.3 %reduce-scatter.5.cloned.1.call-start = ((), (), s32[]{:S(2)}) async-start(), calls=%async_computation.5 | async-start | bytes 13934592 | tf_op jit(solution)/shard_map/reduce_scatter | solution.py:1338
  524.3 1.0 copy-start.15
  524.4 1.2 copy-start.14
  524.4 1.3 copy-start.11
  525.5 76.1 %copy-start = (f32[2,1024,128]{2,1,0:T(8,128)}, f32[2,1024,128]{2,1,0:T(8,128)S(1)}, u32[]{:S(2)}) copy-start(f32[2,1024,128]{2,1,0:T(8,128)S(1)} %broadcast_in_dim.38) | copy-start | bytes 3145732
  525.6 75.9 %copy-start.1 = (f32[2,1024,128]{2,1,0:T(8,128)}, f32[2,1024,128]{2,1,0:T(8,128)S(1)}, u32[]{:S(2)}) copy-start(f32[2,1024,128]{2,1,0:T(8,128)S(1)} %broadcast_in_dim.39) | copy-start | bytes 3145732
  525.6 2.2 copy-start.3
  527.8 1.4 copy-start.6
  601.5 0.8 copy-start.9
  671.8 1.8 copy-start.2
  704.6 9.0 %slice-start = ((s8[9437184]{0:T(1024)(128)(4,1)}), s8[4194304]{0:T(1024)(128)(4,1)S(1)}, s32[]{:S(2)}) async-start(s8[9437184]{0:T(1024)(128)(4,1)} %bitcast.59), calls=%async_computation.6 | async-start | bytes 8388608
  706.4 7.2 slice-start.1
  708.1 5.5 slice-start.2
  (2 other events, 1.2 us)
Sparse Core Ops, SparseCore 0:
  44.8 90.2 all-gather.2
  177.3 27.2 all-gather.4
  524.4 70.1 reduce-scatter.2
  598.6 105.4 reduce-scatter.4

commit v7 on v6

--- a/solution.py
+++ b/solution.py
@@ -41,71 +41,6 @@
     if half == 0:
         return t
     return jnp.where(t < blocks, t, t + rank + 1)
-
-
-def attend_back_kernel(blocks, q_ref, kv_ref, do_ref, l_ref, d_ref, qs_ref, ks_ref,
-                       dq_ref, dkv_ref, dk_acc, dv_acc):
-    rank = lax.axis_index("ctx")
-    size = q_ref.shape[2]
-    head = q_ref.shape[3]
-    row = lax.broadcasted_iota(jnp.int32, (size, size), 0)
-    col = lax.broadcasted_iota(jnp.int32, (size, size), 1)
-    dk_acc[...] = jnp.zeros_like(dk_acc)
-    dv_acc[...] = jnp.zeros_like(dv_acc)
-    for half in range(2):
-        q = q_ref[0, half] * jnp.asarray(SCALE, BF16)
-        do = do_ref[0, half]
-        qseg = qs_ref[0, half]
-        log_mass = l_ref[0, half]
-        delta = d_ref[0, half]
-
-        def part(block, own):
-            rows = pl.ds(pl.multiple_of(block * size, size), size)
-            k = kv_ref[0, rows, :head]
-            v = kv_ref[0, rows, head:]
-            ids = jnp.broadcast_to(ks_ref[0, :, rows], (8, size))
-            allowed = jnp.transpose(ids)[:, 0:1] == qseg
-            if own:
-                order = (row <= col) if half == 0 else (row >= col)
-                allowed = (allowed & order) | (col == row)
-            s = jnp.where(allowed, dot(k, q, NT), NEGATIVE)
-            p = jnp.exp(s - log_mass)
-            ds = (p * (dot(v, do, NT) - delta)).astype(BF16)
-            dv_acc[rows, :] += dot(p.astype(BF16), do)
-            dk_acc[rows, :] += dot(ds, q)
-            return dot(ds, k, TN)
-
-        def step(t, dq):
-            return dq + part(block_starts(half, t, blocks, rank), False)
-
-        dq = part(rank + half * blocks, True)
-        count = rank if half == 0 else 2 * blocks - 1 - rank
-        dq_ref[0, half] = SCALE * lax.fori_loop(0, count, step, dq)
-    dkv_ref[0, :, :head] = dk_acc[...].astype(BF16)
-    dkv_ref[0, :, head:] = dv_acc[...].astype(BF16)
-
-
-def attend_back(q, kv, do, log_mass, delta, qseg, kseg):
-    groups, _, size, head = q.shape
-    length = kv.shape[1]
-    blocks = length // (2 * size)
-    halves = pl.BlockSpec((1, 2, size, head), lambda g: (g, 0, 0, 0))
-    whole = pl.BlockSpec((1, length, 2 * head), lambda g: (g, 0, 0))
-    line = pl.BlockSpec((1, 2, 1, size), lambda g: (g, 0, 0, 0))
-    return pl.pallas_call(
-        functools.partial(attend_back_kernel, blocks),
-        grid=(groups,),
-        out_shape=(
-            jax.ShapeDtypeStruct(q.shape, F32),
-            jax.ShapeDtypeStruct((groups, length, 2 * head), BF16),
-        ),
-        in_specs=[halves, whole, halves, line, line, line,
-                  pl.BlockSpec((1, 1, length), lambda g: (g, 0, 0))],
-        out_specs=(halves, pl.BlockSpec((1, length, 2 * head), lambda g: (g, 0, 0))),
-        scratch_shapes=[pltpu.VMEM((length, head), F32)] * 2,
-        compiler_params=pltpu.CompilerParams(vmem_limit_bytes=56 * 2**20),
-        name="attend_back",
-    )(q, kv, do, log_mass, delta, qseg, kseg)
 
 
 def angles(position, half_size, full_size):
@@ -818,7 +753,7 @@
         spot = pl.ds(half * size + u * tile, tile)
         cosine, sine = cos_ref[spot, :], sin_ref[spot, :]
         hat, _ = norm_parts(x_ref[rows, :].astype(F32))
-        raw = dot((hat * (1.0 + gain_ref[0:1, :])).astype(BF16), w_ref[...])
+        raw = dot((hat * (1.0 + gain_ref[0:1, :])).astype(BF16), w_ref[:, : 3 * head])
         hat, inv = norm_parts(raw[:, :head])
         qhat_ref[rows, :] = hat
         qinv_ref[rows, :] = inv
@@ -1006,86 +941,198 @@
                 self.outwards(c).wait_send()
 
 
-def query_back_kernel(tiles, tile, dq_ref, hat_ref, inv_ref, cos_ref, sin_ref, x_ref, gain_ref, gq_ref, wq_ref,
-                      one_ref, grad_ref, dgain_ref, acc, whole, *sems):
-    i = pl.program_id(0)
-    head = hat_ref.shape[1]
-    line = LineGather(whole, tile, head, sems)
-
-    @pl.when(i == 0)
-    def _():
-        barrier_line(line.z)
-        acc[...] = jnp.zeros_like(acc)
-        dgain_ref[...] = jnp.zeros_like(dgain_ref)
-
-    @pl.when(i < tiles)
-    def _():
-        d_rot = rotate(dq_ref[...], cos_ref[...], -sin_ref[...])
-        d_raw, d_gain = norm_back(d_rot, hat_ref[...], inv_ref[...], gq_ref[...])
-        d_raw = d_raw.astype(BF16)
-        at = pl.ds(pl.multiple_of(line.z * head, head), head)
-        whole[pl.ds(pl.multiple_of(i * tile, tile), tile), at] = d_raw
-        line.forward(i, 0)
+def turned(column, size):
+    return jnp.transpose(jnp.broadcast_to(column, (size, 128)))[0:1, :]
+
+
+def attention_back_kernel(groups, size, q_ref, do_ref, log_ref, delta_ref, qs_ref, ids_ref, hat_ref, inv_ref, cos_ref, sin_ref,
+                          x_ref, gain_ref, gq_ref, go_ref, kv_hbm, all_out, dkv_ref, dgain_ref, grad_ref,
+                          kv, dk, dv, part, near, pair, far, whole, acc, load, store, ss1, rs1, ss2, rs2, *sems):
+    head = q_ref.shape[1]
+    length = kv.shape[1]
+    blocks = length // (2 * size)
+    id_rows = size // 128
+    tiles = 2 * groups
+    group = Shared(False)
+    rank, core = group.me, group.core
+    line = LineGather(whole, size, head, sems)
+    z = line.z
+    others = range(1, group.chips)
+    order = list(others) + [0]
+
+    def fetch(g):
+        return pltpu.make_async_copy(kv_hbm.at[g], kv.at[g], load.at[g])
+
+    for g in range(groups):
+        fetch(g).start()
+    group.greet(z)
+    acc[...] = jnp.zeros_like(acc)
+    dgain_ref[...] = jnp.zeros_like(dgain_ref)
+
+    def rows_of(half, device):
+        return pl.ds(pl.multiple_of(half * (length // 2) + device * size, size), size)
+
+    def within(g, half, k):
+        to = group.other(k) + 1 - 2 * core
+        return group.copy(
+            part.at[g, rows_of(half, to)], near.at[g, half, k], ss1.at[g, half, k], rs1.at[g, half, k], group.partner())
+
+    def between(g, half, k):
+        return group.copy(
+            pair.at[g, half, k - 1], far.at[g, half, k - 1], ss2.at[g, half, k], rs2.at[g, half, k], group.other(k))
+
+    def both_cores(g):
+        for half in range(2):
+            for k in order:
+                within(g, half, k).wait_recv()
+                total = part[g, rows_of(half, group.other(k)), :].astype(F32) + near[g, half, k].astype(F32)
+                if k > 0:
+                    pair[g, half, k - 1] = total.astype(BF16)
+                    between(g, half, k).start()
+                else:
+                    dkv_ref[pl.ds((2 * g + half) * size, size), :] = total.astype(BF16)
+
+    def all_chips(g):
+        for half in range(2):
+            at = pl.ds((2 * g + half) * size, size)
+            total = dkv_ref[at, :].astype(F32)
+            for k in others:
+                between(g, half, k).wait_recv()
+                total = total + far[g, half, k - 1].astype(F32)
+            dkv_ref[at, :] = total.astype(BF16)
+
+    def hops(t):
+        for hop in range(3):
+            if 0 <= t - hop < tiles:
+                line.forward(t - hop, hop)
+
+    def attend(g, half):
+        row = lax.broadcasted_iota(jnp.int32, (size, size), 0)
+        col = lax.broadcasted_iota(jnp.int32, (size, size), 1)
+        own = pl.ds((2 * g + half) * size, size)
+        q = q_ref[own, :] * jnp.asarray(SCALE, BF16)
+        do = do_ref[own, :]
+        qseg = qs_ref[g, half]
+        log_mass = turned(log_ref[g, half], size)
+        delta = turned(delta_ref[own, :], size)
+
+        def step_of(block, mine):
+            at = pl.ds(pl.multiple_of(block * size, size), size)
+            k = kv[g, at, :head]
+            v = kv[g, at, head:]
+            device = lax.axis_index("dp") * lax.axis_size("ctx") + lax.rem(block, blocks)
+            ids = ids_ref[device, pl.ds((2 * g + lax.div(block, blocks)) * id_rows, id_rows), :]
+            ids = jnp.concatenate([ids[j : j + 1] for j in range(id_rows)], axis=1)
+            ids = jnp.transpose(jnp.broadcast_to(jnp.where(ids == 0, -1, ids), (8, size)))[:, 0:1]
+            allowed = ids == qseg
+            if mine:
+                ahead = (row <= col) if half == 0 else (row >= col)
+                allowed = (allowed & ahead) | (col == row)
+            s = jnp.where(allowed, dot(k, q, NT), NEGATIVE)
+            p = jnp.exp(s - log_mass)
+            ds = (p * (dot(v, do, NT) - delta)).astype(BF16)
+            dv[at, :] += dot(p.astype(BF16), do)
+            dk[at, :] += dot(ds, q)
+            return dot(ds, k, TN)
+
+        def step(t, dq):
+            return dq + step_of(block_starts(half, t, blocks, rank), False)
+
+        dq = step_of(rank + half * blocks, True)
+        count = rank if half == 0 else 2 * blocks - 1 - rank
+        dq = SCALE * lax.fori_loop(0, count, step, dq)
+        spot = pl.ds(half * size, size)
+        d_rot = rotate(dq, cos_ref[spot, :], -sin_ref[spot, :])
+        d_raw, d_gain = norm_back(d_rot, hat_ref[own, :], inv_ref[own, :], gq_ref[...])
         dgain_ref[...] += d_gain[None]
-        hat, _ = norm_parts(x_ref[...].astype(F32))
+        whole[own, pl.ds(pl.multiple_of(z * head, head), head)] = d_raw.astype(BF16)
+
+    def weight_gradient(t):
+        own = pl.ds(t * size, size)
+        hat, _ = norm_parts(x_ref[own, :].astype(F32))
         one = (hat * (1.0 + gain_ref[0:1, :])).astype(BF16)
-        acc[...] += dot(one, d_raw, TN)
-
-    @pl.when((i >= 1) & (i <= tiles))
-    def _():
-        line.forward(i - 1, 1)
-
-    @pl.when((i >= 2) & (i <= tiles + 1))
-    def _():
-        line.forward(i - 2, 2)
-
-    @pl.when(i >= 3)
-    def _():
-        line.arrived(i - 3)
-        one_ref[...] = dot(whole[pl.ds(pl.multiple_of((i - 3) * tile, tile), tile), :], wq_ref[...], NT)
-
-    @pl.when(i == tiles + 2)
-    def _():
-        grad_ref[...] = acc[...].astype(BF16)
-        line.finish(tiles)
-
-
-def query_back(dq, hat, inv, cosine, sine, x, gains, gain_query, weights, ident):
-    rows, width = x.shape
-    head = hat.shape[1]
-    tile = 256
-    tiles = rows // tile
-    dma = pltpu.SemaphoreType.DMA((3, tiles))
-
-    def early(cols):
-        return pl.BlockSpec((tile, cols), lambda i: (jnp.minimum(i, tiles - 1), 0))
-
+        acc[...] += dot(one, whole[own, pl.ds(pl.multiple_of(z * head, head), head)], TN)
+
+    def keep(t):
+        at = pl.ds(t * size, size)
+        return pltpu.make_async_copy(whole.at[at], all_out.at[at], store.at[t])
+
+    for g in range(groups):
+        fetch(g).wait()
+        dk[...] = jnp.zeros_like(dk)
+        dv[...] = jnp.zeros_like(dv)
+        for half in range(2):
+            attend(g, half)
+            hops(2 * g + half)
+            if half == 0 and g > 0:
+                both_cores(g - 1)
+        part[g, :, :head] = dk[...].astype(BF16)
+        part[g, :, head:] = dv[...].astype(BF16)
+        for half in range(2):
+            for k in order:
+                within(g, half, k).start()
+        for half in range(2):
+            weight_gradient(2 * g + half)
+        if g > 0:
+            all_chips(g - 1)
+    hops(tiles)
+    both_cores(groups - 1)
+    hops(tiles + 1)
+    grad_ref[:, :head] = acc[...].astype(BF16)
+    grad_ref[:, head:] = go_ref[...]
+    for t in range(tiles):
+        line.arrived(t)
+        keep(t).start()
+    all_chips(groups - 1)
+    for g in range(groups):
+        for half in range(2):
+            for k in others:
+                between(g, half, k).wait_send()
+            for k in order:
+                within(g, half, k).wait_send()
+    line.finish(tiles)
+    for t in range(tiles):
+        keep(t).wait()
+
+
+def attention_back(q, d_heads, log_mass, delta, qseg, ids, hat, inv, cosine, sine, x, gains, gain_query, grad_o, kv, ident):
+    rows, head = q.shape
+    width = x.shape[1]
+    groups, length, _ = kv.shape
+    size = rows // (2 * groups)
+    chips = length // (4 * size)
+    tiles = 2 * groups
+    vmem = pl.BlockSpec(memory_space=pltpu.VMEM)
+    dma = pltpu.SemaphoreType.DMA
     return pl.pallas_call(
-        functools.partial(query_back_kernel, tiles, tile),
-        grid=(tiles + 3,),
+        functools.partial(attention_back_kernel, groups, size),
         out_shape=(
-            jax.ShapeDtypeStruct((rows, width), F32),
-            jax.ShapeDtypeStruct((width, head), BF16),
+            jax.ShapeDtypeStruct((rows, 4 * head), BF16),
+            jax.ShapeDtypeStruct((rows, 2 * head), BF16),
             jax.ShapeDtypeStruct((1, head), F32),
+            jax.ShapeDtypeStruct((width, 2 * head), BF16),
         ),
-        in_specs=[early(head), early(head), early(1), early(head // 2), early(head // 2), early(width),
-                  whole_block(gains.shape), whole_block(gain_query.shape), whole_block(weights.shape)],
-        out_specs=(
-            pl.BlockSpec((tile, width), lambda i: (jnp.maximum(i - 3, 0), 0)),
-            pl.BlockSpec((width, head), lambda i: (0, 0)),
-            pl.BlockSpec((1, head), lambda i: (0, 0)),
-        ),
+        in_specs=[vmem] * 14 + [ANY],
+        out_specs=(ANY, vmem, vmem, vmem),
         scratch_shapes=[
-            pltpu.VMEM((width, head), F32), pltpu.VMEM((rows, 4 * head), BF16)] + [dma] * 4,
+            pltpu.VMEM((groups, length, 2 * head), BF16),
+            pltpu.VMEM((length, head), F32), pltpu.VMEM((length, head), F32),
+            pltpu.VMEM((groups, length, 2 * head), BF16),
+            pltpu.VMEM((groups, 2, chips, size, 2 * head), BF16),
+            pltpu.VMEM((groups, 2, chips - 1, size, 2 * head), BF16),
+            pltpu.VMEM((groups, 2, chips - 1, size, 2 * head), BF16),
+            pltpu.VMEM((rows, 4 * head), BF16),
+            pltpu.VMEM((width, head), F32),
+            dma((groups,)), dma((tiles,))] + [dma((groups, 2, chips))] * 4 + [dma((3, tiles))] * 4,
         compiler_params=pltpu.CompilerParams(
-            collective_id=ident, has_side_effects=True, vmem_limit_bytes=48 * 2**20),
-        name="query_back",
-    )(dq, hat, inv, cosine, sine, x, gains, gain_query, weights)
-
-
-def key_back_kernel(tiles, tile, chunk, own_rows, dkv_ref, hat_ref, inv_ref, cos_ref, sin_ref, x_ref, dm_ref, part_ref,
-                    gain_ref, gk_ref, w_ref, dgq_ref, dg_mid_ref, dg_post_ref, grad_q_ref, grad_o_ref,
-                    dx_ref, last_ref, acc, acc_in, acc_key, w_kv, w_sem, out, own, near, far, *sems):
+            collective_id=ident, has_side_effects=True, vmem_limit_bytes=63 * 2**20),
+        name="attention_back",
+    )(q, d_heads, log_mass, delta, qseg, ids, hat, inv, cosine, sine, x, gains, gain_query, grad_o, kv)
+
+
+def key_back_kernel(tiles, tile, chunk, own_rows, dkv_ref, hat_ref, inv_ref, cos_ref, sin_ref, x_ref, dm_ref, dq_ref,
+                    gain_ref, gk_ref, w_ref, wq_ref, dgq_ref, dg_mid_ref, dg_post_ref, rs_ref,
+                    dx_ref, last_ref, gate_ref, up_ref, down_ref, acc, acc_in, acc_key, w_kv, w_sem, out, own, near, far, *sems):
     i = pl.program_id(0)
     head = hat_ref.shape[1]
     per = tile // chunk
@@ -1118,6 +1165,14 @@
         for j in range(per):
             line.total((i - 2) * per + j)
 
+    @pl.when(i == 0)
+    def _():
+        gate_ref[...] = rs_ref[0].astype(F32)
+        up_ref[...] = rs_ref[1].astype(F32)
+        row = lax.broadcasted_iota(jnp.int32, (own_rows, own_rows), 0)
+        col = lax.broadcasted_iota(jnp.int32, (own_rows, own_rows), 1)
+        down_ref[...] = dot(rs_ref[2], jnp.where(row == col, 1.0, 0.0).astype(BF16), TN)
+
     @pl.when(i == 1)
     def _():
         line.pair(count - 1)
@@ -1135,7 +1190,7 @@
         d_raw, d_gain = norm_back(d_rot, hat_ref[...], inv_ref[...], gk_ref[...])
         acc_key[...] += d_gain[None]
         d_raw = jnp.concatenate([d_raw.astype(BF16), d_kv[:, head:]], axis=1)
-        d_one = part_ref[...] + dot(d_raw, w_kv[...], NT)
+        d_one = dot(dq_ref[...], wq_ref[...], NT) + dot(d_raw, w_kv[...], NT)
         hat, inv = norm_parts(x_ref[...].astype(F32))
         gain = gain_ref[0:1, :]
         d_part, d_gain = norm_back(d_one, hat, inv, gain)
@@ -1148,9 +1203,7 @@
         line.arrived(count - 1)
         width = x_ref.shape[1]
         short = head * own_rows // width
-        last_ref[:, :head] = grad_q_ref[...]
-        last_ref[:, head : 3 * head] = acc[...].astype(BF16)
-        last_ref[:, 3 * head : 4 * head] = grad_o_ref[...]
+        last_ref[:, : 2 * head] = acc[...].astype(BF16)
         d_query = out[pl.ds((count - 1) * chunk, 16), :head][0:1].astype(F32)
         pair = jnp.concatenate([d_query, acc_key[...], jnp.zeros((14, head), F32)], axis=0).astype(BF16)
         col = lax.broadcasted_iota(jnp.int32, (head, width), 1)
@@ -1160,12 +1213,12 @@
         spread = dot(pair, jnp.where(col == spot, 1.0, 0.0).astype(BF16))
         gains = jnp.concatenate(
             [acc_in[...], dg_mid_ref[...], dg_post_ref[...], spread[0:2], jnp.zeros((122, width), F32)], axis=0)
-        last_ref[:, 4 * head :] = jnp.transpose(gains).astype(BF16)
+        last_ref[:, 2 * head :] = jnp.transpose(gains).astype(BF16)
         line.finish()
 
 
-def key_back(d_kv, hat, inv, cosine, sine, x, d_middle, part, gains, gain_key, first, dg_query, dg_mid, dg_post,
-             grad_q, grad_o, own_rows, ident):
+def key_back(d_kv, hat, inv, cosine, sine, x, d_middle, d_query, gains, gain_key, first, w_query, dg_query, dg_mid, dg_post,
+             ffn_grads, own_rows, ident):
     rows, width = x.shape
     head = hat.shape[1]
     tile, chunk = 256, 128
@@ -1176,19 +1229,28 @@
     def late(cols):
         return pl.BlockSpec((tile, cols), lambda i: (jnp.maximum(i - 3, 0), 0))
 
+    def fixed(shape):
+        return pl.BlockSpec(shape, lambda i: (0, 0))
+
+    turns = cosine.shape[0] // tile
+    turn = pl.BlockSpec((tile, head // 2), lambda i: (lax.rem(jnp.maximum(i - 3, 0), turns), 0))
     comm = pltpu.VMEM((count * chunk, 2 * head), BF16)
     return pl.pallas_call(
         functools.partial(key_back_kernel, tiles, tile, chunk, own_rows),
         grid=(tiles + 3,),
         out_shape=(
             jax.ShapeDtypeStruct((rows, width), F32),
-            jax.ShapeDtypeStruct((width, 4 * head + 128), BF16),
+            jax.ShapeDtypeStruct((width, 2 * head + 128), BF16),
+            jax.ShapeDtypeStruct(ffn_grads.shape[1:], F32),
+            jax.ShapeDtypeStruct(ffn_grads.shape[1:], F32),
+            jax.ShapeDtypeStruct(ffn_grads.shape[:0:-1], F32),
         ),
         in_specs=[pl.BlockSpec((tile, 2 * head), lambda i: (jnp.minimum(i, tiles - 1), 0)),
-                  late(head), late(1), late(head // 2), late(head // 2), late(width), late(width), late(width),
+                  late(head), late(1), turn, turn, late(width), late(width), late(4 * head),
                   whole_block(gains.shape), whole_block(gain_key.shape), ANY]
-        + [whole_block(a.shape) for a in (dg_query, dg_mid, dg_post, grad_q, grad_o)],
-        out_specs=(late(width), pl.BlockSpec((width, 4 * head + 128), lambda i: (0, 0))),
+        + [whole_block(a.shape) for a in (w_query, dg_query, dg_mid, dg_post, ffn_grads)],
+        out_specs=(late(width), fixed((width, 2 * head + 128)), fixed(ffn_grads.shape[1:]), fixed(ffn_grads.shape[1:]),
+                   fixed(ffn_grads.shape[:0:-1])),
         scratch_shapes=[
             pltpu.VMEM((width, 2 * head), F32), pltpu.VMEM((1, width), F32), pltpu.VMEM((1, head), F32),
             pltpu.VMEM((width, 2 * head), BF16), pltpu.SemaphoreType.DMA] + [comm] * 4 + [dma] * 7
@@ -1196,7 +1258,7 @@
         compiler_params=pltpu.CompilerParams(
             collective_id=ident, has_side_effects=True, vmem_limit_bytes=56 * 2**20),
         name="key_back",
-    )(d_kv, hat, inv, cosine, sine, x, d_middle, part, gains, gain_key, first, dg_query, dg_mid, dg_post, grad_q, grad_o)
+    )(d_kv, hat, inv, cosine, sine, x, d_middle, d_query, gains, gain_key, first, w_query, dg_query, dg_mid, dg_post, ffn_grads)
 
 
 def scatter_kernel(chips, own_rows, x_ref, o_ref, near, pair, far, *sems):
@@ -1301,7 +1363,6 @@
         rows_of_16(jnp.concatenate([w_query, w_out.T], axis=1)), ids, width // own_rows, 5)
     first = first[:, :own_rows].reshape(width, -1)
     line = line[:own_rows].reshape(own_rows, 4, 2, head).transpose(2, 0, 1, 3).reshape(2, own_rows, 4 * head)
-    mat_qkv = first[:, : 3 * head]
     side = first[:, 3 * head :]
     gain_cols = side[:, :8].astype(F32)
     gain_rows = gain_cols.T
@@ -1309,9 +1370,6 @@
     short = g_query.shape[0]
     gain_query, gain_key = (
         gain_cols[:, i].reshape(-1, own_rows)[:, :short].reshape(-1) for i in (4, 5))
-    key_ids = lax.dynamic_index_in_dim(ids.reshape((-1, ctx) + ids.shape[1:]), lax.axis_index("dp"), 0, keepdims=False)
-    key_ids = key_ids[:, :id_rows].reshape(ctx, groups, 2, size).transpose(1, 2, 0, 3).reshape(groups, length)
-    key_ids = jnp.where(key_ids == 0, -1, key_ids)
 
     wide = wide_of(hidden)
     second = jnp.concatenate(
@@ -1321,51 +1379,43 @@
     offsets = rank * size + jnp.arange(size, dtype=jnp.int32)
     position = jnp.concatenate([offsets, length - 1 - offsets]).astype(F32)
     cosine, sine = angles(position, head // 2, head)
-    turn = (cosine, sine)
-    cosine = jnp.broadcast_to(cosine, (groups, per_group, head // 2)).reshape(rows, head // 2)
-    sine = jnp.broadcast_to(sine, (groups, per_group, head // 2)).reshape(rows, head // 2)
 
     x_rows = tokens.reshape(rows, width)
     dy_rows = cotangent.reshape(rows, width)
     queries, q_hat, q_scale, k_hat, k_scale, heads_own, log_mass, kv, heads_all = attention(
-        x_rows, mat_qkv, gain_rows, gain_query[None], gain_key[None], *turn, own_ids[..., None], ids, length, 0)
+        x_rows, first, gain_rows, gain_query[None], gain_key[None], cosine, sine, own_ids[..., None], ids, length, 0)
 
     line, heads_all = lax.optimization_barrier((line[0], heads_all))
     query_full = lax.all_gather(line, shared, axis=0, tiled=True)
     attn, hidden_two, gate, up, ffn_out = ffn_forward(x_rows, heads_all, gain_rows, weights, hidden, 1)
     output, d_gain_post_ffn, grad_ffn, d_two = ffn_backward(
         x_rows, attn, dy_rows, ffn_out, hidden_two, gate, up, gain_rows, weights, 2)
-    grad_ffn = lax.psum_scatter(grad_ffn, shared, scatter_dimension=1, tiled=True).astype(F32)
+    grad_ffn = lax.psum_scatter(grad_ffn, shared, scatter_dimension=1, tiled=True)
     d_middle, d_heads, delta, d_gain_mid, grad_out_t = middle_back(
         x_rows, attn, dy_rows, d_two, heads_own, gain_rows, weights)
 
-    d_query, d_kv = attend_back(
-        queries.reshape(groups, 2, size, head), kv, d_heads.reshape(groups, 2, size, head),
-        log_mass.reshape(groups, 2, 1, size), delta.reshape(groups, 2, 1, size),
-        own_ids[:, :, None, :], key_ids[:, None, :])
-    d_kv = lax.psum_scatter(
-        d_kv.reshape(groups, 2, length // 2, 2 * head), "ctx", scatter_dimension=2, tiled=True)
-    d_one, grad_q, d_gain_query = query_back(
-        d_query.reshape(rows, head), q_hat, q_scale, cosine, sine, x_rows, gain_rows, gain_query[None], query_full, 4)
-    d_kv, d_one = lax.optimization_barrier((d_kv, d_one))
-    d_tokens, last = key_back(
-        d_kv.reshape(rows, 2 * head), k_hat, k_scale, cosine, sine, x_rows, d_middle, d_one, gain_rows, gain_key[None],
-        first, d_gain_query, d_gain_mid, d_gain_post_ffn, grad_q, grad_out_t, own_rows, 3)
+    d_q_all, d_kv, d_gain_query, grad_qo = attention_back(
+        queries, d_heads, log_mass, delta, own_ids[:, :, None, :], ids, q_hat, q_scale, cosine, sine, x_rows, gain_rows,
+        gain_query[None], grad_out_t, kv, 4)
+    grad_qo = lax.psum_scatter(grad_qo, shared, scatter_dimension=0, tiled=True).astype(F32)
+    d_tokens, last, grad_gate, grad_up, grad_down = key_back(
+        d_kv, k_hat, k_scale, cosine, sine, x_rows, d_middle, d_q_all, gain_rows, gain_key[None],
+        first, query_full, d_gain_query, d_gain_mid, d_gain_post_ffn, grad_ffn, own_rows, 3)
     if own_rows % 16 == 0:
         last = scatter(last, own_rows, 7)
     else:
         last = lax.psum_scatter(last, shared, scatter_dimension=0, tiled=True).astype(F32)
-    g = last[:, 4 * head :]
+    g = last[:, 2 * head :]
     return (
         output.reshape(tokens.shape),
         d_tokens.reshape(tokens.shape),
+        grad_qo[:, :head],
         last[:, :head],
         last[:, head : 2 * head],
-        last[:, 2 * head : 3 * head],
-        last[:, 3 * head : 4 * head].T,
-        grad_ffn[0],
-        grad_ffn[1],
-        grad_ffn[2].T,
+        grad_qo[:, head:].T,
+        grad_gate,
+        grad_up,
+        grad_down,
         g[:, 0],
         g[:, 1],
         g[:, 2],

time: 734 us -> 853 us (1.16)
  waiting for transfers between devices: 0.56 us -> 159 us
  Pallas kernels: 655 us -> 622 us
    reduce_scatter x1, waiting for transfers between devices: 0.01 us -> 95.3 us  [shards(): lax.psum_scatter(grad_ffn, shared, scatter_dimension=1, tiled=True)]
    reduce_scatter x1, waiting for transfers between devices: 0.01 us -> 34.6 us  [shards(): lax.psum_scatter(grad_qo, shared, scatter_dimension=0, tiled=True)]
    all_gather x1, waiting for transfers between devices: 0.02 us -> 27.9 us  [shards(): query_full = lax.all_gather(line, shared, axis=0, tiled=True)]
    pallas_call x1, Pallas kernels: 28.7 us -> 12.6 us  [scatter(): pl.pallas_call(functools.partial(scatter_kernel, chips, own_rows), out_sh...]
    pallas_call x2 -> x1, Pallas kernels: 97.9 us -> 82.3 us  [attention_back(): pl.pallas_call(functools.partial(attention_back_kernel, groups, size), ou...]
    unnamed x48 -> x37, local copies, waits for them, and re-layouts: 20.9 us -> 20.8 us
  transfers between devices with their start and end apart: 4 -> 4, of which waited for: 0 -> 3; matrix products, arithmetic and copies ran while one was open for 2% -> 2% of each run, Pallas kernels for 87% -> 15%
where the time goes in v7:
time: 853 us; the launch traced here: 844 us
  Pallas kernels  622 us (73%)
  waiting for transfers between devices  159 us (19%)
  local copies, waits for them, and re-layouts  38.5 us (5%)
  between operations  14.5 us (2%)
  other arithmetic  9.63 us (1%)
    pallas_call x1, Pallas kernels, ffn_backward(): pl.pallas_call(functools.partial(ffn_backward_kernel, tiles, tile, chunk,...  145 us
    pallas_call x1, Pallas kernels, ffn_forward(): pl.pallas_call(functools.partial(ffn_forward_kernel, tiles, tile, chunk,...  141 us
    pallas_call x1, Pallas kernels, attention(): pl.pallas_call(functools.partial(attention_kernel, groups, size), out_sha...  123 us
    reduce_scatter x1, waiting for transfers between devices, shards(): lax.psum_scatter(grad_ffn, shared, scatter_dimension=1, tiled=True)  95.3 us
    pallas_call x1, Pallas kernels, attention_back(): pl.pallas_call(functools.partial(attention_back_kernel, groups, size), ou...  82.3 us
    pallas_call x1, Pallas kernels, key_back(): pl.pallas_call(functools.partial(key_back_kernel, tiles, tile, chunk, own...  75.8 us
    reduce_scatter x1, waiting for transfers between devices, shards(): lax.psum_scatter(grad_qo, shared, scatter_dimension=0, tiled=True)  34.6 us
    all_gather x1, waiting for transfers between devices, shards(): query_full = lax.all_gather(line, shared, axis=0, tiled=True)  27.9 us
  transfers between devices with their start and end apart: 4, of which 3 were waited for; matrix products, arithmetic and copies ran while one was open for 2% of the time, Pallas kernels for 15%

profile of v7, /device:TPU:0, one launch (start us, length us, event | category | flops | bytes accessed | tf_op | source)
XLA Modules:
  0.0 843.7 jit_solution(8080826367600921682)
XLA Ops:
  11.5 1.3 reshape_reshape.3.i_ref
  12.8 1.6 pad_maximum_fusion.b_ref
  14.4 1.7 fusion.9.a_ref
  16.1 23.4 %first_gather.1 = (bf16[8,144,896]{2,1,0:T(8,128)(2,1)}, bf16[144,2048]{1,0:T(8,128)(2,1)}, s32[8,16,128]{2,1,0:T(8,128)}) custom-call(bf16[144,896]{1,0:T(8,128)(2,1)} %fusion.9.a_ref, bf16[144,512]{1,0:T(8,128)(2,1)} %pad_maximum_fusion.b_ref, s32[16,128]{1,0:T(8,128)} %reshape_reshape.3.i_ref), custom_call_target="tpu_custom_call" | custom-call | tf_op jit(solution)/shard_map/first_gather/pallas_call | solution.py:704
  39.5 2.2 reshape.72
  42.2 1.3 fusion.6
  48.3 1.3 copy.61.qs_ref
  50.4 3.1 multiply_sine_fusion
  53.4 122.8 %attention.1 = (bf16[2048,256]{1,0:T(8,128)(2,1)}, f32[2048,256]{1,0:T(8,128)}, f32[2048,1]{1,0:T(8,128)}, f32[2048,256]{1,0:T(8,128)}, f32[2048,1]{1,0:T(8,128)...) custom-call(bf16[2048,1152]{1,0:T(8,128)(2,1)} %bitcast.25, ...), custom_call_target="tpu_custom_call" | custom-call | tf_op jit(solution)/shard_map/attention/pallas_call | solution.py:887
  176.3 141.1 %ffn_forward.1 = (bf16[2048,1152]{1,0:T(8,128)(2,1)}, bf16[2048,1152]{1,0:T(8,128)(2,1)}, bf16[2048,1728]{1,0:T(8,128)(2,1)}, bf16[2048,1728]{1,0:T(8,128)(2,1)}, bf16[2048,1152]{1,0:T(8,128)(2,1)}) custom-call(bf16[2048,1152]{1,0:T(8,128)(2,1)} %bitcast.26, bf16[2048,1024]{1,0:T(8,128)(2,1)} %get-tuple-element.56.h_ref, f32[8,1152]{1,0:T(8,128)} %copy.60.gain_ref, ...), custom_call_target="tpu_custom_call" | custom-call | tf_op jit(solution)/shard_map/ffn_forward/pallas_call | solution.py:300
  317.4 144.7 %ffn_backward.1 = (bf16[2048,1152]{1,0:T(8,128)(2,1)}, f32[1,1152]{1,0:T(1,128)}, bf16[3,1152,1728]{2,1,0:T(8,128)(2,1)}, bf16[2048,1152]{1,0:T(8,128)(2,1)}) custom-call(bf16[2048,1152]{1,0:T(8,128)(2,1)} %bitcast.27, bf16[2048,1152]{1,0:T(8,128)(2,1)} %get-tuple-element.57.attn_ref, bf16[2048,1152]{1,0:T(8,128)(2,1)} %bitcast.31, ...), custom_call_target="tpu_custom_call" | custom-call | tf_op jit(solution)/shard_map/ffn_backward/pallas_call | solution.py:432
  463.4 19.1 %middle_back.1 = (f32[2048,1152]{1,0:T(8,128)}, bf16[2048,256]{1,0:T(8,128)(2,1)S(1)}, f32[2048,1]{1,0:T(8,128)S(1)}, f32[2,1152]{1,0:T(2,128)S(1)}, bf16[1152,256]{1,0:T(8,128)(2,1)S(1)}) custom-call(bf16[2048,1152]{1,0:T(8,128)(2,1)} %bitcast.28, bf16[2048,1152]{1,0:T(8,128)(2,1)} %get-tuple-element.57.attn_ref, bf16[2048,1152]{1,0:T(8,128)(2,1)} %bitcast.32, ...), custom_call_target="tpu_custom_call" | custom-call | tf_op jit(solution)/shard_map/middle_back/pallas_call | solution.py:491
  485.9 82.3 %attention_back.1 = (bf16[2048,1024]{1,0:T(8,128)(2,1)}, bf16[2048,512]{1,0:T(8,128)(2,1)}, f32[1,256]{1,0:T(1,128)}, bf16[1152,512]{1,0:T(8,128)(2,1)}) custom-call(bf16[2048,256]{1,0:T(8,128)(2,1)} %get-tuple-element.63.q_ref, bf16[2048,256]{1,0:T(8,128)(2,1)} %copy-done.2, f32[2,2,512,1]{3,2,1,0:T(8,128)} %get-tuple-element.67.log_ref, ...), custom_call_target="tpu_custom_call" | custom-call | tf_op jit(solution)/shard_map/attention_back/pallas_call | solution.py:1107
  569.6 34.6 %reduce-scatter.5.cloned.1.call-done = bf16[144,512]{1,0:T(8,128)(2,1)} async-done(((bf16[1152,512]{1,0:T(8,128)(2,1)}), bf16[144,512]{1,0:T(8,128)(2,1)}) %reduce-scatter.5.cloned.1.call-update) | async-done | bytes 147472 | tf_op jit(solution)/shard_map/reduce_scatter | solution.py:1400
  605.1 1.6 slice.86
  607.4 27.9 %all-gather.5.cloned.1.call-done.wq_ref = bf16[1152,1024]{1,0:T(8,128)(2,1)} async-done(((bf16[144,1024]{1,0:T(8,128)(2,1)}), bf16[1152,1024]{1,0:T(8,128)(2,1)}) %all-gather.5.cloned.1.call-update) | async-done | bytes 2359312 | tf_op jit(solution)/shard_map/all_gather | solution.py:1389
  635.3 95.3 %reduce-scatter.3.cloned.1.call-done.rs_ref = bf16[3,144,1728]{2,1,0:T(8,128)(2,1)} async-done(((bf16[3,1152,1728]{2,1,0:T(8,128)(2,1)}), bf16[3,144,1728]{2,1,0:T(8,128)(2,1)}) %reduce-scatter.3.cloned.1.call-update) | async-done | bytes 1493008 | tf_op jit(solution)/shard_map/reduce_scatter | solution.py:1393
  730.6 75.8 %key_back.1 = (f32[2048,1152]{1,0:T(8,128)}, bf16[1152,640]{1,0:T(8,128)(2,1)}, f32[144,1728]{1,0:T(8,128)}, f32[144,1728]{1,0:T(8,128)}, f32[1728,144]{1,0:T(8,128)}) custom-call(bf16[2048,512]{1,0:T(8,128)(2,1)} %get-tuple-element.73.dkv_ref, f32[2048,256]{1,0:T(8,128)} %get-tuple-element.74.hat_ref, f32[2048,1]{1,0:T(8,128)} %get-tuple-element.75.inv_ref, ...), custom_call_target="tpu_custom_call" | custom-call | tf_op jit(solution)/shard_map/key_back/pallas_call | solution.py:1238
  806.4 1.4 copy-done.1
  807.8 12.6 %scatter.1 = f32[144,640]{1,0:T(8,128)S(1)} custom-call(bf16[1152,640]{1,0:T(8,128)(2,1)S(1)} %copy-done.1), custom_call_target="tpu_custom_call" | custom-call | tf_op jit(solution)/shard_map/scatter/pallas_call | solution.py:1322
  822.7 1.5 copy.69
  824.2 5.2 copy.78
  829.4 1.6 copy-done.7
  831.0 3.9 copy.79
  (71 shorter events, 22.0 us)
Async XLA Ops:
  7.2 35.0 %copy-start.11 = (bf16[1728,144]{0,1:T(8,128)(2,1)S(1)}, bf16[1728,144]{0,1:T(8,128)(2,1)}, u32[]{:S(2)}) copy-start(bf16[1728,144]{0,1:T(8,128)(2,1)} %param.25) | copy-start | bytes 1492996
  7.2 35.0 %copy-start.13 = (bf16[144,1728]{1,0:T(8,128)(2,1)S(1)}, bf16[144,1728]{1,0:T(8,128)(2,1)}, u32[]{:S(2)}) copy-start(bf16[144,1728]{1,0:T(8,128)(2,1)} %param.23) | copy-start | bytes 1492996
  7.2 35.0 %copy-start.12 = (bf16[144,1728]{1,0:T(8,128)(2,1)S(1)}, bf16[144,1728]{1,0:T(8,128)(2,1)}, u32[]{:S(2)}) copy-start(bf16[144,1728]{1,0:T(8,128)(2,1)} %param.24) | copy-start | bytes 1492996
  7.2 169.1 %all-gather.3.cloned.1.call-start = ((), (), s32[]{:S(2)}) async-start(), calls=%async_computation.2 | async-start | bytes 16588800 | tf_op jit(solution)/shard_map/all_gather | solution.py:1377
  41.9 1.7 copy-start.14
  43.5 560.7 %reduce-scatter.5.cloned.1.call-start = ((), (), s32[]{:S(2)}) async-start(), calls=%async_computation.5 | async-start | bytes 1327104 | tf_op jit(solution)/shard_map/reduce_scatter | solution.py:1400
  317.4 144.8 %copy-start = (f32[8,1152]{1,0:T(8,128)S(1)}, f32[8,1152]{1,0:T(8,128)}, u32[]{:S(2)}) copy-start(f32[8,1152]{1,0:T(8,128)} %copy.60.gain_ref) | copy-start | bytes 110596
  462.2 1.2 copy-start.4
  482.5 1.0 copy-start.2
  483.5 1.0 copy-start.3
  484.5 0.8 copy-start.5
  485.3 0.6 copy-start.6
  568.3 67.0 %all-gather.5.cloned.1.call-start = ((), (), s32[]{:S(2)}) async-start(), calls=%async_computation.3 | async-start | bytes 2654208 | tf_op jit(solution)/shard_map/all_gather | solution.py:1389
  569.0 161.7 %reduce-scatter.3.cloned.1.call-start = ((), (), s32[]{:S(2)}) async-start(), calls=%async_computation.4 | async-start | bytes 13934592 | tf_op jit(solution)/shard_map/reduce_scatter | solution.py:1393
  806.4 1.4 copy-start.1
  807.8 14.9 %copy-start.8 = (f32[1728,144]{1,0:T(8,128)S(1)}, f32[1728,144]{1,0:T(8,128)}, u32[]{:S(2)}) copy-start(f32[1728,144]{1,0:T(8,128)} %get-tuple-element.127) | copy-start | bytes 2985988
  824.2 6.8 copy-start.7
  831.0 3.9 copy-start.10
  831.0 4.8 copy-start.9
Sparse Core Ops, SparseCore 0:
  43.7 90.2 all-gather.2
  568.4 35.7 reduce-scatter.4
  606.3 29.0 all-gather.4
  639.3 91.3 reduce-scatter.2

commit v8 on v7

--- a/solution.py
+++ b/solution.py
@@ -21,6 +21,10 @@
 
 def dot(a, b, dims=NN):
     return lax.dot_general(a, b, dims, preferred_element_type=F32)
+
+
+def cost(us):
+    return pl.CostEstimate(flops=int(us * 1.1e9), bytes_accessed=0, transcendentals=0)
 
 
 def barrier_line(z):
@@ -319,6 +323,7 @@
         + line_sum_scratch(count, chunk, count, width),
         compiler_params=pltpu.CompilerParams(
             collective_id=ident, has_side_effects=True, vmem_limit_bytes=60 * 2**20),
+        cost_estimate=cost(140),
         name="ffn_forward",
     )(x, heads, gains, weights)
 
@@ -446,6 +451,7 @@
         + line_sum_scratch(count, chunk, slots, width),
         compiler_params=pltpu.CompilerParams(
             collective_id=ident, has_side_effects=True, vmem_limit_bytes=63 * 2**20),
+        cost_estimate=cost(145),
         name="ffn_backward",
     )(x, attn, dy, ffn, two, gate, up, gains, weights)
 
@@ -505,6 +511,7 @@
         ),
         scratch_shapes=[pltpu.VMEM((width, head), F32), pltpu.VMEM((width, head), BF16), pltpu.SemaphoreType.DMA],
         compiler_params=pltpu.CompilerParams(vmem_limit_bytes=48 * 2**20),
+        cost_estimate=cost(19),
         name="middle_back",
     )(x, attn, dy, d_two, heads, gains, weights)
 
@@ -712,6 +719,7 @@
         out_specs=(ANY,) * 3,
         scratch_shapes=[pltpu.SemaphoreType.DMA((3,))] + [dma] * 8 + [hop] * 4,
         compiler_params=pltpu.CompilerParams(collective_id=ident, has_side_effects=True),
+        cost_estimate=cost(20),
         name="first_gather",
     )(a, b, ids)
 
@@ -905,6 +913,7 @@
         + [dma((3, tiles * (chips - 1)))] * 4,
         compiler_params=pltpu.CompilerParams(
             collective_id=ident, has_side_effects=True, vmem_limit_bytes=60 * 2**20),
+        cost_estimate=cost(110),
         name="attention",
     )(x, w, gains, gain_query, gain_key, cosine, sine, qseg, ids)
 
@@ -1126,24 +1135,82 @@
             dma((groups,)), dma((tiles,))] + [dma((groups, 2, chips))] * 4 + [dma((3, tiles))] * 4,
         compiler_params=pltpu.CompilerParams(
             collective_id=ident, has_side_effects=True, vmem_limit_bytes=63 * 2**20),
+        cost_estimate=cost(80),
         name="attention_back",
     )(q, d_heads, log_mass, delta, qseg, ids, hat, inv, cosine, sine, x, gains, gain_query, grad_o, kv)
 
 
-def key_back_kernel(tiles, tile, chunk, own_rows, dkv_ref, hat_ref, inv_ref, cos_ref, sin_ref, x_ref, dm_ref, dq_ref,
-                    gain_ref, gk_ref, w_ref, wq_ref, dgq_ref, dg_mid_ref, dg_post_ref, rs_ref,
-                    dx_ref, last_ref, gate_ref, up_ref, down_ref, acc, acc_in, acc_key, w_kv, w_sem, out, own, near, far, *sems):
+class RowScatter:
+    def __init__(self, group, own_rows, source, near, pair, far, sems):
+        self.group, self.own_rows, self.source = group, own_rows, source
+        self.near, self.pair, self.far, self.sems = near, pair, far, sems
+        self.others = list(range(1, group.chips))
+        self.order = self.others + [0]
+
+    def block(self, device):
+        return pl.ds(pl.multiple_of(device * self.own_rows, 16), self.own_rows)
+
+    def within(self, k):
+        g = self.group
+        return g.copy(self.source.at[self.block(g.other(k) + 1 - 2 * g.core)], self.near.at[k],
+                      self.sems[0].at[k], self.sems[1].at[k], g.partner())
+
+    def between(self, k):
+        g = self.group
+        return g.copy(self.pair.at[k], self.far.at[k], self.sems[2].at[k], self.sems[3].at[k], g.other(k))
+
+    def send(self):
+        for k in self.order:
+            self.within(k).start()
+
+    def middle(self, out):
+        for k in self.order:
+            self.within(k).wait_recv()
+            both = self.source[self.block(self.group.other(k)), :].astype(F32) + self.near[k].astype(F32)
+            if k > 0:
+                self.pair[k] = both.astype(BF16)
+                self.between(k).start()
+            else:
+                out[...] = both
+
+    def final(self, out):
+        for k in self.others:
+            self.between(k).wait_recv()
+            out[...] += self.far[k].astype(F32)
+        for k in self.others:
+            self.between(k).wait_send()
+        for k in self.order:
+            self.within(k).wait_send()
+
+
+def row_scatter_scratch(chips, own_rows, cols):
+    return [pltpu.VMEM((chips, own_rows, cols), BF16)] * 3 + [pltpu.SemaphoreType.DMA((chips,))] * 4
+
+
+def key_back_kernel(tiles, tile, chunk, own_rows, scattered, dkv_ref, hat_ref, inv_ref, cos_ref, sin_ref, x_ref, dm_ref, dq_ref,
+                    gain_ref, gk_ref, w_ref, wq_ref, dgq_ref, dg_mid_ref, dg_post_ref, rs_ref, qo_ref,
+                    dx_ref, last_out, qo_out, gate_ref, up_ref, down_ref, acc, acc_in, acc_key, w_kv, w_sem, last_ref,
+                    out, own, near, far, *sems):
     i = pl.program_id(0)
     head = hat_ref.shape[1]
     per = tile // chunk
     count = tiles * per + 1
-    line = ResidentSum(count, chunk, count, own, near, far, out, sems)
+    line = ResidentSum(count, chunk, count, own, near, far, out, sems[:9])
+    group = Shared(True)
+    if scattered:
+        early = RowScatter(group, own_rows, qo_ref, *sems[9:12], sems[12:16])
+        late = RowScatter(group, own_rows, last_ref, *sems[16:19], sems[19:23])
 
     @pl.when(i == 0)
     def _():
         copy = pltpu.make_async_copy(w_ref.at[:, pl.ds(head, 2 * head)], w_kv, w_sem)
         copy.start()
-        barrier_line(line.z)
+        if scattered:
+            group.greet(line.z)
+            early.send()
+        else:
+            barrier_line(line.z)
+            qo_out[...] = qo_ref[...]
         for ref in (acc, acc_in, acc_key):
             ref[...] = jnp.zeros_like(ref)
         copy.wait()
@@ -1180,6 +1247,13 @@
     @pl.when(i == 2)
     def _():
         line.total(count - 1)
+        if scattered:
+            early.middle(qo_out)
+
+    if scattered:
+        @pl.when(i == tiles)
+        def _():
+            early.final(qo_out)
 
     @pl.when(i >= 3)
     def _():
@@ -1214,11 +1288,18 @@
         gains = jnp.concatenate(
             [acc_in[...], dg_mid_ref[...], dg_post_ref[...], spread[0:2], jnp.zeros((122, width), F32)], axis=0)
         last_ref[:, 2 * head :] = jnp.transpose(gains).astype(BF16)
-        line.finish()
+        if scattered:
+            late.send()
+            line.finish()
+            late.middle(last_out)
+            late.final(last_out)
+        else:
+            last_out[...] = last_ref[...]
+            line.finish()
 
 
 def key_back(d_kv, hat, inv, cosine, sine, x, d_middle, d_query, gains, gain_key, first, w_query, dg_query, dg_mid, dg_post,
-             ffn_grads, own_rows, ident):
+             ffn_grads, grad_qo, own_rows, ident):
     rows, width = x.shape
     head = hat.shape[1]
     tile, chunk = 256, 128
@@ -1235,12 +1316,23 @@
     turns = cosine.shape[0] // tile
     turn = pl.BlockSpec((tile, head // 2), lambda i: (lax.rem(jnp.maximum(i - 3, 0), turns), 0))
     comm = pltpu.VMEM((count * chunk, 2 * head), BF16)
+    scattered = own_rows % 16 == 0
+    chips = width // (2 * own_rows)
+    last = (width, 2 * head + 128)
+    more = []
+    if scattered:
+        last_out, qo_out, kind = (own_rows, last[1]), (own_rows, 2 * head), F32
+        for cols in (2 * head, last[1]):
+            more += row_scatter_scratch(chips, own_rows, cols)
+    else:
+        last_out, qo_out, kind = last, grad_qo.shape, BF16
     return pl.pallas_call(
-        functools.partial(key_back_kernel, tiles, tile, chunk, own_rows),
+        functools.partial(key_back_kernel, tiles, tile, chunk, own_rows, scattered),
         grid=(tiles + 3,),
         out_shape=(
             jax.ShapeDtypeStruct((rows, width), F32),
-            jax.ShapeDtypeStruct((width, 2 * head + 128), BF16),
+            jax.ShapeDtypeStruct(last_out, kind),
+            jax.ShapeDtypeStruct(qo_out, kind),
             jax.ShapeDtypeStruct(ffn_grads.shape[1:], F32),
             jax.ShapeDtypeStruct(ffn_grads.shape[1:], F32),
             jax.ShapeDtypeStruct(ffn_grads.shape[:0:-1], F32),
@@ -1248,87 +1340,18 @@
         in_specs=[pl.BlockSpec((tile, 2 * head), lambda i: (jnp.minimum(i, tiles - 1), 0)),
                   late(head), late(1), turn, turn, late(width), late(width), late(4 * head),
                   whole_block(gains.shape), whole_block(gain_key.shape), ANY]
-        + [whole_block(a.shape) for a in (w_query, dg_query, dg_mid, dg_post, ffn_grads)],
-        out_specs=(late(width), fixed((width, 2 * head + 128)), fixed(ffn_grads.shape[1:]), fixed(ffn_grads.shape[1:]),
+        + [whole_block(a.shape) for a in (w_query, dg_query, dg_mid, dg_post, ffn_grads, grad_qo)],
+        out_specs=(late(width), fixed(last_out), fixed(qo_out), fixed(ffn_grads.shape[1:]), fixed(ffn_grads.shape[1:]),
                    fixed(ffn_grads.shape[:0:-1])),
         scratch_shapes=[
             pltpu.VMEM((width, 2 * head), F32), pltpu.VMEM((1, width), F32), pltpu.VMEM((1, head), F32),
-            pltpu.VMEM((width, 2 * head), BF16), pltpu.SemaphoreType.DMA] + [comm] * 4 + [dma] * 7
-        + [pltpu.SemaphoreType.REGULAR] * 2,
+            pltpu.VMEM((width, 2 * head), BF16), pltpu.SemaphoreType.DMA, pltpu.VMEM(last, BF16)] + [comm] * 4 + [dma] * 7
+        + [pltpu.SemaphoreType.REGULAR] * 2 + more,
         compiler_params=pltpu.CompilerParams(
             collective_id=ident, has_side_effects=True, vmem_limit_bytes=56 * 2**20),
+        cost_estimate=cost(75),
         name="key_back",
-    )(d_kv, hat, inv, cosine, sine, x, d_middle, d_query, gains, gain_key, first, w_query, dg_query, dg_mid, dg_post, ffn_grads)
-
-
-def scatter_kernel(chips, own_rows, x_ref, o_ref, near, pair, far, *sems):
-    ss1, rs1, ss2, rs2 = sems
-    ctx = lax.axis_size("ctx")
-    me = lax.axis_index("dp") * ctx + lax.axis_index("ctx")
-    core = lax.rem(me, 2)
-    chip = lax.div(me, 2)
-    bar = pltpu.get_barrier_semaphore()
-
-    def device(d):
-        return {"dp": lax.div(d, ctx), "ctx": lax.rem(d, ctx)}
-
-    partner = device(2 * chip + 1 - core)
-    pl.semaphore_signal(bar, inc=1, device_id=partner, device_id_type=MESH)
-    for k in range(1, chips):
-        other = lax.rem(chip + k, chips)
-        pl.semaphore_signal(bar, inc=1, device_id=device(2 * other + core), device_id_type=MESH)
-    pl.semaphore_wait(bar, chips)
-
-    def block(d):
-        return pl.ds(pl.multiple_of(d * own_rows, 16), own_rows)
-
-    def within(k):
-        q = lax.rem(chip + k, chips)
-        return pltpu.make_async_remote_copy(
-            x_ref.at[block(2 * q + 1 - core)], near.at[k], ss1.at[k], rs1.at[k], device_id=partner, device_id_type=MESH)
-
-    def between(k):
-        q = lax.rem(chip + k, chips)
-        return pltpu.make_async_remote_copy(
-            pair.at[k], far.at[k], ss2.at[k], rs2.at[k], device_id=device(2 * q + core), device_id_type=MESH)
-
-    order = list(range(1, chips)) + [0]
-    for k in order:
-        within(k).start()
-    for k in order:
-        within(k).wait_recv()
-        q = lax.rem(chip + k, chips)
-        both = x_ref[block(2 * q + core), :].astype(F32) + near[k].astype(F32)
-        if k > 0:
-            pair[k] = both.astype(BF16)
-            between(k).start()
-        else:
-            o_ref[...] = both
-    for k in range(1, chips):
-        between(k).wait_recv()
-        o_ref[...] += far[k].astype(F32)
-    for k in range(1, chips):
-        between(k).wait_send()
-    for k in order:
-        within(k).wait_send()
-
-
-def scatter(x, own_rows, ident):
-    n = x.shape[0] // own_rows
-    chips = n // 2
-    cols = x.shape[1]
-    buf = pltpu.VMEM((chips, own_rows, cols), BF16)
-    vmem = pl.BlockSpec(memory_space=pltpu.VMEM)
-    return pl.pallas_call(
-        functools.partial(scatter_kernel, chips, own_rows),
-        out_shape=jax.ShapeDtypeStruct((own_rows, cols), F32),
-        in_specs=[vmem],
-        out_specs=vmem,
-        scratch_shapes=[buf] * 3 + [pltpu.SemaphoreType.DMA((chips,))] * 4,
-        compiler_params=pltpu.CompilerParams(
-            collective_id=ident, has_side_effects=True, vmem_limit_bytes=40 * 2**20),
-        name="scatter",
-    )(x)
+    )(d_kv, hat, inv, cosine, sine, x, d_middle, d_query, gains, gain_key, first, w_query, dg_query, dg_mid, dg_post, ffn_grads, grad_qo)
 
 
 def shards(tokens, segments, cotangent, w_query, w_key, w_value, w_out, w_gate, w_up, w_down,
@@ -1388,6 +1411,7 @@
     line, heads_all = lax.optimization_barrier((line[0], heads_all))
     query_full = lax.all_gather(line, shared, axis=0, tiled=True)
     attn, hidden_two, gate, up, ffn_out = ffn_forward(x_rows, heads_all, gain_rows, weights, hidden, 1)
+    ffn_out, query_full = lax.optimization_barrier((ffn_out, query_full))
     output, d_gain_post_ffn, grad_ffn, d_two = ffn_backward(
         x_rows, attn, dy_rows, ffn_out, hidden_two, gate, up, gain_rows, weights, 2)
     grad_ffn = lax.psum_scatter(grad_ffn, shared, scatter_dimension=1, tiled=True)
@@ -1397,14 +1421,12 @@
     d_q_all, d_kv, d_gain_query, grad_qo = attention_back(
         queries, d_heads, log_mass, delta, own_ids[:, :, None, :], ids, q_hat, q_scale, cosine, sine, x_rows, gain_rows,
         gain_query[None], grad_out_t, kv, 4)
-    grad_qo = lax.psum_scatter(grad_qo, shared, scatter_dimension=0, tiled=True).astype(F32)
-    d_tokens, last, grad_gate, grad_up, grad_down = key_back(
+    d_tokens, last, grad_qo, grad_gate, grad_up, grad_down = key_back(
         d_kv, k_hat, k_scale, cosine, sine, x_rows, d_middle, d_q_all, gain_rows, gain_key[None],
-        first, query_full, d_gain_query, d_gain_mid, d_gain_post_ffn, grad_ffn, own_rows, 3)
-    if own_rows % 16 == 0:
-        last = scatter(last, own_rows, 7)
-    else:
+        first, query_full, d_gain_query, d_gain_mid, d_gain_post_ffn, grad_ffn, grad_qo, own_rows, 3)
+    if own_rows % 16:
         last = lax.psum_scatter(last, shared, scatter_dimension=0, tiled=True).astype(F32)
+        grad_qo = lax.psum_scatter(grad_qo, shared, scatter_dimension=0, tiled=True).astype(F32)
     g = last[:, 2 * head :]
     return (
         output.reshape(tokens.shape),

time: 853 us -> 712 us (0.83)
  waiting for transfers between devices: 159 us -> 0.11 us
  Pallas kernels: 622 us -> 640 us
    reduce_scatter x1, waiting for transfers between devices: 95.3 us -> 0.02 us  [shards(): lax.psum_scatter(grad_ffn, shared, scatter_dimension=1, tiled=True)]
    reduce_scatter x1 -> x0, waiting for transfers between devices: 34.6 us -> none  [shards(): lax.psum_scatter(grad_qo, shared, scatter_dimension=0, tiled=True)]
    all_gather x1, waiting for transfers between devices: 27.9 us -> 0.02 us  [shards(): query_full = lax.all_gather(line, shared, axis=0, tiled=True)]
    pallas_call x1, Pallas kernels: 82.3 us -> 102 us  [attention_back(): pl.pallas_call(functools.partial(attention_back_kernel, groups, size), ou...]
    pallas_call x1 -> x0, Pallas kernels: 12.6 us -> none  [scatter(): pl.pallas_call(functools.partial(scatter_kernel, chips, own_rows), out_sh...]
    pallas_call x1, Pallas kernels: 75.8 us -> 85.8 us  [key_back(): pl.pallas_call(functools.partial(key_back_kernel, tiles, tile, chunk, own...]
  transfers between devices with their start and end apart: 4 -> 3, of which waited for: 3 -> 0; matrix products, arithmetic and copies ran while one was open for 2% -> 1% of each run, Pallas kernels for 15% -> 55%
where the time goes in v8:
time: 712 us; the launch traced here: 703 us
  Pallas kernels  640 us (90%)
  local copies, waits for them, and re-layouts  39.5 us (6%)
  between operations  14.5 us (2%)
  other arithmetic  8.7 us (1%)
    pallas_call x1, Pallas kernels, ffn_backward(): pl.pallas_call(functools.partial(ffn_backward_kernel, tiles, tile, chunk,...  144 us
    pallas_call x1, Pallas kernels, ffn_forward(): pl.pallas_call(functools.partial(ffn_forward_kernel, tiles, tile, chunk,...  141 us
    pallas_call x1, Pallas kernels, attention(): pl.pallas_call(functools.partial(attention_kernel, groups, size), out_sha...  123 us
    pallas_call x1, Pallas kernels, attention_back(): pl.pallas_call(functools.partial(attention_back_kernel, groups, size), ou...  102 us
    pallas_call x1, Pallas kernels, key_back(): pl.pallas_call(functools.partial(key_back_kernel, tiles, tile, chunk, own...  85.8 us
    pallas_call x1, Pallas kernels, first_gather(): pl.pallas_call(first_gather_kernel, out_shape=(jax.ShapeDtypeStruct((devi...  23.4 us
    pallas_call x1, Pallas kernels, middle_back(): pl.pallas_call(middle_back_kernel, grid=(rows // tile,), out_shape=(jax.S...  20.6 us
    unnamed x37, local copies, waits for them, and re-layouts  20.4 us
  transfers between devices with their start and end apart: 3, of which 0 were waited for; matrix products, arithmetic and copies ran while one was open for 1% of the time, Pallas kernels for 55%

profile of v8, /device:TPU:0, one launch (start us, length us, event | category | flops | bytes accessed | tf_op | source)
XLA Modules:
  0.0 703.2 jit_solution(12630272513883421172)
XLA Ops:
  11.4 1.3 reshape_reshape.3.i_ref
  12.7 1.6 pad_maximum_fusion.b_ref
  14.3 1.7 fusion.9.a_ref
  15.9 23.4 %first_gather.1 = (bf16[8,144,896]{2,1,0:T(8,128)(2,1)}, bf16[144,2048]{1,0:T(8,128)(2,1)}, s32[8,16,128]{2,1,0:T(8,128)}) custom-call(bf16[144,896]{1,0:T(8,128)(2,1)} %fusion.9.a_ref, bf16[144,512]{1,0:T(8,128)(2,1)} %pad_maximum_fusion.b_ref, s32[16,128]{1,0:T(8,128)} %reshape_reshape.3.i_ref), custom_call_target="tpu_custom_call" | custom-call | flops 22000001024 | tf_op jit(solution)/shard_map/first_gather/pallas_call | solution.py:711
  39.4 2.3 reshape.72
  42.2 1.3 fusion.6
  43.6 1.0 slice_convert_fusion
  47.7 1.3 copy.61.qs_ref
  49.8 3.1 multiply_sine_fusion
  52.8 123.1 %attention.1 = (bf16[2048,256]{1,0:T(8,128)(2,1)}, f32[2048,256]{1,0:T(8,128)}, f32[2048,1]{1,0:T(8,128)}, f32[2048,256]{1,0:T(8,128)}, f32[2048,1]{1,0:T(8,128)...) custom-call(bf16[2048,1152]{1,0:T(8,128)(2,1)} %bitcast.40, ...), custom_call_target="tpu_custom_call" | custom-call | flops 121000001536 | tf_op jit(solution)/shard_map/attention/pallas_call | solution.py:895
  176.1 141.2 %ffn_forward.1 = (bf16[2048,1152]{1,0:T(8,128)(2,1)}, bf16[2048,1152]{1,0:T(8,128)(2,1)}, bf16[2048,1728]{1,0:T(8,128)(2,1)}, bf16[2048,1728]{1,0:T(8,128)(2,1)}, bf16[2048,1152]{1,0:T(8,128)(2,1)}) custom-call(bf16[2048,1152]{1,0:T(8,128)(2,1)} %bitcast.41, bf16[2048,1024]{1,0:T(8,128)(2,1)} %get-tuple-element.59.h_ref, f32[8,1152]{1,0:T(8,128)} %copy.60.gain_ref, ...), custom_call_target="tpu_custom_call" | custom-call | flops 153999998976 | tf_op jit(solution)/shard_map/ffn_forward/pallas_call | solution.py:304
  317.3 144.3 %ffn_backward.1 = (bf16[2048,1152]{1,0:T(8,128)(2,1)}, f32[1,1152]{1,0:T(1,128)}, bf16[3,1152,1728]{2,1,0:T(8,128)(2,1)}, bf16[2048,1152]{1,0:T(8,128)(2,1)}) custom-call(bf16[2048,1152]{1,0:T(8,128)(2,1)} %bitcast.42, bf16[2048,1152]{1,0:T(8,128)(2,1)} %get-tuple-element.60.attn_ref, bf16[2048,1152]{1,0:T(8,128)(2,1)} %bitcast.38, ...), custom_call_target="tpu_custom_call" | custom-call | flops 159499993088 | tf_op jit(solution)/shard_map/ffn_backward/pallas_call | solution.py:437
  462.9 20.6 %middle_back.1 = (f32[2048,1152]{1,0:T(8,128)}, bf16[2048,256]{1,0:T(8,128)(2,1)S(1)}, f32[2048,1]{1,0:T(8,128)S(1)}, f32[2,1152]{1,0:T(2,128)S(1)}, bf16[1152,256]{1,0:T(8,128)(2,1)S(1)}) custom-call(bf16[2048,1152]{1,0:T(8,128)(2,1)} %bitcast.43, bf16[2048,1152]{1,0:T(8,128)(2,1)} %get-tuple-element.60.attn_ref, bf16[2048,1152]{1,0:T(8,128)(2,1)} %bitcast.39, ...), custom_call_target="tpu_custom_call" | custom-call | flops 20899999744 | tf_op jit(solution)/shard_map/middle_back/pallas_call | solution.py:497
  483.5 1.0 copy-done.2
  484.5 1.0 copy-done.3
  486.8 102.0 %attention_back.1 = (bf16[2048,1024]{1,0:T(8,128)(2,1)}, bf16[2048,512]{1,0:T(8,128)(2,1)}, f32[1,256]{1,0:T(1,128)}, bf16[1152,512]{1,0:T(8,128)(2,1)}) custom-call(bf16[2048,256]{1,0:T(8,128)(2,1)} %get-tuple-element.68.q_ref, bf16[2048,256]{1,0:T(8,128)(2,1)} %copy-done.2, f32[2,2,512,1]{3,2,1,0:T(8,128)} %get-tuple-element.72.log_ref, ...), custom_call_target="tpu_custom_call" | custom-call | flops 88000004096 | tf_op jit(solution)/shard_map/attention_back/pallas_call | solution.py:1116
  588.9 85.8 %key_back.1 = (f32[2048,1152]{1,0:T(8,128)}, f32[144,640]{1,0:T(8,128)}, f32[144,512]{1,0:T(8,128)}, f32[144,1728]{1,0:T(8,128)}, f32[144,1728]{1,0:T(8,128)}, /*index=5*/f32[1728,144]{1,0:T(8,128)}) custom-call(bf16[2048,512]{1,0:T(8,128)(2,1)} %get-tuple-element.78.dkv_ref, f32[2048,256]{1,0:T(8,128)} %get-tuple-element.79.hat_ref, ...), custom_call_target="tpu_custom_call" | custom-call | flops 82500001792 | tf_op jit(solution)/shard_map/key_back/pallas_call | solution.py:1329
  674.7 1.8 fusion.12
  676.5 2.0 slice_reduce_fusion.2
  678.5 1.5 slice_reduce_fusion.6
  680.0 2.9 copy.69
  683.7 5.2 copy.78
  688.9 1.6 copy-done.6
  690.5 3.9 copy.79
  (65 shorter events, 13.9 us)
Async XLA Ops:
  7.2 168.9 %all-gather.3.cloned.1.call-start = ((), (), s32[]{:S(2)}) async-start(), calls=%async_computation.1 | async-start | bytes 16588800 | tf_op jit(solution)/shard_map/all_gather | solution.py:1400
  39.3 2.9 copy-start.9
  39.3 2.8 copy-start.10
  39.4 2.8 copy-start.11
  42.2 5.4 copy-start.13
  43.6 273.7 %all-gather.5.cloned.1.call-start = ((), (), s32[]{:S(2)}) async-start(), calls=%async_computation.2 | async-start | bytes 2654208 | tf_op jit(solution)/shard_map/all_gather | solution.py:1412
  176.0 412.9 %reduce-scatter.2.cloned.1.call-start = ((), (), s32[]{:S(2)}) async-start(), calls=%async_computation.3 | async-start | bytes 13934592 | tf_op jit(solution)/shard_map/reduce_scatter | solution.py:1417
  461.6 0.7 copy-start.14
  461.6 1.3 copy-start
  461.6 1.3 copy-start.1
  483.5 1.0 copy-start.2
  484.5 1.0 copy-start.3
  485.4 0.8 copy-start.4
  486.2 0.6 copy-start.5
  674.7 8.2 %copy-start.12 = (f32[144,512]{1,0:T(8,128)S(1)}, f32[144,512]{1,0:T(8,128)}, u32[]{:S(2)}) copy-start(f32[144,512]{1,0:T(8,128)} %get-tuple-element.90) | copy-start | bytes 884740
  683.7 6.8 copy-start.6
  690.5 3.9 copy-start.8
  690.5 4.8 copy-start.7
Sparse Core Ops, SparseCore 0:
  43.7 90.2 all-gather.2
  176.1 27.0 all-gather.4
  461.8 116.6 reduce-scatter.1

commit v9 on v8

--- a/solution.py
+++ b/solution.py
@@ -297,7 +297,7 @@
 def ffn_forward(x, heads, gains, weights, hidden, ident):
     rows, width = x.shape
     all_heads = heads.shape[1]
-    tile, chunk = 256, 128
+    tile, chunk = 128, 128
     tiles = rows // tile
     count = rows // chunk
     wide = wide_of(hidden)
@@ -328,9 +328,9 @@
     )(x, heads, gains, weights)
 
 
-def ffn_backward_kernel(tiles, tile, chunk, slots, hidden, x_ref, attn_ref, dy_ref, ffn_ref, two_ref, gate_ref, up_ref,
+def ffn_backward_kernel(tiles, tile, chunk, slots, hidden, dy_ref, ffn_ref, two_ref, gate_ref, up_ref,
                         gain_ref, w_ref,
-                        y_ref, dgain_ref, grad_ref, out_ref, wg_ref, wu_ref, wd_ref, w_sem,
+                        dgain_ref, grad_ref, out_ref, wg_ref, wu_ref, wd_ref, w_sem,
                         acc_g, acc_u, acc_d, keep_g, keep_u, keep_h, stage, stage_sem, own, near, far, *sems):
     i = pl.program_id(0)
     per = tile // chunk
@@ -348,10 +348,8 @@
         for copy in copies:
             copy.wait()
 
-    middle, _, _ = middle_of(x_ref[...], attn_ref[...], gain_ref[1:2, :])
     hat, inv = norm_parts(ffn_ref[...].astype(F32))
     gain = gain_ref[3:4, :]
-    y_ref[...] = (middle + hat * (1.0 + gain)).astype(BF16)
     d_ffn, d_gain = norm_back(dy_ref[...].astype(F32), hat, inv, gain)
     dgain_ref[...] += d_gain[None]
     d_ffn = d_ffn.astype(BF16)
@@ -423,8 +421,8 @@
         line.finish()
 
 
-def ffn_backward(x, attn, dy, ffn, two, gate, up, gains, weights, ident):
-    rows, width = x.shape
+def ffn_backward(dy, ffn, two, gate, up, gains, weights, ident):
+    rows, width = dy.shape
     hidden = gate.shape[1]
     wide = wide_of(hidden)
     tile, chunk = 256, 128
@@ -438,14 +436,13 @@
         functools.partial(ffn_backward_kernel, tiles, tile, chunk, slots, hidden),
         grid=(tiles,),
         out_shape=(
-            jax.ShapeDtypeStruct((rows, width), BF16),
             jax.ShapeDtypeStruct((1, width), F32),
             jax.ShapeDtypeStruct((3, width, hidden), BF16),
             jax.ShapeDtypeStruct((rows, width), BF16),
         ),
-        in_specs=[tile_block(tile, width)] * 5 + [tile_block(tile, hidden)] * 2
+        in_specs=[tile_block(tile, width)] * 3 + [tile_block(tile, hidden)] * 2
         + [whole_block(gains.shape), ANY],
-        out_specs=(tile_block(tile, width), pl.BlockSpec((1, width), lambda i: (0, 0)), ANY, ANY),
+        out_specs=(pl.BlockSpec((1, width), lambda i: (0, 0)), ANY, ANY),
         scratch_shapes=[pltpu.VMEM((width, wide), BF16)] * 3 + [pltpu.SemaphoreType.DMA((3,))] + [acc] * 3 + [keep] * 3
         + [pltpu.VMEM((2, step, hidden), BF16), pltpu.SemaphoreType.DMA((2,))]
         + line_sum_scratch(count, chunk, slots, width),
@@ -453,11 +450,11 @@
             collective_id=ident, has_side_effects=True, vmem_limit_bytes=63 * 2**20),
         cost_estimate=cost(145),
         name="ffn_backward",
-    )(x, attn, dy, ffn, two, gate, up, gains, weights)
-
-
-def middle_back_kernel(x_ref, attn_ref, dy_ref, d2_ref, h_ref, gain_ref, w_ref,
-                       dm_ref, dh_ref, delta_ref, dgain_ref, go_ref, acc, wo_ref, w_sem):
+    )(dy, ffn, two, gate, up, gains, weights)
+
+
+def middle_back_kernel(x_ref, attn_ref, dy_ref, d2_ref, ffn_ref, h_ref, gain_ref, w_ref,
+                       y_ref, dm_ref, dh_ref, delta_ref, dgain_ref, go_ref, acc, wo_ref, w_sem):
     i = pl.program_id(0)
 
     @pl.when(i == 0)
@@ -471,6 +468,8 @@
         dgain_ref[...] = jnp.zeros_like(dgain_ref)
 
     middle, attn_hat, attn_inv = middle_of(x_ref[...], attn_ref[...], gain_ref[1:2, :])
+    hat, _ = norm_parts(ffn_ref[...].astype(F32))
+    y_ref[...] = (middle + hat * (1.0 + gain_ref[3:4, :])).astype(BF16)
     hat, inv = norm_parts(middle)
     d_part, d_gain = norm_back(d2_ref[...].astype(F32), hat, inv, gain_ref[2:3, :])
     dgain_ref[1:2, :] += d_gain[None]
@@ -490,7 +489,7 @@
         go_ref[...] = acc[...].astype(BF16)
 
 
-def middle_back(x, attn, dy, d_two, heads, gains, weights):
+def middle_back(x, attn, dy, d_two, ffn, heads, gains, weights):
     rows, width = x.shape
     head = heads.shape[1]
     tile = 256
@@ -498,22 +497,23 @@
         middle_back_kernel,
         grid=(rows // tile,),
         out_shape=(
+            jax.ShapeDtypeStruct((rows, width), BF16),
             jax.ShapeDtypeStruct((rows, width), F32),
             jax.ShapeDtypeStruct((rows, head), BF16),
             jax.ShapeDtypeStruct((rows, 1), F32),
             jax.ShapeDtypeStruct((2, width), F32),
             jax.ShapeDtypeStruct((width, head), BF16),
         ),
-        in_specs=[tile_block(tile, width)] * 4 + [tile_block(tile, head)] + [whole_block(gains.shape), ANY],
+        in_specs=[tile_block(tile, width)] * 5 + [tile_block(tile, head)] + [whole_block(gains.shape), ANY],
         out_specs=(
-            tile_block(tile, width), tile_block(tile, head), tile_block(tile, 1),
+            tile_block(tile, width), tile_block(tile, width), tile_block(tile, head), tile_block(tile, 1),
             pl.BlockSpec((2, width), lambda i: (0, 0)), pl.BlockSpec((width, head), lambda i: (0, 0)),
         ),
         scratch_shapes=[pltpu.VMEM((width, head), F32), pltpu.VMEM((width, head), BF16), pltpu.SemaphoreType.DMA],
         compiler_params=pltpu.CompilerParams(vmem_limit_bytes=48 * 2**20),
         cost_estimate=cost(19),
         name="middle_back",
-    )(x, attn, dy, d_two, heads, gains, weights)
+    )(x, attn, dy, d_two, ffn, heads, gains, weights)
 
 
 class LineGather:
@@ -649,12 +649,14 @@
             source, target, send, recv, device_id=self.ident(device), device_id_type=MESH)
 
 
-def first_gather_kernel(a_ref, b_ref, i_ref, all_ref, line_ref, ids_ref, lsem, ss1, rs1, ss2, rs2, si1, ri1, si2, ri2, *sems):
+def first_gather_kernel(a_ref, b_ref, c_ref, i_ref, all_ref, line_ref, more_ref, ids_ref, lsem, ss1, rs1, ss2, rs2, si1, ri1, si2, ri2, *sems):
     group = Shared(True)
-    line = LineGather(line_ref, b_ref.shape[0], b_ref.shape[1], sems)
+    line = LineGather(line_ref, b_ref.shape[0], b_ref.shape[1], sems[:4])
+    more = LineGather(more_ref, c_ref.shape[0], c_ref.shape[1], sems[4:])
     width = b_ref.shape[1]
     own = [
         pltpu.make_async_copy(b_ref, line_ref.at[:, pl.ds(pl.multiple_of(line.z * width, width), width)], lsem.at[0]),
+        pltpu.make_async_copy(c_ref, more_ref.at[:, pl.ds(pl.multiple_of(line.z * width, width), width)], lsem.at[3]),
         pltpu.make_async_copy(a_ref, all_ref.at[group.me], lsem.at[1]),
         pltpu.make_async_copy(i_ref, ids_ref.at[group.me], lsem.at[2]),
     ]
@@ -679,23 +681,28 @@
     for k in range(1, group.chips):
         for n in both:
             direct(n, k).start()
+    for n in both:
+        inner(n, 0).start()
     own[0].wait()
     line.forward(0, 0)
-    for n in both:
-        inner(n, 0).start()
+    own[1].wait()
+    more.forward(0, 0)
     for k in range(1, group.chips):
         if k < 3:
             line.forward(0, k)
+            more.forward(0, k)
         for n in both:
             direct(n, k, True).wait_recv()
             inner(n, k).start()
     for hop in range(min(3, group.chips), 3):
         line.forward(0, hop)
+        more.forward(0, hop)
     for k in range(group.chips):
         for n in both:
             inner(n, k, True).wait_recv()
     line.arrived(0)
-    for copy in own[1:]:
+    more.arrived(0)
+    for copy in own[2:]:
         copy.wait()
     for n in both:
         for k in range(1, group.chips):
@@ -703,9 +710,10 @@
         for k in range(group.chips):
             inner(n, k).wait_send()
     line.finish(1)
-
-
-def first_gather(a, b, ids, devices, ident):
+    more.finish(1)
+
+
+def first_gather(a, b, c, ids, devices, ident):
     dma = pltpu.SemaphoreType.DMA((devices // 2,))
     hop = pltpu.SemaphoreType.DMA((3, 1))
     return pl.pallas_call(
@@ -713,15 +721,16 @@
         out_shape=(
             jax.ShapeDtypeStruct((devices,) + a.shape, a.dtype),
             jax.ShapeDtypeStruct((b.shape[0], 4 * b.shape[1]), b.dtype),
+            jax.ShapeDtypeStruct((c.shape[0], 4 * c.shape[1]), c.dtype),
             jax.ShapeDtypeStruct((devices,) + ids.shape, ids.dtype),
         ),
-        in_specs=[ANY] * 3,
-        out_specs=(ANY,) * 3,
-        scratch_shapes=[pltpu.SemaphoreType.DMA((3,))] + [dma] * 8 + [hop] * 4,
+        in_specs=[ANY] * 4,
+        out_specs=(ANY,) * 4,
+        scratch_shapes=[pltpu.SemaphoreType.DMA((4,))] + [dma] * 8 + [hop] * 8,
         compiler_params=pltpu.CompilerParams(collective_id=ident, has_side_effects=True),
         cost_estimate=cost(20),
         name="first_gather",
-    )(a, b, ids)
+    )(a, b, c, ids)
 
 
 def attention_kernel(groups, size, x_ref, w_ref, gain_ref, gq_ref, gk_ref, cos_ref, sin_ref, qs_ref, ks_ref,
@@ -1188,8 +1197,8 @@
 
 
 def key_back_kernel(tiles, tile, chunk, own_rows, scattered, dkv_ref, hat_ref, inv_ref, cos_ref, sin_ref, x_ref, dm_ref, dq_ref,
-                    gain_ref, gk_ref, w_ref, wq_ref, dgq_ref, dg_mid_ref, dg_post_ref, rs_ref, qo_ref,
-                    dx_ref, last_out, qo_out, gate_ref, up_ref, down_ref, acc, acc_in, acc_key, w_kv, w_sem, last_ref,
+                    gain_ref, gk_ref, w_ref, wq_ref, dgq_ref, dg_mid_ref, dg_post_ref, qo_ref,
+                    dx_ref, last_out, qo_out, acc, acc_in, acc_key, w_kv, w_sem, last_ref, part,
                     out, own, near, far, *sems):
     i = pl.program_id(0)
     head = hat_ref.shape[1]
@@ -1221,6 +1230,7 @@
     def _():
         for j in range(per):
             line.put(i * per + j, dkv_ref[j * chunk : (j + 1) * chunk, :])
+        part[pl.ds(pl.multiple_of(i * tile, tile), tile), :] = dot(dq_ref[...], wq_ref[...], NT)
 
     @pl.when((i >= 1) & (i <= tiles))
     def _():
@@ -1231,14 +1241,6 @@
     def _():
         for j in range(per):
             line.total((i - 2) * per + j)
-
-    @pl.when(i == 0)
-    def _():
-        gate_ref[...] = rs_ref[0].astype(F32)
-        up_ref[...] = rs_ref[1].astype(F32)
-        row = lax.broadcasted_iota(jnp.int32, (own_rows, own_rows), 0)
-        col = lax.broadcasted_iota(jnp.int32, (own_rows, own_rows), 1)
-        down_ref[...] = dot(rs_ref[2], jnp.where(row == col, 1.0, 0.0).astype(BF16), TN)
 
     @pl.when(i == 1)
     def _():
@@ -1264,7 +1266,7 @@
         d_raw, d_gain = norm_back(d_rot, hat_ref[...], inv_ref[...], gk_ref[...])
         acc_key[...] += d_gain[None]
         d_raw = jnp.concatenate([d_raw.astype(BF16), d_kv[:, head:]], axis=1)
-        d_one = dot(dq_ref[...], wq_ref[...], NT) + dot(d_raw, w_kv[...], NT)
+        d_one = part[pl.ds(pl.multiple_of((i - 3) * tile, tile), tile), :] + dot(d_raw, w_kv[...], NT)
         hat, inv = norm_parts(x_ref[...].astype(F32))
         gain = gain_ref[0:1, :]
         d_part, d_gain = norm_back(d_one, hat, inv, gain)
@@ -1299,7 +1301,7 @@
 
 
 def key_back(d_kv, hat, inv, cosine, sine, x, d_middle, d_query, gains, gain_key, first, w_query, dg_query, dg_mid, dg_post,
-             ffn_grads, grad_qo, own_rows, ident):
+             grad_qo, own_rows, ident):
     rows, width = x.shape
     head = hat.shape[1]
     tile, chunk = 256, 128
@@ -1333,25 +1335,23 @@
             jax.ShapeDtypeStruct((rows, width), F32),
             jax.ShapeDtypeStruct(last_out, kind),
             jax.ShapeDtypeStruct(qo_out, kind),
-            jax.ShapeDtypeStruct(ffn_grads.shape[1:], F32),
-            jax.ShapeDtypeStruct(ffn_grads.shape[1:], F32),
-            jax.ShapeDtypeStruct(ffn_grads.shape[:0:-1], F32),
         ),
         in_specs=[pl.BlockSpec((tile, 2 * head), lambda i: (jnp.minimum(i, tiles - 1), 0)),
-                  late(head), late(1), turn, turn, late(width), late(width), late(4 * head),
+                  late(head), late(1), turn, turn, late(width), late(width),
+                  pl.BlockSpec((tile, 4 * head), lambda i: (jnp.minimum(i, tiles - 1), 0)),
                   whole_block(gains.shape), whole_block(gain_key.shape), ANY]
-        + [whole_block(a.shape) for a in (w_query, dg_query, dg_mid, dg_post, ffn_grads, grad_qo)],
-        out_specs=(late(width), fixed(last_out), fixed(qo_out), fixed(ffn_grads.shape[1:]), fixed(ffn_grads.shape[1:]),
-                   fixed(ffn_grads.shape[:0:-1])),
+        + [whole_block(a.shape) for a in (w_query, dg_query, dg_mid, dg_post, grad_qo)],
+        out_specs=(late(width), fixed(last_out), fixed(qo_out)),
         scratch_shapes=[
             pltpu.VMEM((width, 2 * head), F32), pltpu.VMEM((1, width), F32), pltpu.VMEM((1, head), F32),
-            pltpu.VMEM((width, 2 * head), BF16), pltpu.SemaphoreType.DMA, pltpu.VMEM(last, BF16)] + [comm] * 4 + [dma] * 7
+            pltpu.VMEM((width, 2 * head), BF16), pltpu.SemaphoreType.DMA, pltpu.VMEM(last, BF16),
+            pltpu.VMEM((rows, width), F32)] + [comm] * 4 + [dma] * 7
         + [pltpu.SemaphoreType.REGULAR] * 2 + more,
         compiler_params=pltpu.CompilerParams(
             collective_id=ident, has_side_effects=True, vmem_limit_bytes=56 * 2**20),
         cost_estimate=cost(75),
         name="key_back",
-    )(d_kv, hat, inv, cosine, sine, x, d_middle, d_query, gains, gain_key, first, w_query, dg_query, dg_mid, dg_post, ffn_grads, grad_qo)
+    )(d_kv, hat, inv, cosine, sine, x, d_middle, d_query, gains, gain_key, first, w_query, dg_query, dg_mid, dg_post, grad_qo)
 
 
 def shards(tokens, segments, cotangent, w_query, w_key, w_value, w_out, w_gate, w_up, w_down,
@@ -1381,11 +1381,10 @@
     def rows_of_16(w):
         return jnp.pad(w, ((0, -own_rows % 16), (0, 0)))
 
-    first, line, ids = first_gather(
+    first, line_query, line_out, ids = first_gather(
         rows_of_16(jnp.concatenate([w_query, w_key, w_value, extra], axis=1)),
-        rows_of_16(jnp.concatenate([w_query, w_out.T], axis=1)), ids, width // own_rows, 5)
+        rows_of_16(w_query), rows_of_16(w_out.T), ids, width // own_rows, 5)
     first = first[:, :own_rows].reshape(width, -1)
-    line = line[:own_rows].reshape(own_rows, 4, 2, head).transpose(2, 0, 1, 3).reshape(2, own_rows, 4 * head)
     side = first[:, 3 * head :]
     gain_cols = side[:, :8].astype(F32)
     gain_rows = gain_cols.T
@@ -1396,7 +1395,7 @@
 
     wide = wide_of(hidden)
     second = jnp.concatenate(
-        [line[1]] + [jnp.pad(w, ((0, 0), (0, wide - hidden))) for w in (w_gate, w_up, w_down.T)], axis=1)
+        [line_out[:own_rows]] + [jnp.pad(w, ((0, 0), (0, wide - hidden))) for w in (w_gate, w_up, w_down.T)], axis=1)
     weights = lax.all_gather(second, shared, axis=0, tiled=True)
 
     offsets = rank * size + jnp.arange(size, dtype=jnp.int32)
@@ -1408,22 +1407,23 @@
     queries, q_hat, q_scale, k_hat, k_scale, heads_own, log_mass, kv, heads_all = attention(
         x_rows, first, gain_rows, gain_query[None], gain_key[None], cosine, sine, own_ids[..., None], ids, length, 0)
 
-    line, heads_all = lax.optimization_barrier((line[0], heads_all))
-    query_full = lax.all_gather(line, shared, axis=0, tiled=True)
+    line_query, heads_all = lax.optimization_barrier((line_query[:own_rows], heads_all))
+    query_full = lax.all_gather(line_query, shared, axis=0, tiled=True)
     attn, hidden_two, gate, up, ffn_out = ffn_forward(x_rows, heads_all, gain_rows, weights, hidden, 1)
     ffn_out, query_full = lax.optimization_barrier((ffn_out, query_full))
-    output, d_gain_post_ffn, grad_ffn, d_two = ffn_backward(
-        x_rows, attn, dy_rows, ffn_out, hidden_two, gate, up, gain_rows, weights, 2)
+    d_gain_post_ffn, grad_ffn, d_two = ffn_backward(
+        dy_rows, ffn_out, hidden_two, gate, up, gain_rows, weights, 2)
     grad_ffn = lax.psum_scatter(grad_ffn, shared, scatter_dimension=1, tiled=True)
-    d_middle, d_heads, delta, d_gain_mid, grad_out_t = middle_back(
-        x_rows, attn, dy_rows, d_two, heads_own, gain_rows, weights)
+    output, d_middle, d_heads, delta, d_gain_mid, grad_out_t = middle_back(
+        x_rows, attn, dy_rows, d_two, ffn_out, heads_own, gain_rows, weights)
 
     d_q_all, d_kv, d_gain_query, grad_qo = attention_back(
         queries, d_heads, log_mass, delta, own_ids[:, :, None, :], ids, q_hat, q_scale, cosine, sine, x_rows, gain_rows,
         gain_query[None], grad_out_t, kv, 4)
-    d_tokens, last, grad_qo, grad_gate, grad_up, grad_down = key_back(
+    d_tokens, last, grad_qo = key_back(
         d_kv, k_hat, k_scale, cosine, sine, x_rows, d_middle, d_q_all, gain_rows, gain_key[None],
-        first, query_full, d_gain_query, d_gain_mid, d_gain_post_ffn, grad_ffn, grad_qo, own_rows, 3)
+        first, query_full, d_gain_query, d_gain_mid, d_gain_post_ffn, grad_qo, own_rows, 3)
+    grad_ffn = grad_ffn.astype(F32)
     if own_rows % 16:
         last = lax.psum_scatter(last, shared, scatter_dimension=0, tiled=True).astype(F32)
         grad_qo = lax.psum_scatter(grad_qo, shared, scatter_dimension=0, tiled=True).astype(F32)
@@ -1435,9 +1435,9 @@
         last[:, :head],
         last[:, head : 2 * head],
         grad_qo[:, head:].T,
-        grad_gate,
-        grad_up,
-        grad_down,
+        grad_ffn[0],
+        grad_ffn[1],
+        grad_ffn[2].T,
         g[:, 0],
         g[:, 1],
         g[:, 2],

time: 712 us -> 687 us (0.965)
  Pallas kernels: 640 us -> 626 us
  local copies, waits for them, and re-layouts: 39.5 us -> 29 us
    pallas_call x1, Pallas kernels: 141 us -> 129 us  [ffn_forward(): pl.pallas_call(functools.partial(ffn_forward_kernel, tiles, tile, chunk,...]
    unnamed x37 -> x23, local copies, waits for them, and re-layouts: 20.4 us -> 10.1 us
  transfers between devices with their start and end apart: 3 -> 3, of which waited for: 0 -> 0; matrix products, arithmetic and copies ran while one was open for 1% -> 2% of each run, Pallas kernels for 55% -> 68%
where the time goes in v9:
time: 687 us; the launch traced here: 679 us
  Pallas kernels  626 us (91%)
  local copies, waits for them, and re-layouts  29 us (4%)
  between operations  14.4 us (2%)
  other arithmetic  9.79 us (1%)
    pallas_call x1, Pallas kernels, ffn_backward(): pl.pallas_call(functools.partial(ffn_backward_kernel, tiles, tile, chunk,...  144 us
    pallas_call x1, Pallas kernels, ffn_forward(): pl.pallas_call(functools.partial(ffn_forward_kernel, tiles, tile, chunk,...  129 us
    pallas_call x1, Pallas kernels, attention(): pl.pallas_call(functools.partial(attention_kernel, groups, size), out_sha...  125 us
    pallas_call x1, Pallas kernels, attention_back(): pl.pallas_call(functools.partial(attention_back_kernel, groups, size), ou...  102 us
    pallas_call x1, Pallas kernels, key_back(): pl.pallas_call(functools.partial(key_back_kernel, tiles, tile, chunk, own...  83.2 us
    pallas_call x1, Pallas kernels, middle_back(): pl.pallas_call(middle_back_kernel, grid=(rows // tile,), out_shape=(jax.S...  23 us
    pallas_call x1, Pallas kernels, first_gather(): pl.pallas_call(first_gather_kernel, out_shape=(jax.ShapeDtypeStruct((devi...  20.2 us
  transfers between devices with their start and end apart: 3, of which 0 were waited for; matrix products, arithmetic and copies ran while one was open for 2% of the time, Pallas kernels for 68%

profile of v9, /device:TPU:0, one launch (start us, length us, event | category | flops | bytes accessed | tf_op | source)
XLA Modules:
  0.0 679.0 jit_solution(14749497927888835889)
XLA Ops:
  11.4 1.3 reshape_reshape.3.i_ref
  12.7 1.7 fusion.9.a_ref
  14.3 20.2 %first_gather.1 = (bf16[8,144,896]{2,1,0:T(8,128)(2,1)}, bf16[144,1024]{1,0:T(8,128)(2,1)}, bf16[144,1024]{1,0:T(8,128)(2,1)}, s32[8,16,128]{2,1,0:T(8,128)}) custom-call(bf16[144,896]{1,0:T(8,128)(2,1)} %fusion.9.a_ref, bf16[144,256]{1,0:T(8,128)(2,1)} %b_ref.1, bf16[144,256]{1,0:T(8,128)(2,1)} %bitcast.37, s32[16,128]{1,0:T(8,128)} %reshape_reshape.3.i_ref), custom_call_target="tpu_custom_call" | custom-call | flops 22000001024 | tf_op jit(solution)/shard_map/first_gather/pallas_call | solution.py:719
  34.6 2.2 fusion.6
  36.9 1.0 slice_convert_fusion
  38.0 0.8 copy.55.gain_ref
  41.0 1.3 copy.56.qs_ref
  42.3 3.1 multiply_sine_fusion
  45.4 125.1 %attention.1 = (bf16[2048,256]{1,0:T(8,128)(2,1)}, f32[2048,256]{1,0:T(8,128)}, f32[2048,1]{1,0:T(8,128)}, f32[2048,256]{1,0:T(8,128)}, f32[2048,1]{1,0:T(8,128)...) custom-call(bf16[2048,1152]{1,0:T(8,128)(2,1)} %bitcast.32, ...), custom_call_target="tpu_custom_call" | custom-call | flops 121000001536 | tf_op jit(solution)/shard_map/attention/pallas_call | solution.py:904
  171.2 128.6 %ffn_forward.1 = (bf16[2048,1152]{1,0:T(8,128)(2,1)}, bf16[2048,1152]{1,0:T(8,128)(2,1)}, bf16[2048,1728]{1,0:T(8,128)(2,1)}, bf16[2048,1728]{1,0:T(8,128)(2,1)}, bf16[2048,1152]{1,0:T(8,128)(2,1)}) custom-call(bf16[2048,1152]{1,0:T(8,128)(2,1)} %bitcast.33, bf16[2048,1024]{1,0:T(8,128)(2,1)} %get-tuple-element.57.h_ref, f32[8,1152]{1,0:T(8,128)} %copy.55.gain_ref, ...), custom_call_target="tpu_custom_call" | custom-call | flops 153999998976 | tf_op jit(solution)/shard_map/ffn_forward/pallas_call | solution.py:304
  299.8 143.5 %ffn_backward.1 = (f32[1,1152]{1,0:T(1,128)}, bf16[3,1152,1728]{2,1,0:T(8,128)(2,1)}, bf16[2048,1152]{1,0:T(8,128)(2,1)}) custom-call(bf16[2048,1152]{1,0:T(8,128)(2,1)} %bitcast.30, bf16[2048,1152]{1,0:T(8,128)(2,1)} %get-tuple-element.62.ffn_ref, bf16[2048,1152]{1,0:T(8,128)(2,1)} %get-tuple-element.63.two_ref, ...), custom_call_target="tpu_custom_call" | custom-call | flops 159499993088 | tf_op jit(solution)/shard_map/ffn_backward/pallas_call | solution.py:435
  444.6 23.0 %middle_back.1 = (bf16[2048,1152]{1,0:T(8,128)(2,1)}, f32[2048,1152]{1,0:T(8,128)}, bf16[2048,256]{1,0:T(8,128)(2,1)S(1)}, f32[2048,1]{1,0:T(8,128)S(1)}, f32[2,...) custom-call(bf16[2048,1152]{1,0:T(8,128)(2,1)} %bitcast.34, bf16[2048,1152]{1,0:T(8,128)(2,1)} %get-tuple-element.59.attn_ref, ...), custom_call_target="tpu_custom_call" | custom-call | flops 20899999744 | tf_op jit(solution)/shard_map/middle_back/pallas_call | solution.py:496
  467.6 1.0 copy-done.2
  468.5 1.0 copy-done.3
  470.9 102.0 %attention_back.1 = (bf16[2048,1024]{1,0:T(8,128)(2,1)}, bf16[2048,512]{1,0:T(8,128)(2,1)}, f32[1,256]{1,0:T(1,128)}, bf16[1152,512]{1,0:T(8,128)(2,1)}) custom-call(bf16[2048,256]{1,0:T(8,128)(2,1)} %get-tuple-element.69.q_ref, bf16[2048,256]{1,0:T(8,128)(2,1)} %copy-done.2, f32[2,2,512,1]{3,2,1,0:T(8,128)} %get-tuple-element.71.log_ref, ...), custom_call_target="tpu_custom_call" | custom-call | flops 88000004096 | tf_op jit(solution)/shard_map/attention_back/pallas_call | solution.py:1125
  572.9 83.2 %key_back.1 = (f32[2048,1152]{1,0:T(8,128)}, f32[144,640]{1,0:T(8,128)}, f32[144,512]{1,0:T(8,128)}) custom-call(bf16[2048,512]{1,0:T(8,128)(2,1)} %get-tuple-element.77.dkv_ref, f32[2048,256]{1,0:T(8,128)} %get-tuple-element.78.hat_ref, f32[2048,1]{1,0:T(8,128)} %get-tuple-element.79.inv_ref, f32[1024,128]{1,0:T(8,128)} %get-tuple-element.154.cos_ref, ...), custom_call_target="tpu_custom_call" | custom-call | flops 82500001792 | tf_op jit(solution)/shard_map/key_back/pallas_call | solution.py:1331
  656.1 1.5 slice_reduce_fusion.6
  657.6 2.0 slice_reduce_fusion.2
  659.6 1.7 fusion.11
  661.3 1.7 slice_bitcast_fusion.3
  663.0 1.8 convert_element_type.24
  664.8 1.7 slice_bitcast_fusion
  666.5 1.8 copy-done.6
  668.3 3.7 copy.65
  (49 shorter events, 9.7 us)
Async XLA Ops:
  7.2 164.0 %all-gather.3.cloned.1.call-start = ((), (), s32[]{:S(2)}) async-start(), calls=%async_computation.1 | async-start | bytes 16588800 | tf_op jit(solution)/shard_map/all_gather | solution.py:1399
  14.3 20.3 %copy-start.7 = (bf16[1728,144]{0,1:T(8,128)(2,1)S(1)}, bf16[1728,144]{0,1:T(8,128)(2,1)}, u32[]{:S(2)}) copy-start(bf16[1728,144]{0,1:T(8,128)(2,1)} %param.25) | copy-start | bytes 1492996
  14.3 20.3 %copy-start.8 = (bf16[144,1728]{1,0:T(8,128)(2,1)S(1)}, bf16[144,1728]{1,0:T(8,128)(2,1)}, u32[]{:S(2)}) copy-start(bf16[144,1728]{1,0:T(8,128)(2,1)} %param.24) | copy-start | bytes 1492996
  14.3 20.3 %copy-start.9 = (bf16[144,1728]{1,0:T(8,128)(2,1)S(1)}, bf16[144,1728]{1,0:T(8,128)(2,1)}, u32[]{:S(2)}) copy-start(bf16[144,1728]{1,0:T(8,128)(2,1)} %param.23) | copy-start | bytes 1492996
  34.6 6.3 copy-start.10
  36.9 262.9 %all-gather.5.cloned.1.call-start = ((), (), s32[]{:S(2)}) async-start(), calls=%async_computation.2 | async-start | bytes 2654208 | tf_op jit(solution)/shard_map/all_gather | solution.py:1411
  170.5 492.5 %reduce-scatter.2.cloned.1.call-start = ((), (), s32[]{:S(2)}) async-start(), calls=%async_computation.3 | async-start | bytes 13934592 | tf_op jit(solution)/shard_map/reduce_scatter | solution.py:1416
  443.3 0.8 copy-start
  443.3 1.2 copy-start.1
  467.6 1.0 copy-start.2
  468.5 1.0 copy-start.3
  469.5 0.8 copy-start.4
  470.3 0.6 copy-start.5
  663.0 5.3 copy-start.6
Sparse Core Ops, SparseCore 0:
  37.0 91.5 all-gather.2
  170.6 27.5 all-gather.4
  443.5 115.4 reduce-scatter.1

commit v10 on v9

--- a/solution.py
+++ b/solution.py
@@ -742,9 +742,10 @@
     blocks = length // (2 * size)
     group = Shared(False)
     rank = group.me
-    line = LineGather(whole, size, head, sems[:4])
+    tile = min(256, size)
+    per = size // tile
+    line = LineGather(whole, tile, head, sems[:4])
     z = line.z
-    tile = min(256, size)
     group.greet(z)
 
     def block(g, half, k, own):
@@ -756,8 +757,13 @@
     def place(g, half, c):
         return kv.at[g, pl.ds(pl.multiple_of(half * (length // 2) + c * size, size), size)]
 
+    def straight(t):
+        return t == 2 * groups - 1
+
     def direct(g, half, k, incoming=False):
         at = keys.quarter(g, half, k, z, own=not incoming)
+        if straight(2 * g + half):
+            at = place(g, half, group.other(-k) if incoming else rank)
         return group.copy(at, at, ss1.at[g, half, k], rs1.at[g, half, k], group.other(k))
 
     def inner(g, half, k, incoming=False):
@@ -825,59 +831,66 @@
     chips = range(1, group.chips)
     tiles = 2 * groups
 
+    def stage(t, n):
+        if not 0 <= t < tiles:
+            return
+        g, half = divmod(t, 2)
+        for k in chips:
+            spot = keys.tile_of(g, half, k)
+            if n == 0:
+                direct(g, half, k).start()
+            elif straight(t):
+                if n == 4:
+                    direct(g, half, k, True).wait_recv()
+                    inner(g, half, k).start()
+            elif n == 4:
+                keys.arrived(spot)
+                inner(g, half, k).start()
+            else:
+                if n == 1:
+                    direct(g, half, k, True).wait_recv()
+                keys.forward(spot, n - 1)
+
     def exchange(t):
-        for stage in (4, 3, 2, 1):
-            if not 0 <= t - stage < tiles:
-                continue
-            g, half = divmod(t - stage, 2)
-            for k in chips:
-                spot = keys.tile_of(g, half, k)
-                if stage == 1:
-                    direct(g, half, k, True).wait_recv()
-                if stage <= 3:
-                    keys.forward(spot, stage - 1)
-                else:
-                    keys.arrived(spot)
-                    inner(g, half, k).start()
+        for n in (4, 3, 2, 1):
+            stage(t - n, n)
 
     def hops(t):
         for hop in range(3):
             if 0 <= t - hop < tiles:
-                line.forward(t - hop, hop)
+                for u in range(per):
+                    line.forward((t - hop) * per + u, hop)
 
     def keep(t):
-        at = pl.ds(t * size, size)
+        at = pl.ds(t * tile, tile)
         return pltpu.make_async_copy(whole.at[at], all_out.at[at], store_all.at[t])
 
     def save(g):
         return pltpu.make_async_copy(kv.at[g], kv_out.at[g], store_kv.at[g])
 
+    def landed(t):
+        g, half = divmod(t, 2)
+        for k in range(group.chips):
+            inner(g, half, k, True).wait_recv()
+
     for t in range(tiles):
         g, half = divmod(t, 2)
-        for u in range(size // tile):
+        for u in range(per):
             project(g, half, u)
-        for k in chips:
-            direct(g, half, k).start()
+        stage(t, 0)
         inner(g, half, 0).start()
         exchange(t)
-    at_step = tiles
+    for t in range(tiles):
+        g, half = divmod(t, 2)
+        exchange(tiles + t)
+        landed(t)
+        attend(g, half)
+        hops(t)
     for g in range(groups):
-        while at_step < min(2 * g + 6, tiles + 4):
-            exchange(at_step)
-            at_step += 1
-        for half in range(2):
-            for k in range(group.chips):
-                inner(g, half, k, True).wait_recv()
         save(g).start()
-        for half in range(2):
-            attend(g, half)
-            if at_step < tiles + 4:
-                exchange(at_step)
-                at_step += 1
-            hops(2 * g + half)
     for t in range(tiles, tiles + 2):
         hops(t)
-    for t in range(tiles):
+    for t in range(tiles * per):
         line.arrived(t)
         keep(t).start()
     for g in range(groups):
@@ -887,9 +900,9 @@
                 direct(g, half, k).wait_send()
             for k in range(group.chips):
                 inner(g, half, k).wait_send()
-    line.finish(tiles)
-    keys.finish(tiles * (group.chips - 1))
-    for t in range(tiles):
+    line.finish(tiles * per)
+    keys.finish((tiles - 1) * (group.chips - 1))
+    for t in range(tiles * per):
         keep(t).wait()
 
 
@@ -899,6 +912,7 @@
     head = gain_query.shape[1]
     chips = length // (4 * size)
     tiles = 2 * groups
+    parts = rows // min(256, size)
     vmem = pl.BlockSpec(memory_space=pltpu.VMEM)
     dma = pltpu.SemaphoreType.DMA
     return pl.pallas_call(
@@ -918,7 +932,7 @@
         out_specs=(vmem,) * 7 + (ANY, ANY),
         scratch_shapes=[
             pltpu.VMEM((groups, length, 2 * head), BF16), pltpu.VMEM((rows, 4 * head), BF16),
-            dma((groups,)), dma((tiles,))] + [dma((groups, 2, chips))] * 4 + [dma((3, tiles))] * 4
+            dma((groups,)), dma((parts,))] + [dma((groups, 2, chips))] * 4 + [dma((3, parts))] * 4
         + [dma((3, tiles * (chips - 1)))] * 4,
         compiler_params=pltpu.CompilerParams(
             collective_id=ident, has_side_effects=True, vmem_limit_bytes=60 * 2**20),
@@ -964,7 +978,7 @@
 
 
 def attention_back_kernel(groups, size, q_ref, do_ref, log_ref, delta_ref, qs_ref, ids_ref, hat_ref, inv_ref, cos_ref, sin_ref,
-                          x_ref, gain_ref, gq_ref, go_ref, kv_hbm, all_out, dkv_ref, dgain_ref, grad_ref,
+                          x_ref, gain_ref, gq_ref, go_ref, kv_hbm, all_out, dkv_ref, rest_ref, dgain_ref, grad_ref,
                           kv, dk, dv, part, near, pair, far, whole, acc, load, store, ss1, rs1, ss2, rs2, *sems):
     head = q_ref.shape[1]
     length = kv.shape[1]
@@ -973,7 +987,9 @@
     tiles = 2 * groups
     group = Shared(False)
     rank, core = group.me, group.core
-    line = LineGather(whole, size, head, sems)
+    tile = min(256, size)
+    per = size // tile
+    line = LineGather(whole, tile, head, sems)
     z = line.z
     others = range(1, group.chips)
     order = list(others) + [0]
@@ -1004,7 +1020,9 @@
             for k in order:
                 within(g, half, k).wait_recv()
                 total = part[g, rows_of(half, group.other(k)), :].astype(F32) + near[g, half, k].astype(F32)
-                if k > 0:
+                if k > 0 and g == groups - 1:
+                    rest_ref[half, k - 1] = total.astype(BF16)
+                elif k > 0:
                     pair[g, half, k - 1] = total.astype(BF16)
                     between(g, half, k).start()
                 else:
@@ -1022,7 +1040,8 @@
     def hops(t):
         for hop in range(3):
             if 0 <= t - hop < tiles:
-                line.forward(t - hop, hop)
+                for u in range(per):
+                    line.forward((t - hop) * per + u, hop)
 
     def attend(g, half):
         row = lax.broadcasted_iota(jnp.int32, (size, size), 0)
@@ -1072,7 +1091,7 @@
         acc[...] += dot(one, whole[own, pl.ds(pl.multiple_of(z * head, head), head)], TN)
 
     def keep(t):
-        at = pl.ds(t * size, size)
+        at = pl.ds(t * tile, tile)
         return pltpu.make_async_copy(whole.at[at], all_out.at[at], store.at[t])
 
     for g in range(groups):
@@ -1098,18 +1117,18 @@
     hops(tiles + 1)
     grad_ref[:, :head] = acc[...].astype(BF16)
     grad_ref[:, head:] = go_ref[...]
-    for t in range(tiles):
+    for t in range(tiles * per):
         line.arrived(t)
         keep(t).start()
-    all_chips(groups - 1)
     for g in range(groups):
         for half in range(2):
-            for k in others:
-                between(g, half, k).wait_send()
+            if g < groups - 1:
+                for k in others:
+                    between(g, half, k).wait_send()
             for k in order:
                 within(g, half, k).wait_send()
-    line.finish(tiles)
-    for t in range(tiles):
+    line.finish(tiles * per)
+    for t in range(tiles * per):
         keep(t).wait()
 
 
@@ -1119,7 +1138,7 @@
     groups, length, _ = kv.shape
     size = rows // (2 * groups)
     chips = length // (4 * size)
-    tiles = 2 * groups
+    parts = rows // min(256, size)
     vmem = pl.BlockSpec(memory_space=pltpu.VMEM)
     dma = pltpu.SemaphoreType.DMA
     return pl.pallas_call(
@@ -1127,11 +1146,12 @@
         out_shape=(
             jax.ShapeDtypeStruct((rows, 4 * head), BF16),
             jax.ShapeDtypeStruct((rows, 2 * head), BF16),
+            jax.ShapeDtypeStruct((2, chips - 1, size, 2 * head), BF16),
             jax.ShapeDtypeStruct((1, head), F32),
             jax.ShapeDtypeStruct((width, 2 * head), BF16),
         ),
         in_specs=[vmem] * 14 + [ANY],
-        out_specs=(ANY, vmem, vmem, vmem),
+        out_specs=(ANY, vmem, vmem, vmem, vmem),
         scratch_shapes=[
             pltpu.VMEM((groups, length, 2 * head), BF16),
             pltpu.VMEM((length, head), F32), pltpu.VMEM((length, head), F32),
@@ -1141,7 +1161,7 @@
             pltpu.VMEM((groups, 2, chips - 1, size, 2 * head), BF16),
             pltpu.VMEM((rows, 4 * head), BF16),
             pltpu.VMEM((width, head), F32),
-            dma((groups,)), dma((tiles,))] + [dma((groups, 2, chips))] * 4 + [dma((3, tiles))] * 4,
+            dma((groups,)), dma((parts,))] + [dma((groups, 2, chips))] * 4 + [dma((3, parts))] * 4,
         compiler_params=pltpu.CompilerParams(
             collective_id=ident, has_side_effects=True, vmem_limit_bytes=63 * 2**20),
         cost_estimate=cost(80),
@@ -1197,15 +1217,22 @@
 
 
 def key_back_kernel(tiles, tile, chunk, own_rows, scattered, dkv_ref, hat_ref, inv_ref, cos_ref, sin_ref, x_ref, dm_ref, dq_ref,
-                    gain_ref, gk_ref, w_ref, wq_ref, dgq_ref, dg_mid_ref, dg_post_ref, qo_ref,
+                    gain_ref, gk_ref, w_ref, wq_ref, dgq_ref, dg_mid_ref, dg_post_ref, qo_ref, rest_ref,
                     dx_ref, last_out, qo_out, acc, acc_in, acc_key, w_kv, w_sem, last_ref, part,
-                    out, own, near, far, *sems):
+                    add, ss, rs, out, own, near, far, *sems):
     i = pl.program_id(0)
     head = hat_ref.shape[1]
     per = tile // chunk
     count = tiles * per + 1
     line = ResidentSum(count, chunk, count, own, near, far, out, sems[:9])
     group = Shared(True)
+    ring = Shared(False)
+    size = rest_ref.shape[2]
+    first = tiles * per - 2 * size // chunk
+
+    def between(half, k):
+        return ring.copy(rest_ref.at[half, k - 1], add.at[half, k - 1], ss.at[half, k], rs.at[half, k], ring.other(k))
+
     if scattered:
         early = RowScatter(group, own_rows, qo_ref, *sems[9:12], sems[12:16])
         late = RowScatter(group, own_rows, last_ref, *sems[16:19], sems[19:23])
@@ -1216,10 +1243,14 @@
         copy.start()
         if scattered:
             group.greet(line.z)
+        else:
+            ring.greet(line.z)
+            qo_out[...] = qo_ref[...]
+        for half in range(2):
+            for k in range(1, ring.chips):
+                between(half, k).start()
+        if scattered:
             early.send()
-        else:
-            barrier_line(line.z)
-            qo_out[...] = qo_ref[...]
         for ref in (acc, acc_in, acc_key):
             ref[...] = jnp.zeros_like(ref)
         copy.wait()
@@ -1229,7 +1260,27 @@
     @pl.when(i < tiles)
     def _():
         for j in range(per):
-            line.put(i * per + j, dkv_ref[j * chunk : (j + 1) * chunk, :])
+            c = i * per + j
+            mine = dkv_ref[j * chunk : (j + 1) * chunk, :]
+
+            @pl.when(c < first)
+            def _():
+                line.put(c, mine)
+
+            @pl.when(c >= first)
+            def _():
+                half = lax.div((c - first) * chunk, size)
+                at = lax.rem((c - first) * chunk, size)
+
+                @pl.when(at == 0)
+                def _():
+                    for k in range(1, ring.chips):
+                        between(half, k).wait_recv()
+
+                total = mine.astype(F32)
+                for k in range(1, ring.chips):
+                    total = total + add[half, k - 1, pl.ds(pl.multiple_of(at, chunk), chunk), :].astype(F32)
+                line.put(c, total.astype(BF16))
         part[pl.ds(pl.multiple_of(i * tile, tile), tile), :] = dot(dq_ref[...], wq_ref[...], NT)
 
     @pl.when((i >= 1) & (i <= tiles))
@@ -1276,6 +1327,9 @@
 
     @pl.when(i == tiles + 2)
     def _():
+        for half in range(2):
+            for k in range(1, ring.chips):
+                between(half, k).wait_send()
         line.arrived(count - 1)
         width = x_ref.shape[1]
         short = head * own_rows // width
@@ -1301,10 +1355,10 @@
 
 
 def key_back(d_kv, hat, inv, cosine, sine, x, d_middle, d_query, gains, gain_key, first, w_query, dg_query, dg_mid, dg_post,
-             grad_qo, own_rows, ident):
+             grad_qo, rest, own_rows, ident):
     rows, width = x.shape
     head = hat.shape[1]
-    tile, chunk = 256, 128
+    tile, chunk = 128, 128
     tiles = rows // tile
     count = rows // chunk + 1
     dma = pltpu.SemaphoreType.DMA((count,))
@@ -1340,18 +1394,19 @@
                   late(head), late(1), turn, turn, late(width), late(width),
                   pl.BlockSpec((tile, 4 * head), lambda i: (jnp.minimum(i, tiles - 1), 0)),
                   whole_block(gains.shape), whole_block(gain_key.shape), ANY]
-        + [whole_block(a.shape) for a in (w_query, dg_query, dg_mid, dg_post, grad_qo)],
+        + [whole_block(a.shape) for a in (w_query, dg_query, dg_mid, dg_post, grad_qo, rest)],
         out_specs=(late(width), fixed(last_out), fixed(qo_out)),
         scratch_shapes=[
             pltpu.VMEM((width, 2 * head), F32), pltpu.VMEM((1, width), F32), pltpu.VMEM((1, head), F32),
             pltpu.VMEM((width, 2 * head), BF16), pltpu.SemaphoreType.DMA, pltpu.VMEM(last, BF16),
-            pltpu.VMEM((rows, width), F32)] + [comm] * 4 + [dma] * 7
+            pltpu.VMEM((rows, width), F32), pltpu.VMEM(rest.shape, BF16)]
+        + [pltpu.SemaphoreType.DMA((2, rest.shape[1] + 1))] * 2 + [comm] * 4 + [dma] * 7
         + [pltpu.SemaphoreType.REGULAR] * 2 + more,
         compiler_params=pltpu.CompilerParams(
             collective_id=ident, has_side_effects=True, vmem_limit_bytes=56 * 2**20),
         cost_estimate=cost(75),
         name="key_back",
-    )(d_kv, hat, inv, cosine, sine, x, d_middle, d_query, gains, gain_key, first, w_query, dg_query, dg_mid, dg_post, grad_qo)
+    )(d_kv, hat, inv, cosine, sine, x, d_middle, d_query, gains, gain_key, first, w_query, dg_query, dg_mid, dg_post, grad_qo, rest)
 
 
 def shards(tokens, segments, cotangent, w_query, w_key, w_value, w_out, w_gate, w_up, w_down,
@@ -1417,12 +1472,12 @@
     output, d_middle, d_heads, delta, d_gain_mid, grad_out_t = middle_back(
         x_rows, attn, dy_rows, d_two, ffn_out, heads_own, gain_rows, weights)
 
-    d_q_all, d_kv, d_gain_query, grad_qo = attention_back(
+    d_q_all, d_kv, rest, d_gain_query, grad_qo = attention_back(
         queries, d_heads, log_mass, delta, own_ids[:, :, None, :], ids, q_hat, q_scale, cosine, sine, x_rows, gain_rows,
         gain_query[None], grad_out_t, kv, 4)
     d_tokens, last, grad_qo = key_back(
         d_kv, k_hat, k_scale, cosine, sine, x_rows, d_middle, d_q_all, gain_rows, gain_key[None],
-        first, query_full, d_gain_query, d_gain_mid, d_gain_post_ffn, grad_qo, own_rows, 3)
+        first, query_full, d_gain_query, d_gain_mid, d_gain_post_ffn, grad_qo, rest, own_rows, 3)
     grad_ffn = grad_ffn.astype(F32)
     if own_rows % 16:
         last = lax.psum_scatter(last, shared, scatter_dimension=0, tiled=True).astype(F32)

time: 687 us -> 676 us (0.984)
  Pallas kernels: 626 us -> 615 us
    pallas_call x1, Pallas kernels: 102 us -> 86.7 us  [attention_back(): pl.pallas_call(functools.partial(attention_back_kernel, groups, size), ou...]
    pallas_call x1, Pallas kernels: 83.2 us -> 96 us  [key_back(): pl.pallas_call(functools.partial(key_back_kernel, tiles, tile, chunk, own...]
    pallas_call x1, Pallas kernels: 125 us -> 117 us  [attention(): pl.pallas_call(functools.partial(attention_kernel, groups, size), out_sha...]
where the time goes in v10:
time: 676 us; the launch traced here: 668 us
  Pallas kernels  615 us (91%)
  local copies, waits for them, and re-layouts  29 us (4%)
  between operations  14.4 us (2%)
  other arithmetic  9.79 us (1%)
    pallas_call x1, Pallas kernels, ffn_backward(): pl.pallas_call(functools.partial(ffn_backward_kernel, tiles, tile, chunk,...  144 us
    pallas_call x1, Pallas kernels, ffn_forward(): pl.pallas_call(functools.partial(ffn_forward_kernel, tiles, tile, chunk,...  129 us
    pallas_call x1, Pallas kernels, attention(): pl.pallas_call(functools.partial(attention_kernel, groups, size), out_sha...  117 us
    pallas_call x1, Pallas kernels, key_back(): pl.pallas_call(functools.partial(key_back_kernel, tiles, tile, chunk, own...  96 us
    pallas_call x1, Pallas kernels, attention_back(): pl.pallas_call(functools.partial(attention_back_kernel, groups, size), ou...  86.7 us
    pallas_call x1, Pallas kernels, middle_back(): pl.pallas_call(middle_back_kernel, grid=(rows // tile,), out_shape=(jax.S...  23 us
    pallas_call x1, Pallas kernels, first_gather(): pl.pallas_call(first_gather_kernel, out_shape=(jax.ShapeDtypeStruct((devi...  20.2 us
  transfers between devices with their start and end apart: 3, of which 0 were waited for; matrix products, arithmetic and copies ran while one was open for 2% of the time, Pallas kernels for 68%

profile of v10, /device:TPU:0, one launch (start us, length us, event | category | flops | bytes accessed | tf_op | source)
XLA Modules:
  0.0 668.3 jit_solution(11508751012331242094)
XLA Ops:
  11.4 1.3 reshape_reshape.3.i_ref
  12.7 1.7 fusion.9.a_ref
  14.3 20.2 %first_gather.1 = (bf16[8,144,896]{2,1,0:T(8,128)(2,1)}, bf16[144,1024]{1,0:T(8,128)(2,1)}, bf16[144,1024]{1,0:T(8,128)(2,1)}, s32[8,16,128]{2,1,0:T(8,128)}) custom-call(bf16[144,896]{1,0:T(8,128)(2,1)} %fusion.9.a_ref, bf16[144,256]{1,0:T(8,128)(2,1)} %b_ref.1, bf16[144,256]{1,0:T(8,128)(2,1)} %bitcast.37, s32[16,128]{1,0:T(8,128)} %reshape_reshape.3.i_ref), custom_call_target="tpu_custom_call" | custom-call | flops 22000001024 | tf_op jit(solution)/shard_map/first_gather/pallas_call | solution.py:719
  34.6 2.2 fusion.6
  36.9 1.0 slice_convert_fusion
  38.0 0.8 copy.55.gain_ref
  41.0 1.3 copy.56.qs_ref
  42.3 3.1 multiply_sine_fusion
  45.4 117.0 %attention.1 = (bf16[2048,256]{1,0:T(8,128)(2,1)}, f32[2048,256]{1,0:T(8,128)}, f32[2048,1]{1,0:T(8,128)}, f32[2048,256]{1,0:T(8,128)}, f32[2048,1]{1,0:T(8,128)...) custom-call(bf16[2048,1152]{1,0:T(8,128)(2,1)} %bitcast.32, ...), custom_call_target="tpu_custom_call" | custom-call | flops 121000001536 | tf_op jit(solution)/shard_map/attention/pallas_call | solution.py:918
  163.0 128.6 %ffn_forward.1 = (bf16[2048,1152]{1,0:T(8,128)(2,1)}, bf16[2048,1152]{1,0:T(8,128)(2,1)}, bf16[2048,1728]{1,0:T(8,128)(2,1)}, bf16[2048,1728]{1,0:T(8,128)(2,1)}, bf16[2048,1152]{1,0:T(8,128)(2,1)}) custom-call(bf16[2048,1152]{1,0:T(8,128)(2,1)} %bitcast.33, bf16[2048,1024]{1,0:T(8,128)(2,1)} %get-tuple-element.58.h_ref, f32[8,1152]{1,0:T(8,128)} %copy.55.gain_ref, ...), custom_call_target="tpu_custom_call" | custom-call | flops 153999998976 | tf_op jit(solution)/shard_map/ffn_forward/pallas_call | solution.py:304
  291.7 143.5 %ffn_backward.1 = (f32[1,1152]{1,0:T(1,128)}, bf16[3,1152,1728]{2,1,0:T(8,128)(2,1)}, bf16[2048,1152]{1,0:T(8,128)(2,1)}) custom-call(bf16[2048,1152]{1,0:T(8,128)(2,1)} %bitcast.30, bf16[2048,1152]{1,0:T(8,128)(2,1)} %get-tuple-element.63.ffn_ref, bf16[2048,1152]{1,0:T(8,128)(2,1)} %get-tuple-element.64.two_ref, ...), custom_call_target="tpu_custom_call" | custom-call | flops 159499993088 | tf_op jit(solution)/shard_map/ffn_backward/pallas_call | solution.py:435
  436.4 23.0 %middle_back.1 = (bf16[2048,1152]{1,0:T(8,128)(2,1)}, f32[2048,1152]{1,0:T(8,128)}, bf16[2048,256]{1,0:T(8,128)(2,1)S(1)}, f32[2048,1]{1,0:T(8,128)S(1)}, f32[2,...) custom-call(bf16[2048,1152]{1,0:T(8,128)(2,1)} %bitcast.34, bf16[2048,1152]{1,0:T(8,128)(2,1)} %get-tuple-element.60.attn_ref, ...), custom_call_target="tpu_custom_call" | custom-call | flops 20899999744 | tf_op jit(solution)/shard_map/middle_back/pallas_call | solution.py:496
  459.4 1.0 copy-done.2
  460.4 1.0 copy-done.3
  462.7 86.7 %attention_back.1 = (bf16[2048,1024]{1,0:T(8,128)(2,1)}, bf16[2048,512]{1,0:T(8,128)(2,1)}, bf16[2,1,512,512]{3,2,1,0:T(8,128)(2,1)}, f32[1,256]{1,0:T(1,128)}, bf16[1152,512]{1,0:T(8,128)(2,1)}) custom-call(bf16[2048,256]{1,0:T(8,128)(2,1)} %get-tuple-element.70.q_ref, bf16[2048,256]{1,0:T(8,128)(2,1)} %copy-done.2, ...), custom_call_target="tpu_custom_call" | custom-call | flops 88000004096 | tf_op jit(solution)/shard_map/attention_back/pallas_call | solution.py:1144
  549.4 96.0 %key_back.1 = (f32[2048,1152]{1,0:T(8,128)}, f32[144,640]{1,0:T(8,128)}, f32[144,512]{1,0:T(8,128)}) custom-call(bf16[2048,512]{1,0:T(8,128)(2,1)} %get-tuple-element.78.dkv_ref, f32[2048,256]{1,0:T(8,128)} %get-tuple-element.79.hat_ref, f32[2048,1]{1,0:T(8,128)} %get-tuple-element.80.inv_ref, f32[1024,128]{1,0:T(8,128)} %get-tuple-element.156.cos_ref, ...), custom_call_target="tpu_custom_call" | custom-call | flops 82500001792 | tf_op jit(solution)/shard_map/key_back/pallas_call | solution.py:1385
  645.4 1.5 slice_reduce_fusion.6
  646.9 2.0 slice_reduce_fusion.2
  648.9 1.7 fusion.11
  650.6 1.7 slice_bitcast_fusion.3
  652.3 1.8 convert_element_type.24
  654.1 1.7 slice_bitcast_fusion
  655.8 1.8 copy-done.6
  657.6 3.7 copy.65
  (49 shorter events, 9.7 us)
Async XLA Ops:
  7.2 155.9 %all-gather.3.cloned.1.call-start = ((), (), s32[]{:S(2)}) async-start(), calls=%async_computation.1 | async-start | bytes 16588800 | tf_op jit(solution)/shard_map/all_gather | solution.py:1454
  14.3 20.3 %copy-start.7 = (bf16[1728,144]{0,1:T(8,128)(2,1)S(1)}, bf16[1728,144]{0,1:T(8,128)(2,1)}, u32[]{:S(2)}) copy-start(bf16[1728,144]{0,1:T(8,128)(2,1)} %param.25) | copy-start | bytes 1492996
  14.3 20.3 %copy-start.8 = (bf16[144,1728]{1,0:T(8,128)(2,1)S(1)}, bf16[144,1728]{1,0:T(8,128)(2,1)}, u32[]{:S(2)}) copy-start(bf16[144,1728]{1,0:T(8,128)(2,1)} %param.24) | copy-start | bytes 1492996
  14.3 20.3 %copy-start.9 = (bf16[144,1728]{1,0:T(8,128)(2,1)S(1)}, bf16[144,1728]{1,0:T(8,128)(2,1)}, u32[]{:S(2)}) copy-start(bf16[144,1728]{1,0:T(8,128)(2,1)} %param.23) | copy-start | bytes 1492996
  34.6 6.3 copy-start.10
  36.9 254.8 %all-gather.5.cloned.1.call-start = ((), (), s32[]{:S(2)}) async-start(), calls=%async_computation.2 | async-start | bytes 2654208 | tf_op jit(solution)/shard_map/all_gather | solution.py:1466
  162.4 489.9 %reduce-scatter.2.cloned.1.call-start = ((), (), s32[]{:S(2)}) async-start(), calls=%async_computation.3 | async-start | bytes 13934592 | tf_op jit(solution)/shard_map/reduce_scatter | solution.py:1471
  435.2 0.8 copy-start
  435.2 1.2 copy-start.1
  459.4 1.0 copy-start.2
  460.4 1.0 copy-start.3
  461.3 0.8 copy-start.4
  462.2 0.6 copy-start.5
  652.3 5.3 copy-start.6
Sparse Core Ops, SparseCore 0:
  37.0 94.7 all-gather.2
  162.5 27.5 all-gather.4
  435.3 105.9 reduce-scatter.1

commit v11 on v10

--- a/solution.py
+++ b/solution.py
@@ -229,15 +229,15 @@
     line = LineSum(tiles * per, chunk, tiles * per, own, near, far, out_ref, sems)
     head = wo_ref.shape[1] // 4
 
+    copies = [pltpu.make_async_copy(w_ref.at[:, pl.ds(0, 4 * head)], wo_ref, w_sem.at[3])]
+    copies += load_ffn_weights(w_ref, (wg_ref, wu_ref, wd_ref), w_sem)
+
     @pl.when(i == 0)
     def _():
-        copies = load_ffn_weights(w_ref, (wg_ref, wu_ref, wd_ref), w_sem)
-        copies.append(pltpu.make_async_copy(w_ref.at[:, pl.ds(0, 4 * head)], wo_ref, w_sem.at[3]))
         for copy in copies:
             copy.start()
         barrier_line(line.z)
-        for copy in copies:
-            copy.wait()
+        copies[0].wait()
 
     attn = dot(h_ref[...], wo_ref[...], NT).astype(BF16)
     attn_ref[...] = attn
@@ -246,6 +246,12 @@
     two = (hat * (1.0 + gain_ref[2:3, :])).astype(BF16)
     two_ref[...] = two
     part = None
+
+    @pl.when(i == 0)
+    def _():
+        for copy in copies[1:]:
+            copy.wait()
+
     for a, b in column_parts(hidden):
         gate = dot(two, wg_ref[:, a:b])
         up = dot(two, wu_ref[:, a:b])
@@ -337,15 +343,15 @@
     last = tiles * per
     line = LineSum(last, chunk, slots, own, near, far, out_ref, sems)
 
+    copies = load_ffn_weights(w_ref, (wg_ref, wu_ref, wd_ref), w_sem)
+
     @pl.when(i == 0)
     def _():
-        copies = load_ffn_weights(w_ref, (wg_ref, wu_ref, wd_ref), w_sem)
-        for copy in copies:
+        for copy in copies[::-1]:
             copy.start()
         barrier_line(line.z)
-        for acc in (acc_g, acc_u, acc_d, dgain_ref):
-            acc[...] = jnp.zeros_like(acc)
-        for copy in copies:
+        dgain_ref[...] = jnp.zeros_like(dgain_ref)
+        for copy in copies[::-1]:
             copy.wait()
 
     hat, inv = norm_parts(ffn_ref[...].astype(F32))
@@ -372,6 +378,11 @@
     def _():
         for j in range(per):
             line.pair((i - 1) * per + j)
+
+    @pl.when(i == 0)
+    def _():
+        for acc in (acc_g, acc_u, acc_d):
+            acc[...] = jnp.zeros_like(acc)
 
     acc_g[...] += dot(two_ref[...], keep_g[...], TN)
     acc_u[...] += dot(two_ref[...], keep_u[...], TN)
@@ -474,7 +485,7 @@
     d_part, d_gain = norm_back(d2_ref[...].astype(F32), hat, inv, gain_ref[2:3, :])
     dgain_ref[1:2, :] += d_gain[None]
     d_middle = dy_ref[...].astype(F32) + d_part
-    dm_ref[...] = d_middle
+    dm_ref[...] = d_middle.astype(BF16)
     d_attn, d_gain = norm_back(d_middle, attn_hat, attn_inv, gain_ref[1:2, :])
     dgain_ref[0:1, :] += d_gain[None]
     d_attn = d_attn.astype(BF16)
@@ -498,7 +509,7 @@
         grid=(rows // tile,),
         out_shape=(
             jax.ShapeDtypeStruct((rows, width), BF16),
-            jax.ShapeDtypeStruct((rows, width), F32),
+            jax.ShapeDtypeStruct((rows, width), BF16),
             jax.ShapeDtypeStruct((rows, head), BF16),
             jax.ShapeDtypeStruct((rows, 1), F32),
             jax.ShapeDtypeStruct((2, width), F32),
@@ -1216,7 +1227,7 @@
     return [pltpu.VMEM((chips, own_rows, cols), BF16)] * 3 + [pltpu.SemaphoreType.DMA((chips,))] * 4
 
 
-def key_back_kernel(tiles, tile, chunk, own_rows, scattered, dkv_ref, hat_ref, inv_ref, cos_ref, sin_ref, x_ref, dm_ref, dq_ref,
+def key_back_kernel(tiles, tile, chunk, own_rows, scattered, dkv_ref, hat_ref, inv_ref, cos_ref, sin_ref, x_ref, dq_ref,
                     gain_ref, gk_ref, w_ref, wq_ref, dgq_ref, dg_mid_ref, dg_post_ref, qo_ref, rest_ref,
                     dx_ref, last_out, qo_out, acc, acc_in, acc_key, w_kv, w_sem, last_ref, part,
                     add, ss, rs, out, own, near, far, *sems):
@@ -1257,75 +1268,80 @@
         line.put(count - 1, jnp.broadcast_to(
             jnp.concatenate([dgq_ref[...], dgq_ref[...]], axis=1).astype(BF16), (chunk, 2 * head)))
 
+    def put_rows(c):
+        return dkv_ref[pl.ds(pl.multiple_of(c * chunk, chunk), chunk), :]
+
+    @pl.when(i == 0)
+    def _():
+        def ready(c, _):
+            line.put(c, put_rows(c))
+            return 0
+
+        lax.fori_loop(0, first, ready, 0)
+
+    for half in range(2):
+        @pl.when(i == max(0, (first * chunk + half * size) // tile - 2))
+        def _():
+            for k in range(1, ring.chips):
+                between(half, k).wait_recv()
+
+            def ready(n, _):
+                c = first + half * (size // chunk) + n
+                total = put_rows(c).astype(F32)
+                for k in range(1, ring.chips):
+                    total = total + add[half, k - 1, pl.ds(pl.multiple_of(n * chunk, chunk), chunk), :].astype(F32)
+                line.put(c, total.astype(BF16))
+                return 0
+
+            lax.fori_loop(0, size // chunk, ready, 0)
+
     @pl.when(i < tiles)
     def _():
+        part[pl.ds(pl.multiple_of(i * tile, tile), tile), :] = dot(dq_ref[...], wq_ref[...], NT)
+
+    @pl.when((i >= 1) & (i <= tiles))
+    def _():
         for j in range(per):
-            c = i * per + j
-            mine = dkv_ref[j * chunk : (j + 1) * chunk, :]
-
-            @pl.when(c < first)
-            def _():
-                line.put(c, mine)
-
-            @pl.when(c >= first)
-            def _():
-                half = lax.div((c - first) * chunk, size)
-                at = lax.rem((c - first) * chunk, size)
-
-                @pl.when(at == 0)
-                def _():
-                    for k in range(1, ring.chips):
-                        between(half, k).wait_recv()
-
-                total = mine.astype(F32)
-                for k in range(1, ring.chips):
-                    total = total + add[half, k - 1, pl.ds(pl.multiple_of(at, chunk), chunk), :].astype(F32)
-                line.put(c, total.astype(BF16))
-        part[pl.ds(pl.multiple_of(i * tile, tile), tile), :] = dot(dq_ref[...], wq_ref[...], NT)
-
-    @pl.when((i >= 1) & (i <= tiles))
+            line.total((i - 1) * per + j)
+
+    @pl.when(i < tiles)
     def _():
         for j in range(per):
-            line.pair((i - 1) * per + j)
-
-    @pl.when((i >= 2) & (i <= tiles + 1))
-    def _():
-        for j in range(per):
-            line.total((i - 2) * per + j)
+            line.pair(i * per + j)
 
     @pl.when(i == 1)
     def _():
         line.pair(count - 1)
-
-    @pl.when(i == 2)
-    def _():
-        line.total(count - 1)
         if scattered:
             early.middle(qo_out)
+
+    @pl.when(i == 2)
+    def _():
+        line.total(count - 1)
 
     if scattered:
         @pl.when(i == tiles)
         def _():
             early.final(qo_out)
 
-    @pl.when(i >= 3)
+    @pl.when(i >= 2)
     def _():
         for j in range(per):
-            line.arrived((i - 3) * per + j)
-        d_kv = out[pl.ds(pl.multiple_of((i - 3) * tile, tile), tile), :]
+            line.arrived((i - 2) * per + j)
+        d_kv = out[pl.ds(pl.multiple_of((i - 2) * tile, tile), tile), :]
         d_rot = rotate(d_kv[:, :head].astype(F32), cos_ref[...], -sin_ref[...])
         d_raw, d_gain = norm_back(d_rot, hat_ref[...], inv_ref[...], gk_ref[...])
         acc_key[...] += d_gain[None]
         d_raw = jnp.concatenate([d_raw.astype(BF16), d_kv[:, head:]], axis=1)
-        d_one = part[pl.ds(pl.multiple_of((i - 3) * tile, tile), tile), :] + dot(d_raw, w_kv[...], NT)
+        d_one = part[pl.ds(pl.multiple_of((i - 2) * tile, tile), tile), :] + dot(d_raw, w_kv[...], NT)
         hat, inv = norm_parts(x_ref[...].astype(F32))
         gain = gain_ref[0:1, :]
         d_part, d_gain = norm_back(d_one, hat, inv, gain)
         acc_in[...] += d_gain[None]
-        dx_ref[...] = dm_ref[...] + d_part
+        dx_ref[...] = d_part.astype(BF16)
         acc[...] += dot((hat * (1.0 + gain)).astype(BF16), d_raw, TN)
 
-    @pl.when(i == tiles + 2)
+    @pl.when(i == tiles + 1)
     def _():
         for half in range(2):
             for k in range(1, ring.chips):
@@ -1354,23 +1370,23 @@
             line.finish()
 
 
-def key_back(d_kv, hat, inv, cosine, sine, x, d_middle, d_query, gains, gain_key, first, w_query, dg_query, dg_mid, dg_post,
+def key_back(d_kv, hat, inv, cosine, sine, x, d_query, gains, gain_key, first, w_query, dg_query, dg_mid, dg_post,
              grad_qo, rest, own_rows, ident):
     rows, width = x.shape
     head = hat.shape[1]
-    tile, chunk = 128, 128
+    tile, chunk = 256, 128
     tiles = rows // tile
     count = rows // chunk + 1
     dma = pltpu.SemaphoreType.DMA((count,))
 
     def late(cols):
-        return pl.BlockSpec((tile, cols), lambda i: (jnp.maximum(i - 3, 0), 0))
+        return pl.BlockSpec((tile, cols), lambda i: (jnp.maximum(i - 2, 0), 0))
 
     def fixed(shape):
         return pl.BlockSpec(shape, lambda i: (0, 0))
 
     turns = cosine.shape[0] // tile
-    turn = pl.BlockSpec((tile, head // 2), lambda i: (lax.rem(jnp.maximum(i - 3, 0), turns), 0))
+    turn = pl.BlockSpec((tile, head // 2), lambda i: (lax.rem(jnp.maximum(i - 2, 0), turns), 0))
     comm = pltpu.VMEM((count * chunk, 2 * head), BF16)
     scattered = own_rows % 16 == 0
     chips = width // (2 * own_rows)
@@ -1384,14 +1400,14 @@
         last_out, qo_out, kind = last, grad_qo.shape, BF16
     return pl.pallas_call(
         functools.partial(key_back_kernel, tiles, tile, chunk, own_rows, scattered),
-        grid=(tiles + 3,),
+        grid=(tiles + 2,),
         out_shape=(
-            jax.ShapeDtypeStruct((rows, width), F32),
+            jax.ShapeDtypeStruct((rows, width), BF16),
             jax.ShapeDtypeStruct(last_out, kind),
             jax.ShapeDtypeStruct(qo_out, kind),
         ),
-        in_specs=[pl.BlockSpec((tile, 2 * head), lambda i: (jnp.minimum(i, tiles - 1), 0)),
-                  late(head), late(1), turn, turn, late(width), late(width),
+        in_specs=[whole_block(d_kv.shape),
+                  late(head), late(1), turn, turn, late(width),
                   pl.BlockSpec((tile, 4 * head), lambda i: (jnp.minimum(i, tiles - 1), 0)),
                   whole_block(gains.shape), whole_block(gain_key.shape), ANY]
         + [whole_block(a.shape) for a in (w_query, dg_query, dg_mid, dg_post, grad_qo, rest)],
@@ -1406,7 +1422,7 @@
             collective_id=ident, has_side_effects=True, vmem_limit_bytes=56 * 2**20),
         cost_estimate=cost(75),
         name="key_back",
-    )(d_kv, hat, inv, cosine, sine, x, d_middle, d_query, gains, gain_key, first, w_query, dg_query, dg_mid, dg_post, grad_qo, rest)
+    )(d_kv, hat, inv, cosine, sine, x, d_query, gains, gain_key, first, w_query, dg_query, dg_mid, dg_post, grad_qo, rest)
 
 
 def shards(tokens, segments, cotangent, w_query, w_key, w_value, w_out, w_gate, w_up, w_down,
@@ -1475,10 +1491,10 @@
     d_q_all, d_kv, rest, d_gain_query, grad_qo = attention_back(
         queries, d_heads, log_mass, delta, own_ids[:, :, None, :], ids, q_hat, q_scale, cosine, sine, x_rows, gain_rows,
         gain_query[None], grad_out_t, kv, 4)
-    d_tokens, last, grad_qo = key_back(
-        d_kv, k_hat, k_scale, cosine, sine, x_rows, d_middle, d_q_all, gain_rows, gain_key[None],
+    d_part, last, grad_qo = key_back(
+        d_kv, k_hat, k_scale, cosine, sine, x_rows, d_q_all, gain_rows, gain_key[None],
         first, query_full, d_gain_query, d_gain_mid, d_gain_post_ffn, grad_qo, rest, own_rows, 3)
-    grad_ffn = grad_ffn.astype(F32)
+    d_tokens = d_middle.astype(F32) + d_part.astype(F32)
     if own_rows % 16:
         last = lax.psum_scatter(last, shared, scatter_dimension=0, tiled=True).astype(F32)
         grad_qo = lax.psum_scatter(grad_qo, shared, scatter_dimension=0, tiled=True).astype(F32)
@@ -1490,9 +1506,9 @@
         last[:, :head],
         last[:, head : 2 * head],
         grad_qo[:, head:].T,
-        grad_ffn[0],
-        grad_ffn[1],
-        grad_ffn[2].T,
+        grad_ffn[0].astype(F32),
+        grad_ffn[1].astype(F32),
+        grad_ffn[2].astype(F32).T,
         g[:, 0],
         g[:, 1],
         g[:, 2],

time: 676 us -> 670 us (level)
  other arithmetic: 9.79 us -> 18.1 us
  Pallas kernels: 615 us -> 607 us
  local copies, waits for them, and re-layouts: 29 us -> 22 us
    add x0 -> x1, other arithmetic: none -> 6.99 us  [shards(): d_tokens = d_middle.astype(F32) + d_part.astype(F32)]
  transfers between devices with their start and end apart: 3 -> 3, of which waited for: 0 -> 0; matrix products, arithmetic and copies ran while one was open for 2% -> 3% of each run, Pallas kernels for 68% -> 67%
where the time goes in v11:
time: 670 us; the launch traced here: 661 us
  Pallas kernels  607 us (91%)
  local copies, waits for them, and re-layouts  22 us (3%)
  other arithmetic  18.1 us (3%)
  between operations  14.1 us (2%)
    pallas_call x1, Pallas kernels, ffn_backward(): pl.pallas_call(functools.partial(ffn_backward_kernel, tiles, tile, chunk,...  144 us
    pallas_call x1, Pallas kernels, ffn_forward(): pl.pallas_call(functools.partial(ffn_forward_kernel, tiles, tile, chunk,...  127 us
    pallas_call x1, Pallas kernels, attention(): pl.pallas_call(functools.partial(attention_kernel, groups, size), out_sha...  117 us
    pallas_call x1, Pallas kernels, key_back(): pl.pallas_call(functools.partial(key_back_kernel, tiles, tile, chunk, own...  89.6 us
    pallas_call x1, Pallas kernels, attention_back(): pl.pallas_call(functools.partial(attention_back_kernel, groups, size), ou...  85.9 us
    pallas_call x1, Pallas kernels, middle_back(): pl.pallas_call(middle_back_kernel, grid=(rows // tile,), out_shape=(jax.S...  22 us
    pallas_call x1, Pallas kernels, first_gather(): pl.pallas_call(first_gather_kernel, out_shape=(jax.ShapeDtypeStruct((devi...  20.2 us
  transfers between devices with their start and end apart: 3, of which 0 were waited for; matrix products, arithmetic and copies ran while one was open for 3% of the time, Pallas kernels for 67%

profile of v11, /device:TPU:0, one launch (start us, length us, event | category | flops | bytes accessed | tf_op | source)
XLA Modules:
  0.0 660.9 jit_solution(10849347932511092637)
XLA Ops:
  11.4 1.3 reshape_reshape.3.i_ref
  12.7 1.7 fusion.11.a_ref
  14.3 20.2 %first_gather.1 = (bf16[8,144,896]{2,1,0:T(8,128)(2,1)}, bf16[144,1024]{1,0:T(8,128)(2,1)}, bf16[144,1024]{1,0:T(8,128)(2,1)}, s32[8,16,128]{2,1,0:T(8,128)}) custom-call(bf16[144,896]{1,0:T(8,128)(2,1)} %fusion.11.a_ref, bf16[144,256]{1,0:T(8,128)(2,1)} %b_ref.1, bf16[144,256]{1,0:T(8,128)(2,1)} %bitcast.48, s32[16,128]{1,0:T(8,128)} %reshape_reshape.3.i_ref), custom_call_target="tpu_custom_call" | custom-call | flops 22000001024 | tf_op jit(solution)/shard_map/first_gather/pallas_call | solution.py:730
  34.6 2.2 fusion.6
  36.9 1.0 slice_convert_fusion
  38.0 0.8 copy.55.gain_ref
  41.0 1.3 copy.56.qs_ref
  42.3 3.1 multiply_sine_fusion
  45.4 117.0 %attention.1 = (bf16[2048,256]{1,0:T(8,128)(2,1)}, f32[2048,256]{1,0:T(8,128)}, f32[2048,1]{1,0:T(8,128)}, f32[2048,256]{1,0:T(8,128)}, f32[2048,1]{1,0:T(8,128)...) custom-call(bf16[2048,1152]{1,0:T(8,128)(2,1)} %bitcast.43, ...), custom_call_target="tpu_custom_call" | custom-call | flops 121000001536 | tf_op jit(solution)/shard_map/attention/pallas_call | solution.py:929
  163.1 127.3 %ffn_forward.1 = (bf16[2048,1152]{1,0:T(8,128)(2,1)}, bf16[2048,1152]{1,0:T(8,128)(2,1)}, bf16[2048,1728]{1,0:T(8,128)(2,1)}, bf16[2048,1728]{1,0:T(8,128)(2,1)}, bf16[2048,1152]{1,0:T(8,128)(2,1)}) custom-call(bf16[2048,1152]{1,0:T(8,128)(2,1)} %bitcast.44, bf16[2048,1024]{1,0:T(8,128)(2,1)} %get-tuple-element.58.h_ref, f32[8,1152]{1,0:T(8,128)} %copy.55.gain_ref, ...), custom_call_target="tpu_custom_call" | custom-call | flops 153999998976 | tf_op jit(solution)/shard_map/ffn_forward/pallas_call | solution.py:310
  290.4 144.4 %ffn_backward.1 = (f32[1,1152]{1,0:T(1,128)}, bf16[3,1152,1728]{2,1,0:T(8,128)(2,1)}, bf16[2048,1152]{1,0:T(8,128)(2,1)}) custom-call(bf16[2048,1152]{1,0:T(8,128)(2,1)} %bitcast.41, bf16[2048,1152]{1,0:T(8,128)(2,1)} %get-tuple-element.63.ffn_ref, bf16[2048,1152]{1,0:T(8,128)(2,1)} %get-tuple-element.64.two_ref, ...), custom_call_target="tpu_custom_call" | custom-call | flops 159499993088 | tf_op jit(solution)/shard_map/ffn_backward/pallas_call | solution.py:446
  434.9 0.7 copy-done
  436.1 22.0 %middle_back.1 = (bf16[2048,1152]{1,0:T(8,128)(2,1)}, bf16[2048,1152]{1,0:T(8,128)(2,1)}, bf16[2048,256]{1,0:T(8,128)(2,1)S(1)}, f32[2048,1]{1,0:T(8,128)S(1)}, ...) custom-call(bf16[2048,1152]{1,0:T(8,128)(2,1)} %bitcast.45, bf16[2048,1152]{1,0:T(8,128)(2,1)} %get-tuple-element.60.attn_ref, ...), custom_call_target="tpu_custom_call" | custom-call | flops 20899999744 | tf_op jit(solution)/shard_map/middle_back/pallas_call | solution.py:507
  458.2 1.0 copy-done.2
  459.1 1.0 copy-done.3
  460.2 0.8 copy-done.4
  461.6 85.9 %attention_back.1 = (bf16[2048,1024]{1,0:T(8,128)(2,1)}, bf16[2048,512]{1,0:T(8,128)(2,1)}, bf16[2,1,512,512]{3,2,1,0:T(8,128)(2,1)}, f32[1,256]{1,0:T(1,128)}, bf16[1152,512]{1,0:T(8,128)(2,1)}) custom-call(bf16[2048,256]{1,0:T(8,128)(2,1)} %get-tuple-element.71.q_ref, bf16[2048,256]{1,0:T(8,128)(2,1)} %copy-done.2, ...), custom_call_target="tpu_custom_call" | custom-call | flops 88000004096 | tf_op jit(solution)/shard_map/attention_back/pallas_call | solution.py:1155
  547.5 89.6 %key_back.1 = (bf16[2048,1152]{1,0:T(8,128)(2,1)}, f32[144,640]{1,0:T(8,128)}, f32[144,512]{1,0:T(8,128)}) custom-call(bf16[2048,512]{1,0:T(8,128)(2,1)} %get-tuple-element.79.dkv_ref, f32[2048,256]{1,0:T(8,128)} %get-tuple-element.80.hat_ref, f32[2048,1]{1,0:T(8,128)} %get-tuple-element.81.inv_ref, f32[1024,128]{1,0:T(8,128)} %get-tuple-element.156.cos_ref, ...), custom_call_target="tpu_custom_call" | custom-call | flops 82500001792 | tf_op jit(solution)/shard_map/key_back/pallas_call | solution.py:1401
  637.1 1.5 slice_reduce_fusion.6
  638.6 2.1 slice_reduce_fusion.2
  640.7 1.7 fusion.13
  642.4 1.7 slice_bitcast_fusion.3
  644.1 7.0 %convert_add_fusion = f32[2048,1152]{1,0:T(8,128)} fusion(bf16[2048,1152]{1,0:T(8,128)(2,1)} %get-tuple-element.89, bf16[2048,1152]{1,0:T(8,128)(2,1)S(1)} %bitcast.35), kind=kLoop, calls=%fused_computation | loop fusion | flops 7077888 | bytes 18874368 | tf_op jit(solution)/shard_map/add | solution.py:1497
  651.1 3.1 convert_bitcast_fusion
  (51 shorter events, 8.2 us)
Async XLA Ops:
  7.2 155.9 %all-gather.3.cloned.1.call-start = ((), (), s32[]{:S(2)}) async-start(), calls=%async_computation.1 | async-start | bytes 16588800 | tf_op jit(solution)/shard_map/all_gather | solution.py:1470
  14.3 20.3 %copy-start.6 = (bf16[1728,144]{0,1:T(8,128)(2,1)S(1)}, bf16[1728,144]{0,1:T(8,128)(2,1)}, u32[]{:S(2)}) copy-start(bf16[1728,144]{0,1:T(8,128)(2,1)} %param.25) | copy-start | bytes 1492996
  14.3 20.3 %copy-start.7 = (bf16[144,1728]{1,0:T(8,128)(2,1)S(1)}, bf16[144,1728]{1,0:T(8,128)(2,1)}, u32[]{:S(2)}) copy-start(bf16[144,1728]{1,0:T(8,128)(2,1)} %param.24) | copy-start | bytes 1492996
  14.3 20.3 %copy-start.8 = (bf16[144,1728]{1,0:T(8,128)(2,1)S(1)}, bf16[144,1728]{1,0:T(8,128)(2,1)}, u32[]{:S(2)}) copy-start(bf16[144,1728]{1,0:T(8,128)(2,1)} %param.23) | copy-start | bytes 1492996
  34.6 6.3 copy-start.9
  36.9 253.6 %all-gather.5.cloned.1.call-start = ((), (), s32[]{:S(2)}) async-start(), calls=%async_computation.2 | async-start | bytes 2654208 | tf_op jit(solution)/shard_map/all_gather | solution.py:1482
  162.4 488.7 %reduce-scatter.2.cloned.1.call-start = ((), (), s32[]{:S(2)}) async-start(), calls=%async_computation.3 | async-start | bytes 13934592 | tf_op jit(solution)/shard_map/reduce_scatter | solution.py:1487
  434.9 0.8 copy-start
  434.9 1.2 copy-start.1
  458.2 1.0 copy-start.2
  459.1 1.0 copy-start.3
  460.2 0.8 copy-start.4
  461.0 0.6 copy-start.5
  547.5 96.6 %slice-start = ((s8[4718592]{0:T(1024)(128)(4,1)}), s8[4194304]{0:T(1024)(128)(4,1)S(1)}, s32[]{:S(2)}) async-start(s8[4718592]{0:T(1024)(128)(4,1)} %bitcast.34), calls=%async_computation.4 | async-start | bytes 8388608
  547.5 96.6 %slice-start.1 = ((s8[4718592]{0:T(1024)(128)(4,1)}), s8[524288]{0:T(1024)(128)(4,1)S(1)}, s32[]{:S(2)}) async-start(s8[4718592]{0:T(1024)(128)(4,1)} %bitcast.34), calls=%async_computation.5 | async-start | bytes 1048576
Sparse Core Ops, SparseCore 0:
  37.0 94.7 all-gather.2
  162.6 27.6 all-gather.4
  435.0 104.8 reduce-scatter.1

commit v12 on v11

--- a/solution.py
+++ b/solution.py
@@ -203,9 +203,8 @@
     return value, slope
 
 
-def column_parts(cols):
-    middle = -(-cols // 256) * 128
-    return [(0, middle), (middle, cols)] if middle < cols else [(0, cols)]
+def column_parts(cols, step):
+    return [(a, min(a + step, cols)) for a in range(0, cols, step)]
 
 
 def middle_of(x, attn, gain_post_attn):
@@ -252,7 +251,7 @@
         for copy in copies[1:]:
             copy.wait()
 
-    for a, b in column_parts(hidden):
+    for a, b in column_parts(hidden, 896):
         gate = dot(two, wg_ref[:, a:b])
         up = dot(two, wu_ref[:, a:b])
         gate_ref[:, a:b] = gate.astype(BF16)
@@ -276,9 +275,11 @@
     @pl.when(i == tiles - 1)
     def _():
         last = tiles * per
-        for j in range(per):
-            line.pair(last - per + j)
-        for c in range(max(0, last - 2 * per), last):
+        for c in range(max(0, last - 2 * per), last - per):
+            line.total(c)
+        for c in range(last - per, last):
+            line.pair(c)
+        for c in range(last - per, last):
             line.total(c)
         for c in range(last):
             line.retire(c)
@@ -360,7 +361,17 @@
     dgain_ref[...] += d_gain[None]
     d_ffn = d_ffn.astype(BF16)
     part = None
-    for a, b in column_parts(hidden):
+
+    def handle(j):
+        @pl.when(i >= 1)
+        def _():
+            line.pair((i - 1) * per + j)
+
+        @pl.when(i >= 2)
+        def _():
+            line.total((i - 2) * per + j)
+
+    for a, b in column_parts(hidden, 512):
         d_hidden = dot(d_ffn, wd_ref[:, a:b])
         up = up_ref[:, a:b].astype(F32)
         value, slope = gelu_parts(gate_ref[:, a:b].astype(F32))
@@ -371,14 +382,11 @@
         keep_u[:, a:b] = d_up
         more = dot(d_gate, wg_ref[:, a:b], NT) + dot(d_up, wu_ref[:, a:b], NT)
         part = more if part is None else part + more
+        if a == 0:
+            handle(0)
     for j in range(per):
         line.put(i * per + j, part[j * chunk : (j + 1) * chunk].astype(BF16))
 
-    @pl.when(i >= 1)
-    def _():
-        for j in range(per):
-            line.pair((i - 1) * per + j)
-
     @pl.when(i == 0)
     def _():
         for acc in (acc_g, acc_u, acc_d):
@@ -386,12 +394,9 @@
 
     acc_g[...] += dot(two_ref[...], keep_g[...], TN)
     acc_u[...] += dot(two_ref[...], keep_u[...], TN)
+    for j in range(1, per):
+        handle(j)
     acc_d[...] += dot(d_ffn, keep_h[...], TN)
-
-    @pl.when(i >= 2)
-    def _():
-        for j in range(per):
-            line.total((i - 2) * per + j)
 
     @pl.when(i >= 3)
     def _():
@@ -400,33 +405,35 @@
 
     @pl.when(i == tiles - 1)
     def _():
-        for j in range(per):
-            line.pair(last - per + j)
         step = stage.shape[1]
         count = acc_g.shape[0] // step
 
-        def piece(acc, out, k, at):
-            @pl.when(k >= 2)
-            def _():
-                pltpu.make_async_copy(stage.at[at], out.at[pl.ds(0, step)], stage_sem.at[at]).wait()
-            rows = pl.ds(pl.multiple_of(k * step, step), step)
-            stage[at] = acc[rows, :].astype(BF16)
-            pltpu.make_async_copy(stage.at[at], out.at[rows], stage_sem.at[at]).start()
-
-        for acc, out in ((acc_g, grad_ref.at[0]), (acc_u, grad_ref.at[1]), (acc_d, grad_ref.at[2])):
+        def write(acc, out):
             def pieces(k, _):
-                piece(acc, out, k, lax.rem(k, 2))
+                at = lax.rem(k, 2)
+                rows = pl.ds(pl.multiple_of(k * step, step), step)
+
+                @pl.when(k >= 2)
+                def _():
+                    pltpu.make_async_copy(stage.at[at], out.at[pl.ds(0, step)], stage_sem.at[at]).wait()
+                stage[at] = acc[rows, :].astype(BF16)
+                pltpu.make_async_copy(stage.at[at], out.at[rows], stage_sem.at[at]).start()
                 return 0
 
             lax.fori_loop(0, count, pieces, 0)
             for at in range(2):
                 pltpu.make_async_copy(stage.at[at], out.at[pl.ds(0, step)], stage_sem.at[at]).wait()
-            if acc is acc_g:
-                for c in range(max(0, last - 2 * per), last - per):
-                    line.total(c)
-            if acc is acc_u:
-                for c in range(last - per, last):
-                    line.total(c)
+
+        for c in range(max(0, last - 2 * per), last - per):
+            line.total(c)
+        write(acc_g, grad_ref.at[0])
+        line.pair(last - per)
+        write(acc_u, grad_ref.at[1])
+        for c in range(last - per + 1, last):
+            line.pair(c)
+            line.total(c - 1)
+        write(acc_d, grad_ref.at[2])
+        line.total(last - 1)
         for c in range(max(0, last - 3 * per), last):
             line.retire(c)
         line.finish()

time: 670 us -> 662 us (0.988)
  Pallas kernels: 607 us -> 600 us
    pallas_call x1, Pallas kernels: 144 us -> 136 us  [ffn_backward(): pl.pallas_call(functools.partial(ffn_backward_kernel, tiles, tile, chunk,...]
  transfers between devices with their start and end apart: 3 -> 3, of which waited for: 0 -> 0; matrix products, arithmetic and copies ran while one was open for 3% -> 4% of each run, Pallas kernels for 67% -> 68%
where the time goes in v12:
time: 662 us; the launch traced here: 654 us
  Pallas kernels  600 us (91%)
  local copies, waits for them, and re-layouts  22 us (3%)
  other arithmetic  18.1 us (3%)
  between operations  14.1 us (2%)
    pallas_call x1, Pallas kernels, ffn_backward(): pl.pallas_call(functools.partial(ffn_backward_kernel, tiles, tile, chunk,...  136 us
    pallas_call x1, Pallas kernels, ffn_forward(): pl.pallas_call(functools.partial(ffn_forward_kernel, tiles, tile, chunk,...  127 us
    pallas_call x1, Pallas kernels, attention(): pl.pallas_call(functools.partial(attention_kernel, groups, size), out_sha...  117 us
    pallas_call x1, Pallas kernels, key_back(): pl.pallas_call(functools.partial(key_back_kernel, tiles, tile, chunk, own...  91.4 us
    pallas_call x1, Pallas kernels, attention_back(): pl.pallas_call(functools.partial(attention_back_kernel, groups, size), ou...  85.7 us
    pallas_call x1, Pallas kernels, middle_back(): pl.pallas_call(middle_back_kernel, grid=(rows // tile,), out_shape=(jax.S...  22.1 us
    pallas_call x1, Pallas kernels, first_gather(): pl.pallas_call(first_gather_kernel, out_shape=(jax.ShapeDtypeStruct((devi...  20.2 us
  transfers between devices with their start and end apart: 3, of which 0 were waited for; matrix products, arithmetic and copies ran while one was open for 4% of the time, Pallas kernels for 68%

profile of v12, /device:TPU:0, one launch (start us, length us, event | category | flops | bytes accessed | tf_op | source)
XLA Modules:
  0.0 653.8 jit_solution(16959805934617812811)
XLA Ops:
  11.4 1.3 reshape_reshape.3.i_ref
  12.7 1.7 fusion.11.a_ref
  14.3 20.2 %first_gather.1 = (bf16[8,144,896]{2,1,0:T(8,128)(2,1)}, bf16[144,1024]{1,0:T(8,128)(2,1)}, bf16[144,1024]{1,0:T(8,128)(2,1)}, s32[8,16,128]{2,1,0:T(8,128)}) custom-call(bf16[144,896]{1,0:T(8,128)(2,1)} %fusion.11.a_ref, bf16[144,256]{1,0:T(8,128)(2,1)} %b_ref.1, bf16[144,256]{1,0:T(8,128)(2,1)} %bitcast.48, s32[16,128]{1,0:T(8,128)} %reshape_reshape.3.i_ref), custom_call_target="tpu_custom_call" | custom-call | flops 22000001024 | tf_op jit(solution)/shard_map/first_gather/pallas_call | solution.py:737
  34.6 2.2 fusion.6
  36.9 1.0 slice_convert_fusion
  38.0 0.8 copy.55.gain_ref
  41.0 1.3 copy.56.qs_ref
  42.3 3.1 multiply_sine_fusion
  45.4 117.0 %attention.1 = (bf16[2048,256]{1,0:T(8,128)(2,1)}, f32[2048,256]{1,0:T(8,128)}, f32[2048,1]{1,0:T(8,128)}, f32[2048,256]{1,0:T(8,128)}, f32[2048,1]{1,0:T(8,128)...) custom-call(bf16[2048,1152]{1,0:T(8,128)(2,1)} %bitcast.43, ...), custom_call_target="tpu_custom_call" | custom-call | flops 121000001536 | tf_op jit(solution)/shard_map/attention/pallas_call | solution.py:936
  163.1 127.4 %ffn_forward.1 = (bf16[2048,1152]{1,0:T(8,128)(2,1)}, bf16[2048,1152]{1,0:T(8,128)(2,1)}, bf16[2048,1728]{1,0:T(8,128)(2,1)}, bf16[2048,1728]{1,0:T(8,128)(2,1)}, bf16[2048,1152]{1,0:T(8,128)(2,1)}) custom-call(bf16[2048,1152]{1,0:T(8,128)(2,1)} %bitcast.44, bf16[2048,1024]{1,0:T(8,128)(2,1)} %get-tuple-element.58.h_ref, f32[8,1152]{1,0:T(8,128)} %copy.55.gain_ref, ...), custom_call_target="tpu_custom_call" | custom-call | flops 153999998976 | tf_op jit(solution)/shard_map/ffn_forward/pallas_call | solution.py:311
  290.5 135.7 %ffn_backward.1 = (f32[1,1152]{1,0:T(1,128)}, bf16[3,1152,1728]{2,1,0:T(8,128)(2,1)}, bf16[2048,1152]{1,0:T(8,128)(2,1)}) custom-call(bf16[2048,1152]{1,0:T(8,128)(2,1)} %bitcast.41, bf16[2048,1152]{1,0:T(8,128)(2,1)} %get-tuple-element.63.ffn_ref, bf16[2048,1152]{1,0:T(8,128)(2,1)} %get-tuple-element.64.two_ref, ...), custom_call_target="tpu_custom_call" | custom-call | flops 159499993088 | tf_op jit(solution)/shard_map/ffn_backward/pallas_call | solution.py:453
  426.2 0.7 copy-done
  427.4 22.1 %middle_back.1 = (bf16[2048,1152]{1,0:T(8,128)(2,1)}, bf16[2048,1152]{1,0:T(8,128)(2,1)}, bf16[2048,256]{1,0:T(8,128)(2,1)S(1)}, f32[2048,1]{1,0:T(8,128)S(1)}, ...) custom-call(bf16[2048,1152]{1,0:T(8,128)(2,1)} %bitcast.45, bf16[2048,1152]{1,0:T(8,128)(2,1)} %get-tuple-element.60.attn_ref, ...), custom_call_target="tpu_custom_call" | custom-call | flops 20899999744 | tf_op jit(solution)/shard_map/middle_back/pallas_call | solution.py:514
  449.5 1.0 copy-done.2
  450.5 1.0 copy-done.3
  451.5 0.8 copy-done.4
  452.9 85.7 %attention_back.1 = (bf16[2048,1024]{1,0:T(8,128)(2,1)}, bf16[2048,512]{1,0:T(8,128)(2,1)}, bf16[2,1,512,512]{3,2,1,0:T(8,128)(2,1)}, f32[1,256]{1,0:T(1,128)}, bf16[1152,512]{1,0:T(8,128)(2,1)}) custom-call(bf16[2048,256]{1,0:T(8,128)(2,1)} %get-tuple-element.71.q_ref, bf16[2048,256]{1,0:T(8,128)(2,1)} %copy-done.2, ...), custom_call_target="tpu_custom_call" | custom-call | flops 88000004096 | tf_op jit(solution)/shard_map/attention_back/pallas_call | solution.py:1162
  538.7 91.4 %key_back.1 = (bf16[2048,1152]{1,0:T(8,128)(2,1)}, f32[144,640]{1,0:T(8,128)}, f32[144,512]{1,0:T(8,128)}) custom-call(bf16[2048,512]{1,0:T(8,128)(2,1)} %get-tuple-element.79.dkv_ref, f32[2048,256]{1,0:T(8,128)} %get-tuple-element.80.hat_ref, f32[2048,1]{1,0:T(8,128)} %get-tuple-element.81.inv_ref, f32[1024,128]{1,0:T(8,128)} %get-tuple-element.156.cos_ref, ...), custom_call_target="tpu_custom_call" | custom-call | flops 82500001792 | tf_op jit(solution)/shard_map/key_back/pallas_call | solution.py:1408
  630.1 1.5 slice_reduce_fusion.6
  631.6 2.1 slice_reduce_fusion.2
  633.7 1.7 fusion.13
  635.4 1.7 slice_bitcast_fusion.3
  637.1 7.0 %convert_add_fusion = f32[2048,1152]{1,0:T(8,128)} fusion(bf16[2048,1152]{1,0:T(8,128)(2,1)} %get-tuple-element.89, bf16[2048,1152]{1,0:T(8,128)(2,1)S(1)} %bitcast.35), kind=kLoop, calls=%fused_computation | loop fusion | flops 7077888 | bytes 18874368 | tf_op jit(solution)/shard_map/add | solution.py:1504
  644.1 3.1 convert_bitcast_fusion
  (51 shorter events, 8.2 us)
Async XLA Ops:
  7.2 155.9 %all-gather.3.cloned.1.call-start = ((), (), s32[]{:S(2)}) async-start(), calls=%async_computation.1 | async-start | bytes 16588800 | tf_op jit(solution)/shard_map/all_gather | solution.py:1477
  14.3 20.3 %copy-start.6 = (bf16[1728,144]{0,1:T(8,128)(2,1)S(1)}, bf16[1728,144]{0,1:T(8,128)(2,1)}, u32[]{:S(2)}) copy-start(bf16[1728,144]{0,1:T(8,128)(2,1)} %param.25) | copy-start | bytes 1492996
  14.3 20.3 %copy-start.7 = (bf16[144,1728]{1,0:T(8,128)(2,1)S(1)}, bf16[144,1728]{1,0:T(8,128)(2,1)}, u32[]{:S(2)}) copy-start(bf16[144,1728]{1,0:T(8,128)(2,1)} %param.24) | copy-start | bytes 1492996
  14.3 20.3 %copy-start.8 = (bf16[144,1728]{1,0:T(8,128)(2,1)S(1)}, bf16[144,1728]{1,0:T(8,128)(2,1)}, u32[]{:S(2)}) copy-start(bf16[144,1728]{1,0:T(8,128)(2,1)} %param.23) | copy-start | bytes 1492996
  34.6 6.3 copy-start.9
  36.9 253.6 %all-gather.5.cloned.1.call-start = ((), (), s32[]{:S(2)}) async-start(), calls=%async_computation.2 | async-start | bytes 2654208 | tf_op jit(solution)/shard_map/all_gather | solution.py:1489
  162.4 481.7 %reduce-scatter.2.cloned.1.call-start = ((), (), s32[]{:S(2)}) async-start(), calls=%async_computation.3 | async-start | bytes 13934592 | tf_op jit(solution)/shard_map/reduce_scatter | solution.py:1494
  426.2 0.8 copy-start
  426.2 1.2 copy-start.1
  449.5 1.0 copy-start.2
  450.5 1.0 copy-start.3
  451.5 0.8 copy-start.4
  452.3 0.6 copy-start.5
  538.6 98.5 %slice-start = ((s8[4718592]{0:T(1024)(128)(4,1)}), s8[4194304]{0:T(1024)(128)(4,1)S(1)}, s32[]{:S(2)}) async-start(s8[4718592]{0:T(1024)(128)(4,1)} %bitcast.34), calls=%async_computation.4 | async-start | bytes 8388608
  538.7 98.4 %slice-start.1 = ((s8[4718592]{0:T(1024)(128)(4,1)}), s8[524288]{0:T(1024)(128)(4,1)S(1)}, s32[]{:S(2)}) async-start(s8[4718592]{0:T(1024)(128)(4,1)} %bitcast.34), calls=%async_computation.5 | async-start | bytes 1048576
Sparse Core Ops, SparseCore 0:
  37.0 94.7 all-gather.2
  162.6 27.6 all-gather.4
  426.4 104.7 reduce-scatter.1

commit v13 on v12

--- a/solution.py
+++ b/solution.py
@@ -1306,15 +1306,17 @@
     def _():
         part[pl.ds(pl.multiple_of(i * tile, tile), tile), :] = dot(dq_ref[...], wq_ref[...], NT)
 
-    @pl.when((i >= 1) & (i <= tiles))
-    def _():
-        for j in range(per):
+    def handle(j):
+        @pl.when((i >= 1) & (i <= tiles))
+        def _():
             line.total((i - 1) * per + j)
 
-    @pl.when(i < tiles)
-    def _():
-        for j in range(per):
+        @pl.when(i < tiles)
+        def _():
             line.pair(i * per + j)
+
+    for j in range(per // 2):
+        handle(j)
 
     @pl.when(i == 1)
     def _():
@@ -1347,6 +1349,9 @@
         acc_in[...] += d_gain[None]
         dx_ref[...] = d_part.astype(BF16)
         acc[...] += dot((hat * (1.0 + gain)).astype(BF16), d_raw, TN)
+
+    for j in range(per // 2, per):
+        handle(j)
 
     @pl.when(i == tiles + 1)
     def _():
@@ -1381,7 +1386,7 @@
              grad_qo, rest, own_rows, ident):
     rows, width = x.shape
     head = hat.shape[1]
-    tile, chunk = 256, 128
+    tile, chunk = 256, 64
     tiles = rows // tile
     count = rows // chunk + 1
     dma = pltpu.SemaphoreType.DMA((count,))

time: 662 us -> 650 us (0.982)
  Pallas kernels: 600 us -> 588 us
    pallas_call x1, Pallas kernels: 91.4 us -> 79.5 us  [key_back(): pl.pallas_call(functools.partial(key_back_kernel, tiles, tile, chunk, own...]
  transfers between devices with their start and end apart: 3 -> 3, of which waited for: 0 -> 0; matrix products, arithmetic and copies ran while one was open for 4% -> 4% of each run, Pallas kernels for 68% -> 67%
where the time goes in v13:
time: 650 us; the launch traced here: 642 us
  Pallas kernels  588 us (90%)
  local copies, waits for them, and re-layouts  22 us (3%)
  other arithmetic  18.1 us (3%)
  between operations  14.1 us (2%)
    pallas_call x1, Pallas kernels, ffn_backward(): pl.pallas_call(functools.partial(ffn_backward_kernel, tiles, tile, chunk,...  136 us
    pallas_call x1, Pallas kernels, ffn_forward(): pl.pallas_call(functools.partial(ffn_forward_kernel, tiles, tile, chunk,...  127 us
    pallas_call x1, Pallas kernels, attention(): pl.pallas_call(functools.partial(attention_kernel, groups, size), out_sha...  117 us
    pallas_call x1, Pallas kernels, attention_back(): pl.pallas_call(functools.partial(attention_back_kernel, groups, size), ou...  85.9 us
    pallas_call x1, Pallas kernels, key_back(): pl.pallas_call(functools.partial(key_back_kernel, tiles, tile, chunk, own...  79.5 us
    pallas_call x1, Pallas kernels, middle_back(): pl.pallas_call(middle_back_kernel, grid=(rows // tile,), out_shape=(jax.S...  22.1 us
    pallas_call x1, Pallas kernels, first_gather(): pl.pallas_call(first_gather_kernel, out_shape=(jax.ShapeDtypeStruct((devi...  20.2 us
  transfers between devices with their start and end apart: 3, of which 0 were waited for; matrix products, arithmetic and copies ran while one was open for 4% of the time, Pallas kernels for 67%

profile of v13, /device:TPU:0, one launch (start us, length us, event | category | flops | bytes accessed | tf_op | source)
XLA Modules:
  0.0 642.1 jit_solution(10719780952876179052)
XLA Ops:
  11.4 1.3 reshape_reshape.3.i_ref
  12.7 1.7 fusion.11.a_ref
  14.3 20.2 %first_gather.1 = (bf16[8,144,896]{2,1,0:T(8,128)(2,1)}, bf16[144,1024]{1,0:T(8,128)(2,1)}, bf16[144,1024]{1,0:T(8,128)(2,1)}, s32[8,16,128]{2,1,0:T(8,128)}) custom-call(bf16[144,896]{1,0:T(8,128)(2,1)} %fusion.11.a_ref, bf16[144,256]{1,0:T(8,128)(2,1)} %b_ref.1, bf16[144,256]{1,0:T(8,128)(2,1)} %bitcast.48, s32[16,128]{1,0:T(8,128)} %reshape_reshape.3.i_ref), custom_call_target="tpu_custom_call" | custom-call | flops 22000001024 | tf_op jit(solution)/shard_map/first_gather/pallas_call | solution.py:737
  34.6 2.2 fusion.6
  36.9 1.0 slice_convert_fusion
  38.0 0.8 copy.55.gain_ref
  41.0 1.3 copy.56.qs_ref
  42.3 3.1 multiply_sine_fusion
  45.4 117.0 %attention.1 = (bf16[2048,256]{1,0:T(8,128)(2,1)}, f32[2048,256]{1,0:T(8,128)}, f32[2048,1]{1,0:T(8,128)}, f32[2048,256]{1,0:T(8,128)}, f32[2048,1]{1,0:T(8,128)...) custom-call(bf16[2048,1152]{1,0:T(8,128)(2,1)} %bitcast.43, ...), custom_call_target="tpu_custom_call" | custom-call | flops 121000001536 | tf_op jit(solution)/shard_map/attention/pallas_call | solution.py:936
  163.1 127.4 %ffn_forward.1 = (bf16[2048,1152]{1,0:T(8,128)(2,1)}, bf16[2048,1152]{1,0:T(8,128)(2,1)}, bf16[2048,1728]{1,0:T(8,128)(2,1)}, bf16[2048,1728]{1,0:T(8,128)(2,1)}, bf16[2048,1152]{1,0:T(8,128)(2,1)}) custom-call(bf16[2048,1152]{1,0:T(8,128)(2,1)} %bitcast.44, bf16[2048,1024]{1,0:T(8,128)(2,1)} %get-tuple-element.58.h_ref, f32[8,1152]{1,0:T(8,128)} %copy.55.gain_ref, ...), custom_call_target="tpu_custom_call" | custom-call | flops 153999998976 | tf_op jit(solution)/shard_map/ffn_forward/pallas_call | solution.py:311
  290.5 135.7 %ffn_backward.1 = (f32[1,1152]{1,0:T(1,128)}, bf16[3,1152,1728]{2,1,0:T(8,128)(2,1)}, bf16[2048,1152]{1,0:T(8,128)(2,1)}) custom-call(bf16[2048,1152]{1,0:T(8,128)(2,1)} %bitcast.41, bf16[2048,1152]{1,0:T(8,128)(2,1)} %get-tuple-element.63.ffn_ref, bf16[2048,1152]{1,0:T(8,128)(2,1)} %get-tuple-element.64.two_ref, ...), custom_call_target="tpu_custom_call" | custom-call | flops 159499993088 | tf_op jit(solution)/shard_map/ffn_backward/pallas_call | solution.py:453
  426.2 0.7 copy-done
  427.4 22.1 %middle_back.1 = (bf16[2048,1152]{1,0:T(8,128)(2,1)}, bf16[2048,1152]{1,0:T(8,128)(2,1)}, bf16[2048,256]{1,0:T(8,128)(2,1)S(1)}, f32[2048,1]{1,0:T(8,128)S(1)}, ...) custom-call(bf16[2048,1152]{1,0:T(8,128)(2,1)} %bitcast.45, bf16[2048,1152]{1,0:T(8,128)(2,1)} %get-tuple-element.60.attn_ref, ...), custom_call_target="tpu_custom_call" | custom-call | flops 20899999744 | tf_op jit(solution)/shard_map/middle_back/pallas_call | solution.py:514
  449.5 1.0 copy-done.2
  450.5 1.0 copy-done.3
  451.5 0.8 copy-done.4
  452.9 85.9 %attention_back.1 = (bf16[2048,1024]{1,0:T(8,128)(2,1)}, bf16[2048,512]{1,0:T(8,128)(2,1)}, bf16[2,1,512,512]{3,2,1,0:T(8,128)(2,1)}, f32[1,256]{1,0:T(1,128)}, bf16[1152,512]{1,0:T(8,128)(2,1)}) custom-call(bf16[2048,256]{1,0:T(8,128)(2,1)} %get-tuple-element.71.q_ref, bf16[2048,256]{1,0:T(8,128)(2,1)} %copy-done.2, ...), custom_call_target="tpu_custom_call" | custom-call | flops 88000004096 | tf_op jit(solution)/shard_map/attention_back/pallas_call | solution.py:1162
  538.8 79.5 %key_back.1 = (bf16[2048,1152]{1,0:T(8,128)(2,1)}, f32[144,640]{1,0:T(8,128)}, f32[144,512]{1,0:T(8,128)}) custom-call(bf16[2048,512]{1,0:T(8,128)(2,1)} %get-tuple-element.79.dkv_ref, f32[2048,256]{1,0:T(8,128)} %get-tuple-element.80.hat_ref, f32[2048,1]{1,0:T(8,128)} %get-tuple-element.81.inv_ref, f32[1024,128]{1,0:T(8,128)} %get-tuple-element.156.cos_ref, ...), custom_call_target="tpu_custom_call" | custom-call | flops 82500001792 | tf_op jit(solution)/shard_map/key_back/pallas_call | solution.py:1413
  618.4 1.5 slice_reduce_fusion.6
  619.9 2.1 slice_reduce_fusion.2
  621.9 1.7 fusion.13
  623.6 1.7 slice_bitcast_fusion.3
  625.4 7.0 %convert_add_fusion = f32[2048,1152]{1,0:T(8,128)} fusion(bf16[2048,1152]{1,0:T(8,128)(2,1)} %get-tuple-element.89, bf16[2048,1152]{1,0:T(8,128)(2,1)S(1)} %bitcast.35), kind=kLoop, calls=%fused_computation | loop fusion | flops 7077888 | bytes 18874368 | tf_op jit(solution)/shard_map/add | solution.py:1509
  632.4 3.1 convert_bitcast_fusion
  (51 shorter events, 8.2 us)
Async XLA Ops:
  7.2 155.9 %all-gather.3.cloned.1.call-start = ((), (), s32[]{:S(2)}) async-start(), calls=%async_computation.1 | async-start | bytes 16588800 | tf_op jit(solution)/shard_map/all_gather | solution.py:1482
  14.3 20.3 %copy-start.6 = (bf16[1728,144]{0,1:T(8,128)(2,1)S(1)}, bf16[1728,144]{0,1:T(8,128)(2,1)}, u32[]{:S(2)}) copy-start(bf16[1728,144]{0,1:T(8,128)(2,1)} %param.25) | copy-start | bytes 1492996
  14.3 20.3 %copy-start.7 = (bf16[144,1728]{1,0:T(8,128)(2,1)S(1)}, bf16[144,1728]{1,0:T(8,128)(2,1)}, u32[]{:S(2)}) copy-start(bf16[144,1728]{1,0:T(8,128)(2,1)} %param.24) | copy-start | bytes 1492996
  14.3 20.3 %copy-start.8 = (bf16[144,1728]{1,0:T(8,128)(2,1)S(1)}, bf16[144,1728]{1,0:T(8,128)(2,1)}, u32[]{:S(2)}) copy-start(bf16[144,1728]{1,0:T(8,128)(2,1)} %param.23) | copy-start | bytes 1492996
  34.6 6.3 copy-start.9
  36.9 253.6 %all-gather.5.cloned.1.call-start = ((), (), s32[]{:S(2)}) async-start(), calls=%async_computation.2 | async-start | bytes 2654208 | tf_op jit(solution)/shard_map/all_gather | solution.py:1494
  162.4 469.9 %reduce-scatter.2.cloned.1.call-start = ((), (), s32[]{:S(2)}) async-start(), calls=%async_computation.3 | async-start | bytes 13934592 | tf_op jit(solution)/shard_map/reduce_scatter | solution.py:1499
  426.2 0.8 copy-start
  426.2 1.2 copy-start.1
  449.5 1.0 copy-start.2
  450.5 1.0 copy-start.3
  451.5 0.8 copy-start.4
  452.3 0.6 copy-start.5
  538.8 86.6 %slice-start = ((s8[4718592]{0:T(1024)(128)(4,1)}), s8[4194304]{0:T(1024)(128)(4,1)S(1)}, s32[]{:S(2)}) async-start(s8[4718592]{0:T(1024)(128)(4,1)} %bitcast.34), calls=%async_computation.4 | async-start | bytes 8388608
  538.8 86.5 %slice-start.1 = ((s8[4718592]{0:T(1024)(128)(4,1)}), s8[524288]{0:T(1024)(128)(4,1)S(1)}, s32[]{:S(2)}) async-start(s8[4718592]{0:T(1024)(128)(4,1)} %bitcast.34), calls=%async_computation.5 | async-start | bytes 1048576
Sparse Core Ops, SparseCore 0:
  37.0 94.7 all-gather.2
  162.6 27.6 all-gather.4
  426.4 104.7 reduce-scatter.1

commit v14 on v13

--- a/solution.py
+++ b/solution.py
@@ -246,6 +246,15 @@
     two_ref[...] = two
     part = None
 
+    def handle(j):
+        @pl.when(i >= 1)
+        def _():
+            line.pair((i - 1) * per + j)
+
+        @pl.when(i >= 2)
+        def _():
+            line.total((i - 2) * per + j)
+
     @pl.when(i == 0)
     def _():
         for copy in copies[1:]:
@@ -259,18 +268,14 @@
         value, _ = gelu_parts(gate)
         more = dot((value * up).astype(BF16), wd_ref[:, a:b], NT)
         part = more if part is None else part + more
+        if a == 0:
+            for j in range(per // 2):
+                handle(j)
     for j in range(per):
         line.put(i * per + j, part[j * chunk : (j + 1) * chunk].astype(BF16))
 
-    @pl.when(i >= 1)
-    def _():
-        for j in range(per):
-            line.pair((i - 1) * per + j)
-
-    @pl.when(i >= 2)
-    def _():
-        for j in range(per):
-            line.total((i - 2) * per + j)
+    for j in range(per // 2, per):
+        handle(j)
 
     @pl.when(i == tiles - 1)
     def _():
@@ -304,7 +309,7 @@
 def ffn_forward(x, heads, gains, weights, hidden, ident):
     rows, width = x.shape
     all_heads = heads.shape[1]
-    tile, chunk = 128, 128
+    tile, chunk = 128, 64
     tiles = rows // tile
     count = rows // chunk
     wide = wide_of(hidden)
@@ -1005,7 +1010,7 @@
     tiles = 2 * groups
     group = Shared(False)
     rank, core = group.me, group.core
-    tile = min(256, size)
+    tile = min(128, size)
     per = size // tile
     line = LineGather(whole, tile, head, sems)
     z = line.z
@@ -1156,7 +1161,7 @@
     groups, length, _ = kv.shape
     size = rows // (2 * groups)
     chips = length // (4 * size)
-    parts = rows // min(256, size)
+    parts = rows // min(128, size)
     vmem = pl.BlockSpec(memory_space=pltpu.VMEM)
     dma = pltpu.SemaphoreType.DMA
     return pl.pallas_call(

time: 650 us -> 649 us (level)
  no operation moved by 1% of the time
where the time goes in v14:
time: 649 us; the launch traced here: 641 us
  Pallas kernels  587 us (90%)
  local copies, waits for them, and re-layouts  22 us (3%)
  other arithmetic  18.1 us (3%)
  between operations  14.1 us (2%)
    pallas_call x1, Pallas kernels, ffn_backward(): pl.pallas_call(functools.partial(ffn_backward_kernel, tiles, tile, chunk,...  137 us
    pallas_call x1, Pallas kernels, ffn_forward(): pl.pallas_call(functools.partial(ffn_forward_kernel, tiles, tile, chunk,...  126 us
    pallas_call x1, Pallas kernels, attention(): pl.pallas_call(functools.partial(attention_kernel, groups, size), out_sha...  117 us
    pallas_call x1, Pallas kernels, attention_back(): pl.pallas_call(functools.partial(attention_back_kernel, groups, size), ou...  85.3 us
    pallas_call x1, Pallas kernels, key_back(): pl.pallas_call(functools.partial(key_back_kernel, tiles, tile, chunk, own...  79 us
    pallas_call x1, Pallas kernels, middle_back(): pl.pallas_call(middle_back_kernel, grid=(rows // tile,), out_shape=(jax.S...  22.5 us
    pallas_call x1, Pallas kernels, first_gather(): pl.pallas_call(first_gather_kernel, out_shape=(jax.ShapeDtypeStruct((devi...  20.2 us
  transfers between devices with their start and end apart: 3, of which 0 were waited for; matrix products, arithmetic and copies ran while one was open for 4% of the time, Pallas kernels for 67%

profile of v14, /device:TPU:0, one launch (start us, length us, event | category | flops | bytes accessed | tf_op | source)
XLA Modules:
  0.0 640.9 jit_solution(9306957120851220618)
XLA Ops:
  11.4 1.3 reshape_reshape.3.i_ref
  12.7 1.7 fusion.11.a_ref
  14.3 20.2 %first_gather.1 = (bf16[8,144,896]{2,1,0:T(8,128)(2,1)}, bf16[144,1024]{1,0:T(8,128)(2,1)}, bf16[144,1024]{1,0:T(8,128)(2,1)}, s32[8,16,128]{2,1,0:T(8,128)}) custom-call(bf16[144,896]{1,0:T(8,128)(2,1)} %fusion.11.a_ref, bf16[144,256]{1,0:T(8,128)(2,1)} %b_ref.1, bf16[144,256]{1,0:T(8,128)(2,1)} %bitcast.48, s32[16,128]{1,0:T(8,128)} %reshape_reshape.3.i_ref), custom_call_target="tpu_custom_call" | custom-call | flops 22000001024 | tf_op jit(solution)/shard_map/first_gather/pallas_call | solution.py:742
  34.6 2.2 fusion.6
  36.9 1.0 slice_convert_fusion
  38.0 0.8 copy.55.gain_ref
  41.0 1.3 copy.56.qs_ref
  42.3 3.1 multiply_sine_fusion
  45.4 117.0 %attention.1 = (bf16[2048,256]{1,0:T(8,128)(2,1)}, f32[2048,256]{1,0:T(8,128)}, f32[2048,1]{1,0:T(8,128)}, f32[2048,256]{1,0:T(8,128)}, f32[2048,1]{1,0:T(8,128)...) custom-call(bf16[2048,1152]{1,0:T(8,128)(2,1)} %bitcast.43, ...), custom_call_target="tpu_custom_call" | custom-call | flops 121000001536 | tf_op jit(solution)/shard_map/attention/pallas_call | solution.py:941
  163.1 125.9 %ffn_forward.1 = (bf16[2048,1152]{1,0:T(8,128)(2,1)}, bf16[2048,1152]{1,0:T(8,128)(2,1)}, bf16[2048,1728]{1,0:T(8,128)(2,1)}, bf16[2048,1728]{1,0:T(8,128)(2,1)}, bf16[2048,1152]{1,0:T(8,128)(2,1)}) custom-call(bf16[2048,1152]{1,0:T(8,128)(2,1)} %bitcast.44, bf16[2048,1024]{1,0:T(8,128)(2,1)} %get-tuple-element.58.h_ref, f32[8,1152]{1,0:T(8,128)} %copy.55.gain_ref, ...), custom_call_target="tpu_custom_call" | custom-call | flops 153999998976 | tf_op jit(solution)/shard_map/ffn_forward/pallas_call | solution.py:316
  289.1 136.5 %ffn_backward.1 = (f32[1,1152]{1,0:T(1,128)}, bf16[3,1152,1728]{2,1,0:T(8,128)(2,1)}, bf16[2048,1152]{1,0:T(8,128)(2,1)}) custom-call(bf16[2048,1152]{1,0:T(8,128)(2,1)} %bitcast.41, bf16[2048,1152]{1,0:T(8,128)(2,1)} %get-tuple-element.63.ffn_ref, bf16[2048,1152]{1,0:T(8,128)(2,1)} %get-tuple-element.64.two_ref, ...), custom_call_target="tpu_custom_call" | custom-call | flops 159499993088 | tf_op jit(solution)/shard_map/ffn_backward/pallas_call | solution.py:458
  425.7 0.7 copy-done
  426.9 22.5 %middle_back.1 = (bf16[2048,1152]{1,0:T(8,128)(2,1)}, bf16[2048,1152]{1,0:T(8,128)(2,1)}, bf16[2048,256]{1,0:T(8,128)(2,1)S(1)}, f32[2048,1]{1,0:T(8,128)S(1)}, ...) custom-call(bf16[2048,1152]{1,0:T(8,128)(2,1)} %bitcast.45, bf16[2048,1152]{1,0:T(8,128)(2,1)} %get-tuple-element.60.attn_ref, ...), custom_call_target="tpu_custom_call" | custom-call | flops 20899999744 | tf_op jit(solution)/shard_map/middle_back/pallas_call | solution.py:519
  449.4 1.0 copy-done.2
  450.4 1.0 copy-done.3
  451.4 0.8 copy-done.4
  452.8 85.3 %attention_back.1 = (bf16[2048,1024]{1,0:T(8,128)(2,1)}, bf16[2048,512]{1,0:T(8,128)(2,1)}, bf16[2,1,512,512]{3,2,1,0:T(8,128)(2,1)}, f32[1,256]{1,0:T(1,128)}, bf16[1152,512]{1,0:T(8,128)(2,1)}) custom-call(bf16[2048,256]{1,0:T(8,128)(2,1)} %get-tuple-element.71.q_ref, bf16[2048,256]{1,0:T(8,128)(2,1)} %copy-done.2, ...), custom_call_target="tpu_custom_call" | custom-call | flops 88000004096 | tf_op jit(solution)/shard_map/attention_back/pallas_call | solution.py:1167
  538.1 79.0 %key_back.1 = (bf16[2048,1152]{1,0:T(8,128)(2,1)}, f32[144,640]{1,0:T(8,128)}, f32[144,512]{1,0:T(8,128)}) custom-call(bf16[2048,512]{1,0:T(8,128)(2,1)} %get-tuple-element.79.dkv_ref, f32[2048,256]{1,0:T(8,128)} %get-tuple-element.80.hat_ref, f32[2048,1]{1,0:T(8,128)} %get-tuple-element.81.inv_ref, f32[1024,128]{1,0:T(8,128)} %get-tuple-element.156.cos_ref, ...), custom_call_target="tpu_custom_call" | custom-call | flops 82500001792 | tf_op jit(solution)/shard_map/key_back/pallas_call | solution.py:1418
  617.1 1.5 slice_reduce_fusion.6
  618.6 2.1 slice_reduce_fusion.2
  620.7 1.7 fusion.13
  622.4 1.7 slice_bitcast_fusion.3
  624.1 7.0 %convert_add_fusion = f32[2048,1152]{1,0:T(8,128)} fusion(bf16[2048,1152]{1,0:T(8,128)(2,1)} %get-tuple-element.89, bf16[2048,1152]{1,0:T(8,128)(2,1)S(1)} %bitcast.35), kind=kLoop, calls=%fused_computation | loop fusion | flops 7077888 | bytes 18874368 | tf_op jit(solution)/shard_map/add | solution.py:1514
  631.1 3.1 convert_bitcast_fusion
  (51 shorter events, 8.2 us)
Async XLA Ops:
  7.2 155.9 %all-gather.3.cloned.1.call-start = ((), (), s32[]{:S(2)}) async-start(), calls=%async_computation.1 | async-start | bytes 16588800 | tf_op jit(solution)/shard_map/all_gather | solution.py:1487
  14.3 20.3 %copy-start.6 = (bf16[1728,144]{0,1:T(8,128)(2,1)S(1)}, bf16[1728,144]{0,1:T(8,128)(2,1)}, u32[]{:S(2)}) copy-start(bf16[1728,144]{0,1:T(8,128)(2,1)} %param.25) | copy-start | bytes 1492996
  14.3 20.3 %copy-start.7 = (bf16[144,1728]{1,0:T(8,128)(2,1)S(1)}, bf16[144,1728]{1,0:T(8,128)(2,1)}, u32[]{:S(2)}) copy-start(bf16[144,1728]{1,0:T(8,128)(2,1)} %param.24) | copy-start | bytes 1492996
  14.3 20.3 %copy-start.8 = (bf16[144,1728]{1,0:T(8,128)(2,1)S(1)}, bf16[144,1728]{1,0:T(8,128)(2,1)}, u32[]{:S(2)}) copy-start(bf16[144,1728]{1,0:T(8,128)(2,1)} %param.23) | copy-start | bytes 1492996
  34.6 6.3 copy-start.9
  36.9 252.2 %all-gather.5.cloned.1.call-start = ((), (), s32[]{:S(2)}) async-start(), calls=%async_computation.2 | async-start | bytes 2654208 | tf_op jit(solution)/shard_map/all_gather | solution.py:1499
  162.4 468.7 %reduce-scatter.2.cloned.1.call-start = ((), (), s32[]{:S(2)}) async-start(), calls=%async_computation.3 | async-start | bytes 13934592 | tf_op jit(solution)/shard_map/reduce_scatter | solution.py:1504
  425.6 0.8 copy-start
  425.6 1.2 copy-start.1
  449.4 1.0 copy-start.2
  450.4 1.0 copy-start.3
  451.4 0.8 copy-start.4
  452.2 0.6 copy-start.5
  538.1 86.0 %slice-start = ((s8[4718592]{0:T(1024)(128)(4,1)}), s8[4194304]{0:T(1024)(128)(4,1)S(1)}, s32[]{:S(2)}) async-start(s8[4718592]{0:T(1024)(128)(4,1)} %bitcast.34), calls=%async_computation.4 | async-start | bytes 8388608
  538.1 86.0 %slice-start.1 = ((s8[4718592]{0:T(1024)(128)(4,1)}), s8[524288]{0:T(1024)(128)(4,1)S(1)}, s32[]{:S(2)}) async-start(s8[4718592]{0:T(1024)(128)(4,1)} %bitcast.34), calls=%async_computation.5 | async-start | bytes 1048576
Sparse Core Ops, SparseCore 0:
  37.0 94.7 all-gather.2
  162.6 27.5 all-gather.4
  425.8 103.6 reduce-scatter.1
